TPU v7x, 32 devices: a whole 2x2x4 slice. The times are simulated.
32 devices in a mesh: section: 2 (over core), ctx: 4 (over z), fsdp: 4 (over y, x).
Axes of the slice: x: 2, y: 2, z: 4, core: 2. Of those that a mesh axis runs over, the one named last changes fastest.
Arguments:
- tokens: bfloat16 [2, 8, 1024, 1024], P(None, 'fsdp', 'ctx'), as said below
- segment_ids: int32 [2, 8, 1024], P(None, 'fsdp', 'ctx'), may hold values from 0 to 1023, as said below
- valid_mask: int32 [2, 8, 1024], P(None, 'fsdp', 'ctx'), may hold values from 0 to 1, as said below
- cotangent: bfloat16 [2, 8, 1024, 1024], P(None, 'fsdp', 'ctx'), may hold values from -6 to 6
- qkv_weight: bfloat16 [2, 3, 1024, 1024], P('section', None, ('ctx', 'fsdp')), may hold values from -0.1875 to 0.1875
- out_proj: bfloat16 [2, 1024, 1024], P('section', ('ctx', 'fsdp')), may hold values from -0.75 to 0.75
- in_weight: bfloat16 [2, 1024, 4096], P('section', ('ctx', 'fsdp')), may hold values from -0.1875 to 0.1875
- out_weight: bfloat16 [2, 4096, 1024], P('section', ('ctx', 'fsdp')), may hold values from -0.09375 to 0.09375
- norm_gain: float32 [2, 2, 1024], P('section'), may hold values from 0.5 to 1.5
- norm_shift: float32 [2, 2, 1024], P('section'), may hold values from -4 to 4
- proj_bias: float32 [2, 4, 1024], P('section'), may hold values from -4 to 4
- ff_bias: float32 [2, 4096], P('section'), may hold values from -6 to 6
Outputs:
- activations: bfloat16 [2, 2, 8, 1024, 1024], P('section', None, 'fsdp', 'ctx')
- input_grads: bfloat16 [2, 2, 8, 1024, 1024], P('section', None, 'fsdp', 'ctx')
- grad_qkv: float32 [2, 3, 1024, 1024], P('section', None, ('ctx', 'fsdp'))
- grad_out_proj: float32 [2, 1024, 1024], P('section', ('ctx', 'fsdp'))
- grad_in: float32 [2, 1024, 4096], P('section', ('ctx', 'fsdp'))
- grad_out: float32 [2, 4096, 1024], P('section', ('ctx', 'fsdp'))
- grad_gain: float32 [2, 2, 1024], P('section', None, ('ctx', 'fsdp'))
- grad_shift: float32 [2, 2, 1024], P('section', None, ('ctx', 'fsdp'))
- grad_proj_bias: float32 [2, 4, 1024], P('section', None, ('ctx', 'fsdp'))
- grad_ff_bias: float32 [2, 4096], P('section', ('ctx', 'fsdp'))
- rms: float32 [2, 4], P('section')
Inputs may be any that keep to these rules, and one draw needn't show every extreme that they name: `tokens`: activations of order one. `segment_ids`: ids never fall along a sequence; a document is a run of equal ids; the last position of each sequence has 1023. Among the 4 sequences of one fsdp index one is a single document without padding. `valid_mask`: each sequence's real tokens are a leading run of at least 3 / 8 of its positions.
All inputs are finite; a program needn't handle non-finite values.
Results may differ from a plain program's by a relative error of at most 0.017.
Values may be sent and summed in bfloat16 or wider, within the bound.
No kernel may reach another device: no remote copies, remote signals or barrier semaphores. Data moves between devices by JAX's collectives and lax.ppermute only.
A program may use at most 384 MiB of HBM per device.

v0:
```python
import math

import jax
import jax.numpy as jnp
from jax import lax
from jax.sharding import PartitionSpec as P

HEADS = 16


norm_eps = 1e-05
masked_score = -1e30


def from_behind(value, axis, steps):
    count = lax.axis_size(axis)
    first, last = (max(0, -steps), min(count, count - steps))
    return lax.ppermute(value, axis, [(source, source + steps) for source in range(first, last)])


def normalize(residual, gain_row, shift_row):
    average = jnp.mean(residual, axis=-1, keepdims=True)
    centred = residual - average
    spread = jnp.mean(centred * centred, axis=-1, keepdims=True)
    return centred * lax.rsqrt(spread + norm_eps) * gain_row + shift_row


def exact_gelu(values):
    return jax.nn.gelu(values, approximate=False)


def project(operand_array, matrix_value):
    return lax.dot_general(
        operand_array,
        matrix_value,
        (((operand_array.ndim - 1,), (0,)), ((), ())),
        preferred_element_type=jnp.float32,
    )


def project_back(operand_array, matrix_value):
    return lax.dot_general(
        operand_array,
        matrix_value,
        (((operand_array.ndim - 1,), (1,)), ((), ())),
        preferred_element_type=jnp.float32,
    )


def token_outer(inputs, grads):
    return lax.dot_general(
        inputs, grads, (((0, 1), (0, 1)), ((), ())), preferred_element_type=jnp.float32
    )


def column_total(grads):
    return jnp.sum(grads.astype(jnp.float32), axis=(0, 1))


def head_block(array, start, group_span, head_dim):
    sliced = lax.dynamic_slice_in_dim(array, start, group_span, 2)
    return sliced.reshape(array.shape[0], array.shape[1], group_span // head_dim, head_dim)


def join_heads(stacked):
    moved = jnp.moveaxis(stacked, 0, 2)
    return moved.reshape(moved.shape[0], moved.shape[1], moved.shape[2] * moved.shape[3])


def attend_forward(queries, full_kv, allowed, head_dim, group_span):
    embedding_width = queries.shape[2]
    score_scale = head_dim ** (-0.5)

    def one_group(group_index):
        start = group_index * group_span
        query_block = head_block(queries, start, group_span, head_dim)
        key_block = head_block(full_kv, start, group_span, head_dim)
        value_block = head_block(full_kv, embedding_width + start, group_span, head_dim)
        scores = (
            jnp.einsum(
                "sqhd,skhd->shqk", query_block, key_block, preferred_element_type=jnp.float32
            )
            * score_scale
        )
        scores = jnp.where(allowed[:, None], scores, masked_score)
        row_top = jnp.max(scores, axis=-1, keepdims=True)
        expo = jnp.exp(scores - row_top)
        expo_total = jnp.sum(expo, axis=-1, keepdims=True)
        probs = (expo / expo_total).astype(jnp.bfloat16)
        mixed = jnp.einsum(
            "shqk,skhd->sqhd", probs, value_block, preferred_element_type=jnp.float32
        )
        return (
            mixed.reshape(mixed.shape[0], mixed.shape[1], group_span),
            (row_top + jnp.log(expo_total))[..., 0],
        )

    stacked, log_total = lax.map(one_group, jnp.arange(embedding_width // group_span))
    return (join_heads(stacked), log_total)


def attend_backward(queries, full_kv, allowed, log_total, grad_mixed, head_dim, group_span):
    embedding_width = queries.shape[2]
    score_scale = head_dim ** (-0.5)

    def one_group(group_index):
        start = group_index * group_span
        query_block = head_block(queries, start, group_span, head_dim)
        key_block = head_block(full_kv, start, group_span, head_dim)
        value_block = head_block(full_kv, embedding_width + start, group_span, head_dim)
        grad_block = head_block(grad_mixed, start, group_span, head_dim)
        group_total = lax.dynamic_index_in_dim(log_total, group_index, 0, False)
        scores = (
            jnp.einsum(
                "sqhd,skhd->shqk", query_block, key_block, preferred_element_type=jnp.float32
            )
            * score_scale
        )
        scores = jnp.where(allowed[:, None], scores, masked_score)
        probs = jnp.exp(scores - group_total[..., None])
        grad_probs = jnp.einsum(
            "sqhd,skhd->shqk", grad_block, value_block, preferred_element_type=jnp.float32
        )
        inner = jnp.sum(probs * grad_probs, axis=-1, keepdims=True)
        grad_scores = (probs * (grad_probs - inner)).astype(jnp.bfloat16)
        grad_query = (
            jnp.einsum(
                "shqk,skhd->sqhd", grad_scores, key_block, preferred_element_type=jnp.float32
            )
            * score_scale
        )
        grad_key = (
            jnp.einsum(
                "shqk,sqhd->skhd", grad_scores, query_block, preferred_element_type=jnp.float32
            )
            * score_scale
        )
        grad_value = jnp.einsum(
            "shqk,sqhd->skhd",
            probs.astype(jnp.bfloat16),
            grad_block,
            preferred_element_type=jnp.float32,
        )
        seq_count = grad_query.shape[0]
        return (
            grad_query.reshape(seq_count, grad_query.shape[1], group_span),
            grad_key.reshape(seq_count, grad_key.shape[1], group_span),
            grad_value.reshape(seq_count, grad_value.shape[1], group_span),
        )

    grad_query, grad_key, grad_value = lax.map(one_group, jnp.arange(embedding_width // group_span))
    return (
        join_heads(grad_query),
        jnp.concatenate([join_heads(grad_key), join_heads(grad_value)], axis=2),
    )


def on_device(
    tokens,
    segment_ids,
    valid_mask,
    cotangent,
    qkv_weight,
    out_proj,
    in_weight,
    out_weight,
    norm_gain,
    norm_shift,
    proj_bias,
    ff_bias,
):
    section_index = lax.axis_index("section")
    context_position = lax.axis_index("ctx")
    micro_count, seq_count, local_rows, embedding_width = tokens.shape
    head_dim = embedding_width // HEADS
    group_span = math.gcd(HEADS, 4) * head_dim
    qkv_full, proj_full, in_full, out_full = (
        lax.all_gather(qkv_weight, ("ctx", "fsdp"), axis=2, tiled=True),
        lax.all_gather(out_proj, ("ctx", "fsdp"), axis=1, tiled=True),
        lax.all_gather(in_weight, ("ctx", "fsdp"), axis=1, tiled=True),
        lax.all_gather(out_weight, ("ctx", "fsdp"), axis=1, tiled=True),
    )
    w_query = qkv_full[0, 0]
    w_key = qkv_full[0, 1]
    w_value = qkv_full[0, 2]
    w_proj = proj_full[0]
    w_in = in_full[0]
    w_out = out_full[0]
    gain_rows = norm_gain[0]
    shift_rows = norm_shift[0]
    bias_rows = proj_bias[0]
    ff_row = ff_bias[0]
    seg_keys, valid_keys = (
        lax.all_gather(segment_ids, "ctx", axis=2, tiled=True),
        lax.all_gather(valid_mask, "ctx", axis=2, tiled=True),
    )
    query_pos = context_position * local_rows + jnp.arange(local_rows)
    key_pos = jnp.arange(seg_keys.shape[2])
    diagonal = query_pos[:, None] == key_pos[None, :]

    def mask_for(pick_index):
        seg_query = lax.dynamic_index_in_dim(segment_ids, pick_index, 0, False)
        seg_key = lax.dynamic_index_in_dim(seg_keys, pick_index, 0, False)
        live_key = lax.dynamic_index_in_dim(valid_keys, pick_index, 0, False)
        same_doc = (seg_query[:, :, None] == seg_key[:, None, :]) & (live_key[:, None, :] == 1)
        return same_doc | diagonal[None]

    received = jnp.zeros(tokens.shape[1:], jnp.bfloat16)
    act_store = jnp.zeros((micro_count + 1,) + tokens.shape[1:], jnp.bfloat16)
    square_sums = jnp.zeros((4,), jnp.float32)
    token_count = jnp.zeros((), jnp.float32)
    stores = None
    for tick_index in range(micro_count + 1):
        micro_index = tick_index - section_index
        live_flag = (micro_index >= 0) & (micro_index < micro_count)
        slot_index = jnp.where(live_flag, micro_index, micro_count)
        pick_index = jnp.clip(micro_index, 0, micro_count - 1)
        own_input = lax.dynamic_index_in_dim(tokens, pick_index, 0, False)
        layer_input = jnp.where(section_index == 0, own_input, received)
        layer_queries = (project(layer_input, w_query) + bias_rows[0]).astype(jnp.bfloat16)
        key_rows = project(layer_input, w_key).astype(jnp.bfloat16)
        value_rows = (project(layer_input, w_value) + bias_rows[1]).astype(jnp.bfloat16)
        local_kv = jnp.concatenate([key_rows, value_rows], axis=2)
        layer_full_kv = lax.all_gather(local_kv, "ctx", axis=1, tiled=True)
        mixed, layer_log_total = attend_forward(
            layer_queries, layer_full_kv, mask_for(pick_index), head_dim, group_span
        )
        layer_mixed_low = mixed.astype(jnp.bfloat16)
        branch_attn = project(layer_mixed_low, w_proj) + bias_rows[2]
        layer_first_sum = layer_input.astype(jnp.float32) + branch_attn
        layer_normed = normalize(layer_first_sum, gain_rows[0], shift_rows[0])
        layer_hidden = project(layer_normed.astype(jnp.bfloat16), w_in) + ff_row
        layer_activated = exact_gelu(layer_hidden).astype(jnp.bfloat16)
        branch_ff = project(layer_activated, w_out) + bias_rows[3]
        layer_second_sum = layer_normed + branch_ff
        output = normalize(layer_second_sum, gain_rows[1], shift_rows[1])
        layer_kept = (
            layer_input,
            layer_queries,
            local_kv,
            layer_mixed_low,
            layer_log_total,
            layer_first_sum,
            layer_hidden,
            layer_second_sum,
        )
        output, branch_attn, branch_ff, kept = (output, branch_attn, branch_ff, layer_kept)
        output_low = output.astype(jnp.bfloat16)
        if tick_index == 0:
            stores = jax.tree.map(
                lambda member: jnp.zeros((micro_count + 1,) + member.shape, member.dtype), kept
            )
        stores = jax.tree.map(
            lambda stored, member: lax.dynamic_update_index_in_dim(stored, member, slot_index, 0),
            stores,
            kept,
        )
        act_store = lax.dynamic_update_index_in_dim(act_store, output_low, slot_index, 0)
        valid_rows = lax.dynamic_index_in_dim(valid_mask, pick_index, 0, False).astype(jnp.float32)[
            ..., None
        ]
        pieces = jnp.stack(
            [
                jnp.sum(valid_rows * member * member)
                for member in (layer_input.astype(jnp.float32), branch_attn, branch_ff, output)
            ]
        )
        square_sums = square_sums + jnp.where(live_flag, pieces, 0.0)
        token_count = token_count + jnp.where(live_flag, jnp.sum(valid_rows), 0.0)
        if tick_index < micro_count:
            received = from_behind(output_low, "section", 1)
    grad_received = jnp.zeros(tokens.shape[1:], jnp.bfloat16)
    grad_store = jnp.zeros((micro_count + 1,) + tokens.shape[1:], jnp.bfloat16)
    grad_totals = None
    for tick_index in range(micro_count + 1):
        micro_index = tick_index - 1 + section_index
        live_flag = (micro_index >= 0) & (micro_index < micro_count)
        slot_index = jnp.where(live_flag, micro_index, micro_count)
        pick_index = jnp.clip(micro_index, 0, micro_count - 1)
        own_grad = lax.dynamic_index_in_dim(cotangent, pick_index, 0, False)
        grad_output = jnp.where(section_index == 1, own_grad, grad_received)
        kept = jax.tree.map(
            lambda stored: lax.dynamic_index_in_dim(stored, slot_index, 0, False), stores
        )
        (
            layer_layer_input,
            queries,
            stored_kv,
            mixed_low,
            log_total,
            first_sum,
            hidden,
            second_sum,
        ) = kept
        full_kv = lax.all_gather(stored_kv, "ctx", axis=1, tiled=True)
        normed, pull_first = jax.vjp(normalize, first_sum, gain_rows[0], shift_rows[0])
        unused_out, pull_second = jax.vjp(normalize, second_sum, gain_rows[1], shift_rows[1])
        grad_second, grad_gain_two, grad_shift_two = pull_second(grad_output.astype(jnp.float32))
        grad_ff = grad_second.astype(jnp.bfloat16)
        activated_full, pull_gelu = jax.vjp(exact_gelu, hidden)
        activated = activated_full.astype(jnp.bfloat16)
        grad_w_out = token_outer(activated, grad_ff)
        grad_b_out = column_total(grad_ff)
        grad_hidden = pull_gelu(project_back(grad_ff, w_out))[0].astype(jnp.bfloat16)
        grad_w_in = token_outer(normed.astype(jnp.bfloat16), grad_hidden)
        grad_ff_row = column_total(grad_hidden)
        grad_normed = grad_second + project_back(grad_hidden, w_in)
        grad_first, grad_gain_one, grad_shift_one = pull_first(grad_normed)
        grad_branch = grad_first.astype(jnp.bfloat16)
        grad_w_proj = token_outer(mixed_low, grad_branch)
        grad_b_proj = column_total(grad_branch)
        grad_mixed = project_back(grad_branch, w_proj).astype(jnp.bfloat16)
        grad_queries, grad_full_kv = attend_backward(
            queries, full_kv, mask_for(pick_index), log_total, grad_mixed, head_dim, group_span
        )
        grad_queries = grad_queries.astype(jnp.bfloat16)
        grad_local_kv = lax.psum_scatter(
            grad_full_kv.astype(jnp.bfloat16), "ctx", scatter_dimension=1, tiled=True
        )
        grad_keys = grad_local_kv[..., :embedding_width]
        grad_values = grad_local_kv[..., embedding_width:]
        grad_input = (
            grad_first
            + project_back(grad_queries, w_query)
            + project_back(grad_keys, w_key)
            + project_back(grad_values, w_value)
        )
        grad_qkv_tick = jnp.stack(
            [
                token_outer(layer_layer_input, grad_queries),
                token_outer(layer_layer_input, grad_keys),
                token_outer(layer_layer_input, grad_values),
            ]
        )[None]
        grad_gain_tick = jnp.stack([grad_gain_one, grad_gain_two])[None]
        grad_shift_tick = jnp.stack([grad_shift_one, grad_shift_two])[None]
        grad_bias_tick = jnp.stack(
            [column_total(grad_queries), column_total(grad_values), grad_b_proj, grad_b_out]
        )[None]
        tick_grads = (
            grad_qkv_tick,
            grad_w_proj[None],
            grad_w_in[None],
            grad_w_out[None],
            grad_gain_tick,
            grad_shift_tick,
            grad_bias_tick,
            grad_ff_row[None],
        )
        grad_input, tick_grads = (grad_input, tick_grads)
        grad_low = grad_input.astype(jnp.bfloat16)
        grad_store = lax.dynamic_update_index_in_dim(grad_store, grad_low, slot_index, 0)
        tick_grads = jax.tree.map(lambda member: jnp.where(live_flag, member, 0.0), tick_grads)
        grad_totals = (
            tick_grads if grad_totals is None else jax.tree.map(jnp.add, grad_totals, tick_grads)
        )
        if tick_index < micro_count:
            grad_received = from_behind(grad_low, "section", -1)
    grad_totals = (
        lax.psum_scatter(grad_totals[0], ("ctx", "fsdp"), scatter_dimension=2, tiled=True),
        lax.psum_scatter(grad_totals[1], ("ctx", "fsdp"), scatter_dimension=1, tiled=True),
        lax.psum_scatter(grad_totals[2], ("ctx", "fsdp"), scatter_dimension=1, tiled=True),
        lax.psum_scatter(grad_totals[3], ("ctx", "fsdp"), scatter_dimension=1, tiled=True),
        lax.psum_scatter(grad_totals[4], ("ctx", "fsdp"), scatter_dimension=2, tiled=True),
        lax.psum_scatter(grad_totals[5], ("ctx", "fsdp"), scatter_dimension=2, tiled=True),
        lax.psum_scatter(grad_totals[6], ("ctx", "fsdp"), scatter_dimension=2, tiled=True),
        lax.psum_scatter(grad_totals[7], ("ctx", "fsdp"), scatter_dimension=1, tiled=True),
    )
    square_totals, count_total = lax.psum((square_sums, token_count), ("ctx", "fsdp"))
    rms = jnp.sqrt(square_totals / (count_total * embedding_width))[None]
    return (
        act_store[:micro_count][None],
        grad_store[:micro_count][None],
        grad_totals[0],
        grad_totals[1],
        grad_totals[2],
        grad_totals[3],
        grad_totals[4],
        grad_totals[5],
        grad_totals[6],
        grad_totals[7],
        rms,
    )


def solution(mesh):
    placed = (
        P(None, "fsdp", "ctx", None),
        P(None, "fsdp", "ctx"),
        P(None, "fsdp", "ctx"),
        P(None, "fsdp", "ctx", None),
        P("section", None, ("ctx", "fsdp"), None),
        P("section", ("ctx", "fsdp"), None),
        P("section", ("ctx", "fsdp"), None),
        P("section", ("ctx", "fsdp"), None),
        P("section", None, None),
        P("section", None, None),
        P("section", None, None),
        P("section", None),
    )
    return jax.shard_map(
        on_device,
        mesh=mesh,
        in_specs=placed,
        out_specs=(
            P("section", None, "fsdp", "ctx", None),
            P("section", None, "fsdp", "ctx", None),
            P("section", None, ("ctx", "fsdp"), None),
            P("section", ("ctx", "fsdp"), None),
            P("section", ("ctx", "fsdp"), None),
            P("section", ("ctx", "fsdp"), None),
            P("section", None, ("ctx", "fsdp")),
            P("section", None, ("ctx", "fsdp")),
            P("section", None, ("ctx", "fsdp")),
            P("section", ("ctx", "fsdp")),
            P("section", None),
        ),
        check_vma=False,
    )
```

profile of v0, /device:TPU:0, one launch (start us, length us, event | category | flops | bytes accessed | tf_op | source)
XLA Modules:
  0.0 3812.0 jit_solution(618795684340836961)
XLA Ops:
  8.9 98.8 %all-gather.14.cloned.1.call-done = bf16[1,3,1024,1024]{3,2,1,0:T(8,128)(2,1)} async-done(((bf16[1,3,64,1024]{3,2,1,0:T(8,128)(2,1)}), bf16[1,3,1024,1024]{3,2,1,0:T(8,128)(2,1)}) %all-gather.14.cloned.1.call-update) | async-done | bytes 6291472 | tf_op jit(solution)/shard_map/all_gather | solution.py:178
  118.7 12.0 all_gather.38
  132.0 18.8 all_gather.39
  159.3 105.9 %all-gather.16.cloned.1.call-done = bf16[2,1024,2048]{2,1,0:T(8,128)(2,1)} async-done(((bf16[2,256,2048]{2,1,0:T(8,128)(2,1)}), bf16[2,1024,2048]{2,1,0:T(8,128)(2,1)}) %all-gather.16.cloned.1.call-update) | async-done | bytes 8388624 | tf_op jit(solution)/shard_map/all_gather | solution.py:224
  265.2 12.1 copy.107
  278.3 49.5 %while.96 = (s32[]{:T(128)}, bf16[4,2,256,256]{2,3,0,1:T(8,128)(2,1)}, f32[4,2,4,256]{3,2,1,0:T(4,128)S(1)}, s32[4]{0:T(128)S(1)}, bf16[2,1024,2048]{1,2,0:T(8,1...) while((s32[]{:T(128)}, ...), condition=%wide.region_3.4_spmd.clone, body=%wide.region_0.3_spmd.clone.sunk | while | flops 563607552 | bytes 35992344 | solution.py:98
  337.4 103.7 %all-gather.20.cloned.1.call-done = bf16[1,1024,4096]{2,1,0:T(8,128)(2,1)} async-done(((bf16[1,64,4096]{2,1,0:T(8,128)(2,1)}), bf16[1,1024,4096]{2,1,0:T(8,128)(2,1)}) %all-gather.20.cloned.1.call-update) | async-done | bytes 8388624 | tf_op jit(solution)/shard_map/all_gather | solution.py:180
  441.1 14.5 fusion.366
  455.6 99.1 %all-gather.22.cloned.1.call-done = bf16[1,4096,1024]{2,1,0:T(8,128)(2,1)} async-done(((bf16[1,256,1024]{2,1,0:T(8,128)(2,1)}), bf16[1,4096,1024]{2,1,0:T(8,128)(2,1)}) %all-gather.22.cloned.1.call-update) | async-done | bytes 8388624 | tf_op jit(solution)/shard_map/all_gather | solution.py:181
  558.2 29.7 bitcast_dynamic-update-slice_fusion.11
  614.4 144.3 %all-gather.24.cloned.1.call-done = bf16[2,1024,2048]{2,1,0:T(8,128)(2,1)} async-done(((bf16[2,256,2048]{2,1,0:T(8,128)(2,1)}), bf16[2,1024,2048]{2,1,0:T(8,128)(2,1)}) %all-gather.24.cloned.1.call-update) | async-done | bytes 8388624 | tf_op jit(solution)/shard_map/all_gather | solution.py:224
  758.7 11.8 copy.111
  771.6 49.5 %while.97 = (s32[]{:T(128)}, bf16[4,2,256,256]{2,3,0,1:T(8,128)(2,1)}, f32[4,2,4,256]{3,2,1,0:T(4,128)S(1)}, s32[4]{0:T(128)S(1)}, bf16[2,1024,2048]{1,2,0:T(8,1...) while((s32[]{:T(128)}, ...), condition=%wide.region_11.12_spmd.clone, body=%wide.region_8.11_spmd.clone.sunk | while | flops 563607552 | bytes 35992344 | solution.py:98
  827.4 10.5 fusion.367
  837.9 30.6 bitcast_dynamic-update-slice_fusion.10
  897.4 11.6 broadcast_in_dim.466
  909.0 8.1 bitcast_dynamic-update-slice_fusion.5
  923.5 8.2 bitcast_dynamic-update-slice_fusion.4
  949.4 86.5 %all-gather.26.cloned.1.call-done = bf16[2,1024,2048]{2,1,0:T(8,128)(2,1)} async-done(((bf16[2,256,2048]{2,1,0:T(8,128)(2,1)}), bf16[2,1024,2048]{2,1,0:T(8,128)(2,1)}) %all-gather.26.cloned.1.call-update) | async-done | bytes 8388624 | tf_op jit(solution)/shard_map/all_gather | solution.py:224
  1036.0 12.3 copy.115
  1049.4 49.6 %while.98 = (s32[]{:T(128)}, bf16[4,2,256,256]{2,3,0,1:T(8,128)(2,1)}, f32[4,2,4,256]{3,2,1,0:T(4,128)S(1)}, s32[4]{0:T(128)S(1)}, bf16[2,1024,2048]{1,2,0:T(8,1...) while((s32[]{:T(128)}, ...), condition=%wide.region_19.20_spmd.clone, body=%wide.region_16.19_spmd.clone.sunk | while | flops 563607552 | bytes 35992344 | solution.py:98
  1105.3 10.3 fusion.368
  1115.7 28.1 bitcast_dynamic-update-slice_fusion.9
  1166.2 26.5 convert_reduce_fusion.2
  1192.7 12.7 multiply_reduce_fusion.5
  1219.5 114.1 %while.99 = (s32[]{:T(128)}, bf16[4,2,256,256]{2,3,0,1:T(8,128)(2,1)}, bf16[4,2,1024,256]{2,3,1,0:T(8,128)(2,1)}, bf16[4,2,1024,256]{2,3,1,0:T(8,128)(2,1)}, s32...) while((s32[]{:T(128)}, ...), condition=%wide.region_34.35_spmd.clone, body=%wide.region_32.34_spmd.clone.sunk | while | flops 1376516096 | bytes 108074384 | solution.py:151
  1341.1 7.7 reshape.1415
  1356.3 7.7 reshape.1416
  1364.0 8.2 pad_maximum_fusion
  1378.5 19.6 fusion.67
  1398.1 117.0 %reduce-scatter.20.cloned.1.call-done = bf16[2,256,2048]{2,1,0:T(8,128)(2,1)} async-done(((bf16[2,1024,2048]{2,1,0:T(8,128)(2,1)}), bf16[2,256,2048]{2,1,0:T(8,128)(2,1)}) %reduce-scatter.20.cloned.1.call-update) | async-done | bytes 2097168 | tf_op jit(solution)/shard_map/reduce_scatter | solution.py:317
  1540.7 14.6 convert_reduce_fusion.1
  1555.3 12.5 multiply_reduce_fusion.4
  1575.8 90.5 %all-gather.30.cloned.1.call-done = bf16[1,2,1024,2048]{2,3,1,0:T(8,128)(2,1)} async-done(((bf16[1,2,256,2048]{2,3,1,0:T(8,128)(2,1)}), bf16[1,2,1024,2048]{2,3,1,0:T(8,128)(2,1)}) %all-gather.30.cloned.1.call-update) | async-done | bytes 8388624 | tf_op jit(solution)/shard_map/all_gather | solution.py:295
  1672.5 116.8 %while.100 = (s32[]{:T(128)}, bf16[4,2,256,256]{2,3,0,1:T(8,128)(2,1)}, bf16[4,2,1024,256]{2,3,1,0:T(8,128)(2,1)}, bf16[4,2,1024,256]{2,3,1,0:T(8,128)(2,1)}, s3...) while((s32[]{:T(128)}, ...), condition=%wide.region_46.47_spmd.clone, body=%wide.region_44.46_spmd.clone.sunk | while | flops 1376516096 | bytes 108074384 | solution.py:151
  1796.9 7.8 reshape.1417
  1812.2 7.7 reshape.1418
  1819.9 8.2 pad_maximum_fusion.1
  1833.7 137.2 %reduce-scatter.22.cloned.1.call-done = bf16[2,256,2048]{2,1,0:T(8,128)(2,1)} async-done(((bf16[2,1024,2048]{2,1,0:T(8,128)(2,1)}), bf16[2,256,2048]{2,1,0:T(8,128)(2,1)}) %reduce-scatter.22.cloned.1.call-update) | async-done | bytes 2097168 | tf_op jit(solution)/shard_map/reduce_scatter | solution.py:317
  1993.5 26.7 convert_reduce_fusion
  2020.2 12.4 multiply_reduce_fusion.3
  2040.5 81.7 %all-gather.32.cloned.1.call-done = bf16[1,2,1024,2048]{2,3,1,0:T(8,128)(2,1)} async-done(((bf16[1,2,256,2048]{2,3,1,0:T(8,128)(2,1)}), bf16[1,2,1024,2048]{2,3,1,0:T(8,128)(2,1)}) %all-gather.32.cloned.1.call-update) | async-done | bytes 8388624 | tf_op jit(solution)/shard_map/all_gather | solution.py:295
  2128.3 116.7 %while.101 = (s32[]{:T(128)}, bf16[4,2,256,256]{2,3,0,1:T(8,128)(2,1)}, bf16[4,2,1024,256]{2,3,1,0:T(8,128)(2,1)}, bf16[4,2,1024,256]{2,3,1,0:T(8,128)(2,1)}, s3...) while((s32[]{:T(128)}, ...), condition=%wide.region_58.59_spmd.clone, body=%wide.region_56.58_spmd.clone.sunk | while | flops 1376516096 | bytes 108074384 | solution.py:151
  2245.0 7.5 copy.138
  2252.5 7.8 reshape.1419
  2260.3 7.5 copy.139
  2267.9 7.8 reshape.1420
  2275.7 8.2 pad_maximum_fusion.2
  2300.7 25.7 fusion.192
  2333.2 14.5 fusion.186
  2355.2 71.5 %reduce-scatter.24.cloned.1.call-done = bf16[2,256,2048]{2,1,0:T(8,128)(2,1)} async-done(((bf16[2,1024,2048]{2,1,0:T(8,128)(2,1)}), bf16[2,256,2048]{2,1,0:T(8,128)(2,1)}) %reduce-scatter.24.cloned.1.call-update) | async-done | bytes 2097168 | tf_op jit(solution)/shard_map/reduce_scatter | solution.py:317
  2436.7 30.7 fusion.46
  2468.1 13.5 fusion.397
  2481.6 10.1 fusion.398
  2491.7 24.4 fusion.49
  2544.7 11.2 fusion.52
  2567.4 7.7 fusion.529
  2578.3 42.1 %all-reduce = (f32[4]{0:T(128)S(1)}, f32[]{:T(128)}) all-reduce(f32[4]{0:T(128)S(1)} %fusion.529, f32[]{:T(128)S(6)} %add.985), channel_id=1, replica_groups=mesh['section'=2,'ctx'=4,'fsdp'=4] {'ctx','fsdp'}, use_global_device_ids=true, to_apply=%region_107.108 | all-reduce | flops 5 | bytes 40 | tf_op jit(solution)/shard_map/psum | solution.py:369
  2629.0 31.7 reduce-scatter.40.cloned.1.call-done
  2671.5 64.7 %reduce-scatter.38.cloned.1.call-done = f32[64,4]{1,0:T(8,128)} async-done(((f32[1024,4]{1,0:T(8,128)}), f32[64,4]{1,0:T(8,128)}) %reduce-scatter.38.cloned.1.call-update) | async-done | bytes 1040
  2737.6 92.9 %reduce-scatter.28.cloned.1.call-done = f32[1,64,1024]{2,1,0:T(8,128)} async-done(((f32[1,1024,1024]{2,1,0:T(8,128)}), f32[1,64,1024]{2,1,0:T(8,128)}) %reduce-scatter.28.cloned.1.call-update) | async-done | bytes 262160 | tf_op jit(solution)/shard_map/reduce_scatter | solution.py:361
  2830.5 348.9 %reduce-scatter.32.cloned.1.call-done = f32[1,256,1024]{2,1,0:T(8,128)} async-done(((f32[1,4096,1024]{2,1,0:T(8,128)}), f32[1,256,1024]{2,1,0:T(8,128)}) %reduce-scatter.32.cloned.1.call-update) | async-done | bytes 1048592 | tf_op jit(solution)/shard_map/reduce_scatter | solution.py:363
  3179.5 354.9 %reduce-scatter.30.cloned.1.call-done = f32[1,64,4096]{2,1,0:T(8,128)} async-done(((f32[1,1024,4096]{2,1,0:T(8,128)}), f32[1,64,4096]{2,1,0:T(8,128)}) %reduce-scatter.30.cloned.1.call-update) | async-done | bytes 1048592 | tf_op jit(solution)/shard_map/reduce_scatter | solution.py:362
  3534.3 270.6 %reduce-scatter.26.cloned.1.call-done = f32[1,3,64,1024]{3,2,1,0:T(8,128)} async-done(((f32[1,3,1024,1024]{3,2,1,0:T(8,128)}), f32[1,3,64,1024]{3,2,1,0:T(8,128)}) %reduce-scatter.26.cloned.1.call-update) | async-done | bytes 786448 | tf_op jit(solution)/shard_map/reduce_scatter | solution.py:360
  (978 shorter events, 841.5 us)
Async XLA Ops:
  7.2 100.5 %all-gather.14.cloned.1.call-start = ((), (), s32[]{:S(2)}) async-start(), calls=%async_computation.11 | async-start | bytes 6684672 | tf_op jit(solution)/shard_map/all_gather | solution.py:178
  7.9 257.3 %all-gather.16.cloned.1.call-start = ((), (), s32[]{:S(2)}) async-start(), calls=%async_computation.12 | async-start | bytes 10485760 | tf_op jit(solution)/shard_map/all_gather | solution.py:224
  8.9 107.8 %copy-start.171 = (f32[1,1,1024]{2,1,0:T(1,128)}, f32[1,1,1024]{2,1,0:T(1,128)S(1)}, u32[]{:S(2)}) copy-start(f32[1,1,1024]{2,1,0:T(1,128)S(1)} %get-tuple-element.1357) | copy-start | bytes 12292
  8.9 146.2 %copy-start.168 = (f32[1,1,1024]{2,1,0:T(1,128)}, f32[1,1,1024]{2,1,0:T(1,128)S(1)}, u32[]{:S(2)}) copy-start(f32[1,1,1024]{2,1,0:T(1,128)S(1)} %get-tuple-element.1356) | copy-start | bytes 12292
  8.9 322.4 %copy-start.63 = (f32[1,1,1024]{2,1,0:T(1,128)}, f32[1,1,1024]{2,1,0:T(1,128)S(1)}, u32[]{:S(2)}) copy-start(f32[1,1,1024]{2,1,0:T(1,128)S(1)} %get-tuple-element.1358) | copy-start | bytes 12292
  8.9 829.0 %copy-start.136 = (f32[1,1,1024]{2,1,0:T(1,128)}, f32[1,1,1024]{2,1,0:T(1,128)S(1)}, u32[]{:S(2)}) copy-start(f32[1,1,1024]{2,1,0:T(1,128)S(1)} %get-tuple-element.1355) | copy-start | bytes 12292
  116.7 211.1 %all-gather.18.cloned.1.call-start = ((), (), s32[]{:S(2)}) async-start(), calls=%async_computation.13 | async-start | bytes 2228224 | tf_op jit(solution)/shard_map/all_gather | solution.py:179
  117.5 323.6 %all-gather.20.cloned.1.call-start = ((), (), s32[]{:S(2)}) async-start(), calls=%async_computation.14 | async-start | bytes 8912896 | tf_op jit(solution)/shard_map/all_gather | solution.py:180
  118.0 436.7 %all-gather.22.cloned.1.call-start = ((), (), s32[]{:S(2)}) async-start(), calls=%async_computation.15 | async-start | bytes 8912896 | tf_op jit(solution)/shard_map/all_gather | solution.py:181
  118.6 640.1 %all-gather.24.cloned.1.call-start = ((), (), s32[]{:S(2)}) async-start(), calls=%async_computation.16 | async-start | bytes 10485760 | tf_op jit(solution)/shard_map/all_gather | solution.py:224
  152.2 1053.2 %copy-start.67 = (f32[1,1,1024]{2,1,0:T(1,128)}, f32[1,1,1024]{2,1,0:T(1,128)S(1)}, u32[]{:S(2)}) copy-start(f32[1,1,1024]{2,1,0:T(1,128)S(1)} %get-tuple-element.1359) | copy-start | bytes 12292
  152.8 962.8 %copy-start.83 = (f32[1,1,1024]{2,1,0:T(1,128)}, f32[1,1,1024]{2,1,0:T(1,128)S(1)}, u32[]{:S(2)}) copy-start(f32[1,1,1024]{2,1,0:T(1,128)S(1)} %get-tuple-element.1361) | copy-start | bytes 12292
  331.3 109.8 %copy-start.76 = (f32[1,4096]{1,0:T(1,128)S(1)}, f32[1,4096]{1,0:T(1,128)}, u32[]{:S(2)}) copy-start(f32[1,4096]{1,0:T(1,128)} %param.35) | copy-start | bytes 49156
  336.9 118.7 %copy-start.12 = (f32[2,256,1024]{2,1,0:T(8,128)}, f32[2,256,1024]{2,1,0:T(8,128)S(1)}, u32[]{:S(2)}) copy-start(f32[2,256,1024]{2,1,0:T(8,128)S(1)} %get-tuple-element.1285) | copy-start | bytes 6291460
  592.0 6.7 collective-permute-start
  610.2 425.8 %all-gather.26.cloned.1.call-start = ((), (), s32[]{:S(2)}) async-start(), calls=%async_computation.17 | async-start | bytes 10485760 | tf_op jit(solution)/shard_map/all_gather | solution.py:224
  614.4 157.2 %copy-start.62 = (s32[2,1024]{1,0:T(2,128)S(1)}, s32[2,1024]{1,0:T(2,128)}, u32[]{:S(2)}) copy-start(s32[2,1024]{1,0:T(2,128)} %get-tuple-element.1942) | copy-start | bytes 24580
  614.4 157.2 %copy-start.75 = (pred[2,1024]{1,0:T(4,128)(4,1)S(1)}, pred[2,1024]{1,0:T(4,128)(4,1)}, u32[]{:S(2)}) copy-start(pred[2,1024]{1,0:T(4,128)(4,1)} %get-tuple-element.1944) | copy-start | bytes 6148
  614.4 157.2 %copy-start.89 = (s32[2,256]{1,0:T(2,128)S(1)}, s32[2,256]{1,0:T(2,128)}, u32[]{:S(2)}) copy-start(s32[2,256]{1,0:T(2,128)} %get-tuple-element.1943) | copy-start | bytes 6148
  871.0 4.4 collective-permute-start.1
  879.1 55.1 %copy-start.25 = (bf16[2,256,1024]{2,1,0:T(8,128)(2,1)}, bf16[2,256,1024]{2,1,0:T(8,128)(2,1)S(1)}, u32[]{:S(2)}) copy-start(bf16[2,256,1024]{2,1,0:T(8,128)(2,1)S(1)} %get-tuple-element.1269) | copy-start | bytes 3145732
  887.7 325.7 %all-gather.28.cloned.1.call-start = ((), (), s32[]{:S(2)}) async-start(), calls=%async_computation.25 | async-start | bytes 10485760 | tf_op jit(solution)/shard_map/all_gather | solution.py:295
  949.3 100.0 %copy-start.61 = (s32[2,1024]{1,0:T(2,128)S(1)}, s32[2,1024]{1,0:T(2,128)}, u32[]{:S(2)}) copy-start(s32[2,1024]{1,0:T(2,128)} %get-tuple-element.1990) | copy-start | bytes 24580
  949.3 100.0 %copy-start.74 = (pred[2,1024]{1,0:T(4,128)(4,1)S(1)}, pred[2,1024]{1,0:T(4,128)(4,1)}, u32[]{:S(2)}) copy-start(pred[2,1024]{1,0:T(4,128)(4,1)} %get-tuple-element.1992) | copy-start | bytes 6148
  949.4 100.0 %copy-start.88 = (s32[2,256]{1,0:T(2,128)S(1)}, s32[2,256]{1,0:T(2,128)}, u32[]{:S(2)}) copy-start(s32[2,256]{1,0:T(2,128)} %get-tuple-element.1991) | copy-start | bytes 6148
  949.4 565.7 %reduce-scatter.20.cloned.1.call-start = ((), (), s32[]{:S(2)}) async-start(), calls=%async_computation.18 | async-start | bytes 10485760 | tf_op jit(solution)/shard_map/reduce_scatter | solution.py:317
  1152.4 53.1 %copy-start.113 = (f32[2,256]{1,0:T(2,128)}, f32[2,256]{1,0:T(2,128)S(1)}, u32[]{:S(2)}) copy-start(f32[2,256]{1,0:T(2,128)S(1)} %broadcast_multiply_fusion.4) | copy-start | bytes 6148
  1372.2 294.1 %all-gather.30.cloned.1.call-start = ((), (), s32[]{:S(2)}) async-start(), calls=%async_computation.26 | async-start | bytes 10485760 | tf_op jit(solution)/shard_map/all_gather | solution.py:295
  1372.9 154.1 %copy-start.121 = (f32[2,256]{1,0:T(2,128)}, f32[2,256]{1,0:T(2,128)S(1)}, u32[]{:S(2)}) copy-start(f32[2,256]{1,0:T(2,128)S(1)} %get-tuple-element.1369) | copy-start | bytes 6148
  1372.9 154.1 %copy-start.123 = (f32[2,256]{1,0:T(2,128)}, f32[2,256]{1,0:T(2,128)S(1)}, u32[]{:S(2)}) copy-start(f32[2,256]{1,0:T(2,128)S(1)} %get-tuple-element.1370) | copy-start | bytes 6148
  1372.9 154.1 %copy-start.125 = (f32[2,256]{1,0:T(2,128)}, f32[2,256]{1,0:T(2,128)S(1)}, u32[]{:S(2)}) copy-start(f32[2,256]{1,0:T(2,128)S(1)} %get-tuple-element.1371) | copy-start | bytes 6148
  1372.9 597.9 %reduce-scatter.22.cloned.1.call-start = ((), (), s32[]{:S(2)}) async-start(), calls=%async_computation.19 | async-start | bytes 10485760 | tf_op jit(solution)/shard_map/reduce_scatter | solution.py:317
  1374.0 153.0 %copy-start.104 = (f32[2,256]{1,0:T(2,128)}, f32[2,256]{1,0:T(2,128)S(1)}, u32[]{:S(2)}) copy-start(f32[2,256]{1,0:T(2,128)S(1)} %broadcast_multiply_fusion.6) | copy-start | bytes 6148
  1398.1 120.8 %copy-start.116 = (f32[2,256]{1,0:T(2,128)S(1)}, f32[2,256]{1,0:T(2,128)}, u32[]{:S(2)}) copy-start(f32[2,256]{1,0:T(2,128)} %copy-done.115) | copy-start | bytes 6148
  1522.3 4.7 collective-permute-start.2
  1572.5 100.0 %copy-start.59 = (s32[2,1024]{1,0:T(2,128)S(1)}, s32[2,1024]{1,0:T(2,128)}, u32[]{:S(2)}) copy-start(s32[2,1024]{1,0:T(2,128)} %get-tuple-element.2101) | copy-start | bytes 24580
  1572.5 100.0 %copy-start.72 = (pred[2,1024]{1,0:T(4,128)(4,1)S(1)}, pred[2,1024]{1,0:T(4,128)(4,1)}, u32[]{:S(2)}) copy-start(pred[2,1024]{1,0:T(4,128)(4,1)} %get-tuple-element.2103) | copy-start | bytes 6148
  1572.5 100.0 %copy-start.86 = (s32[2,256]{1,0:T(2,128)S(1)}, s32[2,256]{1,0:T(2,128)}, u32[]{:S(2)}) copy-start(s32[2,256]{1,0:T(2,128)} %get-tuple-element.2102) | copy-start | bytes 6148
  1828.1 146.0 %copy-start.11 = (f32[2,256,1024]{2,1,0:T(8,128)S(1)}, f32[2,256,1024]{2,1,0:T(8,128)}, u32[]{:S(2)}) copy-start(f32[2,256,1024]{2,1,0:T(8,128)} %copy-done.10) | copy-start | bytes 6291460
  1828.1 294.1 %all-gather.32.cloned.1.call-start = ((), (), s32[]{:S(2)}) async-start(), calls=%async_computation.27 | async-start | bytes 10485760 | tf_op jit(solution)/shard_map/all_gather | solution.py:295
  1828.7 598.0 %reduce-scatter.24.cloned.1.call-start = ((), (), s32[]{:S(2)}) async-start(), calls=%async_computation.20 | async-start | bytes 10485760 | tf_op jit(solution)/shard_map/reduce_scatter | solution.py:317
  1833.7 146.7 %copy-start.154 = (f32[2,256]{1,0:T(2,128)S(1)}, f32[2,256]{1,0:T(2,128)}, u32[]{:S(2)}) copy-start(f32[2,256]{1,0:T(2,128)} %get-tuple-element.1089) | copy-start | bytes 6148
  1979.1 4.5 collective-permute-start.3
  1980.5 52.1 %copy-start.109 = (f32[2,256]{1,0:T(2,128)}, f32[2,256]{1,0:T(2,128)S(1)}, u32[]{:S(2)}) copy-start(f32[2,256]{1,0:T(2,128)S(1)} %fusion.527) | copy-start | bytes 6148
  2037.2 91.1 %copy-start.58 = (s32[2,1024]{1,0:T(2,128)S(1)}, s32[2,1024]{1,0:T(2,128)}, u32[]{:S(2)}) copy-start(s32[2,1024]{1,0:T(2,128)} %get-tuple-element.2161) | copy-start | bytes 24580
  2037.2 91.1 %copy-start.71 = (pred[2,1024]{1,0:T(4,128)(4,1)S(1)}, pred[2,1024]{1,0:T(4,128)(4,1)}, u32[]{:S(2)}) copy-start(pred[2,1024]{1,0:T(4,128)(4,1)} %get-tuple-element.2163) | copy-start | bytes 6148
  2037.2 91.1 %copy-start.85 = (s32[2,256]{1,0:T(2,128)S(1)}, s32[2,256]{1,0:T(2,128)}, u32[]{:S(2)}) copy-start(s32[2,256]{1,0:T(2,128)} %get-tuple-element.2162) | copy-start | bytes 6148
  2283.9 342.3 %reduce-scatter.34.cloned.1.call-start = ((), (), s32[]{:S(2)}) async-start(), calls=%async_computation.28 | async-start | bytes 557056
  2347.7 80.3 %copy-start.129 = (f32[1024]{0:T(1024)S(1)}, f32[1024]{0:T(1024)}, u32[]{:S(2)}) copy-start(f32[1024]{0:T(1024)} %get-tuple-element.1266) | copy-start | bytes 12292
  2347.7 80.3 %copy-start.131 = (f32[1024]{0:T(1024)S(1)}, f32[1024]{0:T(1024)}, u32[]{:S(2)}) copy-start(f32[1024]{0:T(1024)} %get-tuple-element.1262) | copy-start | bytes 12292
  2347.7 80.3 %copy-start.133 = (f32[1024]{0:T(1024)S(1)}, f32[1024]{0:T(1024)}, u32[]{:S(2)}) copy-start(f32[1024]{0:T(1024)} %get-tuple-element.1258) | copy-start | bytes 12292
  2347.7 80.4 %copy-start.142 = (f32[1024]{0:T(1024)S(1)}, f32[1024]{0:T(1024)}, u32[]{:S(2)}) copy-start(f32[1024]{0:T(1024)} %get-tuple-element.1077) | copy-start | bytes 12292
  2347.7 80.4 %copy-start.143 = (f32[1024]{0:T(1024)S(1)}, f32[1024]{0:T(1024)}, u32[]{:S(2)}) copy-start(f32[1024]{0:T(1024)} %get-tuple-element.1264) | copy-start | bytes 12292
  2347.8 80.4 %copy-start.146 = (f32[1024]{0:T(1024)S(1)}, f32[1024]{0:T(1024)}, u32[]{:S(2)}) copy-start(f32[1024]{0:T(1024)} %get-tuple-element.1260) | copy-start | bytes 12292
  2347.8 81.5 %copy-start.38 = (bf16[2,256,1024]{2,1,0:T(8,128)(2,1)S(1)}, bf16[2,256,1024]{2,1,0:T(8,128)(2,1)}, u32[]{:S(2)}) copy-start(bf16[2,256,1024]{2,1,0:T(8,128)(2,1)} %copy-done.37) | copy-start | bytes 3145732
  2349.0 278.5 %reduce-scatter.36.cloned.1.call-start = ((), (), s32[]{:S(2)}) async-start(), calls=%async_computation.29 | async-start | bytes 557056
  2351.5 309.2 %reduce-scatter.40.cloned.1.call-start = ((), (), s32[]{:S(2)}) async-start(), calls=%async_computation.31 | async-start | bytes 2228224
  2355.1 381.1 %reduce-scatter.38.cloned.1.call-start = ((), (), s32[]{:S(2)}) async-start(), calls=%async_computation.30 | async-start | bytes 557056
  2429.3 401.3 %reduce-scatter.28.cloned.1.call-start = ((), (), s32[]{:S(2)}) async-start(), calls=%async_computation.22 | async-start | bytes 4456448 | tf_op jit(solution)/shard_map/reduce_scatter | solution.py:361
  2436.7 742.8 %reduce-scatter.32.cloned.1.call-start = ((), (), s32[]{:S(2)}) async-start(), calls=%async_computation.24 | async-start | bytes 17825792 | tf_op jit(solution)/shard_map/reduce_scatter | solution.py:363
  2467.5 1066.9 %reduce-scatter.30.cloned.1.call-start = ((), (), s32[]{:S(2)}) async-start(), calls=%async_computation.23 | async-start | bytes 17825792 | tf_op jit(solution)/shard_map/reduce_scatter | solution.py:362
  2516.1 1288.9 %reduce-scatter.26.cloned.1.call-start = ((), (), s32[]{:S(2)}) async-start(), calls=%async_computation.21 | async-start | bytes 13369344 | tf_op jit(solution)/shard_map/reduce_scatter | solution.py:360
  2575.1 90.3 %copy-start.28 = (bf16[3,2,256,1024]{3,2,1,0:T(8,128)(2,1)S(1)}, bf16[3,2,256,1024]{3,2,1,0:T(8,128)(2,1)}, u32[]{:S(2)}) copy-start(bf16[3,2,256,1024]{3,2,1,0:T(8,128)(2,1)} %get-tuple-element.1397) | copy-start | bytes 9437188
  2575.1 90.4 %copy-start.161 = (f32[2,256]{1,0:T(2,128)S(1)}, f32[2,256]{1,0:T(2,128)}, u32[]{:S(2)}) copy-start(f32[2,256]{1,0:T(2,128)} %copy-done.160) | copy-start | bytes 6148
  (163 other events, 1976.6 us)
Sparse Core Ops, SparseCore 0:
  10.8 96.8 all-gather.13
  116.8 148.2 all-gather.15
  267.9 58.9 all-gather.17
  329.6 111.4 all-gather.19
  443.7 111.0 all-gather.21
  610.3 148.4 all-gather.23
  887.8 148.1 all-gather.25
  1037.5 147.3 all-gather.27
  1372.3 142.6 reduce-scatter.19
  1516.5 149.8 all-gather.29
  1828.2 142.6 reduce-scatter.21
  1972.3 149.8 all-gather.31
  2284.0 142.6 reduce-scatter.23
  2428.8 77.2 reduce-scatter.33
  2508.3 72.9 reduce-scatter.35
  2583.3 77.2 reduce-scatter.39
  2662.8 73.3 reduce-scatter.37
  2739.0 91.4 reduce-scatter.27
  2833.5 345.9 reduce-scatter.31
  3182.3 352.0 reduce-scatter.29
  3537.3 267.6 reduce-scatter.25
where the time goes:
time: 3830 us; the launch traced here: 3810 us
  waiting for transfers between devices  2310 us (60%)
  matrix products  733 us (19%)
  local copies, waits for them, and re-layouts  382 us (10%)
  other arithmetic  243 us (6%)
  blocking collectives  72.9 us (2%)
  loops' own time  41.8 us (1%)
    reduce_scatter x1, waiting for transfers between devices, on_device(): lax.psum_scatter(grad_totals[2], ('ctx', 'fsdp'), scatter_dimension=1, ti...  355 us
    reduce_scatter x1, waiting for transfers between devices, on_device(): lax.psum_scatter(grad_totals[3], ('ctx', 'fsdp'), scatter_dimension=1, ti...  349 us
    all_gather x3, waiting for transfers between devices, on_device(): layer_full_kv = lax.all_gather(local_kv, 'ctx', axis=1, tiled=True)  337 us
    reduce_scatter x3, waiting for transfers between devices, on_device(): lax.psum_scatter(grad_full_kv.astype(jnp.bfloat16), 'ctx', scatter_dimens...  326 us
    reduce_scatter x1, waiting for transfers between devices, on_device(): lax.psum_scatter(grad_totals[0], ('ctx', 'fsdp'), scatter_dimension=2, ti...  271 us
    all_gather x3, waiting for transfers between devices, on_device(): full_kv = lax.all_gather(stored_kv, 'ctx', axis=1, tiled=True)  172 us
    dot_general x18, matrix products, project(): lax.dot_general(operand_array, matrix_value, (((operand_array.ndim - 1,),...  172 us
    dot_general x18, matrix products, token_outer(): lax.dot_general(inputs, grads, (((0, 1), (0, 1)), ((), ())), preferred_el...  164 us
  transfers between devices with their start and end apart: 25, of which 20 were waited for; matrix products, arithmetic and copies ran while one was open for 19% of the time, Pallas kernels for 0%

commit v1 on v0

v1 whole, which is shorter than its diff:
```python
import math

import jax
import jax.numpy as jnp
from jax import lax
from jax.experimental import pallas as pl
from jax.experimental.pallas import tpu as pltpu
from jax.sharding import PartitionSpec as P

HEADS = 16
NORM_EPS = 1e-05
MASKED = -1e30
BF = jnp.bfloat16
F32 = jnp.float32
VMEM_LIMIT = 48 * 1024 * 1024


def nt_dot(a, b):
    return lax.dot_general(a, b, (((1,), (1,)), ((), ())), preferred_element_type=F32)


def nn_dot(a, b):
    return lax.dot_general(a, b, (((1,), (0,)), ((), ())), preferred_element_type=F32)


def tn_dot(a, b):
    return lax.dot_general(a, b, (((0,), (0,)), ((), ())), preferred_element_type=F32)


def mask_bias(code_k, seg_q, first_query):
    shape = (code_k.shape[0], seg_q.shape[1])
    key_at = lax.broadcasted_iota(jnp.int32, shape, 0)
    query_at = lax.broadcasted_iota(jnp.int32, shape, 1) + first_query
    allowed = (code_k == seg_q) | (key_at == query_at)
    return jnp.where(allowed, 0.0, MASKED)


def head_masked(block, head, head_dim):
    lane = lax.broadcasted_iota(jnp.int32, block.shape, 1)
    inside = (lane >= head * head_dim) & (lane < (head + 1) * head_dim)
    return jnp.where(inside, block, jnp.zeros_like(block))


def attend_forward_kernel(head_dim, q_ref, k_ref, v_ref, code_ref, seg_ref, o_ref, lse_ref, bias_ref):
    block = q_ref.shape[0]
    per = q_ref.shape[1] // head_dim
    scale = head_dim ** (-0.5)

    @pl.when(pl.program_id(1) == 0)
    def _():
        bias_ref[...] = mask_bias(code_ref[...], seg_ref[...], pl.program_id(0) * block)

    query = (q_ref[...].astype(F32) * scale).astype(BF)
    keys = k_ref[...]
    values_t = v_ref[...].astype(F32).T.astype(BF)
    outs, tops = [], []
    for head in range(per):
        scores = nt_dot(keys, head_masked(query, head, head_dim)) + bias_ref[...]
        top = jnp.max(scores, axis=0, keepdims=True)
        expo = jnp.exp(scores - top)
        total = jnp.sum(expo, axis=0, keepdims=True)
        part = nn_dot(values_t[head * head_dim : (head + 1) * head_dim], expo.astype(BF))
        outs.append(part / total)
        tops.append(top + jnp.log(total))
    o_ref[...] = jnp.concatenate(outs, axis=0).T.astype(BF)
    lse_ref[0] = jnp.concatenate(tops, axis=0)


def attend_backward_kernel(
    head_dim, q_ref, k_ref, v_ref, do_ref, lse_ref, code_ref, seg_ref, dq_ref, dk_ref, dv_ref, bias_ref, dk_acc, dv_acc
):
    block = q_ref.shape[0]
    per = q_ref.shape[1] // head_dim
    scale = head_dim ** (-0.5)
    at = pl.program_id(1)

    @pl.when(pl.program_id(0) == 0)
    def _():
        bias_ref[at] = mask_bias(code_ref[...], seg_ref[...], at * block)

    @pl.when(at == 0)
    def _():
        dk_acc[...] = jnp.zeros_like(dk_acc)
        dv_acc[...] = jnp.zeros_like(dv_acc)

    query = (q_ref[...].astype(F32) * scale).astype(BF)
    keys = k_ref[...]
    keys_t = keys.astype(F32).T.astype(BF)
    values = v_ref[...]
    grad_out = do_ref[...]
    outs = []
    for head in range(per):
        query_h = head_masked(query, head, head_dim)
        grad_h = head_masked(grad_out, head, head_dim)
        scores = nt_dot(keys, query_h) + bias_ref[at]
        probs = jnp.exp(scores - lse_ref[0, head : head + 1])
        grad_probs = nt_dot(values, grad_h)
        inner = jnp.sum(probs * grad_probs, axis=0, keepdims=True)
        grad_scores = (probs * (grad_probs - inner)).astype(BF)
        dv_acc[...] += nn_dot(probs.astype(BF), grad_h)
        dk_acc[...] += nn_dot(grad_scores, query_h)
        outs.append(nn_dot(keys_t[head * head_dim : (head + 1) * head_dim], grad_scores) * scale)
    dq_ref[...] = jnp.concatenate(outs, axis=0).T.astype(BF)

    @pl.when(at == pl.num_programs(1) - 1)
    def _():
        dk_ref[...] = dk_acc[...].astype(dk_ref.dtype)
        dv_ref[...] = dv_acc[...].astype(dv_ref.dtype)


def attend_forward(q, k, v, code_k, seg_q, head_dim):
    rows, width = q.shape
    keys = k.shape[0]
    block = min(256, rows)
    pair = 2 * head_dim
    cost = pl.CostEstimate(
        flops=16 * rows * keys * width, bytes_accessed=8 * rows * width, transcendentals=rows * keys * width // head_dim
    )
    return pl.pallas_call(
        lambda *refs: attend_forward_kernel(head_dim, *refs),
        grid=(rows // block, width // pair),
        in_specs=[
            pl.BlockSpec((block, pair), lambda i, h: (i, h)),
            pl.BlockSpec((keys, pair), lambda i, h: (0, h)),
            pl.BlockSpec((keys, pair), lambda i, h: (0, h)),
            pl.BlockSpec((keys, 1), lambda i, h: (0, 0)),
            pl.BlockSpec((1, block), lambda i, h: (0, i)),
        ],
        out_specs=[
            pl.BlockSpec((block, pair), lambda i, h: (i, h)),
            pl.BlockSpec((1, 2, block), lambda i, h: (h, 0, i)),
        ],
        out_shape=[
            jax.ShapeDtypeStruct((rows, width), BF),
            jax.ShapeDtypeStruct((width // pair, 2, rows), F32),
        ],
        scratch_shapes=[pltpu.VMEM((keys, block), F32)],
        compiler_params=pltpu.CompilerParams(vmem_limit_bytes=VMEM_LIMIT),
        cost_estimate=cost,
        name="attend_forward",
    )(q, k, v, code_k, seg_q)


def attend_backward(q, k, v, grad_out, lse, code_k, seg_q, head_dim, kv_type):
    rows, width = q.shape
    keys = k.shape[0]
    block = min(256, rows)
    pair = 2 * head_dim
    cost = pl.CostEstimate(
        flops=40 * rows * keys * width, bytes_accessed=16 * rows * width, transcendentals=rows * keys * width // head_dim
    )
    return pl.pallas_call(
        lambda *refs: attend_backward_kernel(head_dim, *refs),
        grid=(width // pair, rows // block),
        in_specs=[
            pl.BlockSpec((block, pair), lambda h, i: (i, h)),
            pl.BlockSpec((keys, pair), lambda h, i: (0, h)),
            pl.BlockSpec((keys, pair), lambda h, i: (0, h)),
            pl.BlockSpec((block, pair), lambda h, i: (i, h)),
            pl.BlockSpec((1, 2, block), lambda h, i: (h, 0, i)),
            pl.BlockSpec((keys, 1), lambda h, i: (0, 0)),
            pl.BlockSpec((1, block), lambda h, i: (0, i)),
        ],
        out_specs=[
            pl.BlockSpec((block, pair), lambda h, i: (i, h)),
            pl.BlockSpec((keys, pair), lambda h, i: (0, h)),
            pl.BlockSpec((keys, pair), lambda h, i: (0, h)),
        ],
        out_shape=[
            jax.ShapeDtypeStruct((rows, width), BF),
            jax.ShapeDtypeStruct((keys, width), kv_type),
            jax.ShapeDtypeStruct((keys, width), kv_type),
        ],
        scratch_shapes=[
            pltpu.VMEM((rows // block, keys, block), F32),
            pltpu.VMEM((keys, pair), F32),
            pltpu.VMEM((keys, pair), F32),
        ],
        compiler_params=pltpu.CompilerParams(vmem_limit_bytes=VMEM_LIMIT),
        cost_estimate=cost,
        name="attend_backward",
    )(q, k, v, grad_out, lse, code_k, seg_q)


def norm_forward(residual):
    average = jnp.mean(residual, axis=-1, keepdims=True)
    centred = residual - average
    spread = jnp.mean(centred * centred, axis=-1, keepdims=True)
    inverse = lax.rsqrt(spread + NORM_EPS)
    return centred * inverse, inverse


def norm_backward(grad, unit, inverse, gain):
    scaled = grad * gain
    return inverse * (
        scaled
        - jnp.mean(scaled, axis=-1, keepdims=True)
        - unit * jnp.mean(scaled * unit, axis=-1, keepdims=True)
    )


def gelu_pair(values):
    cdf = 0.5 * (1.0 + lax.erf(values * (2.0**-0.5)))
    density = jnp.exp(-0.5 * values * values) * ((2.0 * math.pi) ** -0.5)
    return values * cdf, cdf + values * density


class Place:
    def __init__(self):
        self.section = lax.axis_index("section")
        self.ctx = lax.axis_index("ctx")
        fsdp = lax.axis_index("fsdp")
        self.nz = lax.axis_size("ctx")
        self.nf = lax.axis_size("fsdp")
        side = math.isqrt(self.nf)
        self.nx = side if side * side == self.nf else self.nf
        self.ny = self.nf // self.nx
        self.y = fsdp // self.nx
        self.x = fsdp % self.nx

    def from_x(self, value, steps):
        pairs = []
        for f in range(self.nf):
            y, x = divmod(f, self.nx)
            pairs.append((y * self.nx + (x + steps) % self.nx, f))
        return lax.ppermute(value, "fsdp", pairs)

    def from_y(self, value, steps):
        pairs = []
        for f in range(self.nf):
            y, x = divmod(f, self.nx)
            pairs.append((((y + steps) % self.ny) * self.nx + x, f))
        return lax.ppermute(value, "fsdp", pairs)

    def sibling(self, value):
        return lax.ppermute(value, "section", [(0, 1), (1, 0)])

    def in_order(self, own, other, axis):
        first = self.section == 0
        return jnp.concatenate([jnp.where(first, own, other), jnp.where(first, other, own)], axis=axis)


def place_rotated(pieces, first, count):
    out = jnp.zeros((count,) + pieces[0].shape, pieces[0].dtype)
    for r, piece in enumerate(pieces):
        out = lax.dynamic_update_index_in_dim(out, piece, (first + r) % count, 0)
    return out


def gather_rows(place, shard, x_first):
    rows, cols = shard.shape
    column = lax.all_gather(shard, "ctx", axis=0, tiled=True).reshape(place.nz, rows, cols)
    if x_first:
        line = [column] + [place.from_x(column, r) for r in range(1, place.nx)]
        grid = [line] + [[place.from_y(piece, r) for piece in line] for r in range(1, place.ny)]
    else:
        line = [column] + [place.from_y(column, r) for r in range(1, place.ny)]
        more = [[place.from_x(piece, r) for piece in line] for r in range(1, place.nx)]
        grid = [[line[ry]] + [m[ry] for m in more] for ry in range(place.ny)]
    out = jnp.zeros((place.nz, place.nf, rows, cols), shard.dtype)
    for ry in range(place.ny):
        for rx in range(place.nx):
            at = ((place.y + ry) % place.ny) * place.nx + (place.x + rx) % place.nx
            out = lax.dynamic_update_slice(out, grid[ry][rx][:, None], (0, at, 0, 0))
    return out.reshape(place.nz * place.nf * rows, cols)


def scatter_rows(place, full, y_first):
    cols = full.shape[1]
    parts = full.reshape(place.nz, place.ny, place.nx, -1, cols)

    def along_y(value):
        keep = lax.dynamic_index_in_dim(value, place.y, 1, False).astype(F32)
        for r in range(1, place.ny):
            sent = lax.dynamic_index_in_dim(value, (place.y + r) % place.ny, 1, False)
            keep = keep + place.from_y(sent, -r).astype(F32)
        return keep.astype(BF)

    def along_x(value):
        axis = value.ndim - 3
        keep = lax.dynamic_index_in_dim(value, place.x, axis, False).astype(F32)
        for r in range(1, place.nx):
            sent = lax.dynamic_index_in_dim(value, (place.x + r) % place.nx, axis, False)
            keep = keep + place.from_x(sent, -r).astype(F32)
        return keep.astype(BF)

    if y_first:
        column = along_x(along_y(parts))
    else:
        column = along_y(along_x(parts))
    out = lax.psum_scatter(column.reshape(-1, cols), "ctx", scatter_dimension=0, tiled=True)
    return out.astype(F32)


def to_sequences(place, value):
    count = value.shape[0]
    groups = place.nz // count
    piece_at = place.ctx % count
    kept_seq = place.ctx // groups
    pieces = []
    for k in range(count):
        sent = lax.dynamic_index_in_dim(value, (piece_at + k) % count, 0, False)
        pairs = [(z, ((z % count + k) % count) * groups + z // count) for z in range(place.nz)]
        pieces.append(sent if all(a == b for a, b in pairs) else lax.ppermute(sent, "ctx", pairs))
    return place_rotated([pieces[0]] + pieces[:0:-1], kept_seq, count)


def from_sequences(place, value):
    count = value.shape[0]
    groups = place.nz // count
    kept_seq = place.ctx // groups
    pieces = []
    for k in range(count):
        sent = lax.dynamic_index_in_dim(value, (kept_seq - k) % count, 0, False)
        pairs = [(((z % count + k) % count) * groups + z // count, z) for z in range(place.nz)]
        pieces.append(sent if all(a == b for a, b in pairs) else lax.ppermute(sent, "ctx", pairs))
    return place_rotated(pieces, place.ctx % count, count)


def split_to_sequences(place, value):
    seqs, rows, width = value.shape
    half = rows // 2
    mine = lax.dynamic_slice_in_dim(value, place.section * half, half, 1)
    moved = to_sequences(place, mine)
    other = place.sibling(moved)
    first = place.section == 0
    both = jnp.stack([jnp.where(first, moved, other), jnp.where(first, other, moved)], axis=1)
    return both.reshape(seqs * rows, width)


def on_device(
    tokens,
    segment_ids,
    valid_mask,
    cotangent,
    qkv_weight,
    out_proj,
    in_weight,
    out_weight,
    norm_gain,
    norm_shift,
    proj_bias,
    ff_bias,
):
    place = Place()
    section = place.section
    first_section = section == 0
    micro, seqs, local, width = tokens.shape
    count = micro * seqs
    groups = place.nz // count
    rows = count * local
    head_dim = width // HEADS
    half = width // 2
    ff_width = in_weight.shape[2]
    ff_half = ff_width // 2
    chips = place.nz * place.nf
    ff_rows = out_weight.shape[1]
    ff_split = ff_rows // 2

    def part_of(which):
        qkv_part = lax.dynamic_slice_in_dim(qkv_weight[0], which * half, half, 2)
        proj_part = lax.dynamic_slice_in_dim(out_proj[0], which * half, half, 1)
        in_part = lax.dynamic_index_in_dim(
            in_weight[0].reshape(-1, chips, 2, ff_split), which, 2, False
        ).reshape(-1, ff_half)
        out_part = lax.dynamic_slice_in_dim(out_weight[0], which * ff_split, ff_split, 0)
        attn_part = jnp.concatenate([qkv_part[0], qkv_part[1], qkv_part[2], proj_part], axis=1)
        return (attn_part, in_part, out_part)

    own_parts = part_of(section)
    sent_parts = part_of(1 - section)
    full = [[None] * 3, [None] * 3]
    shards = [[None] * 3, [None] * 3]
    for index in range(3):
        other = place.sibling(sent_parts[index])
        shards[0][index] = jnp.where(first_section, own_parts[index], other)
        shards[1][index] = jnp.where(first_section, other, own_parts[index])
    flip = True
    for layer in range(2):
        for index in range(3):
            full[layer][index] = gather_rows(place, shards[layer][index], flip)
            flip = not flip

    def layer_weights(layer):
        attn, w_in, w_out = full[layer]
        w_qkv = attn[:, : 3 * half]
        columns = attn[:, 3 * half :]
        mine = lax.dynamic_slice_in_dim(columns, section * half, half, 0)
        sent = lax.dynamic_slice_in_dim(columns, (1 - section) * half, half, 0)
        w_proj = place.in_order(mine, place.sibling(sent), 1)
        return w_qkv, w_proj, w_in, w_out

    small_own = jnp.concatenate([norm_gain[0], norm_shift[0], proj_bias[0], ff_bias[0].reshape(-1, width)], axis=0)
    small_other = place.sibling(small_own)
    small = [
        jnp.where(first_section, small_own, small_other),
        jnp.where(first_section, small_other, small_own),
    ]

    def layer_small(layer):
        table = small[layer]
        gains, shifts, biases = table[0:2], table[2:4], table[4:8]
        ff_all = table[8:].reshape(chips, 2, ff_split)
        ff_part = lax.dynamic_index_in_dim(ff_all, section, 1, False).reshape(-1)
        bias_q = lax.dynamic_slice_in_dim(biases[0], section * half, half, 0)
        bias_v = lax.dynamic_slice_in_dim(biases[1], section * half, half, 0)
        bias_qkv = jnp.concatenate([bias_q, jnp.zeros_like(bias_q), bias_v])
        return gains, shifts, biases, ff_part, bias_qkv

    ids = segment_ids.reshape(count, local) * 2 + (valid_mask.reshape(count, local) == 1).astype(jnp.int32)
    ids = to_sequences(place, ids).reshape(rows)
    seg_own = ids // 2
    valid_own = ids % 2

    def over_groups(value, steps):
        pairs = []
        for z in range(place.nz):
            q, g = divmod(z, groups)
            pairs.append((q * groups + (g + steps) % groups, z))
        return lax.ppermute(value, "ctx", pairs)

    def gather_groups(value):
        return jnp.concatenate([value] + [over_groups(value, r) for r in range(1, groups)], axis=0)

    def scatter_groups(value):
        parts = value.reshape(groups, rows, -1)
        total = parts[0]
        for r in range(1, groups):
            total = total + over_groups(parts[r].astype(BF), -r).astype(F32)
        return total.astype(BF)

    code_k = gather_groups(jnp.where(valid_own == 1, seg_own, -1))[:, None]
    seg_q = seg_own[None, :]
    live = valid_own.astype(F32)[:, None]

    layer_input = split_to_sequences(place, tokens.reshape(count, local, width))
    grad_out = split_to_sequences(place, cotangent.reshape(count, local, width))

    saved, acts, squares = [], [], []
    weights = [layer_weights(layer) for layer in range(2)]
    smalls = [layer_small(layer) for layer in range(2)]
    for layer in range(2):
        w_qkv, w_proj, w_in, w_out = weights[layer]
        gains, shifts, biases, ff_part, bias_qkv = smalls[layer]
        qkv = (nn_dot(layer_input, w_qkv) + bias_qkv).astype(BF)
        q, k, v = qkv[:, :half], qkv[:, half : 2 * half], qkv[:, 2 * half :]
        if groups > 1:
            kv = gather_groups(qkv[:, half:])
            k, v = kv[:, :half], kv[:, half:]
        mixed, lse = attend_forward(q, k, v, code_k, seg_q, head_dim)
        part = nn_dot(mixed, w_proj)
        branch_attn = part + place.sibling(part.astype(BF)).astype(F32) + biases[2]
        wide_input = layer_input.astype(F32)
        unit_one, inverse_one = norm_forward(wide_input + branch_attn)
        normed = unit_one * gains[0] + shifts[0]
        normed_low = normed.astype(BF)
        hidden = nn_dot(normed_low, w_in) + ff_part
        activated, slope = gelu_pair(hidden)
        activated = activated.astype(BF)
        slope = slope.astype(BF)
        part = nn_dot(activated, w_out)
        branch_ff = part + place.sibling(part.astype(BF)).astype(F32) + biases[3]
        unit_two, inverse_two = norm_forward(normed + branch_ff)
        output = unit_two * gains[1] + shifts[1]
        squares.append(
            jnp.stack([jnp.sum(live * m * m) for m in (wide_input, branch_attn, branch_ff, output)])
        )
        saved.append(
            (layer_input, q, k, v, mixed, lse, unit_one, inverse_one, normed_low, activated, slope, unit_two, inverse_two)
        )
        layer_input = output.astype(BF)
        acts.append(layer_input)

    def give_back(pair):
        value = jnp.where(first_section, pair[0], pair[1])
        return from_sequences(place, value.reshape(count, local, width)).reshape(1, micro, seqs, local, width)

    activations = give_back(acts)

    square_sum = jnp.where(first_section, squares[0], squares[1])
    totals = lax.psum(jnp.concatenate([square_sum, jnp.sum(live)[None]]), ("ctx", "fsdp"))
    rms = jnp.sqrt(totals[:4] / (totals[4] * width))[None]

    grads = [None, None]
    input_grads = [None, None]
    small_grads = [None, None]
    grad_in = grad_out.astype(F32)
    for layer in (1, 0):
        w_qkv, w_proj, w_in, w_out = weights[layer]
        gains = smalls[layer][0]
        (u, q, k, v, mixed, lse, unit_one, inverse_one, normed_low, activated, slope, unit_two, inverse_two) = saved[layer]
        grad_gain_two = jnp.sum(grad_in * unit_two, axis=0)
        grad_shift_two = jnp.sum(grad_in, axis=0)
        grad_second = norm_backward(grad_in, unit_two, inverse_two, gains[1])
        grad_ff = grad_second.astype(BF)
        grad_w_out = tn_dot(activated, grad_ff).astype(BF)
        out_total = scatter_rows(place, grad_w_out, layer == 1)
        grad_b_out = jnp.sum(grad_ff.astype(F32), axis=0)
        grad_hidden = (nt_dot(grad_ff, w_out) * slope.astype(F32)).astype(BF)
        grad_ff_row = jnp.sum(grad_hidden.astype(F32), axis=0)
        part = nt_dot(grad_hidden, w_in)
        grad_normed = grad_second + part + place.sibling(part.astype(BF)).astype(F32)
        grad_w_in = tn_dot(normed_low, grad_hidden).astype(BF)
        in_total = scatter_rows(place, grad_w_in, layer == 0)
        grad_gain_one = jnp.sum(grad_normed * unit_one, axis=0)
        grad_shift_one = jnp.sum(grad_normed, axis=0)
        grad_first = norm_backward(grad_normed, unit_one, inverse_one, gains[0])
        grad_branch = grad_first.astype(BF)
        grad_b_proj = jnp.sum(grad_branch.astype(F32), axis=0)
        grad_mixed = nt_dot(grad_branch, w_proj).astype(BF)
        grad_w_proj = tn_dot(mixed, grad_branch).astype(BF)
        mine = lax.dynamic_slice_in_dim(grad_w_proj, section * half, half, 1)
        sent = lax.dynamic_slice_in_dim(grad_w_proj, (1 - section) * half, half, 1)
        grad_w_proj = place.in_order(mine, place.sibling(sent), 0)
        dq, dk, dv = attend_backward(
            q, k, v, grad_mixed, lse, code_k, seg_q, head_dim, BF if groups == 1 else F32
        )
        if groups > 1:
            dk, dv = scatter_groups(dk), scatter_groups(dv)
        dqkv = jnp.concatenate([dq, dk, dv], axis=1)
        part = nt_dot(dqkv, w_qkv)
        grad_u = grad_first + part + place.sibling(part.astype(BF)).astype(F32)
        grad_w_qkv = tn_dot(u, dqkv).astype(BF)
        attn_total = scatter_rows(place, jnp.concatenate([grad_w_qkv, grad_w_proj], axis=1), layer == 1)
        dqkv_rows = jnp.sum(dqkv.astype(F32), axis=0)
        grads[layer] = (attn_total, in_total, out_total)
        input_grads[layer] = grad_u.astype(BF)
        grad_in = input_grads[layer].astype(F32)
        here = jnp.where(section == layer, 1.0, 0.0)
        spread = jnp.zeros((2, 2, half), F32)
        spread = lax.dynamic_update_slice(spread, dqkv_rows[:half][None, None], (0, section, 0))
        spread = lax.dynamic_update_slice(spread, dqkv_rows[2 * half :][None, None], (1, section, 0))
        ff_spread = lax.dynamic_update_slice(
            jnp.zeros((chips, 2, ff_split), F32), grad_ff_row.reshape(chips, 1, ff_split), (0, section, 0)
        )
        rest = here * jnp.stack(
            [grad_gain_one, grad_gain_two, grad_shift_one, grad_shift_two, grad_b_proj, grad_b_out]
        )
        by_chip = jnp.concatenate([rest, spread.reshape(2, width)], axis=0).reshape(8, chips, -1)
        by_chip = jnp.moveaxis(by_chip, 1, 0).reshape(chips, -1)
        small_grads[layer] = jnp.concatenate([by_chip, ff_spread.reshape(chips, -1)], axis=1)

    input_grads = give_back(input_grads)

    def to_owner(pair):
        mine = jnp.where(first_section, pair[0], pair[1])
        sent = jnp.where(first_section, pair[1], pair[0])
        return mine, place.sibling(sent)

    def halves(pair):
        mine, other = to_owner(pair)
        return jnp.where(first_section, mine, other), jnp.where(first_section, other, mine)

    low, high = halves([grads[0][0], grads[1][0]])
    attn_rows = width // chips
    low = low.reshape(attn_rows, 4, half)
    high = high.reshape(attn_rows, 4, half)
    attn = jnp.concatenate([low, high], axis=2)
    grad_qkv = jnp.moveaxis(attn[:, :3], 1, 0)[None]
    grad_out_proj = attn[:, 3][None]
    low, high = halves([grads[0][1], grads[1][1]])
    grad_in_weight = jnp.stack(
        [low.reshape(-1, chips, ff_split), high.reshape(-1, chips, ff_split)], axis=2
    ).reshape(1, -1, ff_width)
    low, high = halves([grads[0][2], grads[1][2]])
    grad_out_weight = jnp.concatenate([low, high], axis=0)[None]

    mine, other = to_owner(small_grads)
    total = lax.psum_scatter(mine + other, ("ctx", "fsdp"), scatter_dimension=0, tiled=True)[0]
    per_chip = width // chips
    table = total[: 8 * per_chip].reshape(8, per_chip)
    grad_gain = table[0:2][None]
    grad_shift = table[2:4][None]
    grad_proj_bias = jnp.stack([table[6], table[7], table[4], table[5]])[None]
    grad_ff_bias = total[8 * per_chip :][None]
    return (
        activations,
        input_grads,
        grad_qkv,
        grad_out_proj,
        grad_in_weight,
        grad_out_weight,
        grad_gain,
        grad_shift,
        grad_proj_bias,
        grad_ff_bias,
        rms,
    )


def solution(mesh):
    placed = (
        P(None, "fsdp", "ctx", None),
        P(None, "fsdp", "ctx"),
        P(None, "fsdp", "ctx"),
        P(None, "fsdp", "ctx", None),
        P("section", None, ("ctx", "fsdp"), None),
        P("section", ("ctx", "fsdp"), None),
        P("section", ("ctx", "fsdp"), None),
        P("section", ("ctx", "fsdp"), None),
        P("section", None, None),
        P("section", None, None),
        P("section", None, None),
        P("section", None),
    )
    return jax.shard_map(
        on_device,
        mesh=mesh,
        in_specs=placed,
        out_specs=(
            P("section", None, "fsdp", "ctx", None),
            P("section", None, "fsdp", "ctx", None),
            P("section", None, ("ctx", "fsdp"), None),
            P("section", ("ctx", "fsdp"), None),
            P("section", ("ctx", "fsdp"), None),
            P("section", ("ctx", "fsdp"), None),
            P("section", None, ("ctx", "fsdp")),
            P("section", None, ("ctx", "fsdp")),
            P("section", None, ("ctx", "fsdp")),
            P("section", ("ctx", "fsdp")),
            P("section", None),
        ),
        check_vma=False,
    )
```

time: 3830 us -> 1170 us (0.31)
  waiting for transfers between devices: 2310 us -> 437 us
  matrix products: 733 us -> 146 us
  local copies, waits for them, and re-layouts: 382 us -> 126 us
  Pallas kernels: 0 us -> 128 us
  other arithmetic: 243 us -> 140 us
  starting transfers between devices: 8.85 us -> 84.2 us
  loops' own time: 41.8 us -> 0 us
    reduce_scatter x7 -> x6, waiting for transfers between devices: 1390 us -> 0.12 us  [scatter_rows(): lax.psum_scatter(column.reshape(-1, cols), 'ctx', scatter_dimension=0, ti...]
    all_gather x10 -> x6, waiting for transfers between devices: 811 us -> 80.4 us  [gather_rows(): lax.all_gather(shard, 'ctx', axis=0, tiled=True)]
    dot_general x138 -> x24, matrix products: 733 us -> 146 us  [the longest x8 54.8 us: nt_dot(): lax.dot_general(a, b, (((1,), (1,)), ((), ())), preferred_element_type=F32)]
    ppermute x4 -> x67, waiting for transfers between devices: 8.42 us -> 356 us  [the longest x15 168 us: from_y(): return lax.ppermute(value, 'fsdp', pairs)]
    pallas_call x0 -> x4, Pallas kernels: none -> 128 us  [the longest x2 70.6 us: attend_backward(): pl.pallas_call(lambda *refs: attend_backward_kernel(head_dim, *refs), gri...]
    unnamed x25 -> x12, waiting for transfers between devices: 99.6 us -> 0.7 us
    dynamic_slice x121 -> x14, local copies, waits for them, and re-layouts: 101 us -> 5.96 us  [the longest x1 3.1 us: part_of(): lax.dynamic_index_in_dim(in_weight[0].reshape(-1, chips, 2, ff_split), wh...]
    ppermute x4 -> x67, starting transfers between devices: 6.91 us -> 83.1 us  [the longest x6 28.1 us: from_sequences(): lax.ppermute(sent, 'ctx', pairs)]
  transfers between devices with their start and end apart: 25 -> 79, of which waited for: 20 -> 26; matrix products, arithmetic and copies ran while one was open for 19% -> 27% of each run, Pallas kernels for 0% -> 11%
where the time goes in v1:
time: 1170 us; the launch traced here: 1150 us
  waiting for transfers between devices  437 us (37%)
  matrix products  146 us (12%)
  other arithmetic  140 us (12%)
  Pallas kernels  128 us (11%)
  local copies, waits for them, and re-layouts  126 us (11%)
  starting transfers between devices  84.2 us (7%)
  blocking collectives  76.1 us (7%)
  between operations  18.1 us (2%)
    ppermute x15, waiting for transfers between devices, from_y(): return lax.ppermute(value, 'fsdp', pairs)  168 us
    ppermute x15, waiting for transfers between devices, from_x(): return lax.ppermute(value, 'fsdp', pairs)  106 us
    all_gather x6, waiting for transfers between devices, gather_rows(): lax.all_gather(shard, 'ctx', axis=0, tiled=True)  80.4 us
    unnamed x1, blocking collectives  76.1 us
    pallas_call x2, Pallas kernels, attend_backward(): pl.pallas_call(lambda *refs: attend_backward_kernel(head_dim, *refs), gri...  70.6 us
    pallas_call x2, Pallas kernels, attend_forward(): pl.pallas_call(lambda *refs: attend_forward_kernel(head_dim, *refs), grid...  57 us
    dot_general x8, matrix products, nt_dot(): lax.dot_general(a, b, (((1,), (1,)), ((), ())), preferred_element_type=F32)  54.8 us
    dot_general x8, matrix products, nn_dot(): lax.dot_general(a, b, (((1,), (0,)), ((), ())), preferred_element_type=F32)  46.7 us
  transfers between devices with their start and end apart: 79, of which 26 were waited for; matrix products, arithmetic and copies ran while one was open for 27% of the time, Pallas kernels for 11%

profile of v1, /device:TPU:0, one launch (start us, length us, event | category | flops | bytes accessed | tf_op | source)
XLA Modules:
  0.0 1154.9 jit_solution(3048226198847606708)
XLA Ops:
  13.4 3.1 dynamic-slice_reduce_fusion.1
  24.1 4.8 collective-permute-start.9
  36.7 10.8 collective-permute-done
  47.5 17.9 %collective-permute-done.1 = bf16[128,1024]{1,0:T(8,128)(2,1)S(1)} collective-permute-done((bf16[128,1024]{1,0:T(8,128)(2,1)S(1)}, bf16[128,1024]{1,0:T(8,128)(2,1)S(1)}, u32[]{:S(2)}, u32[]{:S(2)}) %collective-permute-start.1) | collective-permute-done | bytes 262176 | tf_op jit(solution)/shard_map/ppermute | solution.py:304
  75.7 10.9 all-gather.9.cloned.1.call-done
  89.5 26.1 %all-gather.17.cloned.1.call-done = bf16[512,1024]{1,0:T(8,128)(2,1)} async-done(((bf16[128,1024]{1,0:T(8,128)(2,1)}), bf16[512,1024]{1,0:T(8,128)(2,1)}) %all-gather.17.cloned.1.call-update) | async-done | bytes 1048592 | tf_op jit(solution)/shard_map/all_gather | solution.py:252
  126.9 17.6 %all-gather.11.cloned.1.call-done = bf16[512,1024]{1,0:T(8,128)(2,1)} async-done(((bf16[128,1024]{1,0:T(8,128)(2,1)}), bf16[512,1024]{1,0:T(8,128)(2,1)}) %all-gather.11.cloned.1.call-update) | async-done | bytes 1048592 | tf_op jit(solution)/shard_map/all_gather | solution.py:252
  148.2 25.8 %all-gather.13.cloned.1.call-done = bf16[256,2048]{1,0:T(8,128)(2,1)} async-done(((bf16[64,2048]{1,0:T(8,128)(2,1)}), bf16[256,2048]{1,0:T(8,128)(2,1)}) %all-gather.13.cloned.1.call-update) | async-done | bytes 1048592 | tf_op jit(solution)/shard_map/all_gather | solution.py:252
  188.6 36.1 %collective-permute-done.7 = bf16[4,64,2048]{2,1,0:T(8,128)(2,1)S(1)} collective-permute-done((bf16[4,64,2048]{2,1,0:T(8,128)(2,1)}, bf16[4,64,2048]{2,1,0:T(8,128)(2,1)S(1)}, u32[]{:S(2)}, u32[]{:S(2)}) %collective-permute-start.7) | collective-permute-done | bytes 1048608 | tf_op jit(solution)/shard_map/ppermute | solution.py:233
  225.1 3.9 add_convert_fusion.1
  229.3 28.5 %attend_forward.2 = (bf16[1024,512]{1,0:T(8,128)(2,1)S(1)}, f32[4,2,1024]{2,1,0:T(2,128)S(1)}) custom-call(bf16[1024,512]{1,0:T(8,128)(2,1)S(1)} %get-tuple-element.128.refs_0_, bf16[1024,512]{1,0:T(8,128)(2,1)S(1)} %get-tuple-element.127.refs_1_, bf16[1024,512]{1,0:T(8,128)(2,1)S(1)} %get-tuple-element.126.refs_2_, s32[1024,1]{1,0:T(8,128)S(1)} %fusion.56.refs_3_.refs_5_, ...), custom_call_target="tpu_custom_call" | custom-call | flops 8589934592 | bytes 4194304 | tf_op jit(solution)/shard_map/attend_forward/pallas_call | solution.py:119
  272.2 11.8 %collective-permute-done.24 = bf16[4,64,2048]{2,1,0:T(8,128)(2,1)S(1)} collective-permute-done((bf16[4,64,2048]{2,1,0:T(8,128)(2,1)S(1)}, bf16[4,64,2048]{2,1,0:T(8,128)(2,1)S(1)}, u32[]{:S(2)}, u32[]{:S(2)}) %collective-permute-start.24) | collective-permute-done | bytes 1048608 | tf_op jit(solution)/shard_map/ppermute | solution.py:233
  285.4 20.6 %collective-permute-done.21 = bf16[4,128,1024]{2,1,0:T(8,128)(2,1)S(1)} collective-permute-done((bf16[4,128,1024]{2,1,0:T(8,128)(2,1)}, bf16[4,128,1024]{2,1,0:T(8,128)(2,1)S(1)}, u32[]{:S(2)}, u32[]{:S(2)}) %collective-permute-start.21) | collective-permute-done | bytes 1048608 | tf_op jit(solution)/shard_map/ppermute | solution.py:233
  314.0 10.8 multiply_convert_fusion.3
  324.8 10.1 fusion.107
  335.2 20.3 %collective-permute-done.25 = bf16[4,64,2048]{2,1,0:T(8,128)(2,1)S(1)} collective-permute-done((bf16[4,64,2048]{2,1,0:T(8,128)(2,1)S(1)}, bf16[4,64,2048]{2,1,0:T(8,128)(2,1)S(1)}, u32[]{:S(2)}, u32[]{:S(2)}) %collective-permute-start.25) | collective-permute-done | bytes 1048608 | tf_op jit(solution)/shard_map/ppermute | solution.py:226
  369.3 4.8 fusion.96
  375.4 3.0 copy-done.58
  378.4 3.6 add_convert_fusion
  383.1 28.5 %attend_forward.3 = (bf16[1024,512]{1,0:T(8,128)(2,1)S(1)}, f32[4,2,1024]{2,1,0:T(2,128)S(1)}) custom-call(bf16[1024,512]{1,0:T(8,128)(2,1)S(1)} %get-tuple-element.125.refs_0_, bf16[1024,512]{1,0:T(8,128)(2,1)S(1)} %get-tuple-element.124.refs_1_, bf16[1024,512]{1,0:T(8,128)(2,1)S(1)} %get-tuple-element.123.refs_2_, s32[1024,1]{1,0:T(8,128)S(1)} %copy-done.11, ...), custom_call_target="tpu_custom_call" | custom-call | flops 8589934592 | bytes 4194304 | tf_op jit(solution)/shard_map/attend_forward/pallas_call | solution.py:119
  421.7 20.7 %collective-permute-done.30 = bf16[4,64,2048]{2,1,0:T(8,128)(2,1)S(1)} collective-permute-done((bf16[4,64,2048]{2,1,0:T(8,128)(2,1)}, bf16[4,64,2048]{2,1,0:T(8,128)(2,1)S(1)}, u32[]{:S(2)}, u32[]{:S(2)}) %collective-permute-start.30) | collective-permute-done | bytes 1048608 | tf_op jit(solution)/shard_map/ppermute | solution.py:233
  445.2 7.8 multiply_convert_fusion.2
  453.0 8.0 fusion.109
  463.2 3.7 collective-permute-done.41
  472.9 3.1 copy-done.32
  476.0 4.5 fusion.31
  482.2 10.3 convert_reduce_fusion
  492.6 6.7 fusion.110
  499.5 8.5 convolution_convert_fusion.4
  512.4 4.6 multiply_reduce_fusion
  520.8 35.3 %attend_backward.2 = (bf16[1024,512]{1,0:T(8,128)(2,1)S(1)}, bf16[1024,512]{1,0:T(8,128)(2,1)S(1)}, bf16[1024,512]{1,0:T(8,128)(2,1)S(1)}) custom-call(bf16[1024,512]{1,0:T(8,128)(2,1)S(1)} %get-tuple-element.125.refs_0_, bf16[1024,512]{1,0:T(8,128)(2,1)S(1)} %get-tuple-element.124.refs_1_, bf16[1024,512]{1,0:T(8,128)(2,1)} %copy-done.9, ...), custom_call_target="tpu_custom_call" | custom-call | flops 21474836480 | bytes 8388608 | tf_op jit(solution)/shard_map/attend_backward/pallas_call | solution.py:152
  558.3 5.8 fusion.111
  565.3 10.2 convolution_convert_fusion.2
  575.4 3.9 fusion.27
  580.7 11.4 fusion.16
  593.7 13.3 %convert_reduce_fusion.1 = (f32[2048]{0:T(1024)S(1)}, bf16[1024,2048]{1,0:T(8,128)(2,1)}) fusion(f32[1024,2048]{1,0:T(8,128)} %get-tuple-element.212, f32[2048]{0:T(1024)S(1)} %bitcast.502, bf16[2048,1024]{1,0:T(8,128)(2,1)} %bitcast.60, f32[1024,1024]{1,0:T(8,128)S(1)} %get-tuple-element.105), kind=kOutput, calls=%fused_computation.13 | convolution fusion | flops 4327471104 | bytes 20987904 | tf_op jit(solution)/shard_map/dot_general | solution.py:19
  607.0 7.5 convolution_convert_fusion.5
  630.1 3.6 fusion.17
  634.0 5.5 collective-permute-done.35
  640.3 23.4 %collective-permute-start.37 = (bf16[256,1024]{1,0:T(8,128)(2,1)}, bf16[256,1024]{1,0:T(8,128)(2,1)S(1)}, u32[]{:S(2)}, u32[]{:S(2)}) collective-permute-start(bf16[256,1024]{1,0:T(8,128)(2,1)} %get-tuple-element.139), channel_id=1, source_target_pairs={{12,0},{0,4},{4,8},{8,12},{13,1},{1,5},{5,9},{9,13},{14,2},{2,6},{... | collective-permute-start | bytes 1572872 | tf_op jit(solution)/shard_map/ppermute | solution.py:316
  665.6 21.7 %collective-permute-done.59 = bf16[4,64,2048]{2,1,0:T(8,128)(2,1)} collective-permute-done((bf16[4,64,2048]{2,1,0:T(8,128)(2,1)}, bf16[4,64,2048]{2,1,0:T(8,128)(2,1)}, u32[]{:S(2)}, u32[]{:S(2)}) %collective-permute-start.59) | collective-permute-done | bytes 1048608 | tf_op jit(solution)/shard_map/ppermute | solution.py:233
  690.3 3.2 fusion.28
  696.0 35.4 %collective-permute-done.63 = bf16[4,2,128,1024]{3,2,1,0:T(8,128)(2,1)} collective-permute-done((bf16[4,2,128,1024]{3,2,1,0:T(8,128)(2,1)}, bf16[4,2,128,1024]{3,2,1,0:T(8,128)(2,1)}, u32[]{:S(2)}, u32[]{:S(2)}) %collective-permute-start.63) | collective-permute-done | bytes 2097184 | tf_op jit(solution)/shard_map/ppermute | solution.py:233
  739.7 8.2 convolution_convert_fusion.3
  752.0 3.9 convolution_convert_fusion
  757.2 8.0 maximum_maximum_fusion.1
  776.5 28.3 %collective-permute-done.61 = bf16[4,2,128,1024]{3,2,1,0:T(8,128)(2,1)} collective-permute-done((bf16[4,2,128,1024]{3,2,1,0:T(8,128)(2,1)}, bf16[4,2,128,1024]{3,2,1,0:T(8,128)(2,1)}, u32[]{:S(2)}, u32[]{:S(2)}) %collective-permute-start.61) | collective-permute-done | bytes 2097184 | tf_op jit(solution)/shard_map/ppermute | solution.py:226
  804.8 3.2 fusion.26
  809.3 8.7 fusion.112
  818.0 21.6 %collective-permute-done.62 = bf16[4,128,1024]{2,1,0:T(8,128)(2,1)S(1)} collective-permute-done((bf16[4,128,1024]{2,1,0:T(8,128)(2,1)S(1)}, bf16[4,128,1024]{2,1,0:T(8,128)(2,1)S(1)}, u32[]{:S(2)}, u32[]{:S(2)}) %collective-permute-start.62) | collective-permute-done | bytes 1048608 | tf_op jit(solution)/shard_map/ppermute | solution.py:233
  841.1 3.0 fusion.29
  848.8 5.1 broadcast_select_fusion.13
  854.7 17.1 %collective-permute-done.54 = bf16[4,64,2048]{2,1,0:T(8,128)(2,1)} collective-permute-done((bf16[4,64,2048]{2,1,0:T(8,128)(2,1)}, bf16[4,64,2048]{2,1,0:T(8,128)(2,1)}, u32[]{:S(2)}, u32[]{:S(2)}) %collective-permute-start.54) | collective-permute-done | bytes 1048608 | tf_op jit(solution)/shard_map/ppermute | solution.py:226
  874.7 6.8 multiply_reduce_fusion.1
  886.9 35.3 %attend_backward.3 = (bf16[1024,512]{1,0:T(8,128)(2,1)S(1)}, bf16[1024,512]{1,0:T(8,128)(2,1)S(1)}, bf16[1024,512]{1,0:T(8,128)(2,1)S(1)}) custom-call(bf16[1024,512]{1,0:T(8,128)(2,1)S(1)} %copy-done.8, bf16[1024,512]{1,0:T(8,128)(2,1)S(1)} %copy-done.6, bf16[1024,512]{1,0:T(8,128)(2,1)} %copy-done.4, bf16[1024,512]{1,0:T(8,128)(2,1)} %convolution_convert_fusion.8.refs_3_, ...), custom_call_target="tpu_custom_call" | custom-call | flops 21474836480 | bytes 8388608 | tf_op jit(solution)/shard_map/attend_backward/pallas_call | solution.py:152
  923.9 3.8 convolution_convert_fusion.1
  927.9 8.3 maximum_maximum_fusion
  941.5 5.3 fusion.113
  948.5 38.6 %collective-permute-done.50 = bf16[4,2,64,2048]{3,2,1,0:T(8,128)(2,1)} collective-permute-done((bf16[4,2,64,2048]{3,2,1,0:T(8,128)(2,1)}, bf16[4,2,64,2048]{3,2,1,0:T(8,128)(2,1)}, u32[]{:S(2)}, u32[]{:S(2)}) %collective-permute-start.50) | collective-permute-done | bytes 2097184 | tf_op jit(solution)/shard_map/ppermute | solution.py:226
  987.2 3.0 fusion.30
  993.8 76.1 %all-reduce.1 = (f32[16,768]{1,0:T(8,128)S(1)}, f32[5]{0:T(128)S(1)}) all-reduce(f32[16,768]{1,0:T(8,128)S(1)} %select_add_fusion, f32[5]{0:T(128)S(1)} %pad_maximum_fusion.13), channel_id=8, replica_groups=mesh['section'=2,'ctx'=4,'fsdp'=4] {'ctx','fsdp'}, use_global_device_ids=true, to_apply=%region_38.39.clone | all-reduce | flops 12293 | bytes 98344
  1069.8 5.6 fusion.45
  1088.3 12.7 %collective-permute-done.46 = bf16[256,1024]{1,0:T(8,128)(2,1)S(1)} collective-permute-done((bf16[256,1024]{1,0:T(8,128)(2,1)S(1)}, bf16[256,1024]{1,0:T(8,128)(2,1)S(1)}, u32[]{:S(2)}, u32[]{:S(2)}) %collective-permute-start.46) | collective-permute-done | bytes 524320 | tf_op jit(solution)/shard_map/ppermute | solution.py:316
  1103.1 27.7 %collective-permute-done.47 = bf16[256,1024]{1,0:T(8,128)(2,1)} collective-permute-done((bf16[256,1024]{1,0:T(8,128)(2,1)}, bf16[256,1024]{1,0:T(8,128)(2,1)}, u32[]{:S(2)}, u32[]{:S(2)}) %collective-permute-start.47) | collective-permute-done | bytes 524320 | tf_op jit(solution)/shard_map/ppermute | solution.py:316
  (662 shorter events, 249.5 us)
Async XLA Ops:
  7.2 63.8 %all-gather.7.cloned.1.call-start = ((), (), s32[]{:S(2)}) async-start(), calls=%async_computation.6 | async-start | bytes 1310720 | tf_op jit(solution)/shard_map/all_gather | solution.py:252
  11.9 74.7 %all-gather.9.cloned.1.call-start = ((), (), s32[]{:S(2)}) async-start(), calls=%async_computation.7 | async-start | bytes 1310720 | tf_op jit(solution)/shard_map/all_gather | solution.py:252
  19.0 96.6 %all-gather.17.cloned.1.call-start = ((), (), s32[]{:S(2)}) async-start(), calls=%async_computation.11 | async-start | bytes 1310720 | tf_op jit(solution)/shard_map/all_gather | solution.py:252
  21.7 122.8 %all-gather.11.cloned.1.call-start = ((), (), s32[]{:S(2)}) async-start(), calls=%async_computation.8 | async-start | bytes 1310720 | tf_op jit(solution)/shard_map/all_gather | solution.py:252
  22.3 151.7 %all-gather.13.cloned.1.call-start = ((), (), s32[]{:S(2)}) async-start(), calls=%async_computation.9 | async-start | bytes 1310720 | tf_op jit(solution)/shard_map/all_gather | solution.py:252
  23.6 42.9 %collective-permute-start.8 = (f32[12,1024]{1,0:T(8,128)S(1)}, f32[12,1024]{1,0:T(8,128)}, u32[]{:S(2)}, u32[]{:S(2)}) collective-permute-start(f32[12,1024]{1,0:T(8,128)S(1)} %pad_maximum_fusion.10), channel_id=1, source_target_pairs={{0,16},{16,0},{1,17},{17,1},{2,18},{18,2},{3,19},{19,3},{4,20},{20... | collective-permute-start | bytes 147464 | tf_op jit(solution)/shard_map/ppermute | solution.py:236
  31.5 15.9 %collective-permute-start = (bf16[128,1024]{1,0:T(8,128)(2,1)S(1)}, bf16[128,1024]{1,0:T(8,128)(2,1)S(1)}, u32[]{:S(2)}, u32[]{:S(2)}) collective-permute-start(bf16[128,1024]{1,0:T(8,128)(2,1)S(1)} %get-tuple-element.147), channel_id=1, source_target_pairs={{0,12},{4,0},{8,4},{12,8},{1,13},{5,1},{9,5},{13,9},{2,14},{6,2},{... | collective-permute-start | bytes 786440 | tf_op jit(solution)/shard_map/ppermute | solution.py:304
  34.4 30.9 %collective-permute-start.1 = (bf16[128,1024]{1,0:T(8,128)(2,1)S(1)}, bf16[128,1024]{1,0:T(8,128)(2,1)S(1)}, u32[]{:S(2)}, u32[]{:S(2)}) collective-permute-start(bf16[128,1024]{1,0:T(8,128)(2,1)S(1)} %get-tuple-element.146), channel_id=1, source_target_pairs={{0,8},{4,12},{8,0},{12,4},{1,9},{5,13},{9,1},{13,5},{2,10},{6,14},... | collective-permute-start | bytes 786440 | tf_op jit(solution)/shard_map/ppermute | solution.py:304
  35.7 29.7 %collective-permute-start.2 = (bf16[128,1024]{1,0:T(8,128)(2,1)S(1)}, bf16[128,1024]{1,0:T(8,128)(2,1)}, u32[]{:S(2)}, u32[]{:S(2)}) collective-permute-start(bf16[128,1024]{1,0:T(8,128)(2,1)S(1)} %get-tuple-element.145), channel_id=1, source_target_pairs={{0,4},{4,8},{8,12},{12,0},{1,5},{5,9},{9,13},{13,1},{2,6},{6,10},{... | collective-permute-start | bytes 786440 | tf_op jit(solution)/shard_map/ppermute | solution.py:304
  36.6 328.5 %all-gather.15.cloned.1.call-start = ((), (), s32[]{:S(2)}) async-start(), calls=%async_computation.10 | async-start | bytes 1310720 | tf_op jit(solution)/shard_map/all_gather | solution.py:252
  69.0 1032.1 %reduce-scatter.13.cloned.1.call-start = ((), (), s32[]{:S(2)}) async-start(), calls=%async_computation.15 | async-start | bytes 1310720 | tf_op jit(solution)/shard_map/reduce_scatter | solution.py:291
  71.0 105.1 %collective-permute-start.5 = (bf16[4,64,2048]{2,1,0:T(8,128)(2,1)}, bf16[4,64,2048]{2,1,0:T(8,128)(2,1)}, u32[]{:S(2)}, u32[]{:S(2)}) collective-permute-start(bf16[4,64,2048]{2,1,0:T(8,128)(2,1)} %bitcast.20), channel_id=1, source_target_pairs={{1,0},{0,1},{3,2},{2,3},{5,4},{4,5},{7,6},{6,7},{9,8},{8,9},{11,10... | collective-permute-start | bytes 3145736 | tf_op jit(solution)/shard_map/ppermute | solution.py:226
  74.2 112.3 %collective-permute-start.6 = (bf16[4,64,2048]{2,1,0:T(8,128)(2,1)}, bf16[4,64,2048]{2,1,0:T(8,128)(2,1)}, u32[]{:S(2)}, u32[]{:S(2)}) collective-permute-start(bf16[4,64,2048]{2,1,0:T(8,128)(2,1)} %bitcast.20), channel_id=1, source_target_pairs={{2,0},{3,1},{0,2},{1,3},{6,4},{7,5},{4,6},{5,7},{10,8},{11,9},{8,1... | collective-permute-start | bytes 3145736 | tf_op jit(solution)/shard_map/ppermute | solution.py:233
  86.6 96.1 %collective-permute-start.15 = (bf16[4,64,2048]{2,1,0:T(8,128)(2,1)}, bf16[4,64,2048]{2,1,0:T(8,128)(2,1)}, u32[]{:S(2)}, u32[]{:S(2)}) collective-permute-start(bf16[4,64,2048]{2,1,0:T(8,128)(2,1)} %bitcast.428), channel_id=1, source_target_pairs={{1,0},{0,1},{3,2},{2,3},{5,4},{4,5},{7,6},{6,7},{9,8},{8,9},{11,10... | collective-permute-start | bytes 3145736 | tf_op jit(solution)/shard_map/ppermute | solution.py:226
  88.1 174.5 %collective-permute-start.16 = (bf16[4,64,2048]{2,1,0:T(8,128)(2,1)}, bf16[4,64,2048]{2,1,0:T(8,128)(2,1)}, u32[]{:S(2)}, u32[]{:S(2)}) collective-permute-start(bf16[4,64,2048]{2,1,0:T(8,128)(2,1)} %bitcast.429), channel_id=1, source_target_pairs={{2,0},{3,1},{0,2},{1,3},{6,4},{7,5},{4,6},{5,7},{10,8},{11,9},{8,1... | collective-permute-start | bytes 3145736 | tf_op jit(solution)/shard_map/ppermute | solution.py:233
  115.6 63.4 %collective-permute-start.31 = (bf16[4,128,1024]{2,1,0:T(8,128)(2,1)}, bf16[4,128,1024]{2,1,0:T(8,128)(2,1)}, u32[]{:S(2)}, u32[]{:S(2)}) collective-permute-start(bf16[4,128,1024]{2,1,0:T(8,128)(2,1)} %bitcast.434), channel_id=1, source_target_pairs={{1,0},{0,1},{3,2},{2,3},{5,4},{4,5},{7,6},{6,7},{9,8},{8,9},{11,10... | collective-permute-start | bytes 3145736 | tf_op jit(solution)/shard_map/ppermute | solution.py:226
  176.1 84.9 %collective-permute-start.32 = (bf16[4,128,1024]{2,1,0:T(8,128)(2,1)S(1)}, bf16[4,128,1024]{2,1,0:T(8,128)(2,1)S(1)}, u32[]{:S(2)}, u32[]{:S(2)}) collective-permute-start(bf16[4,128,1024]{2,1,0:T(8,128)(2,1)S(1)} %bitcast.436), channel_id=1, source_target_pairs={{2,0},{3,1},{0,2},{1,3},{6,4},{7,5},{4,6},{5,7},{10,8},{11,9},{8,1... | collective-permute-start | bytes 3145736 | tf_op jit(solution)/shard_map/ppermute | solution.py:233
  179.0 45.7 %collective-permute-start.7 = (bf16[4,64,2048]{2,1,0:T(8,128)(2,1)}, bf16[4,64,2048]{2,1,0:T(8,128)(2,1)S(1)}, u32[]{:S(2)}, u32[]{:S(2)}) collective-permute-start(bf16[4,64,2048]{2,1,0:T(8,128)(2,1)} %collective-permute-done.5), channel_id=1, source_target_pairs={{2,0},{3,1},{0,2},{1,3},{6,4},{7,5},{4,6},{5,7},{10,8},{11,9},{8,1... | collective-permute-start | bytes 3145736 | tf_op jit(solution)/shard_map/ppermute | solution.py:233
  182.7 81.4 %collective-permute-start.19 = (bf16[4,128,1024]{2,1,0:T(8,128)(2,1)S(1)}, bf16[4,128,1024]{2,1,0:T(8,128)(2,1)}, u32[]{:S(2)}, u32[]{:S(2)}) collective-permute-start(bf16[4,128,1024]{2,1,0:T(8,128)(2,1)S(1)} %bitcast.432), channel_id=1, source_target_pairs={{1,0},{0,1},{3,2},{2,3},{5,4},{4,5},{7,6},{6,7},{9,8},{8,9},{11,10... | collective-permute-start | bytes 3145736 | tf_op jit(solution)/shard_map/ppermute | solution.py:226
  186.6 80.4 %collective-permute-start.20 = (bf16[4,128,1024]{2,1,0:T(8,128)(2,1)S(1)}, bf16[4,128,1024]{2,1,0:T(8,128)(2,1)}, u32[]{:S(2)}, u32[]{:S(2)}) collective-permute-start(bf16[4,128,1024]{2,1,0:T(8,128)(2,1)S(1)} %bitcast.433), channel_id=1, source_target_pairs={{2,0},{3,1},{0,2},{1,3},{6,4},{7,5},{4,6},{5,7},{10,8},{11,9},{8,1... | collective-permute-start | bytes 3145736 | tf_op jit(solution)/shard_map/ppermute | solution.py:233
  225.0 32.9 %collective-permute-start.12 = (bf16[512,512]{1,0:T(8,128)(2,1)S(1)}, bf16[512,512]{1,0:T(8,128)(2,1)S(1)}, u32[]{:S(2)}, u32[]{:S(2)}) collective-permute-start(bf16[512,512]{1,0:T(8,128)(2,1)S(1)} %constant_dynamic-slice_fusion.7), channel_id=1, source_target_pairs={{0,16},{16,0},{1,17},{17,1},{2,18},{18,2},{3,19},{19,3},{4,20},{20... | collective-permute-start | bytes 1572872 | tf_op jit(solution)/shard_map/ppermute | solution.py:236
  257.9 26.0 %collective-permute-start.24 = (bf16[4,64,2048]{2,1,0:T(8,128)(2,1)S(1)}, bf16[4,64,2048]{2,1,0:T(8,128)(2,1)S(1)}, u32[]{:S(2)}, u32[]{:S(2)}) collective-permute-start(bf16[4,64,2048]{2,1,0:T(8,128)(2,1)S(1)} %bitcast.441), channel_id=1, source_target_pairs={{2,0},{3,1},{0,2},{1,3},{6,4},{7,5},{4,6},{5,7},{10,8},{11,9},{8,1... | collective-permute-start | bytes 3145736 | tf_op jit(solution)/shard_map/ppermute | solution.py:233
  261.0 51.0 %collective-permute-start.13 = (bf16[1024,1024]{1,0:T(8,128)(2,1)S(1)}, bf16[1024,1024]{1,0:T(8,128)(2,1)S(1)}, u32[]{:S(2)}, u32[]{:S(2)}) collective-permute-start(bf16[1024,1024]{1,0:T(8,128)(2,1)S(1)} %get-tuple-element.209), channel_id=1, source_target_pairs={{0,16},{16,0},{1,17},{17,1},{2,18},{18,2},{3,19},{19,3},{4,20},{20... | collective-permute-start | bytes 6291464 | tf_op jit(solution)/shard_map/ppermute | solution.py:236
  262.6 44.9 %collective-permute-start.33 = (bf16[4,128,1024]{2,1,0:T(8,128)(2,1)S(1)}, bf16[4,128,1024]{2,1,0:T(8,128)(2,1)S(1)}, u32[]{:S(2)}, u32[]{:S(2)}) collective-permute-start(bf16[4,128,1024]{2,1,0:T(8,128)(2,1)S(1)} %collective-permute-done.32), channel_id=1, source_target_pairs={{1,0},{0,1},{3,2},{2,3},{5,4},{4,5},{7,6},{6,7},{9,8},{8,9},{11,10... | collective-permute-start | bytes 3145736 | tf_op jit(solution)/shard_map/ppermute | solution.py:226
  264.1 41.9 %collective-permute-start.21 = (bf16[4,128,1024]{2,1,0:T(8,128)(2,1)}, bf16[4,128,1024]{2,1,0:T(8,128)(2,1)S(1)}, u32[]{:S(2)}, u32[]{:S(2)}) collective-permute-start(bf16[4,128,1024]{2,1,0:T(8,128)(2,1)} %collective-permute-done.19), channel_id=1, source_target_pairs={{2,0},{3,1},{0,2},{1,3},{6,4},{7,5},{4,6},{5,7},{10,8},{11,9},{8,1... | collective-permute-start | bytes 3145736 | tf_op jit(solution)/shard_map/ppermute | solution.py:233
  266.9 44.0 %collective-permute-start.17 = (bf16[4,64,2048]{2,1,0:T(8,128)(2,1)}, bf16[4,64,2048]{2,1,0:T(8,128)(2,1)S(1)}, u32[]{:S(2)}, u32[]{:S(2)}) collective-permute-start(bf16[4,64,2048]{2,1,0:T(8,128)(2,1)} %collective-permute-done.16), channel_id=1, source_target_pairs={{1,0},{0,1},{3,2},{2,3},{5,4},{4,5},{7,6},{6,7},{9,8},{8,9},{11,10... | collective-permute-start | bytes 3145736 | tf_op jit(solution)/shard_map/ppermute | solution.py:226
  284.0 51.0 %collective-permute-start.23 = (bf16[4,64,2048]{2,1,0:T(8,128)(2,1)S(1)}, bf16[4,64,2048]{2,1,0:T(8,128)(2,1)S(1)}, u32[]{:S(2)}, u32[]{:S(2)}) collective-permute-start(bf16[4,64,2048]{2,1,0:T(8,128)(2,1)S(1)} %bitcast.442), channel_id=1, source_target_pairs={{1,0},{0,1},{3,2},{2,3},{5,4},{4,5},{7,6},{6,7},{9,8},{8,9},{11,10... | collective-permute-start | bytes 3145736 | tf_op jit(solution)/shard_map/ppermute | solution.py:226
  306.0 49.5 %collective-permute-start.25 = (bf16[4,64,2048]{2,1,0:T(8,128)(2,1)S(1)}, bf16[4,64,2048]{2,1,0:T(8,128)(2,1)S(1)}, u32[]{:S(2)}, u32[]{:S(2)}) collective-permute-start(bf16[4,64,2048]{2,1,0:T(8,128)(2,1)S(1)} %collective-permute-done.24), channel_id=1, source_target_pairs={{1,0},{0,1},{3,2},{2,3},{5,4},{4,5},{7,6},{6,7},{9,8},{8,9},{11,10... | collective-permute-start | bytes 3145736 | tf_op jit(solution)/shard_map/ppermute | solution.py:226
  335.0 33.8 %collective-permute-start.22 = (bf16[1024,1024]{1,0:T(8,128)(2,1)}, bf16[1024,1024]{1,0:T(8,128)(2,1)S(1)}, u32[]{:S(2)}, u32[]{:S(2)}) collective-permute-start(bf16[1024,1024]{1,0:T(8,128)(2,1)} %get-tuple-element.213), channel_id=1, source_target_pairs={{0,16},{16,0},{1,17},{17,1},{2,18},{18,2},{3,19},{19,3},{4,20},{20... | collective-permute-start | bytes 6291464 | tf_op jit(solution)/shard_map/ppermute | solution.py:236
  360.7 52.3 %collective-permute-start.38 = (bf16[128,1024]{1,0:T(8,128)(2,1)}, bf16[128,1024]{1,0:T(8,128)(2,1)}, u32[]{:S(2)}, u32[]{:S(2)}) collective-permute-start(bf16[128,1024]{1,0:T(8,128)(2,1)} %get-tuple-element.137), channel_id=1, source_target_pairs={{0,12},{4,0},{8,4},{12,8},{1,13},{5,1},{9,5},{13,9},{2,14},{6,2},{... | collective-permute-start | bytes 786440 | tf_op jit(solution)/shard_map/ppermute | solution.py:304
  362.9 52.4 %collective-permute-start.39 = (bf16[128,1024]{1,0:T(8,128)(2,1)}, bf16[128,1024]{1,0:T(8,128)(2,1)}, u32[]{:S(2)}, u32[]{:S(2)}) collective-permute-start(bf16[128,1024]{1,0:T(8,128)(2,1)} %get-tuple-element.136), channel_id=1, source_target_pairs={{0,8},{4,12},{8,0},{12,4},{1,9},{5,13},{9,1},{13,5},{2,10},{6,14},... | collective-permute-start | bytes 786440 | tf_op jit(solution)/shard_map/ppermute | solution.py:304
  364.0 97.0 %collective-permute-start.40 = (bf16[128,1024]{1,0:T(8,128)(2,1)S(1)}, bf16[128,1024]{1,0:T(8,128)(2,1)}, u32[]{:S(2)}, u32[]{:S(2)}) collective-permute-start(bf16[128,1024]{1,0:T(8,128)(2,1)S(1)} %get-tuple-element.135), channel_id=1, source_target_pairs={{0,4},{4,8},{8,12},{12,0},{1,5},{5,9},{9,13},{13,1},{2,6},{6,10},{... | collective-permute-start | bytes 786440 | tf_op jit(solution)/shard_map/ppermute | solution.py:304
  365.1 52.0 %collective-permute-start.28 = (bf16[4,64,2048]{2,1,0:T(8,128)(2,1)}, bf16[4,64,2048]{2,1,0:T(8,128)(2,1)}, u32[]{:S(2)}, u32[]{:S(2)}) collective-permute-start(bf16[4,64,2048]{2,1,0:T(8,128)(2,1)} %bitcast.437), channel_id=1, source_target_pairs={{1,0},{0,1},{3,2},{2,3},{5,4},{4,5},{7,6},{6,7},{9,8},{8,9},{11,10... | collective-permute-start | bytes 3145736 | tf_op jit(solution)/shard_map/ppermute | solution.py:226
  368.7 51.6 %collective-permute-start.29 = (bf16[4,64,2048]{2,1,0:T(8,128)(2,1)}, bf16[4,64,2048]{2,1,0:T(8,128)(2,1)}, u32[]{:S(2)}, u32[]{:S(2)}) collective-permute-start(bf16[4,64,2048]{2,1,0:T(8,128)(2,1)} %bitcast.438), channel_id=1, source_target_pairs={{2,0},{3,1},{0,2},{1,3},{6,4},{7,5},{4,6},{5,7},{10,8},{11,9},{8,1... | collective-permute-start | bytes 3145736 | tf_op jit(solution)/shard_map/ppermute | solution.py:233
  413.0 29.5 %collective-permute-start.27 = (bf16[1024,1024]{1,0:T(8,128)(2,1)S(1)}, bf16[1024,1024]{1,0:T(8,128)(2,1)S(1)}, u32[]{:S(2)}, u32[]{:S(2)}) collective-permute-start(bf16[1024,1024]{1,0:T(8,128)(2,1)S(1)} %get-tuple-element.215), channel_id=1, source_target_pairs={{0,16},{16,0},{1,17},{17,1},{2,18},{18,2},{3,19},{19,3},{4,20},{20... | collective-permute-start | bytes 6291464 | tf_op jit(solution)/shard_map/ppermute | solution.py:236
  417.1 25.3 %collective-permute-start.30 = (bf16[4,64,2048]{2,1,0:T(8,128)(2,1)}, bf16[4,64,2048]{2,1,0:T(8,128)(2,1)S(1)}, u32[]{:S(2)}, u32[]{:S(2)}) collective-permute-start(bf16[4,64,2048]{2,1,0:T(8,128)(2,1)} %collective-permute-done.28), channel_id=1, source_target_pairs={{2,0},{3,1},{0,2},{1,3},{6,4},{7,5},{4,6},{5,7},{10,8},{11,9},{8,1... | collective-permute-start | bytes 3145736 | tf_op jit(solution)/shard_map/ppermute | solution.py:233
  509.5 65.9 %collective-permute-start.58 = (bf16[4,2,64,2048]{3,2,1,0:T(8,128)(2,1)}, bf16[4,2,64,2048]{3,2,1,0:T(8,128)(2,1)}, u32[]{:S(2)}, u32[]{:S(2)}) collective-permute-start(bf16[4,2,64,2048]{3,2,1,0:T(8,128)(2,1)} %dynamic-slice_bitcast_fusion.2), channel_id=1, source_target_pairs={{1,0},{0,1},{3,2},{2,3},{5,4},{4,5},{7,6},{6,7},{9,8},{8,9},{11,10... | collective-permute-start | bytes 6291464 | tf_op jit(solution)/shard_map/ppermute | solution.py:226
  616.0 74.3 %collective-permute-start.56 = (bf16[4,2,64,2048]{3,2,1,0:T(8,128)(2,1)}, bf16[4,2,64,2048]{3,2,1,0:T(8,128)(2,1)}, u32[]{:S(2)}, u32[]{:S(2)}) collective-permute-start(bf16[4,2,64,2048]{3,2,1,0:T(8,128)(2,1)} %dynamic-slice_bitcast_fusion.3), channel_id=1, source_target_pairs={{2,0},{3,1},{0,2},{1,3},{6,4},{7,5},{4,6},{5,7},{10,8},{11,9},{8,1... | collective-permute-start | bytes 6291464 | tf_op jit(solution)/shard_map/ppermute | solution.py:233
  618.3 69.0 %collective-permute-start.59 = (bf16[4,64,2048]{2,1,0:T(8,128)(2,1)}, bf16[4,64,2048]{2,1,0:T(8,128)(2,1)}, u32[]{:S(2)}, u32[]{:S(2)}) collective-permute-start(bf16[4,64,2048]{2,1,0:T(8,128)(2,1)} %dynamic-slice_bitcast_fusion.8), channel_id=1, source_target_pairs={{2,0},{3,1},{0,2},{1,3},{6,4},{7,5},{4,6},{5,7},{10,8},{11,9},{8,1... | collective-permute-start | bytes 3145736 | tf_op jit(solution)/shard_map/ppermute | solution.py:233
  624.0 15.5 %collective-permute-start.35 = (bf16[256,1024]{1,0:T(8,128)(2,1)}, bf16[256,1024]{1,0:T(8,128)(2,1)S(1)}, u32[]{:S(2)}, u32[]{:S(2)}) collective-permute-start(bf16[256,1024]{1,0:T(8,128)(2,1)} %get-tuple-element.141), channel_id=1, source_target_pairs={{4,0},{8,4},{12,8},{0,12},{5,1},{9,5},{13,9},{1,13},{6,2},{10,6},{... | collective-permute-start | bytes 1572872 | tf_op jit(solution)/shard_map/ppermute | solution.py:316
  628.3 103.1 %collective-permute-start.63 = (bf16[4,2,128,1024]{3,2,1,0:T(8,128)(2,1)}, bf16[4,2,128,1024]{3,2,1,0:T(8,128)(2,1)}, u32[]{:S(2)}, u32[]{:S(2)}) collective-permute-start(bf16[4,2,128,1024]{3,2,1,0:T(8,128)(2,1)} %dynamic-slice_bitcast_fusion), channel_id=1, source_target_pairs={{2,0},{3,1},{0,2},{1,3},{6,4},{7,5},{4,6},{5,7},{10,8},{11,9},{8,1... | collective-permute-start | bytes 6291464 | tf_op jit(solution)/shard_map/ppermute | solution.py:233
  633.9 60.3 %collective-permute-start.36 = (bf16[256,1024]{1,0:T(8,128)(2,1)}, bf16[256,1024]{1,0:T(8,128)(2,1)}, u32[]{:S(2)}, u32[]{:S(2)}) collective-permute-start(bf16[256,1024]{1,0:T(8,128)(2,1)} %get-tuple-element.140), channel_id=1, source_target_pairs={{8,0},{12,4},{0,8},{4,12},{9,1},{13,5},{1,9},{5,13},{10,2},{14,6},... | collective-permute-start | bytes 1572872 | tf_op jit(solution)/shard_map/ppermute | solution.py:316
  640.3 132.7 %collective-permute-start.37 = (bf16[256,1024]{1,0:T(8,128)(2,1)}, bf16[256,1024]{1,0:T(8,128)(2,1)S(1)}, u32[]{:S(2)}, u32[]{:S(2)}) collective-permute-start(bf16[256,1024]{1,0:T(8,128)(2,1)} %get-tuple-element.139), channel_id=1, source_target_pairs={{12,0},{0,4},{4,8},{8,12},{13,1},{1,5},{5,9},{9,13},{14,2},{2,6},{... | collective-permute-start | bytes 1572872 | tf_op jit(solution)/shard_map/ppermute | solution.py:316
  690.2 410.9 %reduce-scatter.11.cloned.1.call-start = ((), (), s32[]{:S(2)}) async-start(), calls=%async_computation.14 | async-start | bytes 1310720 | tf_op jit(solution)/shard_map/reduce_scatter | solution.py:291
  693.6 44.3 %collective-permute-start.57 = (bf16[4,64,2048]{2,1,0:T(8,128)(2,1)S(1)}, bf16[4,64,2048]{2,1,0:T(8,128)(2,1)S(1)}, u32[]{:S(2)}, u32[]{:S(2)}) collective-permute-start(bf16[4,64,2048]{2,1,0:T(8,128)(2,1)S(1)} %dynamic-slice_bitcast_fusion.9), channel_id=1, source_target_pairs={{1,0},{0,1},{3,2},{2,3},{5,4},{4,5},{7,6},{6,7},{9,8},{8,9},{11,10... | collective-permute-start | bytes 3145736 | tf_op jit(solution)/shard_map/ppermute | solution.py:226
  735.1 35.0 %collective-permute-start.64 = (bf16[4,128,1024]{2,1,0:T(8,128)(2,1)}, bf16[4,128,1024]{2,1,0:T(8,128)(2,1)}, u32[]{:S(2)}, u32[]{:S(2)}) collective-permute-start(bf16[4,128,1024]{2,1,0:T(8,128)(2,1)} %dynamic-slice_bitcast_fusion.6), channel_id=1, source_target_pairs={{1,0},{0,1},{3,2},{2,3},{5,4},{4,5},{7,6},{6,7},{9,8},{8,9},{11,10... | collective-permute-start | bytes 3145736 | tf_op jit(solution)/shard_map/ppermute | solution.py:226
  737.9 18.1 %collective-permute-start.52 = (bf16[512,512]{1,0:T(8,128)(2,1)}, bf16[512,512]{1,0:T(8,128)(2,1)}, u32[]{:S(2)}, u32[]{:S(2)}) collective-permute-start(bf16[512,512]{1,0:T(8,128)(2,1)} %constant_dynamic-slice_fusion), channel_id=1, source_target_pairs={{0,16},{16,0},{1,17},{17,1},{2,18},{18,2},{3,19},{19,3},{4,20},{20... | collective-permute-start | bytes 1572872 | tf_op jit(solution)/shard_map/ppermute | solution.py:236
  739.3 393.7 %reduce-scatter.17.cloned.1.call-start = ((), (), s32[]{:S(2)}) async-start(), calls=%async_computation.17 | async-start | bytes 1310720 | tf_op jit(solution)/shard_map/reduce_scatter | solution.py:291
  749.4 55.3 %collective-permute-start.61 = (bf16[4,2,128,1024]{3,2,1,0:T(8,128)(2,1)}, bf16[4,2,128,1024]{3,2,1,0:T(8,128)(2,1)}, u32[]{:S(2)}, u32[]{:S(2)}) collective-permute-start(bf16[4,2,128,1024]{3,2,1,0:T(8,128)(2,1)} %dynamic-slice_bitcast_fusion.1), channel_id=1, source_target_pairs={{1,0},{0,1},{3,2},{2,3},{5,4},{4,5},{7,6},{6,7},{9,8},{8,9},{11,10... | collective-permute-start | bytes 6291464 | tf_op jit(solution)/shard_map/ppermute | solution.py:226
  768.9 72.2 %collective-permute-start.53 = (bf16[4,2,64,2048]{3,2,1,0:T(8,128)(2,1)}, bf16[4,2,64,2048]{3,2,1,0:T(8,128)(2,1)}, u32[]{:S(2)}, u32[]{:S(2)}) collective-permute-start(bf16[4,2,64,2048]{3,2,1,0:T(8,128)(2,1)} %dynamic-slice_bitcast_fusion.4), channel_id=1, source_target_pairs={{2,0},{3,1},{0,2},{1,3},{6,4},{7,5},{4,6},{5,7},{10,8},{11,9},{8,1... | collective-permute-start | bytes 6291464 | tf_op jit(solution)/shard_map/ppermute | solution.py:233
  772.8 360.2 %reduce-scatter.15.cloned.1.call-start = ((), (), s32[]{:S(2)}) async-start(), calls=%async_computation.16 | async-start | bytes 1310720 | tf_op jit(solution)/shard_map/reduce_scatter | solution.py:291
  808.1 31.6 %collective-permute-start.62 = (bf16[4,128,1024]{2,1,0:T(8,128)(2,1)S(1)}, bf16[4,128,1024]{2,1,0:T(8,128)(2,1)S(1)}, u32[]{:S(2)}, u32[]{:S(2)}) collective-permute-start(bf16[4,128,1024]{2,1,0:T(8,128)(2,1)S(1)} %dynamic-slice_bitcast_fusion.7), channel_id=1, source_target_pairs={{2,0},{3,1},{0,2},{1,3},{6,4},{7,5},{4,6},{5,7},{10,8},{11,9},{8,1... | collective-permute-start | bytes 3145736 | tf_op jit(solution)/shard_map/ppermute | solution.py:233
  818.0 56.7 %collective-permute-start.44 = (bf16[1024,1024]{1,0:T(8,128)(2,1)}, bf16[1024,1024]{1,0:T(8,128)(2,1)}, u32[]{:S(2)}, u32[]{:S(2)}) collective-permute-start(bf16[1024,1024]{1,0:T(8,128)(2,1)} %get-tuple-element.225), channel_id=1, source_target_pairs={{0,16},{16,0},{1,17},{17,1},{2,18},{18,2},{3,19},{19,3},{4,20},{20... | collective-permute-start | bytes 6291464 | tf_op jit(solution)/shard_map/ppermute | solution.py:236
  841.1 294.6 %reduce-scatter.9.cloned.1.call-start = ((), (), s32[]{:S(2)}) async-start(), calls=%async_computation.13 | async-start | bytes 1310720 | tf_op jit(solution)/shard_map/reduce_scatter | solution.py:291
  846.6 25.1 %collective-permute-start.54 = (bf16[4,64,2048]{2,1,0:T(8,128)(2,1)}, bf16[4,64,2048]{2,1,0:T(8,128)(2,1)}, u32[]{:S(2)}, u32[]{:S(2)}) collective-permute-start(bf16[4,64,2048]{2,1,0:T(8,128)(2,1)} %dynamic-slice_bitcast_fusion.10), channel_id=1, source_target_pairs={{1,0},{0,1},{3,2},{2,3},{5,4},{4,5},{7,6},{6,7},{9,8},{8,9},{11,10... | collective-permute-start | bytes 3145736 | tf_op jit(solution)/shard_map/ppermute | solution.py:226
  874.7 261.1 %reduce-scatter.7.cloned.1.call-start = ((), (), s32[]{:S(2)}) async-start(), calls=%async_computation.12 | async-start | bytes 1310720 | tf_op jit(solution)/shard_map/reduce_scatter | solution.py:291
  940.0 47.2 %collective-permute-start.50 = (bf16[4,2,64,2048]{3,2,1,0:T(8,128)(2,1)}, bf16[4,2,64,2048]{3,2,1,0:T(8,128)(2,1)}, u32[]{:S(2)}, u32[]{:S(2)}) collective-permute-start(bf16[4,2,64,2048]{3,2,1,0:T(8,128)(2,1)} %dynamic-slice_bitcast_fusion.5), channel_id=1, source_target_pairs={{1,0},{0,1},{3,2},{2,3},{5,4},{4,5},{7,6},{6,7},{9,8},{8,9},{11,10... | collective-permute-start | bytes 6291464 | tf_op jit(solution)/shard_map/ppermute | solution.py:226
  946.8 123.0 %collective-permute-start.45 = (bf16[1024,1024]{1,0:T(8,128)(2,1)}, bf16[1024,1024]{1,0:T(8,128)(2,1)}, u32[]{:S(2)}, u32[]{:S(2)}) collective-permute-start(bf16[1024,1024]{1,0:T(8,128)(2,1)} %get-tuple-element.227), channel_id=1, source_target_pairs={{0,16},{16,0},{1,17},{17,1},{2,18},{18,2},{3,19},{19,3},{4,20},{20... | collective-permute-start | bytes 6291464 | tf_op jit(solution)/shard_map/ppermute | solution.py:236
  948.0 45.8 %collective-permute-start.66 = (f32[16,768]{1,0:T(8,128)S(1)}, f32[16,768]{1,0:T(8,128)S(1)}, u32[]{:S(2)}, u32[]{:S(2)}) collective-permute-start(f32[16,768]{1,0:T(8,128)S(1)} %broadcast_select_fusion.12), channel_id=1, source_target_pairs={{0,16},{16,0},{1,17},{17,1},{2,18},{18,2},{3,19},{19,3},{4,20},{20... | collective-permute-start | bytes 147464 | tf_op jit(solution)/shard_map/ppermute | solution.py:236
  992.5 84.4 %collective-permute-start.51 = (bf16[4,64,2048]{2,1,0:T(8,128)(2,1)}, bf16[4,64,2048]{2,1,0:T(8,128)(2,1)}, u32[]{:S(2)}, u32[]{:S(2)}) collective-permute-start(bf16[4,64,2048]{2,1,0:T(8,128)(2,1)} %dynamic-slice_bitcast_fusion.11), channel_id=1, source_target_pairs={{2,0},{3,1},{0,2},{1,3},{6,4},{7,5},{4,6},{5,7},{10,8},{11,9},{8,1... | collective-permute-start | bytes 3145736 | tf_op jit(solution)/shard_map/ppermute | solution.py:233
  1076.9 24.1 %collective-permute-start.46 = (bf16[256,1024]{1,0:T(8,128)(2,1)S(1)}, bf16[256,1024]{1,0:T(8,128)(2,1)S(1)}, u32[]{:S(2)}, u32[]{:S(2)}) collective-permute-start(bf16[256,1024]{1,0:T(8,128)(2,1)S(1)} %get-tuple-element.131), channel_id=1, source_target_pairs={{4,0},{8,4},{12,8},{0,12},{5,1},{9,5},{13,9},{1,13},{6,2},{10,6},{... | collective-permute-start | bytes 1572872 | tf_op jit(solution)/shard_map/ppermute | solution.py:316
  1086.5 44.3 %collective-permute-start.47 = (bf16[256,1024]{1,0:T(8,128)(2,1)}, bf16[256,1024]{1,0:T(8,128)(2,1)}, u32[]{:S(2)}, u32[]{:S(2)}) collective-permute-start(bf16[256,1024]{1,0:T(8,128)(2,1)} %get-tuple-element.130), channel_id=1, source_target_pairs={{8,0},{12,4},{0,8},{4,12},{9,1},{13,5},{1,9},{5,13},{10,2},{14,6},... | collective-permute-start | bytes 1572872 | tf_op jit(solution)/shard_map/ppermute | solution.py:316
  1086.5 45.4 %collective-permute-start.48 = (bf16[256,1024]{1,0:T(8,128)(2,1)}, bf16[256,1024]{1,0:T(8,128)(2,1)}, u32[]{:S(2)}, u32[]{:S(2)}) collective-permute-start(bf16[256,1024]{1,0:T(8,128)(2,1)} %get-tuple-element.129), channel_id=1, source_target_pairs={{12,0},{0,4},{4,8},{8,12},{13,1},{1,5},{5,9},{9,13},{14,2},{2,6},{... | collective-permute-start | bytes 1572872 | tf_op jit(solution)/shard_map/ppermute | solution.py:316
  1103.1 32.3 %collective-permute-start.60 = (f32[64,2048]{1,0:T(8,128)}, f32[64,2048]{1,0:T(8,128)S(1)}, u32[]{:S(2)}, u32[]{:S(2)}) collective-permute-start(f32[64,2048]{1,0:T(8,128)} %convert_select_fusion.2), channel_id=1, source_target_pairs={{0,16},{16,0},{1,17},{17,1},{2,18},{18,2},{3,19},{19,3},{4,20},{20... | collective-permute-start | bytes 1572872 | tf_op jit(solution)/shard_map/ppermute | solution.py:236
  (150 other events, 3220.1 us)
Sparse Core Ops, SparseCore 0:
  12.0 33.5 all-gather.6
  47.8 38.7 all-gather.8
  88.2 27.4 all-gather.16
  117.0 27.4 all-gather.10
  146.5 27.4 all-gather.12
  175.9 27.4 all-gather.14
  690.3 26.3 reduce-scatter.12
  739.4 27.4 reduce-scatter.10
  772.9 26.9 reduce-scatter.16
  841.2 27.3 reduce-scatter.14
  874.8 27.3 reduce-scatter.8
  1080.1 45.3 reduce-scatter.6

commit v2 on v1

v2 whole, which is shorter than its diff:
```python
import math

import jax
import jax.numpy as jnp
from jax import lax
from jax.experimental import pallas as pl
from jax.experimental.pallas import tpu as pltpu
from jax.sharding import PartitionSpec as P

HEADS = 16
NORM_EPS = 1e-05
MASKED = -1e30
BF = jnp.bfloat16


def priced(flops, bytes_accessed, transcendentals):
    share = 0.35
    return pl.CostEstimate(
        flops=int(share * flops),
        bytes_accessed=int(share * bytes_accessed),
        transcendentals=int(share * transcendentals),
    )


F32 = jnp.float32
MIB = 1024 * 1024


def nt_dot(a, b):
    return lax.dot_general(a, b, (((1,), (1,)), ((), ())), preferred_element_type=F32)


def nn_dot(a, b):
    return lax.dot_general(a, b, (((1,), (0,)), ((), ())), preferred_element_type=F32)


def tn_dot(a, b):
    return lax.dot_general(a, b, (((0,), (0,)), ((), ())), preferred_element_type=F32)


def mask_bias(code_k, seg_q):
    shape = (code_k.shape[0], seg_q.shape[1])
    key_at = lax.broadcasted_iota(jnp.int32, shape, 0)
    query_at = lax.broadcasted_iota(jnp.int32, shape, 1)
    allowed = (code_k == seg_q) | (key_at == query_at)
    return jnp.where(allowed, 0.0, MASKED)


def head_masked(block, head, head_dim):
    lane = lax.broadcasted_iota(jnp.int32, block.shape, 1)
    inside = (lane >= head * head_dim) & (lane < (head + 1) * head_dim)
    return jnp.where(inside, block, jnp.zeros_like(block))


def attend_forward_kernel(head_dim, q_ref, k_ref, v_ref, code_ref, seg_ref, o_ref, lse_ref, bias_ref):
    per = q_ref.shape[1] // head_dim

    @pl.when(pl.program_id(0) == 0)
    def _():
        bias_ref[...] = mask_bias(code_ref[...], seg_ref[...])

    query = (q_ref[...].astype(F32) * head_dim ** (-0.5)).astype(BF)
    keys = k_ref[...]
    values_t = v_ref[...].T
    outs, tops = [], []
    for head in range(per):
        scores = nt_dot(keys, head_masked(query, head, head_dim)) + bias_ref[...]
        top = jnp.max(scores, axis=0, keepdims=True)
        expo = jnp.exp(scores - top)
        total = jnp.sum(expo, axis=0, keepdims=True)
        part = nn_dot(values_t[head * head_dim : (head + 1) * head_dim], expo.astype(BF))
        outs.append(part / total)
        tops.append(top + jnp.log(total))
    o_ref[...] = jnp.concatenate(outs, axis=0).T.astype(BF)
    lse_ref[0] = jnp.concatenate(tops, axis=0)


def attend_backward_kernel(
    head_dim, q_ref, k_ref, v_ref, do_ref, lse_ref, code_ref, seg_ref, dq_ref, dk_ref, dv_ref, bias_ref
):
    rows = q_ref.shape[0]
    block = min(512, rows)
    per = q_ref.shape[1] // head_dim
    scale = head_dim ** (-0.5)

    @pl.when(pl.program_id(0) == 0)
    def _():
        bias_ref[...] = mask_bias(code_ref[...], seg_ref[...])

    keys = k_ref[...]
    keys_t = keys.T
    values = v_ref[...]
    dk, dv = None, None
    for first in range(0, rows, block):
        span = slice(first, first + block)
        query = (q_ref[span, :].astype(F32) * scale).astype(BF)
        grad_out = do_ref[span, :]
        outs = []
        for head in range(per):
            query_h = head_masked(query, head, head_dim)
            grad_h = head_masked(grad_out, head, head_dim)
            scores = nt_dot(keys, query_h) + bias_ref[:, span]
            probs = jnp.exp(scores - lse_ref[0, head : head + 1, span])
            grad_probs = nt_dot(values, grad_h)
            inner = jnp.sum(probs * grad_probs, axis=0, keepdims=True)
            grad_scores = (probs * (grad_probs - inner)).astype(BF)
            dv_part = nn_dot(probs.astype(BF), grad_h)
            dk_part = nn_dot(grad_scores, query_h)
            dv = dv_part if dv is None else dv + dv_part
            dk = dk_part if dk is None else dk + dk_part
            outs.append(nn_dot(keys_t[head * head_dim : (head + 1) * head_dim], grad_scores) * scale)
        dq_ref[span, :] = jnp.concatenate(outs, axis=0).T.astype(BF)
    dk_ref[...] = dk.astype(dk_ref.dtype)
    dv_ref[...] = dv.astype(dv_ref.dtype)


def attend_forward(q, k, v, code_k, seg_q, head_dim):
    rows, width = q.shape
    keys = k.shape[0]
    pair = 2 * head_dim
    cost = priced(
        flops=16 * rows * keys * width, bytes_accessed=8 * rows * width, transcendentals=rows * keys * width // head_dim
    )
    return pl.pallas_call(
        lambda *refs: attend_forward_kernel(head_dim, *refs),
        grid=(width // pair,),
        in_specs=[
            pl.BlockSpec((rows, pair), lambda h: (0, h)),
            pl.BlockSpec((keys, pair), lambda h: (0, h)),
            pl.BlockSpec((keys, pair), lambda h: (0, h)),
            pl.BlockSpec((keys, 1), lambda h: (0, 0)),
            pl.BlockSpec((1, rows), lambda h: (0, 0)),
        ],
        out_specs=[
            pl.BlockSpec((rows, pair), lambda h: (0, h)),
            pl.BlockSpec((1, 2, rows), lambda h: (h, 0, 0)),
        ],
        out_shape=[
            jax.ShapeDtypeStruct((rows, width), BF),
            jax.ShapeDtypeStruct((width // pair, 2, rows), F32),
        ],
        scratch_shapes=[pltpu.VMEM((keys, rows), F32)],
        compiler_params=pltpu.CompilerParams(vmem_limit_bytes=24 * MIB),
        cost_estimate=cost,
        name="attend_forward",
    )(q, k, v, code_k, seg_q)


def attend_backward(q, k, v, grad_out, lse, code_k, seg_q, head_dim, kv_type):
    rows, width = q.shape
    keys = k.shape[0]
    pair = 2 * head_dim
    cost = priced(
        flops=40 * rows * keys * width, bytes_accessed=16 * rows * width, transcendentals=rows * keys * width // head_dim
    )
    return pl.pallas_call(
        lambda *refs: attend_backward_kernel(head_dim, *refs),
        grid=(width // pair,),
        in_specs=[
            pl.BlockSpec((rows, pair), lambda h: (0, h)),
            pl.BlockSpec((keys, pair), lambda h: (0, h)),
            pl.BlockSpec((keys, pair), lambda h: (0, h)),
            pl.BlockSpec((rows, pair), lambda h: (0, h)),
            pl.BlockSpec((1, 2, rows), lambda h: (h, 0, 0)),
            pl.BlockSpec((keys, 1), lambda h: (0, 0)),
            pl.BlockSpec((1, rows), lambda h: (0, 0)),
        ],
        out_specs=[
            pl.BlockSpec((rows, pair), lambda h: (0, h)),
            pl.BlockSpec((keys, pair), lambda h: (0, h)),
            pl.BlockSpec((keys, pair), lambda h: (0, h)),
        ],
        out_shape=[
            jax.ShapeDtypeStruct((rows, width), BF),
            jax.ShapeDtypeStruct((keys, width), kv_type),
            jax.ShapeDtypeStruct((keys, width), kv_type),
        ],
        scratch_shapes=[pltpu.VMEM((keys, rows), F32)],
        compiler_params=pltpu.CompilerParams(vmem_limit_bytes=24 * MIB),
        cost_estimate=cost,
        name="attend_backward",
    )(q, k, v, grad_out, lse, code_k, seg_q)


def row_product(xs, w, transposed, rows_in, consts, outs, finish, name):
    rows = xs[0].shape[0]
    block = min(256, rows)
    widths = [x.shape[1] for x in xs]
    wide = w.shape[0] if transposed else w.shape[1]

    def body(*refs):
        refs = list(refs)
        x_refs = [refs.pop(0) for _ in xs]
        w_ref = refs.pop(0)
        row_refs = [refs.pop(0) for _ in rows_in]
        const_refs = [refs.pop(0) for _ in consts]
        total, first = None, 0
        for x_ref, depth in zip(x_refs, widths):
            if transposed:
                part = nt_dot(x_ref[...], w_ref[:, first : first + depth])
            else:
                part = nn_dot(x_ref[...], w_ref[first : first + depth, :])
            total = part if total is None else total + part
            first += depth
        results = finish(total, *[r[...] for r in row_refs], *[c[...] for c in const_refs])
        for out_ref, value in zip(refs, results):
            out_ref[...] = value.astype(out_ref.dtype)

    return pl.pallas_call(
        body,
        grid=(rows // block,),
        in_specs=[pl.BlockSpec((block, depth), lambda i: (i, 0)) for depth in widths]
        + [pl.BlockSpec(w.shape, lambda i: (0, 0))]
        + [pl.BlockSpec((block, r.shape[1]), lambda i: (i, 0)) for r in rows_in]
        + [pl.BlockSpec(c.shape, lambda i: (0, 0)) for c in consts],
        out_specs=[pl.BlockSpec((block, columns), lambda i: (i, 0)) for columns, _ in outs],
        out_shape=[jax.ShapeDtypeStruct((rows, columns), kind) for columns, kind in outs],
        compiler_params=pltpu.CompilerParams(vmem_limit_bytes=16 * MIB),
        cost_estimate=priced(
            flops=2 * rows * sum(widths) * wide,
            bytes_accessed=2 * (rows * sum(widths) + w.size) + sum(4 * rows * c for c, _ in outs),
            transcendentals=0,
        ),
        name=name,
    )(*xs, w, *rows_in, *consts)


def norm_rows_forward(part, other, before, live, table):
    rows, width = part.shape
    block = min(256, rows)

    def body(part_ref, other_ref, before_ref, live_ref, table_ref, unit_ref, inverse_ref, low_ref, sums_ref):
        start = before_ref[...].astype(F32)
        branch = part_ref[...].astype(F32) + other_ref[...].astype(F32) + table_ref[0:1, :]
        residual = start + branch
        centred = residual - jnp.mean(residual, axis=-1, keepdims=True)
        spread = jnp.mean(centred * centred, axis=-1, keepdims=True)
        inverse = lax.rsqrt(spread + NORM_EPS)
        unit = centred * inverse
        out = unit * table_ref[1:2, :] + table_ref[2:3, :]
        unit_ref[...] = unit.astype(BF)
        inverse_ref[...] = inverse
        low_ref[...] = out.astype(BF)
        real = live_ref[...]

        @pl.when(pl.program_id(0) == 0)
        def _():
            sums_ref[...] = jnp.zeros_like(sums_ref)

        sums_ref[0:1, :] += jnp.sum(real * start * start, axis=0, keepdims=True)
        sums_ref[1:2, :] += jnp.sum(real * branch * branch, axis=0, keepdims=True)
        sums_ref[2:3, :] += jnp.sum(real * out * out, axis=0, keepdims=True)

    by_row = pl.BlockSpec((block, width), lambda i: (i, 0))
    thin = pl.BlockSpec((block, 1), lambda i: (i, 0))
    fixed = pl.BlockSpec((8, width), lambda i: (0, 0))
    return pl.pallas_call(
        body,
        grid=(rows // block,),
        in_specs=[by_row, by_row, by_row, thin, fixed],
        out_specs=[by_row, thin, by_row, fixed],
        out_shape=[
            jax.ShapeDtypeStruct((rows, width), BF),
            jax.ShapeDtypeStruct((rows, 1), F32),
            jax.ShapeDtypeStruct((rows, width), BF),
            jax.ShapeDtypeStruct((8, width), F32),
        ],
        compiler_params=pltpu.CompilerParams(vmem_limit_bytes=12 * MIB),
        cost_estimate=priced(flops=20 * rows * width, bytes_accessed=10 * rows * width, transcendentals=rows),
        name="norm_forward",
    )(part, other, before, live, table)


def norm_rows_backward(terms, unit, inverse, gain, rounded):
    rows, width = unit.shape
    block = min(256, rows)

    def body(*refs):
        refs = list(refs)
        grad = sum([refs.pop(0)[...].astype(F32) for _ in terms])
        unit_ref, inverse_ref, gain_ref = refs[:3]
        low_ref, sums_ref = refs[3:5]
        if rounded:
            refs[5][...] = grad.astype(BF)
            grad = grad.astype(BF).astype(F32)
        unit_rows = unit_ref[...].astype(F32)
        scaled = grad * gain_ref[...]
        result = inverse_ref[...] * (
            scaled
            - jnp.mean(scaled, axis=-1, keepdims=True)
            - unit_rows * jnp.mean(scaled * unit_rows, axis=-1, keepdims=True)
        )
        low = result.astype(BF)
        low_ref[...] = low

        @pl.when(pl.program_id(0) == 0)
        def _():
            sums_ref[...] = jnp.zeros_like(sums_ref)

        sums_ref[0:1, :] += jnp.sum(grad * unit_rows, axis=0, keepdims=True)
        sums_ref[1:2, :] += jnp.sum(grad, axis=0, keepdims=True)
        sums_ref[2:3, :] += jnp.sum(low.astype(F32), axis=0, keepdims=True)

    by_row = pl.BlockSpec((block, width), lambda i: (i, 0))
    thin = pl.BlockSpec((block, 1), lambda i: (i, 0))
    fixed = pl.BlockSpec((8, width), lambda i: (0, 0))
    low_shape = jax.ShapeDtypeStruct((rows, width), BF)
    return pl.pallas_call(
        body,
        grid=(rows // block,),
        in_specs=[by_row] * len(terms) + [by_row, thin, pl.BlockSpec((1, width), lambda i: (0, 0))],
        out_specs=[by_row, fixed] + [by_row] * rounded,
        out_shape=[low_shape, jax.ShapeDtypeStruct((8, width), F32)] + [low_shape] * rounded,
        compiler_params=pltpu.CompilerParams(vmem_limit_bytes=12 * MIB),
        cost_estimate=priced(flops=20 * rows * width, bytes_accessed=10 * rows * width, transcendentals=0),
        name="norm_backward",
    )(*terms, unit, inverse, gain)


def gelu_pair(values):
    cdf = 0.5 * (1.0 + lax.erf(values * (2.0**-0.5)))
    density = jnp.exp(-0.5 * values * values) * ((2.0 * math.pi) ** -0.5)
    return values * cdf, cdf + values * density


class Place:
    def __init__(self):
        self.section = lax.axis_index("section")
        self.ctx = lax.axis_index("ctx")
        fsdp = lax.axis_index("fsdp")
        self.nz = lax.axis_size("ctx")
        self.nf = lax.axis_size("fsdp")
        side = math.isqrt(self.nf)
        self.nx = side if side * side == self.nf else self.nf
        self.ny = self.nf // self.nx
        self.y = fsdp // self.nx
        self.x = fsdp % self.nx

    def from_x(self, value, steps):
        pairs = []
        for f in range(self.nf):
            y, x = divmod(f, self.nx)
            pairs.append((y * self.nx + (x + steps) % self.nx, f))
        return lax.ppermute(value, "fsdp", pairs)

    def from_y(self, value, steps):
        pairs = []
        for f in range(self.nf):
            y, x = divmod(f, self.nx)
            pairs.append((((y + steps) % self.ny) * self.nx + x, f))
        return lax.ppermute(value, "fsdp", pairs)

    def sibling(self, value):
        return lax.ppermute(value, "section", [(0, 1), (1, 0)])

    def in_order(self, own, other, axis):
        first = self.section == 0
        return jnp.concatenate([jnp.where(first, own, other), jnp.where(first, other, own)], axis=axis)


def place_rotated(pieces, first, count):
    out = jnp.zeros((count,) + pieces[0].shape, pieces[0].dtype)
    for r, piece in enumerate(pieces):
        out = lax.dynamic_update_index_in_dim(out, piece, (first + r) % count, 0)
    return out


def tie(*trees):
    return lax.optimization_barrier(trees)


class Gather:
    def __init__(self, place, shard):
        self.place, self.shard = place, shard

    def along_z(self):
        rows, cols = self.shard.shape
        column = lax.all_gather(self.shard, "ctx", axis=0, tiled=True)
        return column.reshape(self.place.nz, rows, cols)

    def first(self, column):
        place = self.place
        from_x = [place.from_x(column, r) for r in range(1, place.nx)]
        from_y = [place.from_y(column, r) for r in range(1, place.ny)]
        return (from_x, from_y)

    def second(self, got):
        place = self.place
        from_x, from_y = got
        half = self.shard.shape[1] // 2
        left = [[place.from_y(piece[..., :half], r) for piece in from_x] for r in range(1, place.ny)]
        right = [[place.from_x(piece[..., half:], r) for r in range(1, place.nx)] for piece in from_y]
        return (left, right)

    def whole(self, column, got, more, split):
        place = self.place
        from_x, from_y = got
        left, right = more
        nz, rows, cols = column.shape
        nx, ny, nf = place.nx, place.ny, place.nf
        half = cols // 2
        diagonal = [(ry, rx) for ry in range(1, ny) for rx in range(1, nx)]
        pieces = [column] + from_x + from_y
        places = [(0, 0)] + [(0, r) for r in range(1, nx)] + [(r, 0) for r in range(1, ny)]
        lefts = [left[ry - 1][rx - 1] for ry, rx in diagonal]
        rights = [right[ry - 1][rx - 1] for ry, rx in diagonal]
        at = jnp.stack([place.y, place.x]).astype(jnp.int32)

        def assemble(at_ref, *refs):
            outs = refs[len(pieces) + 2 * len(diagonal) :]

            def index(ry, rx):
                return ((at_ref[0] + ry) % ny) * nx + (at_ref[1] + rx) % nx

            def put(to, first, value):
                last = first + value.shape[-1]
                if first < split:
                    stop = min(last, split)
                    outs[0][0, to, :, first:stop] = value[:, : stop - first]
                if last > split:
                    start = max(first, split)
                    outs[1][0, to, :, start - split : last - split] = value[:, start - first :]

            for at_piece, ref in zip(places, refs):
                put(index(*at_piece), 0, ref[0])
            for k, at_piece in enumerate(diagonal):
                put(index(*at_piece), 0, refs[len(pieces) + k][0])
                put(index(*at_piece), half, refs[len(pieces) + len(diagonal) + k][0])

        widths = [split] + [cols - split] * (split < cols)
        out = pl.pallas_call(
            assemble,
            grid_spec=pltpu.PrefetchScalarGridSpec(
                num_scalar_prefetch=1,
                grid=(nz,),
                in_specs=[pl.BlockSpec((1, rows, cols), lambda z, at_ref: (z, 0, 0))] * len(pieces)
                + [pl.BlockSpec((1, rows, half), lambda z, at_ref: (z, 0, 0))] * (2 * len(diagonal)),
                out_specs=[pl.BlockSpec((1, nf, rows, w), lambda z, at_ref: (z, 0, 0, 0)) for w in widths],
            ),
            out_shape=[jax.ShapeDtypeStruct((nz, nf, rows, w), column.dtype) for w in widths],
            compiler_params=pltpu.CompilerParams(vmem_limit_bytes=10 * MIB),
            cost_estimate=priced(flops=0, bytes_accessed=4 * nz * nf * rows * cols, transcendentals=0),
            name="assemble",
        )(at, *pieces, *lefts, *rights)
        return [part.reshape(nz * nf * rows, part.shape[-1]) for part in out]


def scatter_sizes(place):
    return place.nz, place.ny, place.nx


class Scatter:
    def __init__(self, place):
        self.place = place
        self.at = jnp.stack([place.y, place.x]).astype(jnp.int32)

    def product(self, x, grads, ready=None):
        place = self.place
        nz, ny, nx = scatter_sizes(place)
        tokens = x.shape[0]
        span = x.shape[1] // nz
        rows = span // (ny * nx)
        widths = [g.shape[1] for g in grads]
        extra = [] if ready is None else [ready]
        cols = sum(widths) + sum(e.shape[1] for e in extra)
        half = cols // 2

        def body(at_ref, x_ref, *refs):
            refs = list(refs)
            grad_refs = [refs.pop(0) for _ in grads]
            extra_refs = [refs.pop(0) for _ in extra]
            full_ref = refs.pop()
            left_refs = [refs.pop(0) for _ in range(ny)]
            right_refs = [refs.pop(0) for _ in range(nx)]
            sums_ref = refs.pop(0)
            turned = x_ref[...].T
            first = 0
            for ref, wide in zip(grad_refs, widths):
                for start in range(0, wide, 512):
                    stop = min(wide, start + 512)
                    value = nn_dot(turned, ref[:, start:stop]).astype(BF)
                    full_ref[:, :, :, first + start : first + stop] = value.reshape(ny, nx, rows, stop - start)
                first += wide
            for ref in extra_refs:
                full_ref[:, :, :, first:] = ref[...].reshape(ny, nx, rows, cols - first)
            for r, ref in enumerate(left_refs):
                ref[0] = full_ref[(at_ref[0] + r) % ny, :, :, :half]
            for r, ref in enumerate(right_refs):
                for y in range(ny):
                    ref[0, y] = full_ref[y, (at_ref[1] + r) % nx, :, half:]

            @pl.when(pl.program_id(0) == 0)
            def _():
                ones = jnp.ones((8, tokens), BF)
                first = 0
                for ref, wide in zip(grad_refs, widths):
                    sums_ref[:, first : first + wide] = nn_dot(ones, ref[...])
                    first += wide

        out = pl.pallas_call(
            body,
            grid_spec=pltpu.PrefetchScalarGridSpec(
                num_scalar_prefetch=1,
                grid=(nz,),
                in_specs=[pl.BlockSpec((tokens, span), lambda z, at_ref: (0, z))]
                + [pl.BlockSpec((tokens, wide), lambda z, at_ref: (0, 0)) for wide in widths]
                + [pl.BlockSpec((span, e.shape[1]), lambda z, at_ref: (z, 0)) for e in extra],
                out_specs=[pl.BlockSpec((1, nx, rows, half), lambda z, at_ref: (z, 0, 0, 0))] * ny
                + [pl.BlockSpec((1, ny, rows, half), lambda z, at_ref: (z, 0, 0, 0))] * nx
                + [pl.BlockSpec((8, sum(widths)), lambda z, at_ref: (0, 0))],
                scratch_shapes=[pltpu.VMEM((ny, nx, rows, cols), BF)],
            ),
            out_shape=[jax.ShapeDtypeStruct((nz, nx, rows, half), BF)] * ny
            + [jax.ShapeDtypeStruct((nz, ny, rows, half), BF)] * nx
            + [jax.ShapeDtypeStruct((8, sum(widths)), F32)],
            compiler_params=pltpu.CompilerParams(vmem_limit_bytes=20 * MIB),
            cost_estimate=priced(
                flops=2 * tokens * x.shape[1] * sum(widths),
                bytes_accessed=2 * (x.size + tokens * cols + x.shape[1] * cols),
                transcendentals=0,
            ),
            name="weight_grad",
        )(self.at, x, *grads, *extra)
        return (out[:ny], out[ny : ny + nx]), out[-1][0]

    def first(self, parts):
        place = self.place
        left, right = parts
        left = [left[0]] + [place.from_y(left[r], -r) for r in range(1, place.ny)]
        right = [right[0]] + [place.from_x(right[r], -r) for r in range(1, place.nx)]
        return (left, right)

    def second(self, parts):
        place = self.place
        nz, ny, nx = scatter_sizes(place)
        left, right = parts
        rows, half = left[0].shape[2:]

        def body(at_ref, *refs):
            left_in, right_in = refs[:ny], refs[ny : ny + nx]
            left_out, right_out = refs[ny + nx : ny + 2 * nx], refs[ny + 2 * nx :]
            for r, ref in enumerate(left_out):
                to = (at_ref[1] + r) % nx
                ref[...] = sum([piece[:, to].astype(F32) for piece in left_in]).astype(BF)
            for r, ref in enumerate(right_out):
                to = (at_ref[0] + r) % ny
                ref[...] = sum([piece[:, to].astype(F32) for piece in right_in]).astype(BF)

        out = pl.pallas_call(
            body,
            grid_spec=pltpu.PrefetchScalarGridSpec(
                num_scalar_prefetch=1,
                grid=(1,),
                in_specs=[pl.BlockSpec((nz, nx, rows, half), lambda z, at_ref: (0, 0, 0, 0))] * ny
                + [pl.BlockSpec((nz, ny, rows, half), lambda z, at_ref: (0, 0, 0, 0))] * nx,
                out_specs=[pl.BlockSpec((nz, rows, half), lambda z, at_ref: (0, 0, 0))] * (nx + ny),
            ),
            out_shape=[jax.ShapeDtypeStruct((nz, rows, half), BF)] * (nx + ny),
            compiler_params=pltpu.CompilerParams(vmem_limit_bytes=20 * MIB),
            cost_estimate=priced(flops=0, bytes_accessed=8 * nz * nx * ny * rows * half, transcendentals=0),
            name="scatter_add",
        )(self.at, *left, *right)
        left, right = out[:nx], out[nx:]
        left = [left[0]] + [place.from_x(left[r], -r) for r in range(1, nx)]
        right = [right[0]] + [place.from_y(right[r], -r) for r in range(1, ny)]
        return (left, right)

    def third(self, parts):
        left, right = parts
        both = [sum([piece.astype(F32) for piece in side]) for side in (left, right)]
        column = jnp.concatenate(both, axis=-1).astype(BF)
        return column.reshape(-1, column.shape[-1])

    def along_z(self, column):
        return lax.psum_scatter(column, "ctx", scatter_dimension=0, tiled=True)


def small_scatter(place, value):
    value = value.reshape(place.nz, place.ny, place.nx, -1)

    def pick(part, axis, index):
        return lax.dynamic_index_in_dim(part, index, axis, False)

    total = pick(value, 1, place.y)
    for r in range(1, place.ny):
        total = total + place.from_y(pick(value, 1, (place.y + r) % place.ny), -r)
    value = total
    total = pick(value, 1, place.x)
    for r in range(1, place.nx):
        total = total + place.from_x(pick(value, 1, (place.x + r) % place.nx), -r)
    value = total
    total = pick(value, 0, place.ctx)
    for r in range(1, place.nz):
        pairs = [(z, (z + r) % place.nz) for z in range(place.nz)]
        total = total + lax.ppermute(pick(value, 0, (place.ctx + r) % place.nz), "ctx", pairs)
    return total


def to_pieces(place, value, steps):
    count = value.shape[0]
    groups = place.nz // count
    piece_at = place.ctx % count
    pieces = []
    for k in steps:
        sent = lax.dynamic_index_in_dim(value, (piece_at + k) % count, 0, False)
        pairs = [(z, ((z % count + k) % count) * groups + z // count) for z in range(place.nz)]
        pieces.append(sent if all(a == b for a, b in pairs) else lax.ppermute(sent, "ctx", pairs))
    return pieces


def in_positions(place, pieces):
    count = len(pieces)
    kept_seq = place.ctx // (place.nz // count)
    return place_rotated([pieces[0]] + pieces[:0:-1], kept_seq, count)


def from_sequences(place, value, steps, section=None):
    count = value.shape[0]
    groups = place.nz // count
    kept_seq = place.ctx // groups
    pieces = []
    for k in steps:
        sent = lax.dynamic_index_in_dim(value, (kept_seq - k) % count, 0, False)
        pairs = [(((z % count + k) % count) * groups + z // count, z) for z in range(place.nz)]
        if any(a != b for a, b in pairs):
            if section is None:
                sent = lax.ppermute(sent, "ctx", pairs)
            else:
                first = section * place.nz
                sent = lax.ppermute(sent, ("section", "ctx"), [(first + a, first + b) for a, b in pairs])
        pieces.append(sent)
    return pieces


def half_rows(place, value):
    half = value.shape[1] // 2
    return lax.dynamic_slice_in_dim(value, place.section * half, half, 1)


def join_halves(place, moved):
    other = place.sibling(moved)
    first = place.section == 0
    both = jnp.stack([jnp.where(first, moved, other), jnp.where(first, other, moved)], axis=1)
    return both.reshape(-1, moved.shape[-1])


def on_device(
    tokens,
    segment_ids,
    valid_mask,
    cotangent,
    qkv_weight,
    out_proj,
    in_weight,
    out_weight,
    norm_gain,
    norm_shift,
    proj_bias,
    ff_bias,
):
    place = Place()
    section = place.section
    first_section = section == 0
    micro, seqs, local, width = tokens.shape
    count = micro * seqs
    groups = place.nz // count
    rows = count * local
    head_dim = width // HEADS
    half = width // 2
    ff_width = in_weight.shape[2]
    ff_half = ff_width // 2
    chips = place.nz * place.nf
    ff_rows = out_weight.shape[1]
    ff_split = ff_rows // 2

    def part_of(which):
        qkv_part = lax.dynamic_slice_in_dim(qkv_weight[0], which * half, half, 2)
        proj_part = lax.dynamic_slice_in_dim(out_proj[0], which * half, half, 1)
        in_part = lax.dynamic_index_in_dim(
            in_weight[0].reshape(-1, chips, 2, ff_split), which, 2, False
        ).reshape(-1, ff_half)
        out_part = lax.dynamic_slice_in_dim(out_weight[0], which * ff_split, ff_split, 0)
        attn_part = jnp.concatenate([qkv_part[0], qkv_part[1], qkv_part[2], proj_part], axis=1)
        return (attn_part, in_part, out_part)

    own_parts = part_of(section)
    sent_parts = part_of(1 - section)
    shards = [[None] * 3, [None] * 3]
    for index in range(3):
        other = place.sibling(sent_parts[index])
        shards[0][index] = jnp.where(first_section, own_parts[index], other)
        shards[1][index] = jnp.where(first_section, other, own_parts[index])
    gathers = [Gather(place, shard) for layer in shards for shard in layer]

    def proj_whole(columns):
        mine = lax.dynamic_slice_in_dim(columns, section * half, half, 0)
        sent = lax.dynamic_slice_in_dim(columns, (1 - section) * half, half, 0)
        return place.in_order(mine, place.sibling(sent), 1)

    small_own = jnp.concatenate([norm_gain[0], norm_shift[0], proj_bias[0], ff_bias[0].reshape(-1, width)], axis=0)
    small_other = place.sibling(small_own)
    small = [
        jnp.where(first_section, small_own, small_other),
        jnp.where(first_section, small_other, small_own),
    ]

    def layer_small(layer):
        table = small[layer]
        gains, shifts, biases = table[0:2], table[2:4], table[4:8]
        ff_all = table[8:].reshape(chips, 2, ff_split)
        ff_part = lax.dynamic_index_in_dim(ff_all, section, 1, False).reshape(-1)
        bias_q = lax.dynamic_slice_in_dim(biases[0], section * half, half, 0)
        bias_v = lax.dynamic_slice_in_dim(biases[1], section * half, half, 0)
        bias_qkv = jnp.concatenate([bias_q, jnp.zeros_like(bias_q), bias_v])
        return gains, shifts, biases, ff_part, bias_qkv

    ids = segment_ids.reshape(count, local) * 2 + (valid_mask.reshape(count, local) == 1).astype(jnp.int32)
    ids = in_positions(place, to_pieces(place, ids, range(count))).reshape(rows)
    seg_own = ids // 2
    valid_own = ids % 2

    def over_groups(value, steps):
        pairs = []
        for z in range(place.nz):
            q, g = divmod(z, groups)
            pairs.append((q * groups + (g + steps) % groups, z))
        return lax.ppermute(value, "ctx", pairs)

    def gather_groups(value):
        return jnp.concatenate([value] + [over_groups(value, r) for r in range(1, groups)], axis=0)

    def scatter_groups(value):
        parts = value.reshape(groups, rows, -1)
        total = parts[0]
        for r in range(1, groups):
            total = total + over_groups(parts[r].astype(BF), -r).astype(F32)
        return total.astype(BF)

    code_k = gather_groups(jnp.where(valid_own == 1, seg_own, -1))[:, None]
    seg_q = seg_own[None, :]
    live = valid_own.astype(F32)[:, None]

    token_half = half_rows(place, tokens.reshape(count, local, width))
    cot_half = half_rows(place, cotangent.reshape(count, local, width))
    smalls = [layer_small(layer) for layer in range(2)]

    def attention_in(layer_input, w_qkv, layer):
        q, k, v = row_product(
            [layer_input],
            w_qkv,
            False,
            [],
            [smalls[layer][4][None]],
            [(half, BF)] * 3,
            lambda total, bias: jnp.split(total + bias, 3, axis=1),
            "project_qkv",
        )
        if groups > 1:
            k, v = gather_groups(k), gather_groups(v)
        mixed, lse = attend_forward(q, k, v, code_k, seg_q, head_dim)
        return q, k, v, mixed, lse

    def norm_table(*given):
        return jnp.concatenate([row[None] for row in given] + [jnp.zeros((8 - len(given), width), F32)], axis=0)

    def to_width(xs, w, transposed, name):
        (low,) = row_product(xs, w, transposed, [], [], [(width, BF)], lambda total: (total,), name)
        return low

    def attention_norm(layer_input, low, layer):
        gains, shifts, biases = smalls[layer][:3]
        table = norm_table(biases[2], gains[0], shifts[0])
        return norm_rows_forward(low, place.sibling(low), layer_input, live, table)

    def feed_in(normed_low, w_in, layer):
        activated, slope = gelu_pair(nn_dot(normed_low, w_in) + smalls[layer][3])
        return activated.astype(BF), slope.astype(BF)

    def feed_norm(normed_low, low, layer):
        gains, shifts, biases = smalls[layer][:3]
        table = norm_table(biases[3], gains[1], shifts[1])
        return norm_rows_forward(low, place.sibling(low), normed_low, live, table)

    columns, got, whole, more = [None] * 6, [None] * 6, [None] * 6, [None] * 6
    token_pieces = to_pieces(place, token_half, range(2))
    columns[0] = gathers[0].along_z()
    columns[0], token_pieces, token_half, gathers[1].shard = tie(
        columns[0], token_pieces, token_half, gathers[1].shard
    )
    got[0] = gathers[0].first(columns[0])
    token_pieces += to_pieces(place, token_half, range(2, count))
    columns[1] = gathers[1].along_z()
    got[0], token_pieces = tie(got[0], token_pieces)
    more[0] = gathers[0].second(got[0])
    layer_input = join_halves(place, in_positions(place, token_pieces))
    more[0], layer_input, columns[1], gathers[2].shard = tie(more[0], layer_input, columns[1], gathers[2].shard)

    def arrived(step):
        split = 3 * half if step % 3 == 0 else columns[step].shape[2]
        whole[step] = gathers[step].whole(columns[step], got[step], more[step], split)

    arrived(0)
    inputs, attns, projs, outs = [layer_input, None], [None] * 2, [None] * 2, [None] * 2
    norms, feeds, ends = [None] * 2, [None] * 2, [None] * 2
    cot_pieces = []
    for step in range(6):
        layer = step // 3
        if step > 0:
            more[step] = gathers[step].second(got[step])
        if step + 1 < 6:
            got[step + 1] = gathers[step + 1].first(columns[step + 1])
        if step + 2 < 6:
            columns[step + 2] = gathers[step + 2].along_z()
        if step in (0, 4):
            if step == 4:
                ends[0] = feed_norm(norms[0][2], outs[0], 0)
                inputs[1] = ends[0][2]
            layer = step // 4
            w_qkv, columns_proj = whole[3 * layer]
            projs[layer] = proj_whole(columns_proj)
            attns[layer] = attention_in(inputs[layer], w_qkv, layer)
            outs[layer] = to_width([attns[layer][3]], projs[layer], False, "project_out")
        elif step == 1:
            norms[0] = attention_norm(inputs[0], outs[0], 0)
            cot_pieces += to_pieces(place, cot_half, range(2))
        elif step == 2:
            feeds[0] = feed_in(norms[0][2], whole[1][0], 0)
            cot_pieces += to_pieces(place, cot_half, range(2, count - 1))
        elif step == 3:
            outs[0] = to_width([feeds[0][0]], whole[2][0], False, "feed_out")
        elif step == 5:
            norms[1] = attention_norm(inputs[1], outs[1], 1)
            feeds[1] = feed_in(norms[1][2], whole[4][0], 1)
            cot_pieces += to_pieces(place, cot_half, [count - 1])
        shard = gathers[step + 3].shard if step + 3 < 6 else ()
        state = (inputs, attns, projs, outs, norms, feeds, ends, cot_pieces)
        got, more, columns, shard, state, cot_half = tie(got, more, columns, shard, state, cot_half)
        inputs, attns, projs, outs, norms, feeds, ends, cot_pieces = state
        if step + 3 < 6:
            gathers[step + 3].shard = shard
        if step > 0:
            arrived(step)

    outs[1] = to_width([feeds[1][0]], whole[5][0], False, "feed_out")
    outs[1], cot_pieces, norms = tie(outs[1], cot_pieces, norms)
    ends[1] = feed_norm(norms[1][2], outs[1], 1)
    terms = [join_halves(place, in_positions(place, cot_pieces))]

    scatter = Scatter(place)
    columns = [[None] * 3, [None] * 3]
    totals = [[None] * 3, [None] * 3]
    small_grads = [None, None]
    act_value = jnp.where(first_section, ends[0][2], ends[1][2]).reshape(count, local, width)
    attn_parts = back_one = grad_one = None
    act_back = []
    for layer in (1, 0):
        gains = smalls[layer][0]
        u = inputs[layer]
        q, k, v, mixed, lse = attns[layer]
        unit_one, inverse_one, normed_low, sums_one = norms[layer]
        activated, slope = feeds[layer]
        unit_two, inverse_two, output, sums_two = ends[layer]
        w_qkv = whole[3 * layer][0]
        w_proj, w_in, w_out = projs[layer], whole[3 * layer + 1][0], whole[3 * layer + 2][0]

        if layer == 0:
            columns[1][1] = scatter.third(in_parts)
        second = norm_rows_backward(terms, unit_two, inverse_two, gains[1:2], layer == 0)
        grad_ff, second_sums = second[:2]
        out_parts, _ = scatter.product(activated, [grad_ff])
        if layer == 1:
            out_parts, grad_ff, act_value = tie(out_parts, grad_ff, act_value)
            act_back += from_sequences(place, act_value, range(count - 1))
        else:
            grad_one = second[2].reshape(count, local, width)
            out_parts, grad_ff, grad_one, columns = tie(out_parts, grad_ff, grad_one, columns)
            totals[1][1] = scatter.along_z(columns[1][1])
            back_one = from_sequences(place, grad_one, range(2), 1)

        out_parts = scatter.first(out_parts)
        (grad_hidden,) = row_product(
            [grad_ff],
            w_out,
            True,
            [slope],
            [],
            [(ff_half, BF)],
            lambda total, slope: (total * slope.astype(F32),),
            "feed_out_back",
        )
        low = to_width([grad_hidden], w_in, True, "feed_in_back")
        low, grad_hidden, attn_parts = tie(low, grad_hidden, attn_parts)

        if layer == 0:
            attn_parts = scatter.second(attn_parts)
        other = place.sibling(low)
        in_parts, hidden_sums = scatter.product(normed_low, [grad_hidden])
        attn_parts, out_parts, in_parts, low, other = tie(attn_parts, out_parts, in_parts, low, other)

        if layer == 0:
            columns[1][0] = scatter.third(attn_parts)
        out_parts = scatter.second(out_parts)
        in_parts = scatter.first(in_parts)
        grad_branch, first_sums = norm_rows_backward(
            [grad_ff, low, other], unit_one, inverse_one, gains[0:1], False
        )
        (grad_mixed,) = row_product(
            [grad_branch], w_proj, True, [], [], [(half, BF)], lambda total: (total,), "project_out_back"
        )
        grad_w_proj = tn_dot(mixed, grad_branch).astype(BF)
        mine = lax.dynamic_slice_in_dim(grad_w_proj, section * half, half, 1)
        sent = lax.dynamic_slice_in_dim(grad_w_proj, (1 - section) * half, half, 1)
        if layer == 0:
            grad_mixed, columns, sent = tie(grad_mixed, columns, sent)
            totals[1][0] = scatter.along_z(columns[1][0])

        grad_w_proj = place.in_order(mine, place.sibling(sent), 0)
        dq, dk, dv = attend_backward(
            q, k, v, grad_mixed, lse, code_k, seg_q, head_dim, BF if groups == 1 else F32
        )
        if groups > 1:
            dk, dv = scatter_groups(dk), scatter_groups(dv)
        if layer == 1:
            out_parts, in_parts, dq, dk, dv, grad_w_proj, act_back, act_value = tie(
                out_parts, in_parts, dq, dk, dv, grad_w_proj, act_back, act_value
            )
            act_back += from_sequences(place, act_value, [count - 1])
        else:
            out_parts, in_parts, dq, dk, dv, grad_w_proj, back_one, grad_one, totals = tie(
                out_parts, in_parts, dq, dk, dv, grad_w_proj, back_one, grad_one, totals
            )
            back_one += from_sequences(place, grad_one, range(2, count), 1)

        columns[layer][2] = scatter.third(out_parts)
        in_parts = scatter.second(in_parts)
        low = to_width([dq, dk, dv], w_qkv, True, "project_qkv_back")
        low, dq, dk, dv, columns = tie(low, dq, dk, dv, columns)
        totals[layer][2] = scatter.along_z(columns[layer][2])
        other = place.sibling(low)
        attn_parts, dqkv_rows = scatter.product(u, [dq, dk, dv], grad_w_proj)
        in_parts, attn_parts, low, other = tie(in_parts, attn_parts, low, other)
        attn_parts = scatter.first(attn_parts)
        terms = [grad_branch, low, other]

        here = jnp.where(section == layer, 1.0, 0.0)
        spread = jnp.zeros((2, 2, half), F32)
        spread = lax.dynamic_update_slice(spread, dqkv_rows[:half][None, None], (0, section, 0))
        spread = lax.dynamic_update_slice(spread, dqkv_rows[2 * half :][None, None], (1, section, 0))
        ff_spread = lax.dynamic_update_slice(
            jnp.zeros((chips, 2, ff_split), F32), hidden_sums.reshape(chips, 1, ff_split), (0, section, 0)
        )
        rest = jnp.stack(
            [first_sums[0], second_sums[0], first_sums[1], second_sums[1], first_sums[2], second_sums[2]]
        )
        by_chip = jnp.concatenate([here * rest, spread.reshape(2, width)], axis=0).reshape(8, chips, -1)
        by_chip = jnp.moveaxis(by_chip, 1, 0).reshape(chips, -1)
        squares = jnp.concatenate([jnp.sum(sums_one[:2], axis=1), jnp.sum(sums_two[1:3], axis=1)])
        squares = here * jnp.concatenate([squares, jnp.sum(live)[None], jnp.zeros((3,), F32)])
        small_grads[layer] = jnp.concatenate(
            [by_chip, ff_spread.reshape(chips, -1), jnp.broadcast_to(squares, (chips, 8))], axis=1
        )

    totals[0][1] = scatter.along_z(scatter.third(in_parts))
    grad_zero = sum([term.astype(F32) for term in terms]).astype(BF).reshape(count, local, width)
    back_zero = from_sequences(place, grad_zero, range(count), 0)
    mine = jnp.where(first_section, small_grads[0], small_grads[1])
    sent = jnp.where(first_section, small_grads[1], small_grads[0])
    small_rows = mine + place.sibling(sent)
    attn_parts, small_rows, back_one, act_back = tie(attn_parts, small_rows, back_one, act_back)
    attn_parts = scatter.second(attn_parts)
    small_total = small_scatter(place, small_rows)
    totals[0][0] = scatter.along_z(scatter.third(attn_parts))

    def give_back(pieces):
        return place_rotated(pieces, place.ctx % count, count).reshape(1, micro, seqs, local, width)

    activations = give_back(act_back)
    input_grads = give_back([jnp.where(first_section, a, b) for a, b in zip(back_zero, back_one)])

    def halves(index):
        a, b = totals[0][index], totals[1][index]
        mine = jnp.where(first_section, a, b)
        other = place.sibling(jnp.where(first_section, b, a))
        low, high = jnp.where(first_section, mine, other), jnp.where(first_section, other, mine)
        return low.astype(F32), high.astype(F32)

    attn_rows = width // chips
    low, high = halves(0)
    low = low.reshape(attn_rows, 4, half)
    high = high.reshape(attn_rows, 4, half)
    attn = jnp.concatenate([low, high], axis=2)
    grad_qkv = jnp.moveaxis(attn[:, :3], 1, 0)[None]
    grad_out_proj = attn[:, 3][None]
    low, high = halves(1)
    grad_in_weight = jnp.stack(
        [low.reshape(-1, chips, ff_split), high.reshape(-1, chips, ff_split)], axis=2
    ).reshape(1, -1, ff_width)
    low, high = halves(2)
    grad_out_weight = jnp.concatenate([low, high], axis=0)[None]

    per_chip = width // chips
    table = small_total[: 8 * per_chip].reshape(8, per_chip)
    grad_gain = table[0:2][None]
    grad_shift = table[2:4][None]
    grad_proj_bias = jnp.stack([table[6], table[7], table[4], table[5]])[None]
    grad_ff_bias = small_total[8 * per_chip : 8 * per_chip + ff_rows][None]
    sums = small_total[8 * per_chip + ff_rows :]
    rms = jnp.sqrt(sums[:4] / (sums[4] * width))[None]
    return (
        activations,
        input_grads,
        grad_qkv,
        grad_out_proj,
        grad_in_weight,
        grad_out_weight,
        grad_gain,
        grad_shift,
        grad_proj_bias,
        grad_ff_bias,
        rms,
    )


def solution(mesh):
    placed = (
        P(None, "fsdp", "ctx", None),
        P(None, "fsdp", "ctx"),
        P(None, "fsdp", "ctx"),
        P(None, "fsdp", "ctx", None),
        P("section", None, ("ctx", "fsdp"), None),
        P("section", ("ctx", "fsdp"), None),
        P("section", ("ctx", "fsdp"), None),
        P("section", ("ctx", "fsdp"), None),
        P("section", None, None),
        P("section", None, None),
        P("section", None, None),
        P("section", None),
    )
    return jax.shard_map(
        on_device,
        mesh=mesh,
        in_specs=placed,
        out_specs=(
            P("section", None, "fsdp", "ctx", None),
            P("section", None, "fsdp", "ctx", None),
            P("section", None, ("ctx", "fsdp"), None),
            P("section", ("ctx", "fsdp"), None),
            P("section", ("ctx", "fsdp"), None),
            P("section", ("ctx", "fsdp"), None),
            P("section", None, ("ctx", "fsdp")),
            P("section", None, ("ctx", "fsdp")),
            P("section", None, ("ctx", "fsdp")),
            P("section", ("ctx", "fsdp")),
            P("section", None),
        ),
        check_vma=False,
    )
```

time: 1170 us -> 774 us (0.66)
  waiting for transfers between devices: 437 us -> 180 us
  Pallas kernels: 128 us -> 255 us
  matrix products: 146 us -> 19.6 us
  other arithmetic: 140 us -> 45.8 us
  blocking collectives: 76.1 us -> 0 us
  starting transfers between devices: 84.2 us -> 117 us
    pallas_call x0 -> x40, Pallas kernels: none -> 170 us  [the longest x14 58.7 us: row_product(): pl.pallas_call(body, grid=(rows // block,), in_specs=[pl.BlockSpec((block...]
    ppermute x15 -> x25, waiting for transfers between devices: 168 us -> 88.6 us  [from_y(): return lax.ppermute(value, 'fsdp', pairs)]
    ppermute x15 -> x25, waiting for transfers between devices: 106 us -> 27.8 us  [from_x(): return lax.ppermute(value, 'fsdp', pairs)]
    unnamed x1 -> x0, blocking collectives: 76.1 us -> none
    all_gather x6, waiting for transfers between devices: 80.4 us -> 14.9 us  [along_z(): column = lax.all_gather(self.shard, 'ctx', axis=0, tiled=True)]
    dot_general x8 -> x0, matrix products: 54.8 us -> none  [nt_dot(): lax.dot_general(a, b, (((1,), (1,)), ((), ())), preferred_element_type=F32)]
    reduce_sum x20 -> x4, other arithmetic: 52.6 us -> 0.48 us  [the longest x2 0.24 us: on_device(): jnp.sum(sums_two[1:3], axis=1)]
    unnamed x287 -> x423, local copies, waits for them, and re-layouts: 30.6 us -> 81.9 us
  transfers between devices with their start and end apart: 79 -> 105, of which waited for: 26 -> 32; matrix products, arithmetic and copies ran while one was open for 27% -> 13% of each run, Pallas kernels for 11% -> 28%
where the time goes in v2:
time: 774 us; the launch traced here: 765 us
  Pallas kernels  255 us (33%)
  waiting for transfers between devices  180 us (23%)
  local copies, waits for them, and re-layouts  129 us (17%)
  starting transfers between devices  117 us (15%)
  other arithmetic  45.8 us (6%)
  matrix products  19.6 us (3%)
  between operations  18.2 us (2%)
    ppermute x25, waiting for transfers between devices, from_y(): return lax.ppermute(value, 'fsdp', pairs)  88.6 us
    unnamed x423, local copies, waits for them, and re-layouts  81.9 us
    pallas_call x14, Pallas kernels, row_product(): pl.pallas_call(body, grid=(rows // block,), in_specs=[pl.BlockSpec((block...  58.7 us
    pallas_call x2, Pallas kernels, attend_backward(): pl.pallas_call(lambda *refs: attend_backward_kernel(head_dim, *refs), gri...  54.4 us
    pallas_call x6, Pallas kernels, product(): pl.pallas_call(body, grid_spec=pltpu.PrefetchScalarGridSpec(num_scalar_pr...  42.9 us
    ppermute x9, starting transfers between devices, to_pieces(): lax.ppermute(sent, 'ctx', pairs)  34.2 us
    pallas_call x2, Pallas kernels, attend_forward(): pl.pallas_call(lambda *refs: attend_forward_kernel(head_dim, *refs), grid...  29.7 us
    ppermute x9, waiting for transfers between devices, to_pieces(): lax.ppermute(sent, 'ctx', pairs)  28.2 us
  transfers between devices with their start and end apart: 105, of which 32 were waited for; matrix products, arithmetic and copies ran while one was open for 13% of the time, Pallas kernels for 28%

profile of v2, /device:TPU:0, one launch (start us, length us, event | category | flops | bytes accessed | tf_op | source)
XLA Modules:
  0.0 764.8 jit_solution(6906311857035779490)
XLA Ops:
  12.4 3.1 dynamic-slice_reduce_fusion.1
  17.3 2.8 collective-permute-start.1
  24.2 7.1 collective-permute-done.1
  31.4 14.8 %all-gather.7.cloned.1.call-done = bf16[256,2048]{1,0:T(8,128)(2,1)} async-done(((bf16[64,2048]{1,0:T(8,128)(2,1)}), bf16[256,2048]{1,0:T(8,128)(2,1)}) %all-gather.7.cloned.1.call-update) | async-done | bytes 1048592 | tf_op jit(solution)/shard_map/all_gather | solution.py:378
  57.7 11.8 %collective-permute-done.5 = bf16[128,1024]{1,0:T(8,128)(2,1)} collective-permute-done((bf16[128,1024]{1,0:T(8,128)(2,1)}, bf16[128,1024]{1,0:T(8,128)(2,1)}, u32[]{:S(2)}, u32[]{:S(2)}) %collective-permute-start.5) | collective-permute-done | bytes 262176 | tf_op jit(solution)/shard_map/ppermute | solution.py:607
  69.5 19.4 %collective-permute-start.14 = (s32[256]{0:T(256)S(1)}, s32[256]{0:T(256)S(1)}, u32[]{:S(2)}, u32[]{:S(2)}) collective-permute-start(s32[256]{0:T(256)S(1)} %bitcast.385), channel_id=1, source_target_pairs={{0,12},{4,0},{8,4},{12,8},{1,13},{5,1},{9,5},{13,9},{2,14},{6,2},{... | collective-permute-start | bytes 3080 | tf_op jit(solution)/shard_map/ppermute | solution.py:607
  101.0 7.5 collective-permute-done.7.refs_3_
  120.9 4.0 project_qkv.2
  124.9 14.9 %attend_forward.2 = (bf16[1024,512]{1,0:T(8,128)(2,1)S(1)}, f32[4,2,1024]{2,1,0:T(2,128)S(1)}) custom-call(bf16[1024,512]{1,0:T(8,128)(2,1)S(1)} %get-tuple-element.751.refs_0_, bf16[1024,512]{1,0:T(8,128)(2,1)S(1)} %get-tuple-element.752.refs_1_, bf16[1024,512]{1,0:T(8,128)(2,1)S(1)} %get-tuple-element.753.refs_2_, ...), custom_call_target="tpu_custom_call" | custom-call | flops 3006477056 | bytes 1468006 | tf_op jit(solution)/shard_map/attend_forward/pallas_call | solution.py:124
  152.7 2.9 collective-permute-start.23
  155.8 5.1 norm_forward.4
  164.3 3.6 collective-permute-done.23
  167.9 14.4 %collective-permute-done.20.refs_3_ = bf16[4,64,1024]{2,1,0:T(8,128)(2,1)S(1)} collective-permute-done((bf16[4,64,1024]{2,1,0:T(8,128)(2,1)S(1)}, bf16[4,64,1024]{2,1,0:T(8,128)(2,1)S(1)}, u32[]{:S(2)}, u32[]{:S(2)}) %collective-permute-start.20) | collective-permute-done | bytes 524320 | tf_op jit(solution)/shard_map/ppermute | solution.py:351
  195.4 3.0 assemble.7
  198.4 9.3 %fusion.4 = (bf16[1024,2048]{1,0:T(8,128)(2,1)}, bf16[1024,2048]{1,0:T(8,128)(2,1)}) fusion(f32[2048]{0:T(1024)S(1)} %bitcast.378, bf16[1024,1024]{1,0:T(8,128)(2,1)S(1)} %copy-done.29, bf16[1024,2048]{1,0:T(8,128)(2,1)S(1)} %bitcast.292), kind=kOutput, calls=%fused_computation.6 | convolution fusion | flops 4320133120 | bytes 14688256 | tf_op jit(solution)/shard_map/dot_general | solution.py:34
  207.7 3.8 collective-permute-done.28
  211.4 8.4 %collective-permute-done.26.refs_3_ = bf16[4,128,512]{2,1,0:T(8,128)(2,1)S(1)} collective-permute-done((bf16[4,128,512]{2,1,0:T(8,128)(2,1)S(1)}, bf16[4,128,512]{2,1,0:T(8,128)(2,1)S(1)}, u32[]{:S(2)}, u32[]{:S(2)}) %collective-permute-start.26) | collective-permute-done | bytes 524320 | tf_op jit(solution)/shard_map/ppermute | solution.py:351
  226.1 3.3 assemble.8
  229.4 5.0 feed_out.2.part_ref
  234.5 22.7 %collective-permute-done.31.refs_3_ = bf16[4,64,1024]{2,1,0:T(8,128)(2,1)S(1)} collective-permute-done((bf16[4,64,1024]{2,1,0:T(8,128)(2,1)S(1)}, bf16[4,64,1024]{2,1,0:T(8,128)(2,1)S(1)}, u32[]{:S(2)}, u32[]{:S(2)}) %collective-permute-start.31) | collective-permute-done | bytes 524320 | tf_op jit(solution)/shard_map/ppermute | solution.py:351
  273.2 4.0 norm_forward.5
  278.0 3.9 project_qkv.3
  282.0 14.9 %attend_forward.3 = (bf16[1024,512]{1,0:T(8,128)(2,1)S(1)}, f32[4,2,1024]{2,1,0:T(2,128)S(1)}) custom-call(bf16[1024,512]{1,0:T(8,128)(2,1)S(1)} %get-tuple-element.664.refs_0_, bf16[1024,512]{1,0:T(8,128)(2,1)S(1)} %get-tuple-element.665.refs_1_, bf16[1024,512]{1,0:T(8,128)(2,1)S(1)} %get-tuple-element.666.refs_2_, ...), custom_call_target="tpu_custom_call" | custom-call | flops 3006477056 | bytes 1468006 | tf_op jit(solution)/shard_map/attend_forward/pallas_call | solution.py:124
  297.0 2.9 project_out.3.part_ref
  299.9 3.0 collective-permute-done.35.refs_3_
  305.8 3.6 collective-permute-start.42
  313.7 3.0 assemble.10
  316.7 5.5 norm_forward.6
  324.3 7.8 %fusion.9 = (bf16[1024,2048]{1,0:T(8,128)(2,1)S(1)}, bf16[1024,2048]{1,0:T(8,128)(2,1)S(1)}) fusion(f32[2048]{0:T(1024)S(1)} %bitcast.377, bf16[1024,1024]{1,0:T(8,128)(2,1)S(1)} %get-tuple-element.625.before_ref.x_ref, bf16[1024,2048]{1,0:T(8,128)(2,1)S(1)} %bitcast.294), kind=kOutput, calls=%fused_computation.11 | convolution fusion | flops 4320133120 | bytes 14688256 | tf_op jit(solution)/shard_map/dot_general | solution.py:34
  332.2 3.0 assemble.11
  335.2 5.1 feed_out.3.part_ref
  341.4 4.6 collective-permute-done.43
  346.6 4.0 norm_forward.7
  350.6 3.1 norm_backward.4
  353.7 7.7 %weight_grad.6 = (bf16[4,2,128,512]{3,2,1,0:T(8,128)(2,1)S(1)}, bf16[4,2,128,512]{3,2,1,0:T(8,128)(2,1)}, bf16[4,2,128,512]{3,2,1,0:T(8,128)(2,1)S(1)}, bf16[4,2,128,512]{3,2,1,0:T(8,128)(2,1)}, f32[8,1024]{1,0:T(8,128)}) custom-call(s32[2]{0:T(128)S(1)} %pad_add_fusion.at_ref, bf16[1024,2048]{1,0:T(8,128)(2,1)S(1)} %get-tuple-element.602.refs_0_.x_ref, ...), custom_call_target="tpu_custom_call" | custom-call | flops 1503238528 | bytes 3670016 | tf_op jit(solution)/shard_map/weight_grad/pallas_call | solution.py:500
  363.1 5.2 feed_out_back.2.refs_0_
  368.3 6.0 feed_in_back.2.refs_1_
  382.3 7.2 weight_grad.7
  390.5 9.7 %collective-permute-done.45.refs_1_ = bf16[4,2,128,512]{3,2,1,0:T(8,128)(2,1)} collective-permute-done((bf16[4,2,128,512]{3,2,1,0:T(8,128)(2,1)}, bf16[4,2,128,512]{3,2,1,0:T(8,128)(2,1)}, u32[]{:S(2)}, u32[]{:S(2)}) %collective-permute-start.45) | collective-permute-done | bytes 1048608 | tf_op jit(solution)/shard_map/ppermute | solution.py:351
  401.5 5.5 norm_backward.5
  418.4 27.1 %attend_backward.2 = (bf16[1024,512]{1,0:T(8,128)(2,1)S(1)}, bf16[1024,512]{1,0:T(8,128)(2,1)S(1)}, bf16[1024,512]{1,0:T(8,128)(2,1)S(1)}) custom-call(bf16[1024,512]{1,0:T(8,128)(2,1)S(1)} %copy-done.160, bf16[1024,512]{1,0:T(8,128)(2,1)S(1)} %copy-done.162, bf16[1024,512]{1,0:T(8,128)(2,1)S(1)} %copy-done.164, ...), custom_call_target="tpu_custom_call" | custom-call | flops 7516192768 | bytes 2936012 | tf_op jit(solution)/shard_map/attend_backward/pallas_call | solution.py:156
  458.0 5.0 project_qkv_back.2.refs_1_
  472.3 6.6 weight_grad.8
  483.4 5.9 norm_backward.6
  490.7 7.6 weight_grad.9
  507.2 5.2 feed_out_back.3.refs_0_
  512.4 6.0 feed_in_back.3.refs_1_
  523.9 3.0 scatter_add.8
  530.6 7.2 weight_grad.10
  537.9 6.9 collective-permute-done.62.refs_1_
  546.1 10.4 %collective-permute-done.60 = bf16[4,64,1024]{2,1,0:T(8,128)(2,1)S(1)} collective-permute-done((bf16[4,64,1024]{2,1,0:T(8,128)(2,1)S(1)}, bf16[4,64,1024]{2,1,0:T(8,128)(2,1)S(1)}, u32[]{:S(2)}, u32[]{:S(2)}) %collective-permute-start.60) | collective-permute-done | bytes 524320 | tf_op jit(solution)/shard_map/ppermute | solution.py:344
  556.5 5.5 norm_backward.7
  572.7 3.5 scatter_add.9
  581.9 27.3 %attend_backward.3 = (bf16[1024,512]{1,0:T(8,128)(2,1)S(1)}, bf16[1024,512]{1,0:T(8,128)(2,1)S(1)}, bf16[1024,512]{1,0:T(8,128)(2,1)S(1)}) custom-call(bf16[1024,512]{1,0:T(8,128)(2,1)S(1)} %copy-done.154, bf16[1024,512]{1,0:T(8,128)(2,1)S(1)} %copy-done.156, bf16[1024,512]{1,0:T(8,128)(2,1)S(1)} %copy-done.158, bf16[1024,512]{1,0:T(8,128)(2,1)S(1)} %copy-done.114, ...), custom_call_target="tpu_custom_call" | custom-call | flops 7516192768 | bytes 2936012 | tf_op jit(solution)/shard_map/attend_backward/pallas_call | solution.py:156
  625.9 4.9 project_qkv_back.3
  639.3 6.6 weight_grad.11
  656.9 9.9 %collective-permute-done.71 = bf16[4,64,1024]{2,1,0:T(8,128)(2,1)S(1)} collective-permute-done((bf16[4,64,1024]{2,1,0:T(8,128)(2,1)S(1)}, bf16[4,64,1024]{2,1,0:T(8,128)(2,1)S(1)}, u32[]{:S(2)}, u32[]{:S(2)}) %collective-permute-start.71) | collective-permute-done | bytes 524320 | tf_op jit(solution)/shard_map/ppermute | solution.py:344
  673.9 5.0 add_convert_fusion
  681.2 10.4 %collective-permute-done.74.refs_1_ = bf16[4,2,64,1024]{3,2,1,0:T(8,128)(2,1)S(1)} collective-permute-done((bf16[4,2,64,1024]{3,2,1,0:T(8,128)(2,1)}, bf16[4,2,64,1024]{3,2,1,0:T(8,128)(2,1)S(1)}, u32[]{:S(2)}, u32[]{:S(2)}) %collective-permute-start.74) | collective-permute-done | bytes 1048608 | tf_op jit(solution)/shard_map/ppermute | solution.py:351
  699.2 5.5 collective-permute-start.80
  714.8 2.8 collective-permute-start.92
  718.9 7.5 collective-permute-start.82
  733.4 10.1 %collective-permute-done.82 = bf16[256,1024]{1,0:T(8,128)(2,1)} collective-permute-done((bf16[256,1024]{1,0:T(8,128)(2,1)S(1)}, bf16[256,1024]{1,0:T(8,128)(2,1)}, u32[]{:S(2)}, u32[]{:S(2)}) %collective-permute-start.82) | collective-permute-done | bytes 524320 | tf_op jit(solution)/shard_map/ppermute | solution.py:630
  745.6 3.9 reduce-scatter.13.cloned.1.call-done
  (833 shorter events, 276.5 us)
Async XLA Ops:
  7.2 39.0 %all-gather.7.cloned.1.call-start = ((), (), s32[]{:S(2)}) async-start(), calls=%async_computation.6 | async-start | bytes 1310720 | tf_op jit(solution)/shard_map/all_gather | solution.py:378
  12.0 98.6 %all-gather.9.cloned.1.call-start = ((), (), s32[]{:S(2)}) async-start(), calls=%async_computation.7 | async-start | bytes 1310720 | tf_op jit(solution)/shard_map/all_gather | solution.py:378
  46.2 42.6 %collective-permute-start.3 = (bf16[4,64,2048]{2,1,0:T(8,128)(2,1)}, bf16[4,64,2048]{2,1,0:T(8,128)(2,1)S(1)}, u32[]{:S(2)}, u32[]{:S(2)}) collective-permute-start(bf16[4,64,2048]{2,1,0:T(8,128)(2,1)} %bitcast.303), channel_id=1, source_target_pairs={{1,0},{0,1},{3,2},{2,3},{5,4},{4,5},{7,6},{6,7},{9,8},{8,9},{11,10... | collective-permute-start | bytes 3145736 | tf_op jit(solution)/shard_map/ppermute | solution.py:344
  47.7 41.7 %collective-permute-start.4 = (bf16[4,64,2048]{2,1,0:T(8,128)(2,1)}, bf16[4,64,2048]{2,1,0:T(8,128)(2,1)}, u32[]{:S(2)}, u32[]{:S(2)}) collective-permute-start(bf16[4,64,2048]{2,1,0:T(8,128)(2,1)} %bitcast.304), channel_id=1, source_target_pairs={{2,0},{3,1},{0,2},{1,3},{6,4},{7,5},{4,6},{5,7},{10,8},{11,9},{8,1... | collective-permute-start | bytes 3145736 | tf_op jit(solution)/shard_map/ppermute | solution.py:351
  50.9 46.7 %collective-permute-start.10 = (bf16[128,1024]{1,0:T(8,128)(2,1)}, bf16[128,1024]{1,0:T(8,128)(2,1)}, u32[]{:S(2)}, u32[]{:S(2)}) collective-permute-start(bf16[128,1024]{1,0:T(8,128)(2,1)} %dynamic-slice_bitcast_fusion.15), channel_id=1, source_target_pairs={{0,16},{16,0},{1,17},{17,1},{2,18},{18,2},{3,19},{19,3},{4,20},{20... | collective-permute-start | bytes 786440 | tf_op jit(solution)/shard_map/ppermute | solution.py:354
  53.4 35.4 %collective-permute-start.6 = (bf16[128,1024]{1,0:T(8,128)(2,1)}, bf16[128,1024]{1,0:T(8,128)(2,1)}, u32[]{:S(2)}, u32[]{:S(2)}) collective-permute-start(bf16[128,1024]{1,0:T(8,128)(2,1)} %get-tuple-element.920), channel_id=1, source_target_pairs={{0,12},{4,0},{8,4},{12,8},{1,13},{5,1},{9,5},{13,9},{2,14},{6,2},{... | collective-permute-start | bytes 786440 | tf_op jit(solution)/shard_map/ppermute | solution.py:607
  57.7 86.3 %all-gather.11.cloned.1.call-start = ((), (), s32[]{:S(2)}) async-start(), calls=%async_computation.8 | async-start | bytes 1310720 | tf_op jit(solution)/shard_map/all_gather | solution.py:378
  110.7 73.3 %all-gather.13.cloned.1.call-start = ((), (), s32[]{:S(2)}) async-start(), calls=%async_computation.9 | async-start | bytes 1310720 | tf_op jit(solution)/shard_map/all_gather | solution.py:378
  111.3 31.4 %collective-permute-start.11 = (bf16[4,64,2048]{2,1,0:T(8,128)(2,1)}, bf16[4,64,2048]{2,1,0:T(8,128)(2,1)}, u32[]{:S(2)}, u32[]{:S(2)}) collective-permute-start(bf16[4,64,2048]{2,1,0:T(8,128)(2,1)} %bitcast.306), channel_id=1, source_target_pairs={{1,0},{0,1},{3,2},{2,3},{5,4},{4,5},{7,6},{6,7},{9,8},{8,9},{11,10... | collective-permute-start | bytes 3145736 | tf_op jit(solution)/shard_map/ppermute | solution.py:344
  111.7 32.3 %collective-permute-start.12 = (bf16[4,64,2048]{2,1,0:T(8,128)(2,1)}, bf16[4,64,2048]{2,1,0:T(8,128)(2,1)}, u32[]{:S(2)}, u32[]{:S(2)}) collective-permute-start(bf16[4,64,2048]{2,1,0:T(8,128)(2,1)} %bitcast.307), channel_id=1, source_target_pairs={{2,0},{3,1},{0,2},{1,3},{6,4},{7,5},{4,6},{5,7},{10,8},{11,9},{8,1... | collective-permute-start | bytes 3145736 | tf_op jit(solution)/shard_map/ppermute | solution.py:351
  144.4 77.0 %all-gather.15.cloned.1.call-start = ((), (), s32[]{:S(2)}) async-start(), calls=%async_computation.10 | async-start | bytes 1310720 | tf_op jit(solution)/shard_map/all_gather | solution.py:378
  144.5 39.4 %collective-permute-start.18 = (bf16[4,128,1024]{2,1,0:T(8,128)(2,1)}, bf16[4,128,1024]{2,1,0:T(8,128)(2,1)}, u32[]{:S(2)}, u32[]{:S(2)}) collective-permute-start(bf16[4,128,1024]{2,1,0:T(8,128)(2,1)} %bitcast.309), channel_id=1, source_target_pairs={{1,0},{0,1},{3,2},{2,3},{5,4},{4,5},{7,6},{6,7},{9,8},{8,9},{11,10... | collective-permute-start | bytes 3145736 | tf_op jit(solution)/shard_map/ppermute | solution.py:344
  146.1 37.9 %collective-permute-start.19 = (bf16[4,128,1024]{2,1,0:T(8,128)(2,1)}, bf16[4,128,1024]{2,1,0:T(8,128)(2,1)}, u32[]{:S(2)}, u32[]{:S(2)}) collective-permute-start(bf16[4,128,1024]{2,1,0:T(8,128)(2,1)} %bitcast.310), channel_id=1, source_target_pairs={{2,0},{3,1},{0,2},{1,3},{6,4},{7,5},{4,6},{5,7},{10,8},{11,9},{8,1... | collective-permute-start | bytes 3145736 | tf_op jit(solution)/shard_map/ppermute | solution.py:351
  147.6 34.7 %collective-permute-start.20 = (bf16[4,64,1024]{2,1,0:T(8,128)(2,1)S(1)}, bf16[4,64,1024]{2,1,0:T(8,128)(2,1)S(1)}, u32[]{:S(2)}, u32[]{:S(2)}) collective-permute-start(bf16[4,64,1024]{2,1,0:T(8,128)(2,1)S(1)} %slice.291), channel_id=1, source_target_pairs={{2,0},{3,1},{0,2},{1,3},{6,4},{7,5},{4,6},{5,7},{10,8},{11,9},{8,1... | collective-permute-start | bytes 1572872 | tf_op jit(solution)/shard_map/ppermute | solution.py:351
  150.3 32.8 %collective-permute-start.21 = (bf16[4,64,1024]{2,1,0:T(8,128)(2,1)S(1)}, bf16[4,64,1024]{2,1,0:T(8,128)(2,1)S(1)}, u32[]{:S(2)}, u32[]{:S(2)}) collective-permute-start(bf16[4,64,1024]{2,1,0:T(8,128)(2,1)S(1)} %slice.292), channel_id=1, source_target_pairs={{1,0},{0,1},{3,2},{2,3},{5,4},{4,5},{7,6},{6,7},{9,8},{8,9},{11,10... | collective-permute-start | bytes 1572872 | tf_op jit(solution)/shard_map/ppermute | solution.py:344
  184.0 74.9 %all-gather.17.cloned.1.call-start = ((), (), s32[]{:S(2)}) async-start(), calls=%async_computation.11 | async-start | bytes 1310720 | tf_op jit(solution)/shard_map/all_gather | solution.py:378
  184.1 37.3 %collective-permute-start.24 = (bf16[4,64,2048]{2,1,0:T(8,128)(2,1)}, bf16[4,64,2048]{2,1,0:T(8,128)(2,1)S(1)}, u32[]{:S(2)}, u32[]{:S(2)}) collective-permute-start(bf16[4,64,2048]{2,1,0:T(8,128)(2,1)} %bitcast.315), channel_id=1, source_target_pairs={{1,0},{0,1},{3,2},{2,3},{5,4},{4,5},{7,6},{6,7},{9,8},{8,9},{11,10... | collective-permute-start | bytes 3145736 | tf_op jit(solution)/shard_map/ppermute | solution.py:344
  184.7 36.7 %collective-permute-start.25 = (bf16[4,64,2048]{2,1,0:T(8,128)(2,1)}, bf16[4,64,2048]{2,1,0:T(8,128)(2,1)S(1)}, u32[]{:S(2)}, u32[]{:S(2)}) collective-permute-start(bf16[4,64,2048]{2,1,0:T(8,128)(2,1)} %bitcast.316), channel_id=1, source_target_pairs={{2,0},{3,1},{0,2},{1,3},{6,4},{7,5},{4,6},{5,7},{10,8},{11,9},{8,1... | collective-permute-start | bytes 3145736 | tf_op jit(solution)/shard_map/ppermute | solution.py:351
  186.0 25.5 %collective-permute-start.28 = (bf16[128,1024]{1,0:T(8,128)(2,1)S(1)}, bf16[128,1024]{1,0:T(8,128)(2,1)S(1)}, u32[]{:S(2)}, u32[]{:S(2)}) collective-permute-start(bf16[128,1024]{1,0:T(8,128)(2,1)S(1)} %dynamic-slice_bitcast_fusion.12), channel_id=1, source_target_pairs={{0,8},{4,12},{8,0},{12,4},{1,9},{5,13},{9,1},{13,5},{2,10},{6,14},... | collective-permute-start | bytes 786440 | tf_op jit(solution)/shard_map/ppermute | solution.py:607
  189.7 30.1 %collective-permute-start.26 = (bf16[4,128,512]{2,1,0:T(8,128)(2,1)S(1)}, bf16[4,128,512]{2,1,0:T(8,128)(2,1)S(1)}, u32[]{:S(2)}, u32[]{:S(2)}) collective-permute-start(bf16[4,128,512]{2,1,0:T(8,128)(2,1)S(1)} %slice.296), channel_id=1, source_target_pairs={{2,0},{3,1},{0,2},{1,3},{6,4},{7,5},{4,6},{5,7},{10,8},{11,9},{8,1... | collective-permute-start | bytes 1572872 | tf_op jit(solution)/shard_map/ppermute | solution.py:351
  192.5 28.1 %collective-permute-start.27 = (bf16[4,128,512]{2,1,0:T(8,128)(2,1)S(1)}, bf16[4,128,512]{2,1,0:T(8,128)(2,1)S(1)}, u32[]{:S(2)}, u32[]{:S(2)}) collective-permute-start(bf16[4,128,512]{2,1,0:T(8,128)(2,1)S(1)} %slice.297), channel_id=1, source_target_pairs={{1,0},{0,1},{3,2},{2,3},{5,4},{4,5},{7,6},{6,7},{9,8},{8,9},{11,10... | collective-permute-start | bytes 1572872 | tf_op jit(solution)/shard_map/ppermute | solution.py:344
  221.5 393.0 %reduce-scatter.11.cloned.1.call-start = ((), (), s32[]{:S(2)}) async-start(), calls=%async_computation.14 | async-start | bytes 1310720 | tf_op jit(solution)/shard_map/reduce_scatter | solution.py:575
  221.7 37.1 %collective-permute-start.29 = (bf16[4,64,2048]{2,1,0:T(8,128)(2,1)}, bf16[4,64,2048]{2,1,0:T(8,128)(2,1)}, u32[]{:S(2)}, u32[]{:S(2)}) collective-permute-start(bf16[4,64,2048]{2,1,0:T(8,128)(2,1)} %bitcast.312), channel_id=1, source_target_pairs={{1,0},{0,1},{3,2},{2,3},{5,4},{4,5},{7,6},{6,7},{9,8},{8,9},{11,10... | collective-permute-start | bytes 3145736 | tf_op jit(solution)/shard_map/ppermute | solution.py:344
  223.3 35.5 %collective-permute-start.30 = (bf16[4,64,2048]{2,1,0:T(8,128)(2,1)}, bf16[4,64,2048]{2,1,0:T(8,128)(2,1)}, u32[]{:S(2)}, u32[]{:S(2)}) collective-permute-start(bf16[4,64,2048]{2,1,0:T(8,128)(2,1)} %bitcast.313), channel_id=1, source_target_pairs={{2,0},{3,1},{0,2},{1,3},{6,4},{7,5},{4,6},{5,7},{10,8},{11,9},{8,1... | collective-permute-start | bytes 3145736 | tf_op jit(solution)/shard_map/ppermute | solution.py:351
  223.8 33.4 %collective-permute-start.31 = (bf16[4,64,1024]{2,1,0:T(8,128)(2,1)S(1)}, bf16[4,64,1024]{2,1,0:T(8,128)(2,1)S(1)}, u32[]{:S(2)}, u32[]{:S(2)}) collective-permute-start(bf16[4,64,1024]{2,1,0:T(8,128)(2,1)S(1)} %slice.299), channel_id=1, source_target_pairs={{2,0},{3,1},{0,2},{1,3},{6,4},{7,5},{4,6},{5,7},{10,8},{11,9},{8,1... | collective-permute-start | bytes 1572872 | tf_op jit(solution)/shard_map/ppermute | solution.py:351
  225.5 32.5 %collective-permute-start.32 = (bf16[4,64,1024]{2,1,0:T(8,128)(2,1)S(1)}, bf16[4,64,1024]{2,1,0:T(8,128)(2,1)S(1)}, u32[]{:S(2)}, u32[]{:S(2)}) collective-permute-start(bf16[4,64,1024]{2,1,0:T(8,128)(2,1)S(1)} %slice.300), channel_id=1, source_target_pairs={{1,0},{0,1},{3,2},{2,3},{5,4},{4,5},{7,6},{6,7},{9,8},{8,9},{11,10... | collective-permute-start | bytes 1572872 | tf_op jit(solution)/shard_map/ppermute | solution.py:344
  266.2 38.3 %collective-permute-start.33 = (bf16[4,128,1024]{2,1,0:T(8,128)(2,1)S(1)}, bf16[4,128,1024]{2,1,0:T(8,128)(2,1)}, u32[]{:S(2)}, u32[]{:S(2)}) collective-permute-start(bf16[4,128,1024]{2,1,0:T(8,128)(2,1)S(1)} %bitcast.318), channel_id=1, source_target_pairs={{1,0},{0,1},{3,2},{2,3},{5,4},{4,5},{7,6},{6,7},{9,8},{8,9},{11,10... | collective-permute-start | bytes 3145736 | tf_op jit(solution)/shard_map/ppermute | solution.py:344
  266.7 37.8 %collective-permute-start.34 = (bf16[4,128,1024]{2,1,0:T(8,128)(2,1)S(1)}, bf16[4,128,1024]{2,1,0:T(8,128)(2,1)}, u32[]{:S(2)}, u32[]{:S(2)}) collective-permute-start(bf16[4,128,1024]{2,1,0:T(8,128)(2,1)S(1)} %bitcast.319), channel_id=1, source_target_pairs={{2,0},{3,1},{0,2},{1,3},{6,4},{7,5},{4,6},{5,7},{10,8},{11,9},{8,1... | collective-permute-start | bytes 3145736 | tf_op jit(solution)/shard_map/ppermute | solution.py:351
  268.3 34.6 %collective-permute-start.35 = (bf16[4,64,1024]{2,1,0:T(8,128)(2,1)S(1)}, bf16[4,64,1024]{2,1,0:T(8,128)(2,1)S(1)}, u32[]{:S(2)}, u32[]{:S(2)}) collective-permute-start(bf16[4,64,1024]{2,1,0:T(8,128)(2,1)S(1)} %slice.301), channel_id=1, source_target_pairs={{2,0},{3,1},{0,2},{1,3},{6,4},{7,5},{4,6},{5,7},{10,8},{11,9},{8,1... | collective-permute-start | bytes 1572872 | tf_op jit(solution)/shard_map/ppermute | solution.py:351
  271.0 32.7 %collective-permute-start.36 = (bf16[4,64,1024]{2,1,0:T(8,128)(2,1)S(1)}, bf16[4,64,1024]{2,1,0:T(8,128)(2,1)S(1)}, u32[]{:S(2)}, u32[]{:S(2)}) collective-permute-start(bf16[4,64,1024]{2,1,0:T(8,128)(2,1)S(1)} %slice.302), channel_id=1, source_target_pairs={{1,0},{0,1},{3,2},{2,3},{5,4},{4,5},{7,6},{6,7},{9,8},{8,9},{11,10... | collective-permute-start | bytes 1572872 | tf_op jit(solution)/shard_map/ppermute | solution.py:344
  305.8 26.3 %collective-permute-start.42 = (bf16[128,1024]{1,0:T(8,128)(2,1)S(1)}, bf16[128,1024]{1,0:T(8,128)(2,1)S(1)}, u32[]{:S(2)}, u32[]{:S(2)}) collective-permute-start(bf16[128,1024]{1,0:T(8,128)(2,1)S(1)} %dynamic-slice_bitcast_fusion.11), channel_id=1, source_target_pairs={{0,12},{4,0},{8,4},{12,8},{1,13},{5,1},{9,5},{13,9},{2,14},{6,2},{... | collective-permute-start | bytes 786440 | tf_op jit(solution)/shard_map/ppermute | solution.py:607
  374.3 27.2 %collective-permute-start.47 = (bf16[1024,1024]{1,0:T(8,128)(2,1)}, bf16[1024,1024]{1,0:T(8,128)(2,1)}, u32[]{:S(2)}, u32[]{:S(2)}) collective-permute-start(bf16[1024,1024]{1,0:T(8,128)(2,1)} %feed_in_back.2.refs_1_), channel_id=1, source_target_pairs={{0,16},{16,0},{1,17},{17,1},{2,18},{18,2},{3,19},{19,3},{4,20},{20... | collective-permute-start | bytes 6291464 | tf_op jit(solution)/shard_map/ppermute | solution.py:354
  374.5 25.8 %collective-permute-start.45 = (bf16[4,2,128,512]{3,2,1,0:T(8,128)(2,1)}, bf16[4,2,128,512]{3,2,1,0:T(8,128)(2,1)}, u32[]{:S(2)}, u32[]{:S(2)}) collective-permute-start(bf16[4,2,128,512]{3,2,1,0:T(8,128)(2,1)} %get-tuple-element.637), channel_id=1, source_target_pairs={{2,0},{3,1},{0,2},{1,3},{6,4},{7,5},{4,6},{5,7},{10,8},{11,9},{8,1... | collective-permute-start | bytes 3145736 | tf_op jit(solution)/shard_map/ppermute | solution.py:351
  376.0 25.5 %collective-permute-start.46 = (bf16[4,2,128,512]{3,2,1,0:T(8,128)(2,1)}, bf16[4,2,128,512]{3,2,1,0:T(8,128)(2,1)}, u32[]{:S(2)}, u32[]{:S(2)}) collective-permute-start(bf16[4,2,128,512]{3,2,1,0:T(8,128)(2,1)} %get-tuple-element.639), channel_id=1, source_target_pairs={{1,0},{0,1},{3,2},{2,3},{5,4},{4,5},{7,6},{6,7},{9,8},{8,9},{11,10... | collective-permute-start | bytes 3145736 | tf_op jit(solution)/shard_map/ppermute | solution.py:344
  379.0 36.2 %collective-permute-start.53 = (bf16[256,1024]{1,0:T(8,128)(2,1)S(1)}, bf16[256,1024]{1,0:T(8,128)(2,1)S(1)}, u32[]{:S(2)}, u32[]{:S(2)}) collective-permute-start(bf16[256,1024]{1,0:T(8,128)(2,1)S(1)} %get-tuple-element.902), channel_id=1, source_target_pairs={{4,0},{8,4},{12,8},{0,12},{5,1},{9,5},{13,9},{1,13},{6,2},{10,6},{... | collective-permute-start | bytes 1572872 | tf_op jit(solution)/shard_map/ppermute | solution.py:627
  408.5 38.8 %collective-permute-start.54 = (bf16[256,1024]{1,0:T(8,128)(2,1)S(1)}, bf16[256,1024]{1,0:T(8,128)(2,1)S(1)}, u32[]{:S(2)}, u32[]{:S(2)}) collective-permute-start(bf16[256,1024]{1,0:T(8,128)(2,1)S(1)} %get-tuple-element.901), channel_id=1, source_target_pairs={{8,0},{12,4},{0,8},{4,12},{9,1},{13,5},{1,9},{5,13},{10,2},{14,6},... | collective-permute-start | bytes 1572872 | tf_op jit(solution)/shard_map/ppermute | solution.py:627
  412.2 35.1 %collective-permute-start.48 = (bf16[4,128,512]{2,1,0:T(8,128)(2,1)S(1)}, bf16[4,128,512]{2,1,0:T(8,128)(2,1)S(1)}, u32[]{:S(2)}, u32[]{:S(2)}) collective-permute-start(bf16[4,128,512]{2,1,0:T(8,128)(2,1)S(1)} %get-tuple-element.657), channel_id=1, source_target_pairs={{1,0},{0,1},{3,2},{2,3},{5,4},{4,5},{7,6},{6,7},{9,8},{8,9},{11,10... | collective-permute-start | bytes 1572872 | tf_op jit(solution)/shard_map/ppermute | solution.py:344
  412.7 34.5 %collective-permute-start.49 = (bf16[4,128,512]{2,1,0:T(8,128)(2,1)S(1)}, bf16[4,128,512]{2,1,0:T(8,128)(2,1)S(1)}, u32[]{:S(2)}, u32[]{:S(2)}) collective-permute-start(bf16[4,128,512]{2,1,0:T(8,128)(2,1)S(1)} %get-tuple-element.659), channel_id=1, source_target_pairs={{2,0},{3,1},{0,2},{1,3},{6,4},{7,5},{4,6},{5,7},{10,8},{11,9},{8,1... | collective-permute-start | bytes 1572872 | tf_op jit(solution)/shard_map/ppermute | solution.py:351
  415.2 33.8 %collective-permute-start.50 = (bf16[4,2,64,1024]{3,2,1,0:T(8,128)(2,1)S(1)}, bf16[4,2,64,1024]{3,2,1,0:T(8,128)(2,1)S(1)}, u32[]{:S(2)}, u32[]{:S(2)}) collective-permute-start(bf16[4,2,64,1024]{3,2,1,0:T(8,128)(2,1)S(1)} %get-tuple-element.661), channel_id=1, source_target_pairs={{2,0},{3,1},{0,2},{1,3},{6,4},{7,5},{4,6},{5,7},{10,8},{11,9},{8,1... | collective-permute-start | bytes 3145736 | tf_op jit(solution)/shard_map/ppermute | solution.py:351
  416.8 33.2 %collective-permute-start.51 = (bf16[4,2,64,1024]{3,2,1,0:T(8,128)(2,1)S(1)}, bf16[4,2,64,1024]{3,2,1,0:T(8,128)(2,1)S(1)}, u32[]{:S(2)}, u32[]{:S(2)}) collective-permute-start(bf16[4,2,64,1024]{3,2,1,0:T(8,128)(2,1)S(1)} %get-tuple-element.663), channel_id=1, source_target_pairs={{1,0},{0,1},{3,2},{2,3},{5,4},{4,5},{7,6},{6,7},{9,8},{8,9},{11,10... | collective-permute-start | bytes 3145736 | tf_op jit(solution)/shard_map/ppermute | solution.py:344
  468.6 146.0 %reduce-scatter.9.cloned.1.call-start = ((), (), s32[]{:S(2)}) async-start(), calls=%async_computation.13 | async-start | bytes 1310720 | tf_op jit(solution)/shard_map/reduce_scatter | solution.py:575
  482.5 35.9 %collective-permute-start.58 = (bf16[4,2,64,1024]{3,2,1,0:T(8,128)(2,1)}, bf16[4,2,64,1024]{3,2,1,0:T(8,128)(2,1)}, u32[]{:S(2)}, u32[]{:S(2)}) collective-permute-start(bf16[4,2,64,1024]{3,2,1,0:T(8,128)(2,1)} %get-tuple-element.717), channel_id=1, source_target_pairs={{2,0},{3,1},{0,2},{1,3},{6,4},{7,5},{4,6},{5,7},{10,8},{11,9},{8,1... | collective-permute-start | bytes 3145736 | tf_op jit(solution)/shard_map/ppermute | solution.py:351
  482.9 35.5 %collective-permute-start.59 = (bf16[4,2,64,1024]{3,2,1,0:T(8,128)(2,1)}, bf16[4,2,64,1024]{3,2,1,0:T(8,128)(2,1)}, u32[]{:S(2)}, u32[]{:S(2)}) collective-permute-start(bf16[4,2,64,1024]{3,2,1,0:T(8,128)(2,1)} %get-tuple-element.719), channel_id=1, source_target_pairs={{1,0},{0,1},{3,2},{2,3},{5,4},{4,5},{7,6},{6,7},{9,8},{8,9},{11,10... | collective-permute-start | bytes 3145736 | tf_op jit(solution)/shard_map/ppermute | solution.py:344
  518.4 38.1 %collective-permute-start.64 = (bf16[1024,1024]{1,0:T(8,128)(2,1)}, bf16[1024,1024]{1,0:T(8,128)(2,1)}, u32[]{:S(2)}, u32[]{:S(2)}) collective-permute-start(bf16[1024,1024]{1,0:T(8,128)(2,1)} %feed_in_back.3.refs_1_), channel_id=1, source_target_pairs={{0,16},{16,0},{1,17},{17,1},{2,18},{18,2},{3,19},{19,3},{4,20},{20... | collective-permute-start | bytes 6291464 | tf_op jit(solution)/shard_map/ppermute | solution.py:354
  518.5 26.3 %collective-permute-start.62 = (bf16[4,2,128,512]{3,2,1,0:T(8,128)(2,1)}, bf16[4,2,128,512]{3,2,1,0:T(8,128)(2,1)}, u32[]{:S(2)}, u32[]{:S(2)}) collective-permute-start(bf16[4,2,128,512]{3,2,1,0:T(8,128)(2,1)} %get-tuple-element.729), channel_id=1, source_target_pairs={{2,0},{3,1},{0,2},{1,3},{6,4},{7,5},{4,6},{5,7},{10,8},{11,9},{8,1... | collective-permute-start | bytes 3145736 | tf_op jit(solution)/shard_map/ppermute | solution.py:351
  519.8 26.3 %collective-permute-start.63 = (bf16[4,2,128,512]{3,2,1,0:T(8,128)(2,1)}, bf16[4,2,128,512]{3,2,1,0:T(8,128)(2,1)}, u32[]{:S(2)}, u32[]{:S(2)}) collective-permute-start(bf16[4,2,128,512]{3,2,1,0:T(8,128)(2,1)} %get-tuple-element.731), channel_id=1, source_target_pairs={{1,0},{0,1},{3,2},{2,3},{5,4},{4,5},{7,6},{6,7},{9,8},{8,9},{11,10... | collective-permute-start | bytes 3145736 | tf_op jit(solution)/shard_map/ppermute | solution.py:344
  521.3 97.1 %reduce-scatter.7.cloned.1.call-start = ((), (), s32[]{:S(2)}) async-start(), calls=%async_computation.12 | async-start | bytes 1310720 | tf_op jit(solution)/shard_map/reduce_scatter | solution.py:575
  527.0 29.5 %collective-permute-start.60 = (bf16[4,64,1024]{2,1,0:T(8,128)(2,1)S(1)}, bf16[4,64,1024]{2,1,0:T(8,128)(2,1)S(1)}, u32[]{:S(2)}, u32[]{:S(2)}) collective-permute-start(bf16[4,64,1024]{2,1,0:T(8,128)(2,1)S(1)} %get-tuple-element.725), channel_id=1, source_target_pairs={{1,0},{0,1},{3,2},{2,3},{5,4},{4,5},{7,6},{6,7},{9,8},{8,9},{11,10... | collective-permute-start | bytes 1572872 | tf_op jit(solution)/shard_map/ppermute | solution.py:344
  527.3 29.2 %collective-permute-start.61 = (bf16[4,64,1024]{2,1,0:T(8,128)(2,1)S(1)}, bf16[4,64,1024]{2,1,0:T(8,128)(2,1)S(1)}, u32[]{:S(2)}, u32[]{:S(2)}) collective-permute-start(bf16[4,64,1024]{2,1,0:T(8,128)(2,1)S(1)} %get-tuple-element.727), channel_id=1, source_target_pairs={{2,0},{3,1},{0,2},{1,3},{6,4},{7,5},{4,6},{5,7},{10,8},{11,9},{8,1... | collective-permute-start | bytes 1572872 | tf_op jit(solution)/shard_map/ppermute | solution.py:351
  567.7 101.5 %reduce-scatter.17.cloned.1.call-start = ((), (), s32[]{:S(2)}) async-start(), calls=%async_computation.17 | async-start | bytes 1310720 | tf_op jit(solution)/shard_map/reduce_scatter | solution.py:575
  571.1 43.4 %collective-permute-start.70 = (bf16[256,1024]{1,0:T(8,128)(2,1)}, bf16[256,1024]{1,0:T(8,128)(2,1)}, u32[]{:S(2)}, u32[]{:S(2)}) collective-permute-start(bf16[256,1024]{1,0:T(8,128)(2,1)} %get-tuple-element.899), channel_id=1, source_target_pairs={{20,16},{24,20},{28,24},{16,28},{21,17},{25,21},{29,25},{17,29},{2... | collective-permute-start | bytes 1572872 | tf_op jit(solution)/shard_map/ppermute | solution.py:630
  577.8 36.7 %collective-permute-start.65 = (bf16[4,128,512]{2,1,0:T(8,128)(2,1)}, bf16[4,128,512]{2,1,0:T(8,128)(2,1)}, u32[]{:S(2)}, u32[]{:S(2)}) collective-permute-start(bf16[4,128,512]{2,1,0:T(8,128)(2,1)} %get-tuple-element.744), channel_id=1, source_target_pairs={{1,0},{0,1},{3,2},{2,3},{5,4},{4,5},{7,6},{6,7},{9,8},{8,9},{11,10... | collective-permute-start | bytes 1572872 | tf_op jit(solution)/shard_map/ppermute | solution.py:344
  579.4 35.2 %collective-permute-start.66 = (bf16[4,128,512]{2,1,0:T(8,128)(2,1)}, bf16[4,128,512]{2,1,0:T(8,128)(2,1)}, u32[]{:S(2)}, u32[]{:S(2)}) collective-permute-start(bf16[4,128,512]{2,1,0:T(8,128)(2,1)} %get-tuple-element.746), channel_id=1, source_target_pairs={{2,0},{3,1},{0,2},{1,3},{6,4},{7,5},{4,6},{5,7},{10,8},{11,9},{8,1... | collective-permute-start | bytes 1572872 | tf_op jit(solution)/shard_map/ppermute | solution.py:351
  579.8 36.7 %collective-permute-start.67 = (bf16[4,2,64,1024]{3,2,1,0:T(8,128)(2,1)}, bf16[4,2,64,1024]{3,2,1,0:T(8,128)(2,1)S(1)}, u32[]{:S(2)}, u32[]{:S(2)}) collective-permute-start(bf16[4,2,64,1024]{3,2,1,0:T(8,128)(2,1)} %copy-done.166), channel_id=1, source_target_pairs={{2,0},{3,1},{0,2},{1,3},{6,4},{7,5},{4,6},{5,7},{10,8},{11,9},{8,1... | collective-permute-start | bytes 3145736 | tf_op jit(solution)/shard_map/ppermute | solution.py:351
  581.4 36.1 %collective-permute-start.68 = (bf16[4,2,64,1024]{3,2,1,0:T(8,128)(2,1)}, bf16[4,2,64,1024]{3,2,1,0:T(8,128)(2,1)S(1)}, u32[]{:S(2)}, u32[]{:S(2)}) collective-permute-start(bf16[4,2,64,1024]{3,2,1,0:T(8,128)(2,1)} %copy-done.165), channel_id=1, source_target_pairs={{1,0},{0,1},{3,2},{2,3},{5,4},{4,5},{7,6},{6,7},{9,8},{8,9},{11,10... | collective-permute-start | bytes 3145736 | tf_op jit(solution)/shard_map/ppermute | solution.py:344
  630.8 36.5 %collective-permute-start.73 = (bf16[1024,1024]{1,0:T(8,128)(2,1)}, bf16[1024,1024]{1,0:T(8,128)(2,1)}, u32[]{:S(2)}, u32[]{:S(2)}) collective-permute-start(bf16[1024,1024]{1,0:T(8,128)(2,1)} %project_qkv_back.3), channel_id=1, source_target_pairs={{0,16},{16,0},{1,17},{17,1},{2,18},{18,2},{3,19},{19,3},{4,20},{20... | collective-permute-start | bytes 6291464 | tf_op jit(solution)/shard_map/ppermute | solution.py:354
  631.0 113.8 %reduce-scatter.15.cloned.1.call-start = ((), (), s32[]{:S(2)}) async-start(), calls=%async_computation.16 | async-start | bytes 1310720 | tf_op jit(solution)/shard_map/reduce_scatter | solution.py:575
  633.3 47.9 %collective-permute-start.79 = (bf16[256,1024]{1,0:T(8,128)(2,1)}, bf16[256,1024]{1,0:T(8,128)(2,1)}, u32[]{:S(2)}, u32[]{:S(2)}) collective-permute-start(bf16[256,1024]{1,0:T(8,128)(2,1)} %dynamic-slice_bitcast_fusion.3), channel_id=1, source_target_pairs={{12,0},{0,4},{4,8},{8,12},{13,1},{1,5},{5,9},{9,13},{14,2},{2,6},{... | collective-permute-start | bytes 1572872 | tf_op jit(solution)/shard_map/ppermute | solution.py:627
  655.5 25.7 %collective-permute-start.77 = (bf16[256,1024]{1,0:T(8,128)(2,1)}, bf16[256,1024]{1,0:T(8,128)(2,1)}, u32[]{:S(2)}, u32[]{:S(2)}) collective-permute-start(bf16[256,1024]{1,0:T(8,128)(2,1)} %get-tuple-element.898), channel_id=1, source_target_pairs={{24,16},{28,20},{16,24},{20,28},{25,17},{29,21},{17,25},{21,29},{2... | collective-permute-start | bytes 1572872 | tf_op jit(solution)/shard_map/ppermute | solution.py:630
  667.3 24.3 %collective-permute-start.74 = (bf16[4,2,64,1024]{3,2,1,0:T(8,128)(2,1)}, bf16[4,2,64,1024]{3,2,1,0:T(8,128)(2,1)S(1)}, u32[]{:S(2)}, u32[]{:S(2)}) collective-permute-start(bf16[4,2,64,1024]{3,2,1,0:T(8,128)(2,1)} %get-tuple-element.800), channel_id=1, source_target_pairs={{2,0},{3,1},{0,2},{1,3},{6,4},{7,5},{4,6},{5,7},{10,8},{11,9},{8,1... | collective-permute-start | bytes 3145736 | tf_op jit(solution)/shard_map/ppermute | solution.py:351
  672.8 76.7 %reduce-scatter.13.cloned.1.call-start = ((), (), s32[]{:S(2)}) async-start(), calls=%async_computation.15 | async-start | bytes 1310720 | tf_op jit(solution)/shard_map/reduce_scatter | solution.py:575
  699.2 31.6 %collective-permute-start.80 = (bf16[256,1024]{1,0:T(8,128)(2,1)S(1)}, bf16[256,1024]{1,0:T(8,128)(2,1)}, u32[]{:S(2)}, u32[]{:S(2)}) collective-permute-start(bf16[256,1024]{1,0:T(8,128)(2,1)S(1)} %get-tuple-element.895), channel_id=1, source_target_pairs={{4,0},{8,4},{12,8},{0,12},{5,1},{9,5},{13,9},{1,13},{6,2},{10,6},{... | collective-permute-start | bytes 1572872 | tf_op jit(solution)/shard_map/ppermute | solution.py:630
  704.8 27.3 %collective-permute-start.81 = (bf16[256,1024]{1,0:T(8,128)(2,1)}, bf16[256,1024]{1,0:T(8,128)(2,1)}, u32[]{:S(2)}, u32[]{:S(2)}) collective-permute-start(bf16[256,1024]{1,0:T(8,128)(2,1)} %get-tuple-element.894), channel_id=1, source_target_pairs={{8,0},{12,4},{0,8},{4,12},{9,1},{13,5},{1,9},{5,13},{10,2},{14,6},... | collective-permute-start | bytes 1572872 | tf_op jit(solution)/shard_map/ppermute | solution.py:630
  718.9 24.6 %collective-permute-start.82 = (bf16[256,1024]{1,0:T(8,128)(2,1)S(1)}, bf16[256,1024]{1,0:T(8,128)(2,1)}, u32[]{:S(2)}, u32[]{:S(2)}) collective-permute-start(bf16[256,1024]{1,0:T(8,128)(2,1)S(1)} %get-tuple-element.893), channel_id=1, source_target_pairs={{12,0},{0,4},{4,8},{8,12},{13,1},{1,5},{5,9},{9,13},{14,2},{2,6},{... | collective-permute-start | bytes 1572872 | tf_op jit(solution)/shard_map/ppermute | solution.py:630
  (247 other events, 2250.7 us)
Sparse Core Ops, SparseCore 0:
  12.1 34.0 all-gather.6
  57.8 32.6 all-gather.8
  110.8 28.0 all-gather.10
  144.6 34.1 all-gather.12
  184.1 31.5 all-gather.14
  221.6 27.9 all-gather.16
  468.7 25.7 reduce-scatter.10
  521.5 24.8 reduce-scatter.8
  567.8 31.3 reduce-scatter.6
  631.1 36.5 reduce-scatter.16
  672.9 31.9 reduce-scatter.14
  719.0 30.5 reduce-scatter.12

commit v3 on v2

--- a/solution.py
+++ b/solution.py
@@ -452,7 +452,7 @@
 class Scatter:
     def __init__(self, place):
         self.place = place
-        self.at = jnp.stack([place.y, place.x]).astype(jnp.int32)
+        self.at = jnp.stack([place.y, place.x, place.section]).astype(jnp.int32)
 
     def product(self, x, grads, ready=None):
         place = self.place
@@ -461,8 +461,8 @@
         span = x.shape[1] // nz
         rows = span // (ny * nx)
         widths = [g.shape[1] for g in grads]
-        extra = [] if ready is None else [ready]
-        cols = sum(widths) + sum(e.shape[1] for e in extra)
+        extra = [] if ready is None else list(ready)
+        cols = sum(widths) + (extra[0].shape[1] if extra else 0)
         half = cols // 2
 
         def body(at_ref, x_ref, *refs):
@@ -481,8 +481,10 @@
                     value = nn_dot(turned, ref[:, start:stop]).astype(BF)
                     full_ref[:, :, :, first + start : first + stop] = value.reshape(ny, nx, rows, stop - start)
                 first += wide
-            for ref in extra_refs:
-                full_ref[:, :, :, first:] = ref[...].reshape(ny, nx, rows, cols - first)
+            if extra:
+                here = (pl.program_id(0) < nz // 2) == (at_ref[2] == 0)
+                value = jnp.where(here, extra_refs[0][...], extra_refs[1][...])
+                full_ref[:, :, :, first:] = value.reshape(ny, nx, rows, cols - first)
             for r, ref in enumerate(left_refs):
                 ref[0] = full_ref[(at_ref[0] + r) % ny, :, :, :half]
             for r, ref in enumerate(right_refs):
@@ -504,7 +506,7 @@
                 grid=(nz,),
                 in_specs=[pl.BlockSpec((tokens, span), lambda z, at_ref: (0, z))]
                 + [pl.BlockSpec((tokens, wide), lambda z, at_ref: (0, 0)) for wide in widths]
-                + [pl.BlockSpec((span, e.shape[1]), lambda z, at_ref: (z, 0)) for e in extra],
+                + [pl.BlockSpec((span, e.shape[1]), lambda z, at_ref: (z % (nz // 2), 0)) for e in extra],
                 out_specs=[pl.BlockSpec((1, nx, rows, half), lambda z, at_ref: (z, 0, 0, 0))] * ny
                 + [pl.BlockSpec((1, ny, rows, half), lambda z, at_ref: (z, 0, 0, 0))] * nx
                 + [pl.BlockSpec((8, sum(widths)), lambda z, at_ref: (0, 0))],
@@ -744,8 +746,8 @@
     cot_half = half_rows(place, cotangent.reshape(count, local, width))
     smalls = [layer_small(layer) for layer in range(2)]
 
-    def attention_in(layer_input, w_qkv, layer):
-        q, k, v = row_product(
+    def project_in(layer_input, w_qkv, layer):
+        return row_product(
             [layer_input],
             w_qkv,
             False,
@@ -755,6 +757,8 @@
             lambda total, bias: jnp.split(total + bias, 3, axis=1),
             "project_qkv",
         )
+
+    def attention(q, k, v):
         if groups > 1:
             k, v = gather_groups(k), gather_groups(v)
         mixed, lse = attend_forward(q, k, v, code_k, seg_q, head_dim)
@@ -782,77 +786,107 @@
         return norm_rows_forward(low, place.sibling(low), normed_low, live, table)
 
     columns, got, whole, more = [None] * 6, [None] * 6, [None] * 6, [None] * 6
+
+    def near(at):
+        got[at] = gathers[at].first(columns[at])
+
+    def far(at):
+        more[at] = gathers[at].second(got[at])
+
+    def along_z(at):
+        columns[at] = gathers[at].along_z()
+
+    def arrived(at):
+        split = 3 * half if at % 3 == 0 else columns[at].shape[2]
+        whole[at] = gathers[at].whole(columns[at], got[at], more[at], split)
+
+    def step_end(state, known):
+        later = [gathers[at].shard for at in range(3, 6)]
+        held = (got, more, columns[:known], later, state)
+        held = tie(*held)
+        got[:], more[:], columns[:known] = held[0], held[1], held[2]
+        for at in range(3, 6):
+            gathers[at].shard = held[3][at - 3]
+        return held[4]
+
     token_pieces = to_pieces(place, token_half, range(2))
-    columns[0] = gathers[0].along_z()
-    columns[0], token_pieces, token_half, gathers[1].shard = tie(
-        columns[0], token_pieces, token_half, gathers[1].shard
-    )
-    got[0] = gathers[0].first(columns[0])
+    along_z(0)
+    token_pieces, token_half, code_k, seg_q, live = step_end((token_pieces, token_half, code_k, seg_q, live), 1)
+
+    near(0)
+    along_z(1)
     token_pieces += to_pieces(place, token_half, range(2, count))
-    columns[1] = gathers[1].along_z()
-    got[0], token_pieces = tie(got[0], token_pieces)
-    more[0] = gathers[0].second(got[0])
+    token_pieces = step_end(token_pieces, 1)
+
+    far(0)
+    along_z(2)
     layer_input = join_halves(place, in_positions(place, token_pieces))
-    more[0], layer_input, columns[1], gathers[2].shard = tie(more[0], layer_input, columns[1], gathers[2].shard)
-
-    def arrived(step):
-        split = 3 * half if step % 3 == 0 else columns[step].shape[2]
-        whole[step] = gathers[step].whole(columns[step], got[step], more[step], split)
-
+    layer_input = step_end(layer_input, 2)
     arrived(0)
-    inputs, attns, projs, outs = [layer_input, None], [None] * 2, [None] * 2, [None] * 2
-    norms, feeds, ends = [None] * 2, [None] * 2, [None] * 2
-    cot_pieces = []
-    for step in range(6):
-        layer = step // 3
-        if step > 0:
-            more[step] = gathers[step].second(got[step])
-        if step + 1 < 6:
-            got[step + 1] = gathers[step + 1].first(columns[step + 1])
-        if step + 2 < 6:
-            columns[step + 2] = gathers[step + 2].along_z()
-        if step in (0, 4):
-            if step == 4:
-                ends[0] = feed_norm(norms[0][2], outs[0], 0)
-                inputs[1] = ends[0][2]
-            layer = step // 4
-            w_qkv, columns_proj = whole[3 * layer]
-            projs[layer] = proj_whole(columns_proj)
-            attns[layer] = attention_in(inputs[layer], w_qkv, layer)
-            outs[layer] = to_width([attns[layer][3]], projs[layer], False, "project_out")
-        elif step == 1:
-            norms[0] = attention_norm(inputs[0], outs[0], 0)
-            cot_pieces += to_pieces(place, cot_half, range(2))
-        elif step == 2:
-            feeds[0] = feed_in(norms[0][2], whole[1][0], 0)
-            cot_pieces += to_pieces(place, cot_half, range(2, count - 1))
-        elif step == 3:
-            outs[0] = to_width([feeds[0][0]], whole[2][0], False, "feed_out")
-        elif step == 5:
-            norms[1] = attention_norm(inputs[1], outs[1], 1)
-            feeds[1] = feed_in(norms[1][2], whole[4][0], 1)
-            cot_pieces += to_pieces(place, cot_half, [count - 1])
-        shard = gathers[step + 3].shard if step + 3 < 6 else ()
-        state = (inputs, attns, projs, outs, norms, feeds, ends, cot_pieces)
-        got, more, columns, shard, state, cot_half = tie(got, more, columns, shard, state, cot_half)
-        inputs, attns, projs, outs, norms, feeds, ends, cot_pieces = state
-        if step + 3 < 6:
-            gathers[step + 3].shard = shard
-        if step > 0:
-            arrived(step)
+
+    near(1)
+    w_qkv, columns_proj = whole[0]
+    projs = [proj_whole(columns_proj), None]
+    q, k, v = project_in(layer_input, w_qkv, 0)
+    along_z(3)
+    columns[2], q, projs = tie(columns[2], q, projs)
+    near(2)
+    attns = [attention(q, k, v), None]
+    outs = [to_width([attns[0][3]], projs[0], False, "project_out"), None]
+    layer_input, attns, projs, outs = step_end((layer_input, attns, projs, outs), 4)
+    inputs = [layer_input, None]
+
+    far(1)
+    far(2)
+    along_z(4)
+    norms = [attention_norm(inputs[0], outs[0], 0), None]
+    norms, cot_half = step_end((norms, cot_half), 5)
+    arrived(1)
+    arrived(2)
+
+    near(3)
+    along_z(5)
+    feeds = [feed_in(norms[0][2], whole[1][0], 0), None]
+    outs[0] = to_width([feeds[0][0]], whole[2][0], False, "feed_out")
+    cot_pieces = to_pieces(place, cot_half, range(count))
+    feeds, outs, cot_pieces = step_end((feeds, outs, cot_pieces), 5)
+
+    far(3)
+    near(4)
+    ends = [feed_norm(norms[0][2], outs[0], 0), None]
+    ends = step_end(ends, 6)
+    inputs[1] = ends[0][2]
+    arrived(3)
+
+    far(4)
+    near(5)
+    w_qkv, columns_proj = whole[3]
+    projs[1] = proj_whole(columns_proj)
+    q, k, v = project_in(inputs[1], w_qkv, 1)
+    attns[1] = attention(q, k, v)
+    outs[1] = to_width([attns[1][3]], projs[1], False, "project_out")
+    attns, projs, outs, inputs = step_end((attns, projs, outs, inputs), 6)
+    arrived(4)
+
+    far(5)
+    norms[1] = attention_norm(inputs[1], outs[1], 1)
+    feeds[1] = feed_in(norms[1][2], whole[4][0], 1)
+    first_back = from_sequences(place, inputs[1].reshape(count, local, width), range(count - 1), 0)
+    norms, feeds, first_back, first_out = step_end((norms, feeds, first_back, inputs[1]), 6)
+    arrived(5)
 
     outs[1] = to_width([feeds[1][0]], whole[5][0], False, "feed_out")
-    outs[1], cot_pieces, norms = tie(outs[1], cot_pieces, norms)
+    first_back += from_sequences(place, first_out.reshape(count, local, width), [count - 1], 0)
+    outs[1], cot_pieces, norms, first_back = tie(outs[1], cot_pieces, norms, first_back)
     ends[1] = feed_norm(norms[1][2], outs[1], 1)
     terms = [join_halves(place, in_positions(place, cot_pieces))]
 
     scatter = Scatter(place)
-    columns = [[None] * 3, [None] * 3]
     totals = [[None] * 3, [None] * 3]
     small_grads = [None, None]
-    act_value = jnp.where(first_section, ends[0][2], ends[1][2]).reshape(count, local, width)
+    last_out = ends[1][2].reshape(count, local, width)
+    last_back = from_sequences(place, last_out, range(count), 1)
     attn_parts = back_one = grad_one = None
-    act_back = []
     for layer in (1, 0):
         gains = smalls[layer][0]
         u = inputs[layer]
@@ -863,18 +897,14 @@
         w_qkv = whole[3 * layer][0]
         w_proj, w_in, w_out = projs[layer], whole[3 * layer + 1][0], whole[3 * layer + 2][0]
 
-        if layer == 0:
-            columns[1][1] = scatter.third(in_parts)
         second = norm_rows_backward(terms, unit_two, inverse_two, gains[1:2], layer == 0)
         grad_ff, second_sums = second[:2]
         out_parts, _ = scatter.product(activated, [grad_ff])
         if layer == 1:
-            out_parts, grad_ff, act_value = tie(out_parts, grad_ff, act_value)
-            act_back += from_sequences(place, act_value, range(count - 1))
+            out_parts, grad_ff = tie(out_parts, grad_ff)
         else:
             grad_one = second[2].reshape(count, local, width)
-            out_parts, grad_ff, grad_one, columns = tie(out_parts, grad_ff, grad_one, columns)
-            totals[1][1] = scatter.along_z(columns[1][1])
+            out_parts, grad_ff, grad_one = tie(out_parts, grad_ff, grad_one)
             back_one = from_sequences(place, grad_one, range(2), 1)
 
         out_parts = scatter.first(out_parts)
@@ -889,16 +919,12 @@
             "feed_out_back",
         )
         low = to_width([grad_hidden], w_in, True, "feed_in_back")
-        low, grad_hidden, attn_parts = tie(low, grad_hidden, attn_parts)
-
+        in_parts, hidden_sums = scatter.product(normed_low, [grad_hidden])
+        low, in_parts, out_parts, attn_parts, last_back = tie(low, in_parts, out_parts, attn_parts, last_back)
+        other = place.sibling(low)
         if layer == 0:
             attn_parts = scatter.second(attn_parts)
-        other = place.sibling(low)
-        in_parts, hidden_sums = scatter.product(normed_low, [grad_hidden])
-        attn_parts, out_parts, in_parts, low, other = tie(attn_parts, out_parts, in_parts, low, other)
-
-        if layer == 0:
-            columns[1][0] = scatter.third(attn_parts)
+
         out_parts = scatter.second(out_parts)
         in_parts = scatter.first(in_parts)
         grad_branch, first_sums = norm_rows_backward(
@@ -911,35 +937,31 @@
         mine = lax.dynamic_slice_in_dim(grad_w_proj, section * half, half, 1)
         sent = lax.dynamic_slice_in_dim(grad_w_proj, (1 - section) * half, half, 1)
         if layer == 0:
-            grad_mixed, columns, sent = tie(grad_mixed, columns, sent)
-            totals[1][0] = scatter.along_z(columns[1][0])
-
-        grad_w_proj = place.in_order(mine, place.sibling(sent), 0)
+            attn_parts, grad_mixed, sent = tie(attn_parts, grad_mixed, sent)
+            totals[1][0] = scatter.along_z(scatter.third(attn_parts))
+
+        grad_w_proj = (mine, place.sibling(sent))
         dq, dk, dv = attend_backward(
             q, k, v, grad_mixed, lse, code_k, seg_q, head_dim, BF if groups == 1 else F32
         )
         if groups > 1:
             dk, dv = scatter_groups(dk), scatter_groups(dv)
-        if layer == 1:
-            out_parts, in_parts, dq, dk, dv, grad_w_proj, act_back, act_value = tie(
-                out_parts, in_parts, dq, dk, dv, grad_w_proj, act_back, act_value
-            )
-            act_back += from_sequences(place, act_value, [count - 1])
-        else:
-            out_parts, in_parts, dq, dk, dv, grad_w_proj, back_one, grad_one, totals = tie(
-                out_parts, in_parts, dq, dk, dv, grad_w_proj, back_one, grad_one, totals
-            )
+        out_parts, in_parts, dq, dk, dv, grad_w_proj, back_one, grad_one, totals = tie(
+            out_parts, in_parts, dq, dk, dv, grad_w_proj, back_one, grad_one, totals
+        )
+
+        totals[layer][2] = scatter.along_z(scatter.third(out_parts))
+        in_parts = scatter.second(in_parts)
+        if layer == 0:
             back_one += from_sequences(place, grad_one, range(2, count), 1)
-
-        columns[layer][2] = scatter.third(out_parts)
-        in_parts = scatter.second(in_parts)
+        attn_parts, dqkv_rows = scatter.product(u, [dq, dk, dv], grad_w_proj)
+        in_parts, attn_parts, dq, dk, dv = tie(in_parts, attn_parts, dq, dk, dv)
+        attn_parts = scatter.first(attn_parts)
+        in_column = scatter.third(in_parts)
         low = to_width([dq, dk, dv], w_qkv, True, "project_qkv_back")
-        low, dq, dk, dv, columns = tie(low, dq, dk, dv, columns)
-        totals[layer][2] = scatter.along_z(columns[layer][2])
+        low, in_column = tie(low, in_column)
+        totals[layer][1] = scatter.along_z(in_column)
         other = place.sibling(low)
-        attn_parts, dqkv_rows = scatter.product(u, [dq, dk, dv], grad_w_proj)
-        in_parts, attn_parts, low, other = tie(in_parts, attn_parts, low, other)
-        attn_parts = scatter.first(attn_parts)
         terms = [grad_branch, low, other]
 
         here = jnp.where(section == layer, 1.0, 0.0)
@@ -960,21 +982,23 @@
             [by_chip, ff_spread.reshape(chips, -1), jnp.broadcast_to(squares, (chips, 8))], axis=1
         )
 
-    totals[0][1] = scatter.along_z(scatter.third(in_parts))
     grad_zero = sum([term.astype(F32) for term in terms]).astype(BF).reshape(count, local, width)
     back_zero = from_sequences(place, grad_zero, range(count), 0)
     mine = jnp.where(first_section, small_grads[0], small_grads[1])
     sent = jnp.where(first_section, small_grads[1], small_grads[0])
     small_rows = mine + place.sibling(sent)
-    attn_parts, small_rows, back_one, act_back = tie(attn_parts, small_rows, back_one, act_back)
+    attn_parts, small_rows, first_back, last_back, back_one, grad_zero = tie(
+        attn_parts, small_rows, first_back, last_back, back_one, grad_zero
+    )
     attn_parts = scatter.second(attn_parts)
     small_total = small_scatter(place, small_rows)
+    attn_parts, back_zero = tie(attn_parts, back_zero)
     totals[0][0] = scatter.along_z(scatter.third(attn_parts))
 
     def give_back(pieces):
         return place_rotated(pieces, place.ctx % count, count).reshape(1, micro, seqs, local, width)
 
-    activations = give_back(act_back)
+    activations = give_back([jnp.where(first_section, a, b) for a, b in zip(first_back, last_back)])
     input_grads = give_back([jnp.where(first_section, a, b) for a, b in zip(back_zero, back_one)])
 
     def halves(index):

time: 774 us -> 750 us (0.969)
  waiting for transfers between devices: 180 us -> 149 us
  local copies, waits for them, and re-layouts: 129 us -> 142 us
    ppermute x25, waiting for transfers between devices: 88.6 us -> 52.9 us  [from_y(): return lax.ppermute(value, 'fsdp', pairs)]
    ppermute x9, starting transfers between devices: 34.2 us -> 14.5 us  [to_pieces(): lax.ppermute(sent, 'ctx', pairs)]
    reduce_scatter x6, waiting for transfers between devices: 3.92 us -> 14.7 us  [along_z(): return lax.psum_scatter(column, 'ctx', scatter_dimension=0, tiled=True)]
    ppermute x22, starting transfers between devices: 4.7 us -> 14.1 us  [sibling(): return lax.ppermute(value, 'section', [(0, 1), (1, 0)])]
    ppermute x6 -> x12, starting transfers between devices: 19.2 us -> 28.3 us  [from_sequences(): lax.ppermute(sent, ('section', 'ctx'), [(first + a, first + b) for a, b i...]
    unnamed x423 -> x355, local copies, waits for them, and re-layouts: 81.9 us -> 80.1 us
  transfers between devices with their start and end apart: 105 -> 108, of which waited for: 32 -> 29; matrix products, arithmetic and copies ran while one was open for 13% -> 17% of each run, Pallas kernels for 28% -> 32%
where the time goes in v3:
time: 750 us; the launch traced here: 740 us
  Pallas kernels  254 us (34%)
  waiting for transfers between devices  149 us (20%)
  local copies, waits for them, and re-layouts  142 us (19%)
  starting transfers between devices  110 us (15%)
  other arithmetic  46.9 us (6%)
  matrix products  19.7 us (3%)
  between operations  18.1 us (2%)
    unnamed x355, local copies, waits for them, and re-layouts  80.1 us
    pallas_call x14, Pallas kernels, row_product(): pl.pallas_call(body, grid=(rows // block,), in_specs=[pl.BlockSpec((block...  57.2 us
    pallas_call x2, Pallas kernels, attend_backward(): pl.pallas_call(lambda *refs: attend_backward_kernel(head_dim, *refs), gri...  54.5 us
    ppermute x25, waiting for transfers between devices, from_y(): return lax.ppermute(value, 'fsdp', pairs)  52.9 us
    pallas_call x6, Pallas kernels, product(): pl.pallas_call(body, grid_spec=pltpu.PrefetchScalarGridSpec(num_scalar_pr...  43.9 us
    ppermute x9, waiting for transfers between devices, to_pieces(): lax.ppermute(sent, 'ctx', pairs)  30.8 us
    pallas_call x2, Pallas kernels, attend_forward(): pl.pallas_call(lambda *refs: attend_forward_kernel(head_dim, *refs), grid...  29.7 us
    ppermute x12, starting transfers between devices, from_sequences(): lax.ppermute(sent, ('section', 'ctx'), [(first + a, first + b) for a, b i...  28.3 us
  transfers between devices with their start and end apart: 108, of which 29 were waited for; matrix products, arithmetic and copies ran while one was open for 17% of the time, Pallas kernels for 32%

profile of v3, /device:TPU:0, one launch (start us, length us, event | category | flops | bytes accessed | tf_op | source)
XLA Modules:
  0.0 740.5 jit_solution(7981970453316580611)
XLA Ops:
  10.6 4.7 collective-permute-start.4
  23.3 3.8 dynamic-slice_reduce_fusion
  38.1 8.3 %all-gather.7.cloned.1.call-done = bf16[256,2048]{1,0:T(8,128)(2,1)} async-done(((bf16[64,2048]{1,0:T(8,128)(2,1)}), bf16[256,2048]{1,0:T(8,128)(2,1)}) %all-gather.7.cloned.1.call-update) | async-done | bytes 1048592 | tf_op jit(solution)/shard_map/all_gather | solution.py:378
  53.7 6.3 collective-permute-done.10
  60.0 24.4 %collective-permute-done.9 = bf16[128,1024]{1,0:T(8,128)(2,1)} collective-permute-done((bf16[128,1024]{1,0:T(8,128)(2,1)}, bf16[128,1024]{1,0:T(8,128)(2,1)}, u32[]{:S(2)}, u32[]{:S(2)}) %collective-permute-start.9) | collective-permute-done | bytes 262176 | tf_op jit(solution)/shard_map/ppermute | solution.py:609
  103.2 8.2 %collective-permute-done.11.refs_3_ = bf16[4,64,1024]{2,1,0:T(8,128)(2,1)} collective-permute-done((bf16[4,64,1024]{2,1,0:T(8,128)(2,1)}, bf16[4,64,1024]{2,1,0:T(8,128)(2,1)}, u32[]{:S(2)}, u32[]{:S(2)}) %collective-permute-start.11) | collective-permute-done | bytes 524320 | tf_op jit(solution)/shard_map/ppermute | solution.py:351
  114.8 3.2 assemble.6
  127.7 3.9 project_qkv.2
  141.1 14.8 %attend_forward.2 = (bf16[1024,512]{1,0:T(8,128)(2,1)S(1)}, f32[4,2,1024]{2,1,0:T(2,128)S(1)}) custom-call(bf16[1024,512]{1,0:T(8,128)(2,1)S(1)} %copy-done.110, bf16[1024,512]{1,0:T(8,128)(2,1)S(1)} %copy-done.113, bf16[1024,512]{1,0:T(8,128)(2,1)S(1)} %copy-done.116, s32[1024,1]{1,0:T(8,128)S(1)} %get-tuple-element.425.refs_3_.refs_5_, ...), custom_call_target="tpu_custom_call" | custom-call | flops 3006477056 | bytes 1468006 | tf_op jit(solution)/shard_map/attend_forward/pallas_call | solution.py:124
  159.1 11.4 %collective-permute-done.18.refs_1_ = bf16[4,128,1024]{2,1,0:T(8,128)(2,1)} collective-permute-done((bf16[4,128,1024]{2,1,0:T(8,128)(2,1)}, bf16[4,128,1024]{2,1,0:T(8,128)(2,1)}, u32[]{:S(2)}, u32[]{:S(2)}) %collective-permute-start.18) | collective-permute-done | bytes 1048608 | tf_op jit(solution)/shard_map/ppermute | solution.py:344
  187.1 5.1 norm_forward.4
  194.4 4.3 collective-permute-done.22.refs_3_
  198.7 3.0 collective-permute-done.23.refs_4_
  206.4 3.2 collective-permute-start.28
  209.7 3.2 assemble.7
  213.0 9.3 %fusion.4 = (bf16[1024,2048]{1,0:T(8,128)(2,1)}, bf16[1024,2048]{1,0:T(8,128)(2,1)S(1)}) fusion(f32[2048]{0:T(1024)S(1)} %bitcast.386, bf16[1024,1024]{1,0:T(8,128)(2,1)S(1)} %get-tuple-element.619.before_ref.x_ref, bf16[1024,2048]{1,0:T(8,128)(2,1)S(1)} %bitcast.303), kind=kOutput, calls=%fused_computation.6 | convolution fusion | flops 4320133120 | bytes 14688256 | tf_op jit(solution)/shard_map/dot_general | solution.py:34
  222.4 4.2 assemble.8
  226.6 5.2 feed_out.2.part_ref
  243.2 5.1 norm_forward.5
  250.4 20.5 %collective-permute-done.32.refs_3_ = bf16[4,64,1024]{2,1,0:T(8,128)(2,1)S(1)} collective-permute-done((bf16[4,64,1024]{2,1,0:T(8,128)(2,1)S(1)}, bf16[4,64,1024]{2,1,0:T(8,128)(2,1)S(1)}, u32[]{:S(2)}, u32[]{:S(2)}) %collective-permute-start.32) | collective-permute-done | bytes 524320 | tf_op jit(solution)/shard_map/ppermute | solution.py:351
  286.2 3.9 project_qkv.3
  290.2 14.9 %attend_forward.3 = (bf16[1024,512]{1,0:T(8,128)(2,1)S(1)}, f32[4,2,1024]{2,1,0:T(2,128)S(1)}) custom-call(bf16[1024,512]{1,0:T(8,128)(2,1)S(1)} %get-tuple-element.575.refs_0_, bf16[1024,512]{1,0:T(8,128)(2,1)S(1)} %get-tuple-element.576.refs_1_, bf16[1024,512]{1,0:T(8,128)(2,1)S(1)} %get-tuple-element.577.refs_2_, ...), custom_call_target="tpu_custom_call" | custom-call | flops 3006477056 | bytes 1468006 | tf_op jit(solution)/shard_map/attend_forward/pallas_call | solution.py:124
  306.0 2.9 project_out.3.part_ref
  312.4 3.1 collective-permute-start.43
  315.6 4.0 collective-permute-start.44
  324.1 3.0 assemble.10
  327.1 5.5 norm_forward.6
  332.6 7.8 %fusion.9 = (bf16[1024,2048]{1,0:T(8,128)(2,1)S(1)}, bf16[1024,2048]{1,0:T(8,128)(2,1)S(1)}) fusion(f32[2048]{0:T(1024)S(1)} %bitcast.387, bf16[1024,1024]{1,0:T(8,128)(2,1)S(1)} %get-tuple-element.540.before_ref.x_ref, bf16[1024,2048]{1,0:T(8,128)(2,1)S(1)} %bitcast.305), kind=kOutput, calls=%fused_computation.11 | convolution fusion | flops 4320133120 | bytes 14688256 | tf_op jit(solution)/shard_map/dot_general | solution.py:34
  343.3 3.0 assemble.11
  346.3 5.1 feed_out.3.part_ref
  354.4 4.7 collective-permute-done.46
  359.8 4.1 norm_forward.7
  363.9 3.1 norm_backward.4
  367.0 7.4 weight_grad.6
  379.3 5.3 feed_out_back.2.refs_0_
  384.6 7.2 weight_grad.7
  391.8 5.2 feed_in_back.2.refs_1_
  399.8 3.0 collective-permute-start.53
  408.8 3.9 norm_backward.5
  417.1 27.3 %attend_backward.2 = (bf16[1024,512]{1,0:T(8,128)(2,1)S(1)}, bf16[1024,512]{1,0:T(8,128)(2,1)S(1)}, bf16[1024,512]{1,0:T(8,128)(2,1)S(1)}) custom-call(bf16[1024,512]{1,0:T(8,128)(2,1)S(1)} %copy-done.119, bf16[1024,512]{1,0:T(8,128)(2,1)S(1)} %copy-done.121, bf16[1024,512]{1,0:T(8,128)(2,1)S(1)} %copy-done.123, ...), custom_call_target="tpu_custom_call" | custom-call | flops 7516192768 | bytes 2936012 | tf_op jit(solution)/shard_map/attend_backward/pallas_call | solution.py:156
  448.0 6.6 weight_grad.8
  464.8 4.1 project_qkv_back.2.refs_1_
  473.1 4.2 norm_backward.6
  478.6 7.8 %weight_grad.9 = (bf16[4,2,128,512]{3,2,1,0:T(8,128)(2,1)S(1)}, bf16[4,2,128,512]{3,2,1,0:T(8,128)(2,1)}, bf16[4,2,128,512]{3,2,1,0:T(8,128)(2,1)S(1)}, bf16[4,2,128,512]{3,2,1,0:T(8,128)(2,1)}, f32[8,1024]{1,0:T(8,128)}) custom-call(s32[3]{0:T(128)S(1)} %pad_add_fusion.at_ref, bf16[1024,2048]{1,0:T(8,128)(2,1)S(1)} %copy-done.14, ...), custom_call_target="tpu_custom_call" | custom-call | flops 1503238528 | bytes 3670016 | tf_op jit(solution)/shard_map/weight_grad/pallas_call | solution.py:502
  497.0 5.2 feed_out_back.3.refs_0_
  502.2 6.0 feed_in_back.3.refs_1_
  508.1 7.9 %weight_grad.10 = (bf16[4,2,64,1024]{3,2,1,0:T(8,128)(2,1)S(1)}, bf16[4,2,64,1024]{3,2,1,0:T(8,128)(2,1)}, bf16[4,2,64,1024]{3,2,1,0:T(8,128)(2,1)S(1)}, bf16[4,2,64,1024]{3,2,1,0:T(8,128)(2,1)}, f32[8,2048]{1,0:T(8,128)S(1)}) custom-call(s32[3]{0:T(128)S(1)} %pad_add_fusion.at_ref, bf16[1024,1024]{1,0:T(8,128)(2,1)S(1)} %copy-done.26, ...), custom_call_target="tpu_custom_call" | custom-call | flops 1503238528 | bytes 3670016 | tf_op jit(solution)/shard_map/weight_grad/pallas_call | solution.py:502
  521.3 2.8 scatter_add.9
  526.0 5.4 norm_backward.7
  535.6 2.8 collective-permute-done.70
  550.1 3.8 scatter_add.8
  559.8 27.1 %attend_backward.3 = (bf16[1024,512]{1,0:T(8,128)(2,1)S(1)}, bf16[1024,512]{1,0:T(8,128)(2,1)S(1)}, bf16[1024,512]{1,0:T(8,128)(2,1)S(1)}) custom-call(bf16[1024,512]{1,0:T(8,128)(2,1)S(1)} %copy-done.111, bf16[1024,512]{1,0:T(8,128)(2,1)S(1)} %copy-done.114, bf16[1024,512]{1,0:T(8,128)(2,1)S(1)} %copy-done.117, bf16[1024,512]{1,0:T(8,128)(2,1)S(1)} %copy-done.86, ...), custom_call_target="tpu_custom_call" | custom-call | flops 7516192768 | bytes 2936012 | tf_op jit(solution)/shard_map/attend_backward/pallas_call | solution.py:156
  596.0 3.7 scatter_add.10
  606.6 7.0 weight_grad.11
  615.0 4.9 project_qkv_back.3
  633.0 5.0 add_convert_fusion
  638.0 14.2 %collective-permute-done.77.refs_1_ = bf16[4,2,64,1024]{3,2,1,0:T(8,128)(2,1)S(1)} collective-permute-done((bf16[4,2,64,1024]{3,2,1,0:T(8,128)(2,1)}, bf16[4,2,64,1024]{3,2,1,0:T(8,128)(2,1)S(1)}, u32[]{:S(2)}, u32[]{:S(2)}) %collective-permute-start.77) | collective-permute-done | bytes 1048608 | tf_op jit(solution)/shard_map/ppermute | solution.py:351
  665.9 5.6 collective-permute-start.85
  671.5 3.8 collective-permute-start.86
  678.9 3.1 collective-permute-done.92
  681.9 3.9 collective-permute-start.87
  686.4 4.7 collective-permute-start.89
  691.2 6.8 collective-permute-done.86
  713.1 14.6 %reduce-scatter.13.cloned.1.call-done = bf16[64,2048]{1,0:T(8,128)(2,1)} async-done(((bf16[256,2048]{1,0:T(8,128)(2,1)}), bf16[64,2048]{1,0:T(8,128)(2,1)}) %reduce-scatter.13.cloned.1.call-update) | async-done | bytes 262160 | tf_op jit(solution)/shard_map/reduce_scatter | solution.py:577
  (767 shorter events, 284.7 us)
Async XLA Ops:
  7.2 39.3 %all-gather.7.cloned.1.call-start = ((), (), s32[]{:S(2)}) async-start(), calls=%async_computation.6 | async-start | bytes 1310720 | tf_op jit(solution)/shard_map/all_gather | solution.py:378
  10.6 20.3 %collective-permute-start.4 = (s32[256]{0:T(256)S(1)}, s32[256]{0:T(256)S(1)}, u32[]{:S(2)}, u32[]{:S(2)}) collective-permute-start(s32[256]{0:T(256)S(1)} %bitcast.397), channel_id=1, source_target_pairs={{0,12},{4,0},{8,4},{12,8},{1,13},{5,1},{9,5},{13,9},{2,14},{6,2},{... | collective-permute-start | bytes 3080 | tf_op jit(solution)/shard_map/ppermute | solution.py:609
  17.3 85.9 %all-gather.9.cloned.1.call-start = ((), (), s32[]{:S(2)}) async-start(), calls=%async_computation.7 | async-start | bytes 1310720 | tf_op jit(solution)/shard_map/all_gather | solution.py:378
  46.5 38.0 %collective-permute-start.7 = (bf16[4,64,2048]{2,1,0:T(8,128)(2,1)}, bf16[4,64,2048]{2,1,0:T(8,128)(2,1)}, u32[]{:S(2)}, u32[]{:S(2)}) collective-permute-start(bf16[4,64,2048]{2,1,0:T(8,128)(2,1)} %bitcast.315), channel_id=1, source_target_pairs={{1,0},{0,1},{3,2},{2,3},{5,4},{4,5},{7,6},{6,7},{9,8},{8,9},{11,10... | collective-permute-start | bytes 3145736 | tf_op jit(solution)/shard_map/ppermute | solution.py:344
  48.0 36.4 %collective-permute-start.8 = (bf16[4,64,2048]{2,1,0:T(8,128)(2,1)}, bf16[4,64,2048]{2,1,0:T(8,128)(2,1)}, u32[]{:S(2)}, u32[]{:S(2)}) collective-permute-start(bf16[4,64,2048]{2,1,0:T(8,128)(2,1)} %bitcast.316), channel_id=1, source_target_pairs={{2,0},{3,1},{0,2},{1,3},{6,4},{7,5},{4,6},{5,7},{10,8},{11,9},{8,1... | collective-permute-start | bytes 3145736 | tf_op jit(solution)/shard_map/ppermute | solution.py:351
  52.7 31.8 %collective-permute-start.9 = (bf16[128,1024]{1,0:T(8,128)(2,1)}, bf16[128,1024]{1,0:T(8,128)(2,1)}, u32[]{:S(2)}, u32[]{:S(2)}) collective-permute-start(bf16[128,1024]{1,0:T(8,128)(2,1)} %get-tuple-element.849), channel_id=1, source_target_pairs={{0,8},{4,12},{8,0},{12,4},{1,9},{5,13},{9,1},{13,5},{2,10},{6,14},... | collective-permute-start | bytes 786440 | tf_op jit(solution)/shard_map/ppermute | solution.py:609
  53.7 81.8 %all-gather.11.cloned.1.call-start = ((), (), s32[]{:S(2)}) async-start(), calls=%async_computation.8 | async-start | bytes 1310720 | tf_op jit(solution)/shard_map/all_gather | solution.py:378
  94.1 76.8 %all-gather.13.cloned.1.call-start = ((), (), s32[]{:S(2)}) async-start(), calls=%async_computation.9 | async-start | bytes 1310720 | tf_op jit(solution)/shard_map/all_gather | solution.py:378
  121.5 80.2 %all-gather.15.cloned.1.call-start = ((), (), s32[]{:S(2)}) async-start(), calls=%async_computation.10 | async-start | bytes 1310720 | tf_op jit(solution)/shard_map/all_gather | solution.py:378
  122.1 37.0 %collective-permute-start.14 = (bf16[4,64,2048]{2,1,0:T(8,128)(2,1)}, bf16[4,64,2048]{2,1,0:T(8,128)(2,1)}, u32[]{:S(2)}, u32[]{:S(2)}) collective-permute-start(bf16[4,64,2048]{2,1,0:T(8,128)(2,1)} %bitcast.321), channel_id=1, source_target_pairs={{1,0},{0,1},{3,2},{2,3},{5,4},{4,5},{7,6},{6,7},{9,8},{8,9},{11,10... | collective-permute-start | bytes 3145736 | tf_op jit(solution)/shard_map/ppermute | solution.py:344
  122.8 36.3 %collective-permute-start.15 = (bf16[4,64,2048]{2,1,0:T(8,128)(2,1)}, bf16[4,64,2048]{2,1,0:T(8,128)(2,1)}, u32[]{:S(2)}, u32[]{:S(2)}) collective-permute-start(bf16[4,64,2048]{2,1,0:T(8,128)(2,1)} %bitcast.322), channel_id=1, source_target_pairs={{2,0},{3,1},{0,2},{1,3},{6,4},{7,5},{4,6},{5,7},{10,8},{11,9},{8,1... | collective-permute-start | bytes 3145736 | tf_op jit(solution)/shard_map/ppermute | solution.py:351
  135.4 35.1 %collective-permute-start.18 = (bf16[4,128,1024]{2,1,0:T(8,128)(2,1)}, bf16[4,128,1024]{2,1,0:T(8,128)(2,1)}, u32[]{:S(2)}, u32[]{:S(2)}) collective-permute-start(bf16[4,128,1024]{2,1,0:T(8,128)(2,1)} %bitcast.327), channel_id=1, source_target_pairs={{1,0},{0,1},{3,2},{2,3},{5,4},{4,5},{7,6},{6,7},{9,8},{8,9},{11,10... | collective-permute-start | bytes 3145736 | tf_op jit(solution)/shard_map/ppermute | solution.py:344
  137.0 33.9 %collective-permute-start.19 = (bf16[4,128,1024]{2,1,0:T(8,128)(2,1)}, bf16[4,128,1024]{2,1,0:T(8,128)(2,1)}, u32[]{:S(2)}, u32[]{:S(2)}) collective-permute-start(bf16[4,128,1024]{2,1,0:T(8,128)(2,1)} %bitcast.328), channel_id=1, source_target_pairs={{2,0},{3,1},{0,2},{1,3},{6,4},{7,5},{4,6},{5,7},{10,8},{11,9},{8,1... | collective-permute-start | bytes 3145736 | tf_op jit(solution)/shard_map/ppermute | solution.py:351
  170.9 101.6 %all-gather.17.cloned.1.call-start = ((), (), s32[]{:S(2)}) async-start(), calls=%async_computation.11 | async-start | bytes 1310720 | tf_op jit(solution)/shard_map/all_gather | solution.py:378
  172.8 21.6 %collective-permute-start.20 = (bf16[4,64,1024]{2,1,0:T(8,128)(2,1)}, bf16[4,64,1024]{2,1,0:T(8,128)(2,1)}, u32[]{:S(2)}, u32[]{:S(2)}) collective-permute-start(bf16[4,64,1024]{2,1,0:T(8,128)(2,1)} %slice.291), channel_id=1, source_target_pairs={{2,0},{3,1},{0,2},{1,3},{6,4},{7,5},{4,6},{5,7},{10,8},{11,9},{8,1... | collective-permute-start | bytes 1572872 | tf_op jit(solution)/shard_map/ppermute | solution.py:351
  182.0 19.7 %collective-permute-start.23 = (bf16[4,128,512]{2,1,0:T(8,128)(2,1)}, bf16[4,128,512]{2,1,0:T(8,128)(2,1)}, u32[]{:S(2)}, u32[]{:S(2)}) collective-permute-start(bf16[4,128,512]{2,1,0:T(8,128)(2,1)} %slice.294), channel_id=1, source_target_pairs={{1,0},{0,1},{3,2},{2,3},{5,4},{4,5},{7,6},{6,7},{9,8},{8,9},{11,10... | collective-permute-start | bytes 1572872 | tf_op jit(solution)/shard_map/ppermute | solution.py:344
  201.7 30.1 %collective-permute-start.25 = (bf16[4,64,2048]{2,1,0:T(8,128)(2,1)}, bf16[4,64,2048]{2,1,0:T(8,128)(2,1)S(1)}, u32[]{:S(2)}, u32[]{:S(2)}) collective-permute-start(bf16[4,64,2048]{2,1,0:T(8,128)(2,1)} %bitcast.324), channel_id=1, source_target_pairs={{1,0},{0,1},{3,2},{2,3},{5,4},{4,5},{7,6},{6,7},{9,8},{8,9},{11,10... | collective-permute-start | bytes 3145736 | tf_op jit(solution)/shard_map/ppermute | solution.py:344
  203.2 28.6 %collective-permute-start.26 = (bf16[4,64,2048]{2,1,0:T(8,128)(2,1)}, bf16[4,64,2048]{2,1,0:T(8,128)(2,1)S(1)}, u32[]{:S(2)}, u32[]{:S(2)}) collective-permute-start(bf16[4,64,2048]{2,1,0:T(8,128)(2,1)} %bitcast.325), channel_id=1, source_target_pairs={{2,0},{3,1},{0,2},{1,3},{6,4},{7,5},{4,6},{5,7},{10,8},{11,9},{8,1... | collective-permute-start | bytes 3145736 | tf_op jit(solution)/shard_map/ppermute | solution.py:351
  205.7 26.0 %collective-permute-start.27 = (bf16[128,1024]{1,0:T(8,128)(2,1)S(1)}, bf16[128,1024]{1,0:T(8,128)(2,1)S(1)}, u32[]{:S(2)}, u32[]{:S(2)}) collective-permute-start(bf16[128,1024]{1,0:T(8,128)(2,1)S(1)} %get-tuple-element.846), channel_id=1, source_target_pairs={{0,4},{4,8},{8,12},{12,0},{1,5},{5,9},{9,13},{13,1},{2,6},{6,10},{... | collective-permute-start | bytes 786440 | tf_op jit(solution)/shard_map/ppermute | solution.py:609
  206.4 25.4 %collective-permute-start.28 = (bf16[128,1024]{1,0:T(8,128)(2,1)S(1)}, bf16[128,1024]{1,0:T(8,128)(2,1)S(1)}, u32[]{:S(2)}, u32[]{:S(2)}) collective-permute-start(bf16[128,1024]{1,0:T(8,128)(2,1)S(1)} %get-tuple-element.845), channel_id=1, source_target_pairs={{0,8},{4,12},{8,0},{12,4},{1,9},{5,13},{9,1},{13,5},{2,10},{6,14},... | collective-permute-start | bytes 786440 | tf_op jit(solution)/shard_map/ppermute | solution.py:609
  209.5 22.3 %collective-permute-start.29 = (bf16[128,1024]{1,0:T(8,128)(2,1)S(1)}, bf16[128,1024]{1,0:T(8,128)(2,1)S(1)}, u32[]{:S(2)}, u32[]{:S(2)}) collective-permute-start(bf16[128,1024]{1,0:T(8,128)(2,1)S(1)} %get-tuple-element.844), channel_id=1, source_target_pairs={{0,12},{4,0},{8,4},{12,8},{1,13},{5,1},{9,5},{13,9},{2,14},{6,2},{... | collective-permute-start | bytes 786440 | tf_op jit(solution)/shard_map/ppermute | solution.py:609
  233.4 356.5 %reduce-scatter.11.cloned.1.call-start = ((), (), s32[]{:S(2)}) async-start(), calls=%async_computation.14 | async-start | bytes 1310720 | tf_op jit(solution)/shard_map/reduce_scatter | solution.py:577
  233.6 38.9 %collective-permute-start.30 = (bf16[4,64,2048]{2,1,0:T(8,128)(2,1)}, bf16[4,64,2048]{2,1,0:T(8,128)(2,1)}, u32[]{:S(2)}, u32[]{:S(2)}) collective-permute-start(bf16[4,64,2048]{2,1,0:T(8,128)(2,1)} %bitcast.318), channel_id=1, source_target_pairs={{1,0},{0,1},{3,2},{2,3},{5,4},{4,5},{7,6},{6,7},{9,8},{8,9},{11,10... | collective-permute-start | bytes 3145736 | tf_op jit(solution)/shard_map/ppermute | solution.py:344
  234.2 38.3 %collective-permute-start.31 = (bf16[4,64,2048]{2,1,0:T(8,128)(2,1)}, bf16[4,64,2048]{2,1,0:T(8,128)(2,1)}, u32[]{:S(2)}, u32[]{:S(2)}) collective-permute-start(bf16[4,64,2048]{2,1,0:T(8,128)(2,1)} %bitcast.319), channel_id=1, source_target_pairs={{2,0},{3,1},{0,2},{1,3},{6,4},{7,5},{4,6},{5,7},{10,8},{11,9},{8,1... | collective-permute-start | bytes 3145736 | tf_op jit(solution)/shard_map/ppermute | solution.py:351
  236.6 34.3 %collective-permute-start.32 = (bf16[4,64,1024]{2,1,0:T(8,128)(2,1)S(1)}, bf16[4,64,1024]{2,1,0:T(8,128)(2,1)S(1)}, u32[]{:S(2)}, u32[]{:S(2)}) collective-permute-start(bf16[4,64,1024]{2,1,0:T(8,128)(2,1)S(1)} %slice.299), channel_id=1, source_target_pairs={{2,0},{3,1},{0,2},{1,3},{6,4},{7,5},{4,6},{5,7},{10,8},{11,9},{8,1... | collective-permute-start | bytes 1572872 | tf_op jit(solution)/shard_map/ppermute | solution.py:351
  238.4 33.3 %collective-permute-start.33 = (bf16[4,64,1024]{2,1,0:T(8,128)(2,1)S(1)}, bf16[4,64,1024]{2,1,0:T(8,128)(2,1)S(1)}, u32[]{:S(2)}, u32[]{:S(2)}) collective-permute-start(bf16[4,64,1024]{2,1,0:T(8,128)(2,1)S(1)} %slice.300), channel_id=1, source_target_pairs={{1,0},{0,1},{3,2},{2,3},{5,4},{4,5},{7,6},{6,7},{9,8},{8,9},{11,10... | collective-permute-start | bytes 1572872 | tf_op jit(solution)/shard_map/ppermute | solution.py:344
  272.5 38.8 %collective-permute-start.35 = (bf16[4,128,1024]{2,1,0:T(8,128)(2,1)}, bf16[4,128,1024]{2,1,0:T(8,128)(2,1)}, u32[]{:S(2)}, u32[]{:S(2)}) collective-permute-start(bf16[4,128,1024]{2,1,0:T(8,128)(2,1)} %bitcast.330), channel_id=1, source_target_pairs={{1,0},{0,1},{3,2},{2,3},{5,4},{4,5},{7,6},{6,7},{9,8},{8,9},{11,10... | collective-permute-start | bytes 3145736 | tf_op jit(solution)/shard_map/ppermute | solution.py:344
  274.1 37.3 %collective-permute-start.36 = (bf16[4,128,1024]{2,1,0:T(8,128)(2,1)}, bf16[4,128,1024]{2,1,0:T(8,128)(2,1)}, u32[]{:S(2)}, u32[]{:S(2)}) collective-permute-start(bf16[4,128,1024]{2,1,0:T(8,128)(2,1)} %bitcast.331), channel_id=1, source_target_pairs={{2,0},{3,1},{0,2},{1,3},{6,4},{7,5},{4,6},{5,7},{10,8},{11,9},{8,1... | collective-permute-start | bytes 3145736 | tf_op jit(solution)/shard_map/ppermute | solution.py:351
  282.2 22.9 %collective-permute-start.39 = (bf16[512,512]{1,0:T(8,128)(2,1)S(1)}, bf16[512,512]{1,0:T(8,128)(2,1)S(1)}, u32[]{:S(2)}, u32[]{:S(2)}) collective-permute-start(bf16[512,512]{1,0:T(8,128)(2,1)S(1)} %constant_dynamic-slice_fusion.11), channel_id=1, source_target_pairs={{0,16},{16,0},{1,17},{17,1},{2,18},{18,2},{3,19},{19,3},{4,20},{20... | collective-permute-start | bytes 1572872 | tf_op jit(solution)/shard_map/ppermute | solution.py:354
  283.7 26.0 %collective-permute-start.37 = (bf16[4,64,1024]{2,1,0:T(8,128)(2,1)S(1)}, bf16[4,64,1024]{2,1,0:T(8,128)(2,1)S(1)}, u32[]{:S(2)}, u32[]{:S(2)}) collective-permute-start(bf16[4,64,1024]{2,1,0:T(8,128)(2,1)S(1)} %slice.304), channel_id=1, source_target_pairs={{2,0},{3,1},{0,2},{1,3},{6,4},{7,5},{4,6},{5,7},{10,8},{11,9},{8,1... | collective-permute-start | bytes 1572872 | tf_op jit(solution)/shard_map/ppermute | solution.py:351
  285.6 25.0 %collective-permute-start.38 = (bf16[4,64,1024]{2,1,0:T(8,128)(2,1)S(1)}, bf16[4,64,1024]{2,1,0:T(8,128)(2,1)S(1)}, u32[]{:S(2)}, u32[]{:S(2)}) collective-permute-start(bf16[4,64,1024]{2,1,0:T(8,128)(2,1)S(1)} %slice.305), channel_id=1, source_target_pairs={{1,0},{0,1},{3,2},{2,3},{5,4},{4,5},{7,6},{6,7},{9,8},{8,9},{11,10... | collective-permute-start | bytes 1572872 | tf_op jit(solution)/shard_map/ppermute | solution.py:344
  312.4 28.0 %collective-permute-start.43 = (bf16[256,1024]{1,0:T(8,128)(2,1)S(1)}, bf16[256,1024]{1,0:T(8,128)(2,1)S(1)}, u32[]{:S(2)}, u32[]{:S(2)}) collective-permute-start(bf16[256,1024]{1,0:T(8,128)(2,1)S(1)} %get-tuple-element.830), channel_id=1, source_target_pairs={{4,0},{8,4},{12,8},{0,12},{5,1},{9,5},{13,9},{1,13},{6,2},{10,6},{... | collective-permute-start | bytes 1572872 | tf_op jit(solution)/shard_map/ppermute | solution.py:632
  315.6 24.9 %collective-permute-start.44 = (bf16[256,1024]{1,0:T(8,128)(2,1)S(1)}, bf16[256,1024]{1,0:T(8,128)(2,1)S(1)}, u32[]{:S(2)}, u32[]{:S(2)}) collective-permute-start(bf16[256,1024]{1,0:T(8,128)(2,1)S(1)} %get-tuple-element.829), channel_id=1, source_target_pairs={{8,0},{12,4},{0,8},{4,12},{9,1},{13,5},{1,9},{5,13},{10,2},{14,6},... | collective-permute-start | bytes 1572872 | tf_op jit(solution)/shard_map/ppermute | solution.py:632
  320.6 19.9 %collective-permute-start.40 = (bf16[4,128,512]{2,1,0:T(8,128)(2,1)S(1)}, bf16[4,128,512]{2,1,0:T(8,128)(2,1)S(1)}, u32[]{:S(2)}, u32[]{:S(2)}) collective-permute-start(bf16[4,128,512]{2,1,0:T(8,128)(2,1)S(1)} %slice.308), channel_id=1, source_target_pairs={{2,0},{3,1},{0,2},{1,3},{6,4},{7,5},{4,6},{5,7},{10,8},{11,9},{8,1... | collective-permute-start | bytes 1572872 | tf_op jit(solution)/shard_map/ppermute | solution.py:351
  374.4 25.2 %collective-permute-start.48 = (bf16[4,2,128,512]{3,2,1,0:T(8,128)(2,1)S(1)}, bf16[4,2,128,512]{3,2,1,0:T(8,128)(2,1)S(1)}, u32[]{:S(2)}, u32[]{:S(2)}) collective-permute-start(bf16[4,2,128,512]{3,2,1,0:T(8,128)(2,1)S(1)} %get-tuple-element.555), channel_id=1, source_target_pairs={{2,0},{3,1},{0,2},{1,3},{6,4},{7,5},{4,6},{5,7},{10,8},{11,9},{8,1... | collective-permute-start | bytes 3145736 | tf_op jit(solution)/shard_map/ppermute | solution.py:351
  374.9 24.9 %collective-permute-start.49 = (bf16[4,2,128,512]{3,2,1,0:T(8,128)(2,1)S(1)}, bf16[4,2,128,512]{3,2,1,0:T(8,128)(2,1)S(1)}, u32[]{:S(2)}, u32[]{:S(2)}) collective-permute-start(bf16[4,2,128,512]{3,2,1,0:T(8,128)(2,1)S(1)} %get-tuple-element.557), channel_id=1, source_target_pairs={{1,0},{0,1},{3,2},{2,3},{5,4},{4,5},{7,6},{6,7},{9,8},{8,9},{11,10... | collective-permute-start | bytes 3145736 | tf_op jit(solution)/shard_map/ppermute | solution.py:344
  377.2 19.7 %collective-permute-start.50 = (bf16[256,1024]{1,0:T(8,128)(2,1)S(1)}, bf16[256,1024]{1,0:T(8,128)(2,1)S(1)}, u32[]{:S(2)}, u32[]{:S(2)}) collective-permute-start(bf16[256,1024]{1,0:T(8,128)(2,1)S(1)} %get-tuple-element.825), channel_id=1, source_target_pairs={{20,16},{24,20},{28,24},{16,28},{21,17},{25,21},{29,25},{17,29},{2... | collective-permute-start | bytes 1572872 | tf_op jit(solution)/shard_map/ppermute | solution.py:632
  404.7 39.8 %collective-permute-start.54 = (bf16[4,128,512]{2,1,0:T(8,128)(2,1)S(1)}, bf16[4,128,512]{2,1,0:T(8,128)(2,1)S(1)}, u32[]{:S(2)}, u32[]{:S(2)}) collective-permute-start(bf16[4,128,512]{2,1,0:T(8,128)(2,1)S(1)} %get-tuple-element.568), channel_id=1, source_target_pairs={{1,0},{0,1},{3,2},{2,3},{5,4},{4,5},{7,6},{6,7},{9,8},{8,9},{11,10... | collective-permute-start | bytes 1572872 | tf_op jit(solution)/shard_map/ppermute | solution.py:344
  405.4 39.1 %collective-permute-start.55 = (bf16[4,128,512]{2,1,0:T(8,128)(2,1)S(1)}, bf16[4,128,512]{2,1,0:T(8,128)(2,1)S(1)}, u32[]{:S(2)}, u32[]{:S(2)}) collective-permute-start(bf16[4,128,512]{2,1,0:T(8,128)(2,1)S(1)} %get-tuple-element.570), channel_id=1, source_target_pairs={{2,0},{3,1},{0,2},{1,3},{6,4},{7,5},{4,6},{5,7},{10,8},{11,9},{8,1... | collective-permute-start | bytes 1572872 | tf_op jit(solution)/shard_map/ppermute | solution.py:351
  407.0 37.6 %collective-permute-start.56 = (bf16[4,2,64,1024]{3,2,1,0:T(8,128)(2,1)S(1)}, bf16[4,2,64,1024]{3,2,1,0:T(8,128)(2,1)S(1)}, u32[]{:S(2)}, u32[]{:S(2)}) collective-permute-start(bf16[4,2,64,1024]{3,2,1,0:T(8,128)(2,1)S(1)} %get-tuple-element.572), channel_id=1, source_target_pairs={{2,0},{3,1},{0,2},{1,3},{6,4},{7,5},{4,6},{5,7},{10,8},{11,9},{8,1... | collective-permute-start | bytes 3145736 | tf_op jit(solution)/shard_map/ppermute | solution.py:351
  407.5 37.1 %collective-permute-start.57 = (bf16[4,2,64,1024]{3,2,1,0:T(8,128)(2,1)S(1)}, bf16[4,2,64,1024]{3,2,1,0:T(8,128)(2,1)S(1)}, u32[]{:S(2)}, u32[]{:S(2)}) collective-permute-start(bf16[4,2,64,1024]{3,2,1,0:T(8,128)(2,1)S(1)} %get-tuple-element.574), channel_id=1, source_target_pairs={{1,0},{0,1},{3,2},{2,3},{5,4},{4,5},{7,6},{6,7},{9,8},{8,9},{11,10... | collective-permute-start | bytes 3145736 | tf_op jit(solution)/shard_map/ppermute | solution.py:344
  414.1 30.4 %collective-permute-start.58 = (bf16[512,512]{1,0:T(8,128)(2,1)S(1)}, bf16[512,512]{1,0:T(8,128)(2,1)S(1)}, u32[]{:S(2)}, u32[]{:S(2)}) collective-permute-start(bf16[512,512]{1,0:T(8,128)(2,1)S(1)} %get-tuple-element.842), channel_id=1, source_target_pairs={{0,16},{16,0},{1,17},{17,1},{2,18},{18,2},{3,19},{19,3},{4,20},{20... | collective-permute-start | bytes 1572872 | tf_op jit(solution)/shard_map/ppermute | solution.py:354
  469.1 49.6 %collective-permute-start.64 = (bf16[4,2,64,1024]{3,2,1,0:T(8,128)(2,1)}, bf16[4,2,64,1024]{3,2,1,0:T(8,128)(2,1)}, u32[]{:S(2)}, u32[]{:S(2)}) collective-permute-start(bf16[4,2,64,1024]{3,2,1,0:T(8,128)(2,1)} %get-tuple-element.629), channel_id=1, source_target_pairs={{2,0},{3,1},{0,2},{1,3},{6,4},{7,5},{4,6},{5,7},{10,8},{11,9},{8,1... | collective-permute-start | bytes 3145736 | tf_op jit(solution)/shard_map/ppermute | solution.py:351
  470.7 48.0 %collective-permute-start.65 = (bf16[4,2,64,1024]{3,2,1,0:T(8,128)(2,1)}, bf16[4,2,64,1024]{3,2,1,0:T(8,128)(2,1)}, u32[]{:S(2)}, u32[]{:S(2)}) collective-permute-start(bf16[4,2,64,1024]{3,2,1,0:T(8,128)(2,1)} %get-tuple-element.631), channel_id=1, source_target_pairs={{1,0},{0,1},{3,2},{2,3},{5,4},{4,5},{7,6},{6,7},{9,8},{8,9},{11,10... | collective-permute-start | bytes 3145736 | tf_op jit(solution)/shard_map/ppermute | solution.py:344
  488.4 30.3 %collective-permute-start.62 = (bf16[4,2,128,512]{3,2,1,0:T(8,128)(2,1)}, bf16[4,2,128,512]{3,2,1,0:T(8,128)(2,1)}, u32[]{:S(2)}, u32[]{:S(2)}) collective-permute-start(bf16[4,2,128,512]{3,2,1,0:T(8,128)(2,1)} %get-tuple-element.625), channel_id=1, source_target_pairs={{2,0},{3,1},{0,2},{1,3},{6,4},{7,5},{4,6},{5,7},{10,8},{11,9},{8,1... | collective-permute-start | bytes 3145736 | tf_op jit(solution)/shard_map/ppermute | solution.py:351
  489.9 28.8 %collective-permute-start.63 = (bf16[4,2,128,512]{3,2,1,0:T(8,128)(2,1)}, bf16[4,2,128,512]{3,2,1,0:T(8,128)(2,1)}, u32[]{:S(2)}, u32[]{:S(2)}) collective-permute-start(bf16[4,2,128,512]{3,2,1,0:T(8,128)(2,1)} %get-tuple-element.627), channel_id=1, source_target_pairs={{1,0},{0,1},{3,2},{2,3},{5,4},{4,5},{7,6},{6,7},{9,8},{8,9},{11,10... | collective-permute-start | bytes 3145736 | tf_op jit(solution)/shard_map/ppermute | solution.py:344
  492.5 97.4 %reduce-scatter.9.cloned.1.call-start = ((), (), s32[]{:S(2)}) async-start(), calls=%async_computation.13 | async-start | bytes 1310720 | tf_op jit(solution)/shard_map/reduce_scatter | solution.py:577
  518.8 71.2 %reduce-scatter.7.cloned.1.call-start = ((), (), s32[]{:S(2)}) async-start(), calls=%async_computation.12 | async-start | bytes 1310720 | tf_op jit(solution)/shard_map/reduce_scatter | solution.py:577
  541.0 84.8 %reduce-scatter.17.cloned.1.call-start = ((), (), s32[]{:S(2)}) async-start(), calls=%async_computation.17 | async-start | bytes 1310720 | tf_op jit(solution)/shard_map/reduce_scatter | solution.py:577
  546.2 43.8 %collective-permute-start.68 = (bf16[4,2,64,1024]{3,2,1,0:T(8,128)(2,1)}, bf16[4,2,64,1024]{3,2,1,0:T(8,128)(2,1)}, u32[]{:S(2)}, u32[]{:S(2)}) collective-permute-start(bf16[4,2,64,1024]{3,2,1,0:T(8,128)(2,1)} %get-tuple-element.645), channel_id=1, source_target_pairs={{2,0},{3,1},{0,2},{1,3},{6,4},{7,5},{4,6},{5,7},{10,8},{11,9},{8,1... | collective-permute-start | bytes 3145736 | tf_op jit(solution)/shard_map/ppermute | solution.py:351
  546.7 43.2 %collective-permute-start.69 = (bf16[4,2,64,1024]{3,2,1,0:T(8,128)(2,1)}, bf16[4,2,64,1024]{3,2,1,0:T(8,128)(2,1)}, u32[]{:S(2)}, u32[]{:S(2)}) collective-permute-start(bf16[4,2,64,1024]{3,2,1,0:T(8,128)(2,1)} %get-tuple-element.647), channel_id=1, source_target_pairs={{1,0},{0,1},{3,2},{2,3},{5,4},{4,5},{7,6},{6,7},{9,8},{8,9},{11,10... | collective-permute-start | bytes 3145736 | tf_op jit(solution)/shard_map/ppermute | solution.py:344
  555.5 34.4 %collective-permute-start.66 = (bf16[4,128,512]{2,1,0:T(8,128)(2,1)}, bf16[4,128,512]{2,1,0:T(8,128)(2,1)S(1)}, u32[]{:S(2)}, u32[]{:S(2)}) collective-permute-start(bf16[4,128,512]{2,1,0:T(8,128)(2,1)} %get-tuple-element.641), channel_id=1, source_target_pairs={{1,0},{0,1},{3,2},{2,3},{5,4},{4,5},{7,6},{6,7},{9,8},{8,9},{11,10... | collective-permute-start | bytes 1572872 | tf_op jit(solution)/shard_map/ppermute | solution.py:344
  556.8 33.1 %collective-permute-start.67 = (bf16[4,128,512]{2,1,0:T(8,128)(2,1)}, bf16[4,128,512]{2,1,0:T(8,128)(2,1)S(1)}, u32[]{:S(2)}, u32[]{:S(2)}) collective-permute-start(bf16[4,128,512]{2,1,0:T(8,128)(2,1)} %get-tuple-element.643), channel_id=1, source_target_pairs={{2,0},{3,1},{0,2},{1,3},{6,4},{7,5},{4,6},{5,7},{10,8},{11,9},{8,1... | collective-permute-start | bytes 1572872 | tf_op jit(solution)/shard_map/ppermute | solution.py:351
  558.3 31.6 %collective-permute-start.73 = (bf16[512,512]{1,0:T(8,128)(2,1)}, bf16[512,512]{1,0:T(8,128)(2,1)}, u32[]{:S(2)}, u32[]{:S(2)}) collective-permute-start(bf16[512,512]{1,0:T(8,128)(2,1)} %get-tuple-element.670), channel_id=1, source_target_pairs={{0,16},{16,0},{1,17},{17,1},{2,18},{18,2},{3,19},{19,3},{4,20},{20... | collective-permute-start | bytes 1572872 | tf_op jit(solution)/shard_map/ppermute | solution.py:354
  593.5 81.8 %reduce-scatter.15.cloned.1.call-start = ((), (), s32[]{:S(2)}) async-start(), calls=%async_computation.16 | async-start | bytes 1310720 | tf_op jit(solution)/shard_map/reduce_scatter | solution.py:577
  624.8 102.9 %reduce-scatter.13.cloned.1.call-start = ((), (), s32[]{:S(2)}) async-start(), calls=%async_computation.15 | async-start | bytes 1310720 | tf_op jit(solution)/shard_map/reduce_scatter | solution.py:577
  628.9 23.3 %collective-permute-start.77 = (bf16[4,2,64,1024]{3,2,1,0:T(8,128)(2,1)}, bf16[4,2,64,1024]{3,2,1,0:T(8,128)(2,1)S(1)}, u32[]{:S(2)}, u32[]{:S(2)}) collective-permute-start(bf16[4,2,64,1024]{3,2,1,0:T(8,128)(2,1)} %copy-done.125), channel_id=1, source_target_pairs={{2,0},{3,1},{0,2},{1,3},{6,4},{7,5},{4,6},{5,7},{10,8},{11,9},{8,1... | collective-permute-start | bytes 3145736 | tf_op jit(solution)/shard_map/ppermute | solution.py:351
  629.5 23.7 %collective-permute-start.78 = (bf16[4,2,64,1024]{3,2,1,0:T(8,128)(2,1)}, bf16[4,2,64,1024]{3,2,1,0:T(8,128)(2,1)S(1)}, u32[]{:S(2)}, u32[]{:S(2)}) collective-permute-start(bf16[4,2,64,1024]{3,2,1,0:T(8,128)(2,1)} %copy-done.124), channel_id=1, source_target_pairs={{1,0},{0,1},{3,2},{2,3},{5,4},{4,5},{7,6},{6,7},{9,8},{8,9},{11,10... | collective-permute-start | bytes 3145736 | tf_op jit(solution)/shard_map/ppermute | solution.py:344
  654.3 23.5 %collective-permute-start.91 = (f32[4,2,776]{2,1,0:T(2,128)S(1)}, f32[4,2,776]{2,1,0:T(2,128)S(1)}, u32[]{:S(2)}, u32[]{:S(2)}) collective-permute-start(f32[4,2,776]{2,1,0:T(2,128)S(1)} %dynamic-slice_bitcast_fusion.33), channel_id=1, source_target_pairs={{2,0},{3,1},{0,2},{1,3},{6,4},{7,5},{4,6},{5,7},{10,8},{11,9},{8,1... | collective-permute-start | bytes 74504 | tf_op jit(solution)/shard_map/ppermute | solution.py:351
  662.6 23.8 %collective-permute-start.83 = (bf16[4,64,1024]{2,1,0:T(8,128)(2,1)}, bf16[4,64,1024]{2,1,0:T(8,128)(2,1)}, u32[]{:S(2)}, u32[]{:S(2)}) collective-permute-start(bf16[4,64,1024]{2,1,0:T(8,128)(2,1)} %get-tuple-element.747), channel_id=1, source_target_pairs={{1,0},{0,1},{3,2},{2,3},{5,4},{4,5},{7,6},{6,7},{9,8},{8,9},{11,10... | collective-permute-start | bytes 1572872 | tf_op jit(solution)/shard_map/ppermute | solution.py:344
  663.9 27.2 %collective-permute-start.84 = (bf16[4,64,1024]{2,1,0:T(8,128)(2,1)}, bf16[4,64,1024]{2,1,0:T(8,128)(2,1)}, u32[]{:S(2)}, u32[]{:S(2)}) collective-permute-start(bf16[4,64,1024]{2,1,0:T(8,128)(2,1)} %get-tuple-element.749), channel_id=1, source_target_pairs={{2,0},{3,1},{0,2},{1,3},{6,4},{7,5},{4,6},{5,7},{10,8},{11,9},{8,1... | collective-permute-start | bytes 1572872 | tf_op jit(solution)/shard_map/ppermute | solution.py:351
  665.9 25.2 %collective-permute-start.85 = (bf16[256,1024]{1,0:T(8,128)(2,1)}, bf16[256,1024]{1,0:T(8,128)(2,1)}, u32[]{:S(2)}, u32[]{:S(2)}) collective-permute-start(bf16[256,1024]{1,0:T(8,128)(2,1)} %get-tuple-element.817), channel_id=1, source_target_pairs={{4,0},{8,4},{12,8},{0,12},{5,1},{9,5},{13,9},{1,13},{6,2},{10,6},{... | collective-permute-start | bytes 1572872 | tf_op jit(solution)/shard_map/ppermute | solution.py:632
  671.5 26.4 %collective-permute-start.86 = (bf16[256,1024]{1,0:T(8,128)(2,1)}, bf16[256,1024]{1,0:T(8,128)(2,1)}, u32[]{:S(2)}, u32[]{:S(2)}) collective-permute-start(bf16[256,1024]{1,0:T(8,128)(2,1)} %get-tuple-element.816), channel_id=1, source_target_pairs={{8,0},{12,4},{0,8},{4,12},{9,1},{13,5},{1,9},{5,13},{10,2},{14,6},... | collective-permute-start | bytes 1572872 | tf_op jit(solution)/shard_map/ppermute | solution.py:632
  686.4 19.7 %collective-permute-start.89 = (bf16[64,2048]{1,0:T(8,128)(2,1)}, bf16[64,2048]{1,0:T(8,128)(2,1)}, u32[]{:S(2)}, u32[]{:S(2)}) collective-permute-start(bf16[64,2048]{1,0:T(8,128)(2,1)} %broadcast_select_fusion.8), channel_id=1, source_target_pairs={{0,16},{16,0},{1,17},{17,1},{2,18},{18,2},{3,19},{19,3},{4,20},{20... | collective-permute-start | bytes 786440 | tf_op jit(solution)/shard_map/ppermute | solution.py:354
  (216 other events, 1611.3 us)
Sparse Core Ops, SparseCore 0:
  17.4 28.9 all-gather.6
  53.8 33.3 all-gather.8
  94.2 26.9 all-gather.10
  122.7 27.4 all-gather.12
  171.0 28.8 all-gather.14
  233.5 26.6 all-gather.16
  492.7 26.7 reduce-scatter.10
  521.9 25.7 reduce-scatter.8
  550.0 25.7 reduce-scatter.6
  593.6 25.5 reduce-scatter.16
  624.9 38.9 reduce-scatter.14
  701.9 25.7 reduce-scatter.12

commit v4 on v3

--- a/solution.py
+++ b/solution.py
@@ -639,6 +639,36 @@
     return lax.dynamic_slice_in_dim(value, place.section * half, half, 1)
 
 
+def join_pieces(place, pieces):
+    count = len(pieces)
+    half, width = pieces[0].shape
+    mine = jnp.stack(pieces)
+    other = place.sibling(mine)
+    at = jnp.stack([place.ctx // (place.nz // count), place.section]).astype(jnp.int32)
+
+    def body(at_ref, mine_ref, other_ref, out_ref):
+        out_ref[0, at_ref[1]] = mine_ref[0]
+        out_ref[0, 1 - at_ref[1]] = other_ref[0]
+
+    piece = pl.BlockSpec((1, half, width), lambda k, at_ref: (k, 0, 0))
+    out = pl.pallas_call(
+        body,
+        grid_spec=pltpu.PrefetchScalarGridSpec(
+            num_scalar_prefetch=1,
+            grid=(count,),
+            in_specs=[piece, piece],
+            out_specs=pl.BlockSpec(
+                (1, 2, half, width), lambda k, at_ref: ((at_ref[0] + count - k) % count, 0, 0, 0)
+            ),
+        ),
+        out_shape=jax.ShapeDtypeStruct((count, 2, half, width), mine.dtype),
+        compiler_params=pltpu.CompilerParams(vmem_limit_bytes=10 * MIB),
+        cost_estimate=priced(flops=0, bytes_accessed=8 * mine.size, transcendentals=0),
+        name="join_pieces",
+    )(at, mine, other)
+    return out.reshape(count * 2 * half, width)
+
+
 def join_halves(place, moved):
     other = place.sibling(moved)
     first = place.section == 0
@@ -814,13 +844,14 @@
     token_pieces, token_half, code_k, seg_q, live = step_end((token_pieces, token_half, code_k, seg_q, live), 1)
 
     near(0)
+    token_pieces += to_pieces(place, token_half, range(2, count))
+    held = (token_pieces, gathers[1].shard, gathers[2].shard)
+    token_pieces, gathers[1].shard, gathers[2].shard = step_end(held, 1)
+
+    far(0)
     along_z(1)
-    token_pieces += to_pieces(place, token_half, range(2, count))
-    token_pieces = step_end(token_pieces, 1)
-
-    far(0)
     along_z(2)
-    layer_input = join_halves(place, in_positions(place, token_pieces))
+    layer_input = join_pieces(place, token_pieces)
     layer_input = step_end(layer_input, 2)
     arrived(0)
 
@@ -829,7 +860,7 @@
     projs = [proj_whole(columns_proj), None]
     q, k, v = project_in(layer_input, w_qkv, 0)
     along_z(3)
-    columns[2], q, projs = tie(columns[2], q, projs)
+    columns[2], q, projs, got[1] = tie(columns[2], q, projs, got[1])
     near(2)
     attns = [attention(q, k, v), None]
     outs = [to_width([attns[0][3]], projs[0], False, "project_out"), None]
@@ -879,7 +910,7 @@
     first_back += from_sequences(place, first_out.reshape(count, local, width), [count - 1], 0)
     outs[1], cot_pieces, norms, first_back = tie(outs[1], cot_pieces, norms, first_back)
     ends[1] = feed_norm(norms[1][2], outs[1], 1)
-    terms = [join_halves(place, in_positions(place, cot_pieces))]
+    terms = [join_pieces(place, cot_pieces)]
 
     scatter = Scatter(place)
     totals = [[None] * 3, [None] * 3]

time: 750 us -> 735 us (0.980)
  waiting for transfers between devices: 149 us -> 135 us
    ppermute x9, waiting for transfers between devices: 30.8 us -> 16.8 us  [to_pieces(): lax.ppermute(sent, 'ctx', pairs)]
    all_gather x6, waiting for transfers between devices: 8.35 us -> 18.9 us  [along_z(): column = lax.all_gather(self.shard, 'ctx', axis=0, tiled=True)]
    ppermute x25, waiting for transfers between devices: 26.2 us -> 16.8 us  [from_x(): return lax.ppermute(value, 'fsdp', pairs)]
    unnamed x355 -> x369, local copies, waits for them, and re-layouts: 80.1 us -> 86.2 us
  transfers between devices with their start and end apart: 108 -> 108, of which waited for: 29 -> 30; matrix products, arithmetic and copies ran while one was open for 17% -> 15% of each run, Pallas kernels for 32% -> 33%
where the time goes in v4:
time: 735 us; the launch traced here: 726 us
  Pallas kernels  257 us (35%)
  local copies, waits for them, and re-layouts  138 us (19%)
  waiting for transfers between devices  135 us (18%)
  starting transfers between devices  112 us (15%)
  other arithmetic  45.7 us (6%)
  matrix products  19.7 us (3%)
  between operations  18.1 us (2%)
    unnamed x369, local copies, waits for them, and re-layouts  86.2 us
    pallas_call x14, Pallas kernels, row_product(): pl.pallas_call(body, grid=(rows // block,), in_specs=[pl.BlockSpec((block...  57.2 us
    pallas_call x2, Pallas kernels, attend_backward(): pl.pallas_call(lambda *refs: attend_backward_kernel(head_dim, *refs), gri...  54.4 us
    ppermute x25, waiting for transfers between devices, from_y(): return lax.ppermute(value, 'fsdp', pairs)  52.9 us
    pallas_call x6, Pallas kernels, product(): pl.pallas_call(body, grid_spec=pltpu.PrefetchScalarGridSpec(num_scalar_pr...  43.9 us
    pallas_call x2, Pallas kernels, attend_forward(): pl.pallas_call(lambda *refs: attend_forward_kernel(head_dim, *refs), grid...  29.7 us
    ppermute x25, starting transfers between devices, from_x(): return lax.ppermute(value, 'fsdp', pairs)  27.6 us
    ppermute x25, starting transfers between devices, from_y(): return lax.ppermute(value, 'fsdp', pairs)  27.1 us
  transfers between devices with their start and end apart: 108, of which 30 were waited for; matrix products, arithmetic and copies ran while one was open for 15% of the time, Pallas kernels for 33%

profile of v4, /device:TPU:0, one launch (start us, length us, event | category | flops | bytes accessed | tf_op | source)
XLA Modules:
  0.0 725.5 jit_solution(10996773765265416677)
XLA Ops:
  10.6 4.7 collective-permute-start.4
  23.3 3.8 dynamic-slice_reduce_fusion
  38.1 8.3 %all-gather.7.cloned.1.call-done = bf16[256,2048]{1,0:T(8,128)(2,1)} async-done(((bf16[64,2048]{1,0:T(8,128)(2,1)}), bf16[256,2048]{1,0:T(8,128)(2,1)}) %all-gather.7.cloned.1.call-update) | async-done | bytes 1048592 | tf_op jit(solution)/shard_map/all_gather | solution.py:378
  52.8 6.1 collective-permute-done.10
  58.9 10.7 %collective-permute-done.9 = bf16[128,1024]{1,0:T(8,128)(2,1)S(1)} collective-permute-done((bf16[128,1024]{1,0:T(8,128)(2,1)S(1)}, bf16[128,1024]{1,0:T(8,128)(2,1)S(1)}, u32[]{:S(2)}, u32[]{:S(2)}) %collective-permute-start.9) | collective-permute-done | bytes 262176 | tf_op jit(solution)/shard_map/ppermute | solution.py:609
  82.7 2.9 join_pieces.2
  86.9 6.3 collective-permute-done.11.refs_3_
  96.4 2.8 all-gather.9.cloned.1.call-done
  105.5 3.0 assemble.6
  116.1 3.9 project_qkv.2
  123.8 4.5 all-gather.11.cloned.1.call-done
  134.9 14.8 %attend_forward.2 = (bf16[1024,512]{1,0:T(8,128)(2,1)S(1)}, f32[4,2,1024]{2,1,0:T(2,128)S(1)}) custom-call(bf16[1024,512]{1,0:T(8,128)(2,1)S(1)} %copy-done.115, bf16[1024,512]{1,0:T(8,128)(2,1)S(1)} %copy-done.118, bf16[1024,512]{1,0:T(8,128)(2,1)S(1)} %copy-done.121, s32[1024,1]{1,0:T(8,128)S(1)} %get-tuple-element.433.refs_3_.refs_5_, ...), custom_call_target="tpu_custom_call" | custom-call | flops 3006477056 | bytes 1468006 | tf_op jit(solution)/shard_map/attend_forward/pallas_call | solution.py:124
  153.8 3.3 all-gather.13.cloned.1.call-done
  173.2 5.1 norm_forward.4
  180.5 4.5 collective-permute-done.22.refs_3_
  185.0 3.1 collective-permute-done.23.refs_4_
  196.9 3.2 assemble.7
  200.2 9.4 %fusion.4 = (bf16[1024,2048]{1,0:T(8,128)(2,1)}, bf16[1024,2048]{1,0:T(8,128)(2,1)S(1)}) fusion(f32[2048]{0:T(1024)S(1)} %bitcast.376, bf16[1024,1024]{1,0:T(8,128)(2,1)S(1)} %get-tuple-element.627.before_ref.x_ref, bf16[1024,2048]{1,0:T(8,128)(2,1)S(1)} %bitcast.286), kind=kOutput, calls=%fused_computation.6 | convolution fusion | flops 4320133120 | bytes 14688256 | tf_op jit(solution)/shard_map/dot_general | solution.py:34
  209.6 4.2 assemble.8
  213.7 5.1 feed_out.2.part_ref
  230.4 5.1 norm_forward.5
  237.6 20.5 %collective-permute-done.32.refs_3_ = bf16[4,64,1024]{2,1,0:T(8,128)(2,1)S(1)} collective-permute-done((bf16[4,64,1024]{2,1,0:T(8,128)(2,1)S(1)}, bf16[4,64,1024]{2,1,0:T(8,128)(2,1)S(1)}, u32[]{:S(2)}, u32[]{:S(2)}) %collective-permute-start.32) | collective-permute-done | bytes 524320 | tf_op jit(solution)/shard_map/ppermute | solution.py:351
  273.4 3.9 project_qkv.3
  277.3 14.9 %attend_forward.3 = (bf16[1024,512]{1,0:T(8,128)(2,1)S(1)}, f32[4,2,1024]{2,1,0:T(2,128)S(1)}) custom-call(bf16[1024,512]{1,0:T(8,128)(2,1)S(1)} %get-tuple-element.583.refs_0_, bf16[1024,512]{1,0:T(8,128)(2,1)S(1)} %get-tuple-element.584.refs_1_, bf16[1024,512]{1,0:T(8,128)(2,1)S(1)} %get-tuple-element.585.refs_2_, ...), custom_call_target="tpu_custom_call" | custom-call | flops 3006477056 | bytes 1468006 | tf_op jit(solution)/shard_map/attend_forward/pallas_call | solution.py:124
  293.2 2.9 project_out.3.part_ref
  299.6 2.9 collective-permute-start.43
  309.1 3.0 assemble.10
  312.1 5.5 norm_forward.6
  317.6 7.8 %fusion.9 = (bf16[1024,2048]{1,0:T(8,128)(2,1)S(1)}, bf16[1024,2048]{1,0:T(8,128)(2,1)S(1)}) fusion(f32[2048]{0:T(1024)S(1)} %bitcast.377, bf16[1024,1024]{1,0:T(8,128)(2,1)S(1)} %get-tuple-element.548.before_ref.x_ref, bf16[1024,2048]{1,0:T(8,128)(2,1)S(1)} %bitcast.288), kind=kOutput, calls=%fused_computation.11 | convolution fusion | flops 4320133120 | bytes 14688256 | tf_op jit(solution)/shard_map/dot_general | solution.py:34
  325.5 4.0 collective-permute-start.45
  329.6 3.0 assemble.11
  332.6 5.2 feed_out.3.part_ref
  339.2 4.9 collective-permute-done.46.other_ref
  344.9 4.0 norm_forward.7
  348.9 3.2 norm_backward.4
  352.1 7.4 %weight_grad.6 = (bf16[4,2,128,512]{3,2,1,0:T(8,128)(2,1)S(1)}, bf16[4,2,128,512]{3,2,1,0:T(8,128)(2,1)S(1)}, bf16[4,2,128,512]{3,2,1,0:T(8,128)(2,1)S(1)}, bf16...) custom-call(s32[3]{0:T(128)S(1)} %pad_add_fusion.at_ref, bf16[1024,2048]{1,0:T(8,128)(2,1)S(1)} %get-tuple-element.521.refs_0_.x_ref, ...), custom_call_target="tpu_custom_call" | custom-call | flops 1503238528 | bytes 3670016 | tf_op jit(solution)/shard_map/weight_grad/pallas_call | solution.py:502
  364.4 5.2 feed_out_back.2.refs_0_
  369.7 7.2 weight_grad.7
  376.8 5.2 feed_in_back.2.refs_1_
  385.0 5.0 collective-permute-start.53
  395.8 3.9 norm_backward.5
  404.2 27.3 %attend_backward.2 = (bf16[1024,512]{1,0:T(8,128)(2,1)S(1)}, bf16[1024,512]{1,0:T(8,128)(2,1)S(1)}, bf16[1024,512]{1,0:T(8,128)(2,1)S(1)}) custom-call(bf16[1024,512]{1,0:T(8,128)(2,1)S(1)} %copy-done.124, bf16[1024,512]{1,0:T(8,128)(2,1)S(1)} %copy-done.126, bf16[1024,512]{1,0:T(8,128)(2,1)S(1)} %copy-done.128, ...), custom_call_target="tpu_custom_call" | custom-call | flops 7516192768 | bytes 2936012 | tf_op jit(solution)/shard_map/attend_backward/pallas_call | solution.py:156
  434.9 6.6 weight_grad.8
  451.8 4.1 project_qkv_back.2.refs_1_
  460.1 4.2 norm_backward.6
  465.7 7.8 %weight_grad.9 = (bf16[4,2,128,512]{3,2,1,0:T(8,128)(2,1)S(1)}, bf16[4,2,128,512]{3,2,1,0:T(8,128)(2,1)}, bf16[4,2,128,512]{3,2,1,0:T(8,128)(2,1)S(1)}, bf16[4,2,128,512]{3,2,1,0:T(8,128)(2,1)}, f32[8,1024]{1,0:T(8,128)}) custom-call(s32[3]{0:T(128)S(1)} %pad_add_fusion.at_ref, bf16[1024,2048]{1,0:T(8,128)(2,1)S(1)} %copy-done.15, ...), custom_call_target="tpu_custom_call" | custom-call | flops 1503238528 | bytes 3670016 | tf_op jit(solution)/shard_map/weight_grad/pallas_call | solution.py:502
  484.1 5.2 feed_out_back.3.refs_0_
  489.3 6.0 feed_in_back.3.refs_1_
  495.3 7.9 %weight_grad.10 = (bf16[4,2,64,1024]{3,2,1,0:T(8,128)(2,1)S(1)}, bf16[4,2,64,1024]{3,2,1,0:T(8,128)(2,1)}, bf16[4,2,64,1024]{3,2,1,0:T(8,128)(2,1)S(1)}, bf16[4,2,64,1024]{3,2,1,0:T(8,128)(2,1)}, f32[8,2048]{1,0:T(8,128)S(1)}) custom-call(s32[3]{0:T(128)S(1)} %pad_add_fusion.at_ref, bf16[1024,1024]{1,0:T(8,128)(2,1)S(1)} %copy-done.27, ...), custom_call_target="tpu_custom_call" | custom-call | flops 1503238528 | bytes 3670016 | tf_op jit(solution)/shard_map/weight_grad/pallas_call | solution.py:502
  508.4 2.8 scatter_add.9
  513.0 5.4 norm_backward.7
  522.6 3.0 collective-permute-done.70
  537.1 3.8 scatter_add.8
  545.6 27.1 %attend_backward.3 = (bf16[1024,512]{1,0:T(8,128)(2,1)S(1)}, bf16[1024,512]{1,0:T(8,128)(2,1)S(1)}, bf16[1024,512]{1,0:T(8,128)(2,1)S(1)}) custom-call(bf16[1024,512]{1,0:T(8,128)(2,1)S(1)} %copy-done.116, bf16[1024,512]{1,0:T(8,128)(2,1)S(1)} %copy-done.119, bf16[1024,512]{1,0:T(8,128)(2,1)S(1)} %copy-done.122, bf16[1024,512]{1,0:T(8,128)(2,1)S(1)} %copy-done.87, ...), custom_call_target="tpu_custom_call" | custom-call | flops 7516192768 | bytes 2936012 | tf_op jit(solution)/shard_map/attend_backward/pallas_call | solution.py:156
  581.8 3.7 scatter_add.10
  592.5 7.0 weight_grad.11
  601.2 4.9 project_qkv_back.3
  619.0 5.0 add_convert_fusion
  624.0 15.4 %collective-permute-done.77.refs_1_ = bf16[4,2,64,1024]{3,2,1,0:T(8,128)(2,1)S(1)} collective-permute-done((bf16[4,2,64,1024]{3,2,1,0:T(8,128)(2,1)}, bf16[4,2,64,1024]{3,2,1,0:T(8,128)(2,1)S(1)}, u32[]{:S(2)}, u32[]{:S(2)}) %collective-permute-start.77) | collective-permute-done | bytes 1048608 | tf_op jit(solution)/shard_map/ppermute | solution.py:351
  653.1 4.2 collective-permute-start.85
  666.0 4.0 collective-permute-start.87
  670.6 5.6 collective-permute-start.89
  676.3 5.8 collective-permute-done.86
  697.2 15.5 %reduce-scatter.13.cloned.1.call-done = bf16[64,2048]{1,0:T(8,128)(2,1)} async-done(((bf16[256,2048]{1,0:T(8,128)(2,1)}), bf16[64,2048]{1,0:T(8,128)(2,1)}) %reduce-scatter.13.cloned.1.call-update) | async-done | bytes 262160 | tf_op jit(solution)/shard_map/reduce_scatter | solution.py:577
  (771 shorter events, 290.7 us)
Async XLA Ops:
  7.2 39.3 %all-gather.7.cloned.1.call-start = ((), (), s32[]{:S(2)}) async-start(), calls=%async_computation.6 | async-start | bytes 1310720 | tf_op jit(solution)/shard_map/all_gather | solution.py:378
  10.6 20.2 %collective-permute-start.4 = (s32[256]{0:T(256)S(1)}, s32[256]{0:T(256)S(1)}, u32[]{:S(2)}, u32[]{:S(2)}) collective-permute-start(s32[256]{0:T(256)S(1)} %bitcast.387), channel_id=1, source_target_pairs={{0,12},{4,0},{8,4},{12,8},{1,13},{5,1},{9,5},{13,9},{2,14},{6,2},{... | collective-permute-start | bytes 3080 | tf_op jit(solution)/shard_map/ppermute | solution.py:609
  17.3 81.9 %all-gather.9.cloned.1.call-start = ((), (), s32[]{:S(2)}) async-start(), calls=%async_computation.7 | async-start | bytes 1310720 | tf_op jit(solution)/shard_map/all_gather | solution.py:378
  46.5 25.4 %collective-permute-start.7 = (bf16[4,64,2048]{2,1,0:T(8,128)(2,1)}, bf16[4,64,2048]{2,1,0:T(8,128)(2,1)}, u32[]{:S(2)}, u32[]{:S(2)}) collective-permute-start(bf16[4,64,2048]{2,1,0:T(8,128)(2,1)} %bitcast.301), channel_id=1, source_target_pairs={{1,0},{0,1},{3,2},{2,3},{5,4},{4,5},{7,6},{6,7},{9,8},{8,9},{11,10... | collective-permute-start | bytes 3145736 | tf_op jit(solution)/shard_map/ppermute | solution.py:344
  47.9 25.2 %collective-permute-start.8 = (bf16[4,64,2048]{2,1,0:T(8,128)(2,1)}, bf16[4,64,2048]{2,1,0:T(8,128)(2,1)}, u32[]{:S(2)}, u32[]{:S(2)}) collective-permute-start(bf16[4,64,2048]{2,1,0:T(8,128)(2,1)} %bitcast.302), channel_id=1, source_target_pairs={{2,0},{3,1},{0,2},{1,3},{6,4},{7,5},{4,6},{5,7},{10,8},{11,9},{8,1... | collective-permute-start | bytes 3145736 | tf_op jit(solution)/shard_map/ppermute | solution.py:351
  73.1 55.1 %all-gather.11.cloned.1.call-start = ((), (), s32[]{:S(2)}) async-start(), calls=%async_computation.8 | async-start | bytes 1310720 | tf_op jit(solution)/shard_map/all_gather | solution.py:378
  73.9 83.3 %all-gather.13.cloned.1.call-start = ((), (), s32[]{:S(2)}) async-start(), calls=%async_computation.9 | async-start | bytes 1310720 | tf_op jit(solution)/shard_map/all_gather | solution.py:378
  99.2 29.0 %collective-permute-start.16 = (bf16[4,64,2048]{2,1,0:T(8,128)(2,1)}, bf16[4,64,2048]{2,1,0:T(8,128)(2,1)}, u32[]{:S(2)}, u32[]{:S(2)}) collective-permute-start(bf16[4,64,2048]{2,1,0:T(8,128)(2,1)} %bitcast.307), channel_id=1, source_target_pairs={{1,0},{0,1},{3,2},{2,3},{5,4},{4,5},{7,6},{6,7},{9,8},{8,9},{11,10... | collective-permute-start | bytes 3145736 | tf_op jit(solution)/shard_map/ppermute | solution.py:344
  100.7 27.6 %collective-permute-start.17 = (bf16[4,64,2048]{2,1,0:T(8,128)(2,1)}, bf16[4,64,2048]{2,1,0:T(8,128)(2,1)}, u32[]{:S(2)}, u32[]{:S(2)}) collective-permute-start(bf16[4,64,2048]{2,1,0:T(8,128)(2,1)} %bitcast.308), channel_id=1, source_target_pairs={{2,0},{3,1},{0,2},{1,3},{6,4},{7,5},{4,6},{5,7},{10,8},{11,9},{8,1... | collective-permute-start | bytes 3145736 | tf_op jit(solution)/shard_map/ppermute | solution.py:351
  112.0 76.0 %all-gather.15.cloned.1.call-start = ((), (), s32[]{:S(2)}) async-start(), calls=%async_computation.10 | async-start | bytes 1310720 | tf_op jit(solution)/shard_map/all_gather | solution.py:378
  128.2 28.9 %collective-permute-start.18 = (bf16[4,128,1024]{2,1,0:T(8,128)(2,1)}, bf16[4,128,1024]{2,1,0:T(8,128)(2,1)}, u32[]{:S(2)}, u32[]{:S(2)}) collective-permute-start(bf16[4,128,1024]{2,1,0:T(8,128)(2,1)} %bitcast.304), channel_id=1, source_target_pairs={{1,0},{0,1},{3,2},{2,3},{5,4},{4,5},{7,6},{6,7},{9,8},{8,9},{11,10... | collective-permute-start | bytes 3145736 | tf_op jit(solution)/shard_map/ppermute | solution.py:344
  129.7 27.4 %collective-permute-start.19 = (bf16[4,128,1024]{2,1,0:T(8,128)(2,1)}, bf16[4,128,1024]{2,1,0:T(8,128)(2,1)}, u32[]{:S(2)}, u32[]{:S(2)}) collective-permute-start(bf16[4,128,1024]{2,1,0:T(8,128)(2,1)} %bitcast.305), channel_id=1, source_target_pairs={{2,0},{3,1},{0,2},{1,3},{6,4},{7,5},{4,6},{5,7},{10,8},{11,9},{8,1... | collective-permute-start | bytes 3145736 | tf_op jit(solution)/shard_map/ppermute | solution.py:351
  157.2 102.5 %all-gather.17.cloned.1.call-start = ((), (), s32[]{:S(2)}) async-start(), calls=%async_computation.11 | async-start | bytes 1310720 | tf_op jit(solution)/shard_map/all_gather | solution.py:378
  159.1 21.4 %collective-permute-start.20 = (bf16[4,64,1024]{2,1,0:T(8,128)(2,1)}, bf16[4,64,1024]{2,1,0:T(8,128)(2,1)}, u32[]{:S(2)}, u32[]{:S(2)}) collective-permute-start(bf16[4,64,1024]{2,1,0:T(8,128)(2,1)} %slice.291), channel_id=1, source_target_pairs={{2,0},{3,1},{0,2},{1,3},{6,4},{7,5},{4,6},{5,7},{10,8},{11,9},{8,1... | collective-permute-start | bytes 1572872 | tf_op jit(solution)/shard_map/ppermute | solution.py:351
  165.8 19.2 %collective-permute-start.22 = (bf16[4,128,512]{2,1,0:T(8,128)(2,1)}, bf16[4,128,512]{2,1,0:T(8,128)(2,1)}, u32[]{:S(2)}, u32[]{:S(2)}) collective-permute-start(bf16[4,128,512]{2,1,0:T(8,128)(2,1)} %slice.293), channel_id=1, source_target_pairs={{2,0},{3,1},{0,2},{1,3},{6,4},{7,5},{4,6},{5,7},{10,8},{11,9},{8,1... | collective-permute-start | bytes 1572872 | tf_op jit(solution)/shard_map/ppermute | solution.py:351
  168.2 19.9 %collective-permute-start.23 = (bf16[4,128,512]{2,1,0:T(8,128)(2,1)}, bf16[4,128,512]{2,1,0:T(8,128)(2,1)}, u32[]{:S(2)}, u32[]{:S(2)}) collective-permute-start(bf16[4,128,512]{2,1,0:T(8,128)(2,1)} %slice.294), channel_id=1, source_target_pairs={{1,0},{0,1},{3,2},{2,3},{5,4},{4,5},{7,6},{6,7},{9,8},{8,9},{11,10... | collective-permute-start | bytes 1572872 | tf_op jit(solution)/shard_map/ppermute | solution.py:344
  188.1 30.9 %collective-permute-start.25 = (bf16[4,64,2048]{2,1,0:T(8,128)(2,1)}, bf16[4,64,2048]{2,1,0:T(8,128)(2,1)S(1)}, u32[]{:S(2)}, u32[]{:S(2)}) collective-permute-start(bf16[4,64,2048]{2,1,0:T(8,128)(2,1)} %bitcast.310), channel_id=1, source_target_pairs={{1,0},{0,1},{3,2},{2,3},{5,4},{4,5},{7,6},{6,7},{9,8},{8,9},{11,10... | collective-permute-start | bytes 3145736 | tf_op jit(solution)/shard_map/ppermute | solution.py:344
  189.5 29.5 %collective-permute-start.26 = (bf16[4,64,2048]{2,1,0:T(8,128)(2,1)}, bf16[4,64,2048]{2,1,0:T(8,128)(2,1)S(1)}, u32[]{:S(2)}, u32[]{:S(2)}) collective-permute-start(bf16[4,64,2048]{2,1,0:T(8,128)(2,1)} %bitcast.311), channel_id=1, source_target_pairs={{2,0},{3,1},{0,2},{1,3},{6,4},{7,5},{4,6},{5,7},{10,8},{11,9},{8,1... | collective-permute-start | bytes 3145736 | tf_op jit(solution)/shard_map/ppermute | solution.py:351
  192.1 26.8 %collective-permute-start.27 = (bf16[128,1024]{1,0:T(8,128)(2,1)S(1)}, bf16[128,1024]{1,0:T(8,128)(2,1)S(1)}, u32[]{:S(2)}, u32[]{:S(2)}) collective-permute-start(bf16[128,1024]{1,0:T(8,128)(2,1)S(1)} %get-tuple-element.850), channel_id=1, source_target_pairs={{0,4},{4,8},{8,12},{12,0},{1,5},{5,9},{9,13},{13,1},{2,6},{6,10},{... | collective-permute-start | bytes 786440 | tf_op jit(solution)/shard_map/ppermute | solution.py:609
  193.5 25.4 %collective-permute-start.28 = (bf16[128,1024]{1,0:T(8,128)(2,1)S(1)}, bf16[128,1024]{1,0:T(8,128)(2,1)S(1)}, u32[]{:S(2)}, u32[]{:S(2)}) collective-permute-start(bf16[128,1024]{1,0:T(8,128)(2,1)S(1)} %get-tuple-element.849), channel_id=1, source_target_pairs={{0,8},{4,12},{8,0},{12,4},{1,9},{5,13},{9,1},{13,5},{2,10},{6,14},... | collective-permute-start | bytes 786440 | tf_op jit(solution)/shard_map/ppermute | solution.py:609
  194.5 24.4 %collective-permute-start.29 = (bf16[128,1024]{1,0:T(8,128)(2,1)S(1)}, bf16[128,1024]{1,0:T(8,128)(2,1)S(1)}, u32[]{:S(2)}, u32[]{:S(2)}) collective-permute-start(bf16[128,1024]{1,0:T(8,128)(2,1)S(1)} %get-tuple-element.848), channel_id=1, source_target_pairs={{0,12},{4,0},{8,4},{12,8},{1,13},{5,1},{9,5},{13,9},{2,14},{6,2},{... | collective-permute-start | bytes 786440 | tf_op jit(solution)/shard_map/ppermute | solution.py:609
  220.5 355.1 %reduce-scatter.11.cloned.1.call-start = ((), (), s32[]{:S(2)}) async-start(), calls=%async_computation.14 | async-start | bytes 1310720 | tf_op jit(solution)/shard_map/reduce_scatter | solution.py:577
  220.8 38.9 %collective-permute-start.30 = (bf16[4,64,2048]{2,1,0:T(8,128)(2,1)}, bf16[4,64,2048]{2,1,0:T(8,128)(2,1)}, u32[]{:S(2)}, u32[]{:S(2)}) collective-permute-start(bf16[4,64,2048]{2,1,0:T(8,128)(2,1)} %bitcast.298), channel_id=1, source_target_pairs={{1,0},{0,1},{3,2},{2,3},{5,4},{4,5},{7,6},{6,7},{9,8},{8,9},{11,10... | collective-permute-start | bytes 3145736 | tf_op jit(solution)/shard_map/ppermute | solution.py:344
  221.4 38.3 %collective-permute-start.31 = (bf16[4,64,2048]{2,1,0:T(8,128)(2,1)}, bf16[4,64,2048]{2,1,0:T(8,128)(2,1)}, u32[]{:S(2)}, u32[]{:S(2)}) collective-permute-start(bf16[4,64,2048]{2,1,0:T(8,128)(2,1)} %bitcast.299), channel_id=1, source_target_pairs={{2,0},{3,1},{0,2},{1,3},{6,4},{7,5},{4,6},{5,7},{10,8},{11,9},{8,1... | collective-permute-start | bytes 3145736 | tf_op jit(solution)/shard_map/ppermute | solution.py:351
  223.9 34.2 %collective-permute-start.32 = (bf16[4,64,1024]{2,1,0:T(8,128)(2,1)S(1)}, bf16[4,64,1024]{2,1,0:T(8,128)(2,1)S(1)}, u32[]{:S(2)}, u32[]{:S(2)}) collective-permute-start(bf16[4,64,1024]{2,1,0:T(8,128)(2,1)S(1)} %slice.299), channel_id=1, source_target_pairs={{2,0},{3,1},{0,2},{1,3},{6,4},{7,5},{4,6},{5,7},{10,8},{11,9},{8,1... | collective-permute-start | bytes 1572872 | tf_op jit(solution)/shard_map/ppermute | solution.py:351
  225.6 33.3 %collective-permute-start.33 = (bf16[4,64,1024]{2,1,0:T(8,128)(2,1)S(1)}, bf16[4,64,1024]{2,1,0:T(8,128)(2,1)S(1)}, u32[]{:S(2)}, u32[]{:S(2)}) collective-permute-start(bf16[4,64,1024]{2,1,0:T(8,128)(2,1)S(1)} %slice.300), channel_id=1, source_target_pairs={{1,0},{0,1},{3,2},{2,3},{5,4},{4,5},{7,6},{6,7},{9,8},{8,9},{11,10... | collective-permute-start | bytes 1572872 | tf_op jit(solution)/shard_map/ppermute | solution.py:344
  259.7 38.8 %collective-permute-start.35 = (bf16[4,128,1024]{2,1,0:T(8,128)(2,1)}, bf16[4,128,1024]{2,1,0:T(8,128)(2,1)}, u32[]{:S(2)}, u32[]{:S(2)}) collective-permute-start(bf16[4,128,1024]{2,1,0:T(8,128)(2,1)} %bitcast.313), channel_id=1, source_target_pairs={{1,0},{0,1},{3,2},{2,3},{5,4},{4,5},{7,6},{6,7},{9,8},{8,9},{11,10... | collective-permute-start | bytes 3145736 | tf_op jit(solution)/shard_map/ppermute | solution.py:344
  261.3 37.3 %collective-permute-start.36 = (bf16[4,128,1024]{2,1,0:T(8,128)(2,1)}, bf16[4,128,1024]{2,1,0:T(8,128)(2,1)}, u32[]{:S(2)}, u32[]{:S(2)}) collective-permute-start(bf16[4,128,1024]{2,1,0:T(8,128)(2,1)} %bitcast.314), channel_id=1, source_target_pairs={{2,0},{3,1},{0,2},{1,3},{6,4},{7,5},{4,6},{5,7},{10,8},{11,9},{8,1... | collective-permute-start | bytes 3145736 | tf_op jit(solution)/shard_map/ppermute | solution.py:351
  269.5 22.8 %collective-permute-start.39 = (bf16[512,512]{1,0:T(8,128)(2,1)S(1)}, bf16[512,512]{1,0:T(8,128)(2,1)S(1)}, u32[]{:S(2)}, u32[]{:S(2)}) collective-permute-start(bf16[512,512]{1,0:T(8,128)(2,1)S(1)} %constant_dynamic-slice_fusion.11), channel_id=1, source_target_pairs={{0,16},{16,0},{1,17},{17,1},{2,18},{18,2},{3,19},{19,3},{4,20},{20... | collective-permute-start | bytes 1572872 | tf_op jit(solution)/shard_map/ppermute | solution.py:354
  271.0 25.9 %collective-permute-start.37 = (bf16[4,64,1024]{2,1,0:T(8,128)(2,1)S(1)}, bf16[4,64,1024]{2,1,0:T(8,128)(2,1)S(1)}, u32[]{:S(2)}, u32[]{:S(2)}) collective-permute-start(bf16[4,64,1024]{2,1,0:T(8,128)(2,1)S(1)} %slice.304), channel_id=1, source_target_pairs={{2,0},{3,1},{0,2},{1,3},{6,4},{7,5},{4,6},{5,7},{10,8},{11,9},{8,1... | collective-permute-start | bytes 1572872 | tf_op jit(solution)/shard_map/ppermute | solution.py:351
  272.7 25.0 %collective-permute-start.38 = (bf16[4,64,1024]{2,1,0:T(8,128)(2,1)S(1)}, bf16[4,64,1024]{2,1,0:T(8,128)(2,1)S(1)}, u32[]{:S(2)}, u32[]{:S(2)}) collective-permute-start(bf16[4,64,1024]{2,1,0:T(8,128)(2,1)S(1)} %slice.305), channel_id=1, source_target_pairs={{1,0},{0,1},{3,2},{2,3},{5,4},{4,5},{7,6},{6,7},{9,8},{8,9},{11,10... | collective-permute-start | bytes 1572872 | tf_op jit(solution)/shard_map/ppermute | solution.py:344
  299.6 25.8 %collective-permute-start.43 = (bf16[256,1024]{1,0:T(8,128)(2,1)S(1)}, bf16[256,1024]{1,0:T(8,128)(2,1)S(1)}, u32[]{:S(2)}, u32[]{:S(2)}) collective-permute-start(bf16[256,1024]{1,0:T(8,128)(2,1)S(1)} %get-tuple-element.836), channel_id=1, source_target_pairs={{4,0},{8,4},{12,8},{0,12},{5,1},{9,5},{13,9},{1,13},{6,2},{10,6},{... | collective-permute-start | bytes 1572872 | tf_op jit(solution)/shard_map/ppermute | solution.py:632
  302.5 22.9 %collective-permute-start.44 = (bf16[256,1024]{1,0:T(8,128)(2,1)S(1)}, bf16[256,1024]{1,0:T(8,128)(2,1)S(1)}, u32[]{:S(2)}, u32[]{:S(2)}) collective-permute-start(bf16[256,1024]{1,0:T(8,128)(2,1)S(1)} %get-tuple-element.835), channel_id=1, source_target_pairs={{8,0},{12,4},{0,8},{4,12},{9,1},{13,5},{1,9},{5,13},{10,2},{14,6},... | collective-permute-start | bytes 1572872 | tf_op jit(solution)/shard_map/ppermute | solution.py:632
  305.6 19.8 %collective-permute-start.40 = (bf16[4,128,512]{2,1,0:T(8,128)(2,1)S(1)}, bf16[4,128,512]{2,1,0:T(8,128)(2,1)S(1)}, u32[]{:S(2)}, u32[]{:S(2)}) collective-permute-start(bf16[4,128,512]{2,1,0:T(8,128)(2,1)S(1)} %slice.308), channel_id=1, source_target_pairs={{2,0},{3,1},{0,2},{1,3},{6,4},{7,5},{4,6},{5,7},{10,8},{11,9},{8,1... | collective-permute-start | bytes 1572872 | tf_op jit(solution)/shard_map/ppermute | solution.py:351
  359.5 25.2 %collective-permute-start.48 = (bf16[4,2,128,512]{3,2,1,0:T(8,128)(2,1)S(1)}, bf16[4,2,128,512]{3,2,1,0:T(8,128)(2,1)S(1)}, u32[]{:S(2)}, u32[]{:S(2)}) collective-permute-start(bf16[4,2,128,512]{3,2,1,0:T(8,128)(2,1)S(1)} %get-tuple-element.563), channel_id=1, source_target_pairs={{2,0},{3,1},{0,2},{1,3},{6,4},{7,5},{4,6},{5,7},{10,8},{11,9},{8,1... | collective-permute-start | bytes 3145736 | tf_op jit(solution)/shard_map/ppermute | solution.py:351
  360.0 24.9 %collective-permute-start.49 = (bf16[4,2,128,512]{3,2,1,0:T(8,128)(2,1)S(1)}, bf16[4,2,128,512]{3,2,1,0:T(8,128)(2,1)S(1)}, u32[]{:S(2)}, u32[]{:S(2)}) collective-permute-start(bf16[4,2,128,512]{3,2,1,0:T(8,128)(2,1)S(1)} %get-tuple-element.565), channel_id=1, source_target_pairs={{1,0},{0,1},{3,2},{2,3},{5,4},{4,5},{7,6},{6,7},{9,8},{8,9},{11,10... | collective-permute-start | bytes 3145736 | tf_op jit(solution)/shard_map/ppermute | solution.py:344
  362.4 19.7 %collective-permute-start.50 = (bf16[256,1024]{1,0:T(8,128)(2,1)S(1)}, bf16[256,1024]{1,0:T(8,128)(2,1)S(1)}, u32[]{:S(2)}, u32[]{:S(2)}) collective-permute-start(bf16[256,1024]{1,0:T(8,128)(2,1)S(1)} %get-tuple-element.833), channel_id=1, source_target_pairs={{20,16},{24,20},{28,24},{16,28},{21,17},{25,21},{29,25},{17,29},{2... | collective-permute-start | bytes 1572872 | tf_op jit(solution)/shard_map/ppermute | solution.py:632
  391.8 39.8 %collective-permute-start.54 = (bf16[4,128,512]{2,1,0:T(8,128)(2,1)S(1)}, bf16[4,128,512]{2,1,0:T(8,128)(2,1)S(1)}, u32[]{:S(2)}, u32[]{:S(2)}) collective-permute-start(bf16[4,128,512]{2,1,0:T(8,128)(2,1)S(1)} %get-tuple-element.576), channel_id=1, source_target_pairs={{1,0},{0,1},{3,2},{2,3},{5,4},{4,5},{7,6},{6,7},{9,8},{8,9},{11,10... | collective-permute-start | bytes 1572872 | tf_op jit(solution)/shard_map/ppermute | solution.py:344
  392.5 39.0 %collective-permute-start.55 = (bf16[4,128,512]{2,1,0:T(8,128)(2,1)S(1)}, bf16[4,128,512]{2,1,0:T(8,128)(2,1)S(1)}, u32[]{:S(2)}, u32[]{:S(2)}) collective-permute-start(bf16[4,128,512]{2,1,0:T(8,128)(2,1)S(1)} %get-tuple-element.578), channel_id=1, source_target_pairs={{2,0},{3,1},{0,2},{1,3},{6,4},{7,5},{4,6},{5,7},{10,8},{11,9},{8,1... | collective-permute-start | bytes 1572872 | tf_op jit(solution)/shard_map/ppermute | solution.py:351
  394.0 37.6 %collective-permute-start.56 = (bf16[4,2,64,1024]{3,2,1,0:T(8,128)(2,1)S(1)}, bf16[4,2,64,1024]{3,2,1,0:T(8,128)(2,1)S(1)}, u32[]{:S(2)}, u32[]{:S(2)}) collective-permute-start(bf16[4,2,64,1024]{3,2,1,0:T(8,128)(2,1)S(1)} %get-tuple-element.580), channel_id=1, source_target_pairs={{2,0},{3,1},{0,2},{1,3},{6,4},{7,5},{4,6},{5,7},{10,8},{11,9},{8,1... | collective-permute-start | bytes 3145736 | tf_op jit(solution)/shard_map/ppermute | solution.py:351
  394.5 37.1 %collective-permute-start.57 = (bf16[4,2,64,1024]{3,2,1,0:T(8,128)(2,1)S(1)}, bf16[4,2,64,1024]{3,2,1,0:T(8,128)(2,1)S(1)}, u32[]{:S(2)}, u32[]{:S(2)}) collective-permute-start(bf16[4,2,64,1024]{3,2,1,0:T(8,128)(2,1)S(1)} %get-tuple-element.582), channel_id=1, source_target_pairs={{1,0},{0,1},{3,2},{2,3},{5,4},{4,5},{7,6},{6,7},{9,8},{8,9},{11,10... | collective-permute-start | bytes 3145736 | tf_op jit(solution)/shard_map/ppermute | solution.py:344
  401.2 30.4 %collective-permute-start.58 = (bf16[512,512]{1,0:T(8,128)(2,1)S(1)}, bf16[512,512]{1,0:T(8,128)(2,1)S(1)}, u32[]{:S(2)}, u32[]{:S(2)}) collective-permute-start(bf16[512,512]{1,0:T(8,128)(2,1)S(1)} %get-tuple-element.846), channel_id=1, source_target_pairs={{0,16},{16,0},{1,17},{17,1},{2,18},{18,2},{3,19},{19,3},{4,20},{20... | collective-permute-start | bytes 1572872 | tf_op jit(solution)/shard_map/ppermute | solution.py:354
  456.1 49.7 %collective-permute-start.64 = (bf16[4,2,64,1024]{3,2,1,0:T(8,128)(2,1)}, bf16[4,2,64,1024]{3,2,1,0:T(8,128)(2,1)}, u32[]{:S(2)}, u32[]{:S(2)}) collective-permute-start(bf16[4,2,64,1024]{3,2,1,0:T(8,128)(2,1)} %get-tuple-element.637), channel_id=1, source_target_pairs={{2,0},{3,1},{0,2},{1,3},{6,4},{7,5},{4,6},{5,7},{10,8},{11,9},{8,1... | collective-permute-start | bytes 3145736 | tf_op jit(solution)/shard_map/ppermute | solution.py:351
  457.7 48.1 %collective-permute-start.65 = (bf16[4,2,64,1024]{3,2,1,0:T(8,128)(2,1)}, bf16[4,2,64,1024]{3,2,1,0:T(8,128)(2,1)}, u32[]{:S(2)}, u32[]{:S(2)}) collective-permute-start(bf16[4,2,64,1024]{3,2,1,0:T(8,128)(2,1)} %get-tuple-element.639), channel_id=1, source_target_pairs={{1,0},{0,1},{3,2},{2,3},{5,4},{4,5},{7,6},{6,7},{9,8},{8,9},{11,10... | collective-permute-start | bytes 3145736 | tf_op jit(solution)/shard_map/ppermute | solution.py:344
  475.5 30.3 %collective-permute-start.62 = (bf16[4,2,128,512]{3,2,1,0:T(8,128)(2,1)}, bf16[4,2,128,512]{3,2,1,0:T(8,128)(2,1)}, u32[]{:S(2)}, u32[]{:S(2)}) collective-permute-start(bf16[4,2,128,512]{3,2,1,0:T(8,128)(2,1)} %get-tuple-element.633), channel_id=1, source_target_pairs={{2,0},{3,1},{0,2},{1,3},{6,4},{7,5},{4,6},{5,7},{10,8},{11,9},{8,1... | collective-permute-start | bytes 3145736 | tf_op jit(solution)/shard_map/ppermute | solution.py:351
  476.9 28.9 %collective-permute-start.63 = (bf16[4,2,128,512]{3,2,1,0:T(8,128)(2,1)}, bf16[4,2,128,512]{3,2,1,0:T(8,128)(2,1)}, u32[]{:S(2)}, u32[]{:S(2)}) collective-permute-start(bf16[4,2,128,512]{3,2,1,0:T(8,128)(2,1)} %get-tuple-element.635), channel_id=1, source_target_pairs={{1,0},{0,1},{3,2},{2,3},{5,4},{4,5},{7,6},{6,7},{9,8},{8,9},{11,10... | collective-permute-start | bytes 3145736 | tf_op jit(solution)/shard_map/ppermute | solution.py:344
  479.5 96.2 %reduce-scatter.9.cloned.1.call-start = ((), (), s32[]{:S(2)}) async-start(), calls=%async_computation.13 | async-start | bytes 1310720 | tf_op jit(solution)/shard_map/reduce_scatter | solution.py:577
  505.9 69.8 %reduce-scatter.7.cloned.1.call-start = ((), (), s32[]{:S(2)}) async-start(), calls=%async_computation.12 | async-start | bytes 1310720 | tf_op jit(solution)/shard_map/reduce_scatter | solution.py:577
  528.0 84.0 %reduce-scatter.17.cloned.1.call-start = ((), (), s32[]{:S(2)}) async-start(), calls=%async_computation.17 | async-start | bytes 1310720 | tf_op jit(solution)/shard_map/reduce_scatter | solution.py:577
  533.1 42.6 %collective-permute-start.68 = (bf16[4,2,64,1024]{3,2,1,0:T(8,128)(2,1)}, bf16[4,2,64,1024]{3,2,1,0:T(8,128)(2,1)}, u32[]{:S(2)}, u32[]{:S(2)}) collective-permute-start(bf16[4,2,64,1024]{3,2,1,0:T(8,128)(2,1)} %get-tuple-element.653), channel_id=1, source_target_pairs={{2,0},{3,1},{0,2},{1,3},{6,4},{7,5},{4,6},{5,7},{10,8},{11,9},{8,1... | collective-permute-start | bytes 3145736 | tf_op jit(solution)/shard_map/ppermute | solution.py:351
  533.7 42.0 %collective-permute-start.69 = (bf16[4,2,64,1024]{3,2,1,0:T(8,128)(2,1)}, bf16[4,2,64,1024]{3,2,1,0:T(8,128)(2,1)}, u32[]{:S(2)}, u32[]{:S(2)}) collective-permute-start(bf16[4,2,64,1024]{3,2,1,0:T(8,128)(2,1)} %get-tuple-element.655), channel_id=1, source_target_pairs={{1,0},{0,1},{3,2},{2,3},{5,4},{4,5},{7,6},{6,7},{9,8},{8,9},{11,10... | collective-permute-start | bytes 3145736 | tf_op jit(solution)/shard_map/ppermute | solution.py:344
  542.5 33.2 %collective-permute-start.66 = (bf16[4,128,512]{2,1,0:T(8,128)(2,1)}, bf16[4,128,512]{2,1,0:T(8,128)(2,1)S(1)}, u32[]{:S(2)}, u32[]{:S(2)}) collective-permute-start(bf16[4,128,512]{2,1,0:T(8,128)(2,1)} %get-tuple-element.649), channel_id=1, source_target_pairs={{1,0},{0,1},{3,2},{2,3},{5,4},{4,5},{7,6},{6,7},{9,8},{8,9},{11,10... | collective-permute-start | bytes 1572872 | tf_op jit(solution)/shard_map/ppermute | solution.py:344
  543.8 31.9 %collective-permute-start.67 = (bf16[4,128,512]{2,1,0:T(8,128)(2,1)}, bf16[4,128,512]{2,1,0:T(8,128)(2,1)S(1)}, u32[]{:S(2)}, u32[]{:S(2)}) collective-permute-start(bf16[4,128,512]{2,1,0:T(8,128)(2,1)} %get-tuple-element.651), channel_id=1, source_target_pairs={{2,0},{3,1},{0,2},{1,3},{6,4},{7,5},{4,6},{5,7},{10,8},{11,9},{8,1... | collective-permute-start | bytes 1572872 | tf_op jit(solution)/shard_map/ppermute | solution.py:351
  545.3 30.4 %collective-permute-start.73 = (bf16[512,512]{1,0:T(8,128)(2,1)}, bf16[512,512]{1,0:T(8,128)(2,1)}, u32[]{:S(2)}, u32[]{:S(2)}) collective-permute-start(bf16[512,512]{1,0:T(8,128)(2,1)} %get-tuple-element.678), channel_id=1, source_target_pairs={{0,16},{16,0},{1,17},{17,1},{2,18},{18,2},{3,19},{19,3},{4,20},{20... | collective-permute-start | bytes 1572872 | tf_op jit(solution)/shard_map/ppermute | solution.py:354
  579.3 80.3 %reduce-scatter.15.cloned.1.call-start = ((), (), s32[]{:S(2)}) async-start(), calls=%async_computation.16 | async-start | bytes 1310720 | tf_op jit(solution)/shard_map/reduce_scatter | solution.py:577
  611.0 101.8 %reduce-scatter.13.cloned.1.call-start = ((), (), s32[]{:S(2)}) async-start(), calls=%async_computation.15 | async-start | bytes 1310720 | tf_op jit(solution)/shard_map/reduce_scatter | solution.py:577
  615.1 24.3 %collective-permute-start.77 = (bf16[4,2,64,1024]{3,2,1,0:T(8,128)(2,1)}, bf16[4,2,64,1024]{3,2,1,0:T(8,128)(2,1)S(1)}, u32[]{:S(2)}, u32[]{:S(2)}) collective-permute-start(bf16[4,2,64,1024]{3,2,1,0:T(8,128)(2,1)} %copy-done.130), channel_id=1, source_target_pairs={{2,0},{3,1},{0,2},{1,3},{6,4},{7,5},{4,6},{5,7},{10,8},{11,9},{8,1... | collective-permute-start | bytes 3145736 | tf_op jit(solution)/shard_map/ppermute | solution.py:351
  615.5 24.8 %collective-permute-start.78 = (bf16[4,2,64,1024]{3,2,1,0:T(8,128)(2,1)}, bf16[4,2,64,1024]{3,2,1,0:T(8,128)(2,1)S(1)}, u32[]{:S(2)}, u32[]{:S(2)}) collective-permute-start(bf16[4,2,64,1024]{3,2,1,0:T(8,128)(2,1)} %copy-done.129), channel_id=1, source_target_pairs={{1,0},{0,1},{3,2},{2,3},{5,4},{4,5},{7,6},{6,7},{9,8},{8,9},{11,10... | collective-permute-start | bytes 3145736 | tf_op jit(solution)/shard_map/ppermute | solution.py:344
  641.5 20.6 %collective-permute-start.91 = (f32[4,2,776]{2,1,0:T(2,128)S(1)}, f32[4,2,776]{2,1,0:T(2,128)S(1)}, u32[]{:S(2)}, u32[]{:S(2)}) collective-permute-start(f32[4,2,776]{2,1,0:T(2,128)S(1)} %dynamic-slice_bitcast_fusion.33), channel_id=1, source_target_pairs={{2,0},{3,1},{0,2},{1,3},{6,4},{7,5},{4,6},{5,7},{10,8},{11,9},{8,1... | collective-permute-start | bytes 74504 | tf_op jit(solution)/shard_map/ppermute | solution.py:351
  649.8 20.9 %collective-permute-start.83 = (bf16[4,64,1024]{2,1,0:T(8,128)(2,1)}, bf16[4,64,1024]{2,1,0:T(8,128)(2,1)}, u32[]{:S(2)}, u32[]{:S(2)}) collective-permute-start(bf16[4,64,1024]{2,1,0:T(8,128)(2,1)} %get-tuple-element.755), channel_id=1, source_target_pairs={{1,0},{0,1},{3,2},{2,3},{5,4},{4,5},{7,6},{6,7},{9,8},{8,9},{11,10... | collective-permute-start | bytes 1572872 | tf_op jit(solution)/shard_map/ppermute | solution.py:344
  651.0 25.2 %collective-permute-start.84 = (bf16[4,64,1024]{2,1,0:T(8,128)(2,1)}, bf16[4,64,1024]{2,1,0:T(8,128)(2,1)}, u32[]{:S(2)}, u32[]{:S(2)}) collective-permute-start(bf16[4,64,1024]{2,1,0:T(8,128)(2,1)} %get-tuple-element.757), channel_id=1, source_target_pairs={{2,0},{3,1},{0,2},{1,3},{6,4},{7,5},{4,6},{5,7},{10,8},{11,9},{8,1... | collective-permute-start | bytes 1572872 | tf_op jit(solution)/shard_map/ppermute | solution.py:351
  653.1 23.1 %collective-permute-start.85 = (bf16[256,1024]{1,0:T(8,128)(2,1)}, bf16[256,1024]{1,0:T(8,128)(2,1)}, u32[]{:S(2)}, u32[]{:S(2)}) collective-permute-start(bf16[256,1024]{1,0:T(8,128)(2,1)} %get-tuple-element.825), channel_id=1, source_target_pairs={{4,0},{8,4},{12,8},{0,12},{5,1},{9,5},{13,9},{1,13},{6,2},{10,6},{... | collective-permute-start | bytes 1572872 | tf_op jit(solution)/shard_map/ppermute | solution.py:632
  657.3 24.8 %collective-permute-start.86 = (bf16[256,1024]{1,0:T(8,128)(2,1)}, bf16[256,1024]{1,0:T(8,128)(2,1)}, u32[]{:S(2)}, u32[]{:S(2)}) collective-permute-start(bf16[256,1024]{1,0:T(8,128)(2,1)} %get-tuple-element.824), channel_id=1, source_target_pairs={{8,0},{12,4},{0,8},{4,12},{9,1},{13,5},{1,9},{5,13},{10,2},{14,6},... | collective-permute-start | bytes 1572872 | tf_op jit(solution)/shard_map/ppermute | solution.py:632
  670.6 19.7 %collective-permute-start.89 = (bf16[64,2048]{1,0:T(8,128)(2,1)}, bf16[64,2048]{1,0:T(8,128)(2,1)}, u32[]{:S(2)}, u32[]{:S(2)}) collective-permute-start(bf16[64,2048]{1,0:T(8,128)(2,1)} %broadcast_select_fusion.8), channel_id=1, source_target_pairs={{0,16},{16,0},{1,17},{17,1},{2,18},{18,2},{3,19},{19,3},{4,20},{20... | collective-permute-start | bytes 786440 | tf_op jit(solution)/shard_map/ppermute | solution.py:354
  (223 other events, 1582.8 us)
Sparse Core Ops, SparseCore 0:
  17.4 28.9 all-gather.6
  73.2 25.9 all-gather.8
  100.8 27.4 all-gather.10
  129.7 27.4 all-gather.12
  158.5 27.4 all-gather.14
  220.7 25.7 all-gather.16
  479.6 25.0 reduce-scatter.10
  507.1 25.8 reduce-scatter.8
  535.3 25.7 reduce-scatter.6
  579.4 24.9 reduce-scatter.16
  611.1 37.6 reduce-scatter.14
  686.1 26.6 reduce-scatter.12

commit v5 on v4

--- a/solution.py
+++ b/solution.py
@@ -454,7 +454,7 @@
         self.place = place
         self.at = jnp.stack([place.y, place.x, place.section]).astype(jnp.int32)
 
-    def product(self, x, grads, ready=None):
+    def product(self, x, grads, ready=None, sums=True):
         place = self.place
         nz, ny, nx = scatter_sizes(place)
         tokens = x.shape[0]
@@ -493,6 +493,9 @@
 
             @pl.when(pl.program_id(0) == 0)
             def _():
+                if not sums:
+                    sums_ref[...] = jnp.zeros_like(sums_ref)
+                    return
                 ones = jnp.ones((8, tokens), BF)
                 first = 0
                 for ref, wide in zip(grad_refs, widths):
@@ -930,7 +933,7 @@
 
         second = norm_rows_backward(terms, unit_two, inverse_two, gains[1:2], layer == 0)
         grad_ff, second_sums = second[:2]
-        out_parts, _ = scatter.product(activated, [grad_ff])
+        out_parts, _ = scatter.product(activated, [grad_ff], sums=False)
         if layer == 1:
             out_parts, grad_ff = tie(out_parts, grad_ff)
         else:

time: 735 us -> 735 us (level)
  transfers between devices with their start and end apart: 108 -> 108, of which waited for: 30 -> 31; matrix products, arithmetic and copies ran while one was open for 15% -> 15% of each run, Pallas kernels for 33% -> 33%
where the time goes in v5:
time: 735 us; the launch traced here: 725 us
  Pallas kernels  256 us (35%)
  local copies, waits for them, and re-layouts  138 us (19%)
  waiting for transfers between devices  135 us (18%)
  starting transfers between devices  112 us (15%)
  other arithmetic  45.7 us (6%)
  matrix products  19.7 us (3%)
  between operations  18.1 us (2%)
    unnamed x369, local copies, waits for them, and re-layouts  86.2 us
    pallas_call x14, Pallas kernels, row_product(): pl.pallas_call(body, grid=(rows // block,), in_specs=[pl.BlockSpec((block...  57.2 us
    pallas_call x2, Pallas kernels, attend_backward(): pl.pallas_call(lambda *refs: attend_backward_kernel(head_dim, *refs), gri...  54.5 us
    ppermute x25, waiting for transfers between devices, from_y(): return lax.ppermute(value, 'fsdp', pairs)  52.5 us
    pallas_call x6, Pallas kernels, product(): pl.pallas_call(body, grid_spec=pltpu.PrefetchScalarGridSpec(num_scalar_pr...  43.1 us
    pallas_call x2, Pallas kernels, attend_forward(): pl.pallas_call(lambda *refs: attend_forward_kernel(head_dim, *refs), grid...  29.7 us
    ppermute x25, starting transfers between devices, from_x(): return lax.ppermute(value, 'fsdp', pairs)  28.1 us
    ppermute x25, starting transfers between devices, from_y(): return lax.ppermute(value, 'fsdp', pairs)  27.4 us
  transfers between devices with their start and end apart: 108, of which 31 were waited for; matrix products, arithmetic and copies ran while one was open for 15% of the time, Pallas kernels for 33%

profile of v5, /device:TPU:0, one launch (start us, length us, event | category | flops | bytes accessed | tf_op | source)
XLA Modules:
  0.0 725.1 jit_solution(1249616990549005878)
XLA Ops:
  10.6 4.7 collective-permute-start.4
  23.3 3.8 dynamic-slice_reduce_fusion
  38.1 8.3 %all-gather.7.cloned.1.call-done = bf16[256,2048]{1,0:T(8,128)(2,1)} async-done(((bf16[64,2048]{1,0:T(8,128)(2,1)}), bf16[256,2048]{1,0:T(8,128)(2,1)}) %all-gather.7.cloned.1.call-update) | async-done | bytes 1048592 | tf_op jit(solution)/shard_map/all_gather | solution.py:378
  52.8 6.1 collective-permute-done.10
  58.9 10.7 %collective-permute-done.9 = bf16[128,1024]{1,0:T(8,128)(2,1)S(1)} collective-permute-done((bf16[128,1024]{1,0:T(8,128)(2,1)S(1)}, bf16[128,1024]{1,0:T(8,128)(2,1)S(1)}, u32[]{:S(2)}, u32[]{:S(2)}) %collective-permute-start.9) | collective-permute-done | bytes 262176 | tf_op jit(solution)/shard_map/ppermute | solution.py:612
  82.7 2.9 join_pieces.2
  86.9 6.3 collective-permute-done.11.refs_3_
  105.5 3.0 assemble.6
  116.1 3.9 project_qkv.2
  123.8 4.5 all-gather.11.cloned.1.call-done
  134.9 14.8 %attend_forward.2 = (bf16[1024,512]{1,0:T(8,128)(2,1)S(1)}, f32[4,2,1024]{2,1,0:T(2,128)S(1)}) custom-call(bf16[1024,512]{1,0:T(8,128)(2,1)S(1)} %copy-done.115, bf16[1024,512]{1,0:T(8,128)(2,1)S(1)} %copy-done.118, bf16[1024,512]{1,0:T(8,128)(2,1)S(1)} %copy-done.121, s32[1024,1]{1,0:T(8,128)S(1)} %get-tuple-element.433.refs_3_.refs_5_, ...), custom_call_target="tpu_custom_call" | custom-call | flops 3006477056 | bytes 1468006 | tf_op jit(solution)/shard_map/attend_forward/pallas_call | solution.py:124
  153.8 3.3 all-gather.13.cloned.1.call-done
  173.2 5.1 norm_forward.4
  180.5 4.5 collective-permute-done.22.refs_3_
  185.0 3.1 collective-permute-done.23.refs_4_
  196.9 3.2 assemble.7
  200.2 9.4 %fusion.4 = (bf16[1024,2048]{1,0:T(8,128)(2,1)}, bf16[1024,2048]{1,0:T(8,128)(2,1)S(1)}) fusion(f32[2048]{0:T(1024)S(1)} %bitcast.376, bf16[1024,1024]{1,0:T(8,128)(2,1)S(1)} %get-tuple-element.627.before_ref.x_ref, bf16[1024,2048]{1,0:T(8,128)(2,1)S(1)} %bitcast.286), kind=kOutput, calls=%fused_computation.6 | convolution fusion | flops 4320133120 | bytes 14688256 | tf_op jit(solution)/shard_map/dot_general | solution.py:34
  209.6 4.2 assemble.8
  213.7 5.1 feed_out.2.part_ref
  230.4 5.1 norm_forward.5
  237.6 20.5 %collective-permute-done.32.refs_3_ = bf16[4,64,1024]{2,1,0:T(8,128)(2,1)S(1)} collective-permute-done((bf16[4,64,1024]{2,1,0:T(8,128)(2,1)S(1)}, bf16[4,64,1024]{2,1,0:T(8,128)(2,1)S(1)}, u32[]{:S(2)}, u32[]{:S(2)}) %collective-permute-start.32) | collective-permute-done | bytes 524320 | tf_op jit(solution)/shard_map/ppermute | solution.py:351
  273.4 3.9 project_qkv.3
  277.3 14.9 %attend_forward.3 = (bf16[1024,512]{1,0:T(8,128)(2,1)S(1)}, f32[4,2,1024]{2,1,0:T(2,128)S(1)}) custom-call(bf16[1024,512]{1,0:T(8,128)(2,1)S(1)} %get-tuple-element.583.refs_0_, bf16[1024,512]{1,0:T(8,128)(2,1)S(1)} %get-tuple-element.584.refs_1_, bf16[1024,512]{1,0:T(8,128)(2,1)S(1)} %get-tuple-element.585.refs_2_, ...), custom_call_target="tpu_custom_call" | custom-call | flops 3006477056 | bytes 1468006 | tf_op jit(solution)/shard_map/attend_forward/pallas_call | solution.py:124
  293.2 2.9 project_out.3.part_ref
  299.6 2.9 collective-permute-start.43
  309.1 3.0 assemble.10
  312.1 5.5 norm_forward.6
  317.6 7.8 %fusion.9 = (bf16[1024,2048]{1,0:T(8,128)(2,1)S(1)}, bf16[1024,2048]{1,0:T(8,128)(2,1)S(1)}) fusion(f32[2048]{0:T(1024)S(1)} %bitcast.377, bf16[1024,1024]{1,0:T(8,128)(2,1)S(1)} %get-tuple-element.548.before_ref.x_ref, bf16[1024,2048]{1,0:T(8,128)(2,1)S(1)} %bitcast.288), kind=kOutput, calls=%fused_computation.11 | convolution fusion | flops 4320133120 | bytes 14688256 | tf_op jit(solution)/shard_map/dot_general | solution.py:34
  325.5 4.0 collective-permute-start.45
  329.6 3.0 assemble.11
  332.6 5.2 feed_out.3.part_ref
  339.2 4.9 collective-permute-done.46.other_ref
  344.9 4.0 norm_forward.7
  348.9 3.2 norm_backward.4
  352.1 7.0 weight_grad.6
  364.1 5.2 feed_out_back.2.refs_0_
  369.3 7.2 weight_grad.7
  376.5 5.2 feed_in_back.2.refs_1_
  384.6 5.0 collective-permute-start.53
  395.5 3.9 norm_backward.5
  403.8 27.3 %attend_backward.2 = (bf16[1024,512]{1,0:T(8,128)(2,1)S(1)}, bf16[1024,512]{1,0:T(8,128)(2,1)S(1)}, bf16[1024,512]{1,0:T(8,128)(2,1)S(1)}) custom-call(bf16[1024,512]{1,0:T(8,128)(2,1)S(1)} %copy-done.124, bf16[1024,512]{1,0:T(8,128)(2,1)S(1)} %copy-done.126, bf16[1024,512]{1,0:T(8,128)(2,1)S(1)} %copy-done.128, ...), custom_call_target="tpu_custom_call" | custom-call | flops 7516192768 | bytes 2936012 | tf_op jit(solution)/shard_map/attend_backward/pallas_call | solution.py:156
  434.6 6.6 weight_grad.8
  451.4 4.1 project_qkv_back.2.refs_1_
  459.7 4.2 norm_backward.6
  465.3 7.4 %weight_grad.9 = (bf16[4,2,128,512]{3,2,1,0:T(8,128)(2,1)S(1)}, bf16[4,2,128,512]{3,2,1,0:T(8,128)(2,1)}, bf16[4,2,128,512]{3,2,1,0:T(8,128)(2,1)S(1)}, bf16[4,2,128,512]{3,2,1,0:T(8,128)(2,1)}, f32[8,1024]{1,0:T(8,128)}) custom-call(s32[3]{0:T(128)S(1)} %pad_add_fusion.at_ref, bf16[1024,2048]{1,0:T(8,128)(2,1)S(1)} %copy-done.15, ...), custom_call_target="tpu_custom_call" | custom-call | flops 1503238528 | bytes 3670016 | tf_op jit(solution)/shard_map/weight_grad/pallas_call | solution.py:505
  483.3 5.2 feed_out_back.3.refs_0_
  488.5 6.0 feed_in_back.3.refs_1_
  494.5 7.9 %weight_grad.10 = (bf16[4,2,64,1024]{3,2,1,0:T(8,128)(2,1)S(1)}, bf16[4,2,64,1024]{3,2,1,0:T(8,128)(2,1)}, bf16[4,2,64,1024]{3,2,1,0:T(8,128)(2,1)S(1)}, bf16[4,2,64,1024]{3,2,1,0:T(8,128)(2,1)}, f32[8,2048]{1,0:T(8,128)S(1)}) custom-call(s32[3]{0:T(128)S(1)} %pad_add_fusion.at_ref, bf16[1024,1024]{1,0:T(8,128)(2,1)S(1)} %copy-done.27, ...), custom_call_target="tpu_custom_call" | custom-call | flops 1503238528 | bytes 3670016 | tf_op jit(solution)/shard_map/weight_grad/pallas_call | solution.py:505
  507.9 2.8 scatter_add.9
  512.6 5.4 norm_backward.7
  522.2 2.9 collective-permute-done.70
  536.7 3.9 scatter_add.8
  545.2 27.1 %attend_backward.3 = (bf16[1024,512]{1,0:T(8,128)(2,1)S(1)}, bf16[1024,512]{1,0:T(8,128)(2,1)S(1)}, bf16[1024,512]{1,0:T(8,128)(2,1)S(1)}) custom-call(bf16[1024,512]{1,0:T(8,128)(2,1)S(1)} %copy-done.116, bf16[1024,512]{1,0:T(8,128)(2,1)S(1)} %copy-done.119, bf16[1024,512]{1,0:T(8,128)(2,1)S(1)} %copy-done.122, bf16[1024,512]{1,0:T(8,128)(2,1)S(1)} %copy-done.87, ...), custom_call_target="tpu_custom_call" | custom-call | flops 7516192768 | bytes 2936012 | tf_op jit(solution)/shard_map/attend_backward/pallas_call | solution.py:156
  581.5 3.7 scatter_add.10
  592.3 7.0 weight_grad.11
  600.6 4.9 project_qkv_back.3
  618.6 5.0 add_convert_fusion
  623.6 15.0 %collective-permute-done.77.refs_1_ = bf16[4,2,64,1024]{3,2,1,0:T(8,128)(2,1)S(1)} collective-permute-done((bf16[4,2,64,1024]{3,2,1,0:T(8,128)(2,1)}, bf16[4,2,64,1024]{3,2,1,0:T(8,128)(2,1)S(1)}, u32[]{:S(2)}, u32[]{:S(2)}) %collective-permute-start.77) | collective-permute-done | bytes 1048608 | tf_op jit(solution)/shard_map/ppermute | solution.py:351
  652.7 4.2 collective-permute-start.85
  662.9 2.8 collective-permute-done.92
  665.7 4.1 collective-permute-start.87
  670.3 5.5 collective-permute-start.89
  675.9 5.9 collective-permute-done.86
  696.9 15.4 %reduce-scatter.13.cloned.1.call-done = bf16[64,2048]{1,0:T(8,128)(2,1)} async-done(((bf16[256,2048]{1,0:T(8,128)(2,1)}), bf16[64,2048]{1,0:T(8,128)(2,1)}) %reduce-scatter.13.cloned.1.call-update) | async-done | bytes 262160 | tf_op jit(solution)/shard_map/reduce_scatter | solution.py:580
  (771 shorter events, 291.6 us)
Async XLA Ops:
  7.2 39.3 %all-gather.7.cloned.1.call-start = ((), (), s32[]{:S(2)}) async-start(), calls=%async_computation.6 | async-start | bytes 1310720 | tf_op jit(solution)/shard_map/all_gather | solution.py:378
  10.6 20.2 %collective-permute-start.4 = (s32[256]{0:T(256)S(1)}, s32[256]{0:T(256)S(1)}, u32[]{:S(2)}, u32[]{:S(2)}) collective-permute-start(s32[256]{0:T(256)S(1)} %bitcast.387), channel_id=1, source_target_pairs={{0,12},{4,0},{8,4},{12,8},{1,13},{5,1},{9,5},{13,9},{2,14},{6,2},{... | collective-permute-start | bytes 3080 | tf_op jit(solution)/shard_map/ppermute | solution.py:612
  17.3 81.9 %all-gather.9.cloned.1.call-start = ((), (), s32[]{:S(2)}) async-start(), calls=%async_computation.7 | async-start | bytes 1310720 | tf_op jit(solution)/shard_map/all_gather | solution.py:378
  46.5 25.4 %collective-permute-start.7 = (bf16[4,64,2048]{2,1,0:T(8,128)(2,1)}, bf16[4,64,2048]{2,1,0:T(8,128)(2,1)}, u32[]{:S(2)}, u32[]{:S(2)}) collective-permute-start(bf16[4,64,2048]{2,1,0:T(8,128)(2,1)} %bitcast.301), channel_id=1, source_target_pairs={{1,0},{0,1},{3,2},{2,3},{5,4},{4,5},{7,6},{6,7},{9,8},{8,9},{11,10... | collective-permute-start | bytes 3145736 | tf_op jit(solution)/shard_map/ppermute | solution.py:344
  47.9 25.2 %collective-permute-start.8 = (bf16[4,64,2048]{2,1,0:T(8,128)(2,1)}, bf16[4,64,2048]{2,1,0:T(8,128)(2,1)}, u32[]{:S(2)}, u32[]{:S(2)}) collective-permute-start(bf16[4,64,2048]{2,1,0:T(8,128)(2,1)} %bitcast.302), channel_id=1, source_target_pairs={{2,0},{3,1},{0,2},{1,3},{6,4},{7,5},{4,6},{5,7},{10,8},{11,9},{8,1... | collective-permute-start | bytes 3145736 | tf_op jit(solution)/shard_map/ppermute | solution.py:351
  73.1 55.1 %all-gather.11.cloned.1.call-start = ((), (), s32[]{:S(2)}) async-start(), calls=%async_computation.8 | async-start | bytes 1310720 | tf_op jit(solution)/shard_map/all_gather | solution.py:378
  73.9 83.3 %all-gather.13.cloned.1.call-start = ((), (), s32[]{:S(2)}) async-start(), calls=%async_computation.9 | async-start | bytes 1310720 | tf_op jit(solution)/shard_map/all_gather | solution.py:378
  99.2 29.0 %collective-permute-start.16 = (bf16[4,64,2048]{2,1,0:T(8,128)(2,1)}, bf16[4,64,2048]{2,1,0:T(8,128)(2,1)}, u32[]{:S(2)}, u32[]{:S(2)}) collective-permute-start(bf16[4,64,2048]{2,1,0:T(8,128)(2,1)} %bitcast.307), channel_id=1, source_target_pairs={{1,0},{0,1},{3,2},{2,3},{5,4},{4,5},{7,6},{6,7},{9,8},{8,9},{11,10... | collective-permute-start | bytes 3145736 | tf_op jit(solution)/shard_map/ppermute | solution.py:344
  100.7 27.6 %collective-permute-start.17 = (bf16[4,64,2048]{2,1,0:T(8,128)(2,1)}, bf16[4,64,2048]{2,1,0:T(8,128)(2,1)}, u32[]{:S(2)}, u32[]{:S(2)}) collective-permute-start(bf16[4,64,2048]{2,1,0:T(8,128)(2,1)} %bitcast.308), channel_id=1, source_target_pairs={{2,0},{3,1},{0,2},{1,3},{6,4},{7,5},{4,6},{5,7},{10,8},{11,9},{8,1... | collective-permute-start | bytes 3145736 | tf_op jit(solution)/shard_map/ppermute | solution.py:351
  112.0 76.0 %all-gather.15.cloned.1.call-start = ((), (), s32[]{:S(2)}) async-start(), calls=%async_computation.10 | async-start | bytes 1310720 | tf_op jit(solution)/shard_map/all_gather | solution.py:378
  128.2 28.9 %collective-permute-start.18 = (bf16[4,128,1024]{2,1,0:T(8,128)(2,1)}, bf16[4,128,1024]{2,1,0:T(8,128)(2,1)}, u32[]{:S(2)}, u32[]{:S(2)}) collective-permute-start(bf16[4,128,1024]{2,1,0:T(8,128)(2,1)} %bitcast.304), channel_id=1, source_target_pairs={{1,0},{0,1},{3,2},{2,3},{5,4},{4,5},{7,6},{6,7},{9,8},{8,9},{11,10... | collective-permute-start | bytes 3145736 | tf_op jit(solution)/shard_map/ppermute | solution.py:344
  129.7 27.4 %collective-permute-start.19 = (bf16[4,128,1024]{2,1,0:T(8,128)(2,1)}, bf16[4,128,1024]{2,1,0:T(8,128)(2,1)}, u32[]{:S(2)}, u32[]{:S(2)}) collective-permute-start(bf16[4,128,1024]{2,1,0:T(8,128)(2,1)} %bitcast.305), channel_id=1, source_target_pairs={{2,0},{3,1},{0,2},{1,3},{6,4},{7,5},{4,6},{5,7},{10,8},{11,9},{8,1... | collective-permute-start | bytes 3145736 | tf_op jit(solution)/shard_map/ppermute | solution.py:351
  157.2 102.5 %all-gather.17.cloned.1.call-start = ((), (), s32[]{:S(2)}) async-start(), calls=%async_computation.11 | async-start | bytes 1310720 | tf_op jit(solution)/shard_map/all_gather | solution.py:378
  159.1 21.4 %collective-permute-start.20 = (bf16[4,64,1024]{2,1,0:T(8,128)(2,1)}, bf16[4,64,1024]{2,1,0:T(8,128)(2,1)}, u32[]{:S(2)}, u32[]{:S(2)}) collective-permute-start(bf16[4,64,1024]{2,1,0:T(8,128)(2,1)} %slice.291), channel_id=1, source_target_pairs={{2,0},{3,1},{0,2},{1,3},{6,4},{7,5},{4,6},{5,7},{10,8},{11,9},{8,1... | collective-permute-start | bytes 1572872 | tf_op jit(solution)/shard_map/ppermute | solution.py:351
  165.8 19.2 %collective-permute-start.22 = (bf16[4,128,512]{2,1,0:T(8,128)(2,1)}, bf16[4,128,512]{2,1,0:T(8,128)(2,1)}, u32[]{:S(2)}, u32[]{:S(2)}) collective-permute-start(bf16[4,128,512]{2,1,0:T(8,128)(2,1)} %slice.293), channel_id=1, source_target_pairs={{2,0},{3,1},{0,2},{1,3},{6,4},{7,5},{4,6},{5,7},{10,8},{11,9},{8,1... | collective-permute-start | bytes 1572872 | tf_op jit(solution)/shard_map/ppermute | solution.py:351
  168.2 19.9 %collective-permute-start.23 = (bf16[4,128,512]{2,1,0:T(8,128)(2,1)}, bf16[4,128,512]{2,1,0:T(8,128)(2,1)}, u32[]{:S(2)}, u32[]{:S(2)}) collective-permute-start(bf16[4,128,512]{2,1,0:T(8,128)(2,1)} %slice.294), channel_id=1, source_target_pairs={{1,0},{0,1},{3,2},{2,3},{5,4},{4,5},{7,6},{6,7},{9,8},{8,9},{11,10... | collective-permute-start | bytes 1572872 | tf_op jit(solution)/shard_map/ppermute | solution.py:344
  188.1 30.9 %collective-permute-start.25 = (bf16[4,64,2048]{2,1,0:T(8,128)(2,1)}, bf16[4,64,2048]{2,1,0:T(8,128)(2,1)S(1)}, u32[]{:S(2)}, u32[]{:S(2)}) collective-permute-start(bf16[4,64,2048]{2,1,0:T(8,128)(2,1)} %bitcast.310), channel_id=1, source_target_pairs={{1,0},{0,1},{3,2},{2,3},{5,4},{4,5},{7,6},{6,7},{9,8},{8,9},{11,10... | collective-permute-start | bytes 3145736 | tf_op jit(solution)/shard_map/ppermute | solution.py:344
  189.5 29.5 %collective-permute-start.26 = (bf16[4,64,2048]{2,1,0:T(8,128)(2,1)}, bf16[4,64,2048]{2,1,0:T(8,128)(2,1)S(1)}, u32[]{:S(2)}, u32[]{:S(2)}) collective-permute-start(bf16[4,64,2048]{2,1,0:T(8,128)(2,1)} %bitcast.311), channel_id=1, source_target_pairs={{2,0},{3,1},{0,2},{1,3},{6,4},{7,5},{4,6},{5,7},{10,8},{11,9},{8,1... | collective-permute-start | bytes 3145736 | tf_op jit(solution)/shard_map/ppermute | solution.py:351
  192.1 26.8 %collective-permute-start.27 = (bf16[128,1024]{1,0:T(8,128)(2,1)S(1)}, bf16[128,1024]{1,0:T(8,128)(2,1)S(1)}, u32[]{:S(2)}, u32[]{:S(2)}) collective-permute-start(bf16[128,1024]{1,0:T(8,128)(2,1)S(1)} %get-tuple-element.850), channel_id=1, source_target_pairs={{0,4},{4,8},{8,12},{12,0},{1,5},{5,9},{9,13},{13,1},{2,6},{6,10},{... | collective-permute-start | bytes 786440 | tf_op jit(solution)/shard_map/ppermute | solution.py:612
  193.5 25.4 %collective-permute-start.28 = (bf16[128,1024]{1,0:T(8,128)(2,1)S(1)}, bf16[128,1024]{1,0:T(8,128)(2,1)S(1)}, u32[]{:S(2)}, u32[]{:S(2)}) collective-permute-start(bf16[128,1024]{1,0:T(8,128)(2,1)S(1)} %get-tuple-element.849), channel_id=1, source_target_pairs={{0,8},{4,12},{8,0},{12,4},{1,9},{5,13},{9,1},{13,5},{2,10},{6,14},... | collective-permute-start | bytes 786440 | tf_op jit(solution)/shard_map/ppermute | solution.py:612
  194.5 24.4 %collective-permute-start.29 = (bf16[128,1024]{1,0:T(8,128)(2,1)S(1)}, bf16[128,1024]{1,0:T(8,128)(2,1)S(1)}, u32[]{:S(2)}, u32[]{:S(2)}) collective-permute-start(bf16[128,1024]{1,0:T(8,128)(2,1)S(1)} %get-tuple-element.848), channel_id=1, source_target_pairs={{0,12},{4,0},{8,4},{12,8},{1,13},{5,1},{9,5},{13,9},{2,14},{6,2},{... | collective-permute-start | bytes 786440 | tf_op jit(solution)/shard_map/ppermute | solution.py:612
  220.5 354.8 %reduce-scatter.11.cloned.1.call-start = ((), (), s32[]{:S(2)}) async-start(), calls=%async_computation.14 | async-start | bytes 1310720 | tf_op jit(solution)/shard_map/reduce_scatter | solution.py:580
  220.8 38.9 %collective-permute-start.30 = (bf16[4,64,2048]{2,1,0:T(8,128)(2,1)}, bf16[4,64,2048]{2,1,0:T(8,128)(2,1)}, u32[]{:S(2)}, u32[]{:S(2)}) collective-permute-start(bf16[4,64,2048]{2,1,0:T(8,128)(2,1)} %bitcast.298), channel_id=1, source_target_pairs={{1,0},{0,1},{3,2},{2,3},{5,4},{4,5},{7,6},{6,7},{9,8},{8,9},{11,10... | collective-permute-start | bytes 3145736 | tf_op jit(solution)/shard_map/ppermute | solution.py:344
  221.4 38.3 %collective-permute-start.31 = (bf16[4,64,2048]{2,1,0:T(8,128)(2,1)}, bf16[4,64,2048]{2,1,0:T(8,128)(2,1)}, u32[]{:S(2)}, u32[]{:S(2)}) collective-permute-start(bf16[4,64,2048]{2,1,0:T(8,128)(2,1)} %bitcast.299), channel_id=1, source_target_pairs={{2,0},{3,1},{0,2},{1,3},{6,4},{7,5},{4,6},{5,7},{10,8},{11,9},{8,1... | collective-permute-start | bytes 3145736 | tf_op jit(solution)/shard_map/ppermute | solution.py:351
  223.9 34.2 %collective-permute-start.32 = (bf16[4,64,1024]{2,1,0:T(8,128)(2,1)S(1)}, bf16[4,64,1024]{2,1,0:T(8,128)(2,1)S(1)}, u32[]{:S(2)}, u32[]{:S(2)}) collective-permute-start(bf16[4,64,1024]{2,1,0:T(8,128)(2,1)S(1)} %slice.299), channel_id=1, source_target_pairs={{2,0},{3,1},{0,2},{1,3},{6,4},{7,5},{4,6},{5,7},{10,8},{11,9},{8,1... | collective-permute-start | bytes 1572872 | tf_op jit(solution)/shard_map/ppermute | solution.py:351
  225.6 33.3 %collective-permute-start.33 = (bf16[4,64,1024]{2,1,0:T(8,128)(2,1)S(1)}, bf16[4,64,1024]{2,1,0:T(8,128)(2,1)S(1)}, u32[]{:S(2)}, u32[]{:S(2)}) collective-permute-start(bf16[4,64,1024]{2,1,0:T(8,128)(2,1)S(1)} %slice.300), channel_id=1, source_target_pairs={{1,0},{0,1},{3,2},{2,3},{5,4},{4,5},{7,6},{6,7},{9,8},{8,9},{11,10... | collective-permute-start | bytes 1572872 | tf_op jit(solution)/shard_map/ppermute | solution.py:344
  259.7 38.8 %collective-permute-start.35 = (bf16[4,128,1024]{2,1,0:T(8,128)(2,1)}, bf16[4,128,1024]{2,1,0:T(8,128)(2,1)}, u32[]{:S(2)}, u32[]{:S(2)}) collective-permute-start(bf16[4,128,1024]{2,1,0:T(8,128)(2,1)} %bitcast.313), channel_id=1, source_target_pairs={{1,0},{0,1},{3,2},{2,3},{5,4},{4,5},{7,6},{6,7},{9,8},{8,9},{11,10... | collective-permute-start | bytes 3145736 | tf_op jit(solution)/shard_map/ppermute | solution.py:344
  261.3 37.3 %collective-permute-start.36 = (bf16[4,128,1024]{2,1,0:T(8,128)(2,1)}, bf16[4,128,1024]{2,1,0:T(8,128)(2,1)}, u32[]{:S(2)}, u32[]{:S(2)}) collective-permute-start(bf16[4,128,1024]{2,1,0:T(8,128)(2,1)} %bitcast.314), channel_id=1, source_target_pairs={{2,0},{3,1},{0,2},{1,3},{6,4},{7,5},{4,6},{5,7},{10,8},{11,9},{8,1... | collective-permute-start | bytes 3145736 | tf_op jit(solution)/shard_map/ppermute | solution.py:351
  269.5 22.8 %collective-permute-start.39 = (bf16[512,512]{1,0:T(8,128)(2,1)S(1)}, bf16[512,512]{1,0:T(8,128)(2,1)S(1)}, u32[]{:S(2)}, u32[]{:S(2)}) collective-permute-start(bf16[512,512]{1,0:T(8,128)(2,1)S(1)} %constant_dynamic-slice_fusion.11), channel_id=1, source_target_pairs={{0,16},{16,0},{1,17},{17,1},{2,18},{18,2},{3,19},{19,3},{4,20},{20... | collective-permute-start | bytes 1572872 | tf_op jit(solution)/shard_map/ppermute | solution.py:354
  271.0 25.9 %collective-permute-start.37 = (bf16[4,64,1024]{2,1,0:T(8,128)(2,1)S(1)}, bf16[4,64,1024]{2,1,0:T(8,128)(2,1)S(1)}, u32[]{:S(2)}, u32[]{:S(2)}) collective-permute-start(bf16[4,64,1024]{2,1,0:T(8,128)(2,1)S(1)} %slice.304), channel_id=1, source_target_pairs={{2,0},{3,1},{0,2},{1,3},{6,4},{7,5},{4,6},{5,7},{10,8},{11,9},{8,1... | collective-permute-start | bytes 1572872 | tf_op jit(solution)/shard_map/ppermute | solution.py:351
  272.7 25.0 %collective-permute-start.38 = (bf16[4,64,1024]{2,1,0:T(8,128)(2,1)S(1)}, bf16[4,64,1024]{2,1,0:T(8,128)(2,1)S(1)}, u32[]{:S(2)}, u32[]{:S(2)}) collective-permute-start(bf16[4,64,1024]{2,1,0:T(8,128)(2,1)S(1)} %slice.305), channel_id=1, source_target_pairs={{1,0},{0,1},{3,2},{2,3},{5,4},{4,5},{7,6},{6,7},{9,8},{8,9},{11,10... | collective-permute-start | bytes 1572872 | tf_op jit(solution)/shard_map/ppermute | solution.py:344
  299.6 25.8 %collective-permute-start.43 = (bf16[256,1024]{1,0:T(8,128)(2,1)S(1)}, bf16[256,1024]{1,0:T(8,128)(2,1)S(1)}, u32[]{:S(2)}, u32[]{:S(2)}) collective-permute-start(bf16[256,1024]{1,0:T(8,128)(2,1)S(1)} %get-tuple-element.836), channel_id=1, source_target_pairs={{4,0},{8,4},{12,8},{0,12},{5,1},{9,5},{13,9},{1,13},{6,2},{10,6},{... | collective-permute-start | bytes 1572872 | tf_op jit(solution)/shard_map/ppermute | solution.py:635
  302.5 22.9 %collective-permute-start.44 = (bf16[256,1024]{1,0:T(8,128)(2,1)S(1)}, bf16[256,1024]{1,0:T(8,128)(2,1)S(1)}, u32[]{:S(2)}, u32[]{:S(2)}) collective-permute-start(bf16[256,1024]{1,0:T(8,128)(2,1)S(1)} %get-tuple-element.835), channel_id=1, source_target_pairs={{8,0},{12,4},{0,8},{4,12},{9,1},{13,5},{1,9},{5,13},{10,2},{14,6},... | collective-permute-start | bytes 1572872 | tf_op jit(solution)/shard_map/ppermute | solution.py:635
  305.6 19.8 %collective-permute-start.40 = (bf16[4,128,512]{2,1,0:T(8,128)(2,1)S(1)}, bf16[4,128,512]{2,1,0:T(8,128)(2,1)S(1)}, u32[]{:S(2)}, u32[]{:S(2)}) collective-permute-start(bf16[4,128,512]{2,1,0:T(8,128)(2,1)S(1)} %slice.308), channel_id=1, source_target_pairs={{2,0},{3,1},{0,2},{1,3},{6,4},{7,5},{4,6},{5,7},{10,8},{11,9},{8,1... | collective-permute-start | bytes 1572872 | tf_op jit(solution)/shard_map/ppermute | solution.py:351
  359.1 25.2 %collective-permute-start.48 = (bf16[4,2,128,512]{3,2,1,0:T(8,128)(2,1)S(1)}, bf16[4,2,128,512]{3,2,1,0:T(8,128)(2,1)S(1)}, u32[]{:S(2)}, u32[]{:S(2)}) collective-permute-start(bf16[4,2,128,512]{3,2,1,0:T(8,128)(2,1)S(1)} %get-tuple-element.563), channel_id=1, source_target_pairs={{2,0},{3,1},{0,2},{1,3},{6,4},{7,5},{4,6},{5,7},{10,8},{11,9},{8,1... | collective-permute-start | bytes 3145736 | tf_op jit(solution)/shard_map/ppermute | solution.py:351
  359.6 24.9 %collective-permute-start.49 = (bf16[4,2,128,512]{3,2,1,0:T(8,128)(2,1)S(1)}, bf16[4,2,128,512]{3,2,1,0:T(8,128)(2,1)S(1)}, u32[]{:S(2)}, u32[]{:S(2)}) collective-permute-start(bf16[4,2,128,512]{3,2,1,0:T(8,128)(2,1)S(1)} %get-tuple-element.565), channel_id=1, source_target_pairs={{1,0},{0,1},{3,2},{2,3},{5,4},{4,5},{7,6},{6,7},{9,8},{8,9},{11,10... | collective-permute-start | bytes 3145736 | tf_op jit(solution)/shard_map/ppermute | solution.py:344
  362.0 19.7 %collective-permute-start.50 = (bf16[256,1024]{1,0:T(8,128)(2,1)S(1)}, bf16[256,1024]{1,0:T(8,128)(2,1)S(1)}, u32[]{:S(2)}, u32[]{:S(2)}) collective-permute-start(bf16[256,1024]{1,0:T(8,128)(2,1)S(1)} %get-tuple-element.833), channel_id=1, source_target_pairs={{20,16},{24,20},{28,24},{16,28},{21,17},{25,21},{29,25},{17,29},{2... | collective-permute-start | bytes 1572872 | tf_op jit(solution)/shard_map/ppermute | solution.py:635
  391.4 39.8 %collective-permute-start.54 = (bf16[4,128,512]{2,1,0:T(8,128)(2,1)S(1)}, bf16[4,128,512]{2,1,0:T(8,128)(2,1)S(1)}, u32[]{:S(2)}, u32[]{:S(2)}) collective-permute-start(bf16[4,128,512]{2,1,0:T(8,128)(2,1)S(1)} %get-tuple-element.576), channel_id=1, source_target_pairs={{1,0},{0,1},{3,2},{2,3},{5,4},{4,5},{7,6},{6,7},{9,8},{8,9},{11,10... | collective-permute-start | bytes 1572872 | tf_op jit(solution)/shard_map/ppermute | solution.py:344
  392.1 39.1 %collective-permute-start.55 = (bf16[4,128,512]{2,1,0:T(8,128)(2,1)S(1)}, bf16[4,128,512]{2,1,0:T(8,128)(2,1)S(1)}, u32[]{:S(2)}, u32[]{:S(2)}) collective-permute-start(bf16[4,128,512]{2,1,0:T(8,128)(2,1)S(1)} %get-tuple-element.578), channel_id=1, source_target_pairs={{2,0},{3,1},{0,2},{1,3},{6,4},{7,5},{4,6},{5,7},{10,8},{11,9},{8,1... | collective-permute-start | bytes 1572872 | tf_op jit(solution)/shard_map/ppermute | solution.py:351
  393.6 37.6 %collective-permute-start.56 = (bf16[4,2,64,1024]{3,2,1,0:T(8,128)(2,1)S(1)}, bf16[4,2,64,1024]{3,2,1,0:T(8,128)(2,1)S(1)}, u32[]{:S(2)}, u32[]{:S(2)}) collective-permute-start(bf16[4,2,64,1024]{3,2,1,0:T(8,128)(2,1)S(1)} %get-tuple-element.580), channel_id=1, source_target_pairs={{2,0},{3,1},{0,2},{1,3},{6,4},{7,5},{4,6},{5,7},{10,8},{11,9},{8,1... | collective-permute-start | bytes 3145736 | tf_op jit(solution)/shard_map/ppermute | solution.py:351
  394.1 37.1 %collective-permute-start.57 = (bf16[4,2,64,1024]{3,2,1,0:T(8,128)(2,1)S(1)}, bf16[4,2,64,1024]{3,2,1,0:T(8,128)(2,1)S(1)}, u32[]{:S(2)}, u32[]{:S(2)}) collective-permute-start(bf16[4,2,64,1024]{3,2,1,0:T(8,128)(2,1)S(1)} %get-tuple-element.582), channel_id=1, source_target_pairs={{1,0},{0,1},{3,2},{2,3},{5,4},{4,5},{7,6},{6,7},{9,8},{8,9},{11,10... | collective-permute-start | bytes 3145736 | tf_op jit(solution)/shard_map/ppermute | solution.py:344
  400.8 30.4 %collective-permute-start.58 = (bf16[512,512]{1,0:T(8,128)(2,1)S(1)}, bf16[512,512]{1,0:T(8,128)(2,1)S(1)}, u32[]{:S(2)}, u32[]{:S(2)}) collective-permute-start(bf16[512,512]{1,0:T(8,128)(2,1)S(1)} %get-tuple-element.846), channel_id=1, source_target_pairs={{0,16},{16,0},{1,17},{17,1},{2,18},{18,2},{3,19},{19,3},{4,20},{20... | collective-permute-start | bytes 1572872 | tf_op jit(solution)/shard_map/ppermute | solution.py:354
  455.7 49.3 %collective-permute-start.64 = (bf16[4,2,64,1024]{3,2,1,0:T(8,128)(2,1)}, bf16[4,2,64,1024]{3,2,1,0:T(8,128)(2,1)}, u32[]{:S(2)}, u32[]{:S(2)}) collective-permute-start(bf16[4,2,64,1024]{3,2,1,0:T(8,128)(2,1)} %get-tuple-element.637), channel_id=1, source_target_pairs={{2,0},{3,1},{0,2},{1,3},{6,4},{7,5},{4,6},{5,7},{10,8},{11,9},{8,1... | collective-permute-start | bytes 3145736 | tf_op jit(solution)/shard_map/ppermute | solution.py:351
  457.3 47.8 %collective-permute-start.65 = (bf16[4,2,64,1024]{3,2,1,0:T(8,128)(2,1)}, bf16[4,2,64,1024]{3,2,1,0:T(8,128)(2,1)}, u32[]{:S(2)}, u32[]{:S(2)}) collective-permute-start(bf16[4,2,64,1024]{3,2,1,0:T(8,128)(2,1)} %get-tuple-element.639), channel_id=1, source_target_pairs={{1,0},{0,1},{3,2},{2,3},{5,4},{4,5},{7,6},{6,7},{9,8},{8,9},{11,10... | collective-permute-start | bytes 3145736 | tf_op jit(solution)/shard_map/ppermute | solution.py:344
  474.7 30.4 %collective-permute-start.62 = (bf16[4,2,128,512]{3,2,1,0:T(8,128)(2,1)}, bf16[4,2,128,512]{3,2,1,0:T(8,128)(2,1)}, u32[]{:S(2)}, u32[]{:S(2)}) collective-permute-start(bf16[4,2,128,512]{3,2,1,0:T(8,128)(2,1)} %get-tuple-element.633), channel_id=1, source_target_pairs={{2,0},{3,1},{0,2},{1,3},{6,4},{7,5},{4,6},{5,7},{10,8},{11,9},{8,1... | collective-permute-start | bytes 3145736 | tf_op jit(solution)/shard_map/ppermute | solution.py:351
  476.1 29.2 %collective-permute-start.63 = (bf16[4,2,128,512]{3,2,1,0:T(8,128)(2,1)}, bf16[4,2,128,512]{3,2,1,0:T(8,128)(2,1)}, u32[]{:S(2)}, u32[]{:S(2)}) collective-permute-start(bf16[4,2,128,512]{3,2,1,0:T(8,128)(2,1)} %get-tuple-element.635), channel_id=1, source_target_pairs={{1,0},{0,1},{3,2},{2,3},{5,4},{4,5},{7,6},{6,7},{9,8},{8,9},{11,10... | collective-permute-start | bytes 3145736 | tf_op jit(solution)/shard_map/ppermute | solution.py:344
  478.7 96.6 %reduce-scatter.9.cloned.1.call-start = ((), (), s32[]{:S(2)}) async-start(), calls=%async_computation.13 | async-start | bytes 1310720 | tf_op jit(solution)/shard_map/reduce_scatter | solution.py:580
  505.3 70.1 %reduce-scatter.7.cloned.1.call-start = ((), (), s32[]{:S(2)}) async-start(), calls=%async_computation.12 | async-start | bytes 1310720 | tf_op jit(solution)/shard_map/reduce_scatter | solution.py:580
  527.6 83.8 %reduce-scatter.17.cloned.1.call-start = ((), (), s32[]{:S(2)}) async-start(), calls=%async_computation.17 | async-start | bytes 1310720 | tf_op jit(solution)/shard_map/reduce_scatter | solution.py:580
  532.7 42.6 %collective-permute-start.68 = (bf16[4,2,64,1024]{3,2,1,0:T(8,128)(2,1)}, bf16[4,2,64,1024]{3,2,1,0:T(8,128)(2,1)}, u32[]{:S(2)}, u32[]{:S(2)}) collective-permute-start(bf16[4,2,64,1024]{3,2,1,0:T(8,128)(2,1)} %get-tuple-element.653), channel_id=1, source_target_pairs={{2,0},{3,1},{0,2},{1,3},{6,4},{7,5},{4,6},{5,7},{10,8},{11,9},{8,1... | collective-permute-start | bytes 3145736 | tf_op jit(solution)/shard_map/ppermute | solution.py:351
  533.3 42.0 %collective-permute-start.69 = (bf16[4,2,64,1024]{3,2,1,0:T(8,128)(2,1)}, bf16[4,2,64,1024]{3,2,1,0:T(8,128)(2,1)}, u32[]{:S(2)}, u32[]{:S(2)}) collective-permute-start(bf16[4,2,64,1024]{3,2,1,0:T(8,128)(2,1)} %get-tuple-element.655), channel_id=1, source_target_pairs={{1,0},{0,1},{3,2},{2,3},{5,4},{4,5},{7,6},{6,7},{9,8},{8,9},{11,10... | collective-permute-start | bytes 3145736 | tf_op jit(solution)/shard_map/ppermute | solution.py:344
  542.2 33.2 %collective-permute-start.66 = (bf16[4,128,512]{2,1,0:T(8,128)(2,1)}, bf16[4,128,512]{2,1,0:T(8,128)(2,1)S(1)}, u32[]{:S(2)}, u32[]{:S(2)}) collective-permute-start(bf16[4,128,512]{2,1,0:T(8,128)(2,1)} %get-tuple-element.649), channel_id=1, source_target_pairs={{1,0},{0,1},{3,2},{2,3},{5,4},{4,5},{7,6},{6,7},{9,8},{8,9},{11,10... | collective-permute-start | bytes 1572872 | tf_op jit(solution)/shard_map/ppermute | solution.py:344
  543.4 31.9 %collective-permute-start.67 = (bf16[4,128,512]{2,1,0:T(8,128)(2,1)}, bf16[4,128,512]{2,1,0:T(8,128)(2,1)S(1)}, u32[]{:S(2)}, u32[]{:S(2)}) collective-permute-start(bf16[4,128,512]{2,1,0:T(8,128)(2,1)} %get-tuple-element.651), channel_id=1, source_target_pairs={{2,0},{3,1},{0,2},{1,3},{6,4},{7,5},{4,6},{5,7},{10,8},{11,9},{8,1... | collective-permute-start | bytes 1572872 | tf_op jit(solution)/shard_map/ppermute | solution.py:351
  544.9 30.5 %collective-permute-start.73 = (bf16[512,512]{1,0:T(8,128)(2,1)}, bf16[512,512]{1,0:T(8,128)(2,1)}, u32[]{:S(2)}, u32[]{:S(2)}) collective-permute-start(bf16[512,512]{1,0:T(8,128)(2,1)} %get-tuple-element.678), channel_id=1, source_target_pairs={{0,16},{16,0},{1,17},{17,1},{2,18},{18,2},{3,19},{19,3},{4,20},{20... | collective-permute-start | bytes 1572872 | tf_op jit(solution)/shard_map/ppermute | solution.py:354
  579.0 80.3 %reduce-scatter.15.cloned.1.call-start = ((), (), s32[]{:S(2)}) async-start(), calls=%async_computation.16 | async-start | bytes 1310720 | tf_op jit(solution)/shard_map/reduce_scatter | solution.py:580
  610.4 102.0 %reduce-scatter.13.cloned.1.call-start = ((), (), s32[]{:S(2)}) async-start(), calls=%async_computation.15 | async-start | bytes 1310720 | tf_op jit(solution)/shard_map/reduce_scatter | solution.py:580
  614.5 24.1 %collective-permute-start.77 = (bf16[4,2,64,1024]{3,2,1,0:T(8,128)(2,1)}, bf16[4,2,64,1024]{3,2,1,0:T(8,128)(2,1)S(1)}, u32[]{:S(2)}, u32[]{:S(2)}) collective-permute-start(bf16[4,2,64,1024]{3,2,1,0:T(8,128)(2,1)} %copy-done.130), channel_id=1, source_target_pairs={{2,0},{3,1},{0,2},{1,3},{6,4},{7,5},{4,6},{5,7},{10,8},{11,9},{8,1... | collective-permute-start | bytes 3145736 | tf_op jit(solution)/shard_map/ppermute | solution.py:351
  615.2 24.4 %collective-permute-start.78 = (bf16[4,2,64,1024]{3,2,1,0:T(8,128)(2,1)}, bf16[4,2,64,1024]{3,2,1,0:T(8,128)(2,1)S(1)}, u32[]{:S(2)}, u32[]{:S(2)}) collective-permute-start(bf16[4,2,64,1024]{3,2,1,0:T(8,128)(2,1)} %copy-done.129), channel_id=1, source_target_pairs={{1,0},{0,1},{3,2},{2,3},{5,4},{4,5},{7,6},{6,7},{9,8},{8,9},{11,10... | collective-permute-start | bytes 3145736 | tf_op jit(solution)/shard_map/ppermute | solution.py:344
  640.7 21.1 %collective-permute-start.91 = (f32[4,2,776]{2,1,0:T(2,128)S(1)}, f32[4,2,776]{2,1,0:T(2,128)S(1)}, u32[]{:S(2)}, u32[]{:S(2)}) collective-permute-start(f32[4,2,776]{2,1,0:T(2,128)S(1)} %dynamic-slice_bitcast_fusion.33), channel_id=1, source_target_pairs={{2,0},{3,1},{0,2},{1,3},{6,4},{7,5},{4,6},{5,7},{10,8},{11,9},{8,1... | collective-permute-start | bytes 74504 | tf_op jit(solution)/shard_map/ppermute | solution.py:351
  649.0 21.3 %collective-permute-start.83 = (bf16[4,64,1024]{2,1,0:T(8,128)(2,1)}, bf16[4,64,1024]{2,1,0:T(8,128)(2,1)}, u32[]{:S(2)}, u32[]{:S(2)}) collective-permute-start(bf16[4,64,1024]{2,1,0:T(8,128)(2,1)} %get-tuple-element.755), channel_id=1, source_target_pairs={{1,0},{0,1},{3,2},{2,3},{5,4},{4,5},{7,6},{6,7},{9,8},{8,9},{11,10... | collective-permute-start | bytes 1572872 | tf_op jit(solution)/shard_map/ppermute | solution.py:344
  650.7 25.1 %collective-permute-start.84 = (bf16[4,64,1024]{2,1,0:T(8,128)(2,1)}, bf16[4,64,1024]{2,1,0:T(8,128)(2,1)}, u32[]{:S(2)}, u32[]{:S(2)}) collective-permute-start(bf16[4,64,1024]{2,1,0:T(8,128)(2,1)} %get-tuple-element.757), channel_id=1, source_target_pairs={{2,0},{3,1},{0,2},{1,3},{6,4},{7,5},{4,6},{5,7},{10,8},{11,9},{8,1... | collective-permute-start | bytes 1572872 | tf_op jit(solution)/shard_map/ppermute | solution.py:351
  652.7 23.1 %collective-permute-start.85 = (bf16[256,1024]{1,0:T(8,128)(2,1)}, bf16[256,1024]{1,0:T(8,128)(2,1)}, u32[]{:S(2)}, u32[]{:S(2)}) collective-permute-start(bf16[256,1024]{1,0:T(8,128)(2,1)} %get-tuple-element.825), channel_id=1, source_target_pairs={{4,0},{8,4},{12,8},{0,12},{5,1},{9,5},{13,9},{1,13},{6,2},{10,6},{... | collective-permute-start | bytes 1572872 | tf_op jit(solution)/shard_map/ppermute | solution.py:635
  657.0 24.9 %collective-permute-start.86 = (bf16[256,1024]{1,0:T(8,128)(2,1)}, bf16[256,1024]{1,0:T(8,128)(2,1)}, u32[]{:S(2)}, u32[]{:S(2)}) collective-permute-start(bf16[256,1024]{1,0:T(8,128)(2,1)} %get-tuple-element.824), channel_id=1, source_target_pairs={{8,0},{12,4},{0,8},{4,12},{9,1},{13,5},{1,9},{5,13},{10,2},{14,6},... | collective-permute-start | bytes 1572872 | tf_op jit(solution)/shard_map/ppermute | solution.py:635
  670.3 19.7 %collective-permute-start.89 = (bf16[64,2048]{1,0:T(8,128)(2,1)}, bf16[64,2048]{1,0:T(8,128)(2,1)}, u32[]{:S(2)}, u32[]{:S(2)}) collective-permute-start(bf16[64,2048]{1,0:T(8,128)(2,1)} %broadcast_select_fusion.8), channel_id=1, source_target_pairs={{0,16},{16,0},{1,17},{17,1},{2,18},{18,2},{3,19},{19,3},{4,20},{20... | collective-permute-start | bytes 786440 | tf_op jit(solution)/shard_map/ppermute | solution.py:354
  (223 other events, 1581.5 us)
Sparse Core Ops, SparseCore 0:
  17.4 28.9 all-gather.6
  73.2 25.9 all-gather.8
  100.8 27.4 all-gather.10
  129.7 27.4 all-gather.12
  158.5 27.4 all-gather.14
  220.7 25.7 all-gather.16
  478.9 25.0 reduce-scatter.10
  506.3 25.7 reduce-scatter.8
  534.5 25.7 reduce-scatter.6
  579.1 24.8 reduce-scatter.16
  610.5 37.8 reduce-scatter.14
  685.8 26.5 reduce-scatter.12
